TPU v7x, 32 devices: a whole 2x2x4 slice. The times are simulated.
32 devices in a mesh: ctx: 8 (over z, y), wa: 4 (over x, core).
Axes of the slice: x: 2, y: 2, z: 4, core: 2. Of those that a mesh axis runs over, the one named last changes fastest.
Arguments:
- tokens: bfloat16 [4, 2048, 896], P('wa', 'ctx'), may hold values from -6 to 6
- neighbours: bfloat16 [4, 32, 2, 128, 896], P('wa', 'ctx'), may hold values from -6 to 6
- cotangent: bfloat16 [4, 2048, 896], P('wa', 'ctx'), may hold values from -6 to 6
- selfnorm: bfloat16 [896], P('wa'), may hold values from 0.099609375 to 1.8984375
- selfquery: bfloat16 [896, 1024], P('wa'), may hold values from -0.1875 to 0.1875
- selfkey: bfloat16 [896, 1024], P('wa'), may hold values from -0.1875 to 0.1875
- selfvalue: bfloat16 [896, 1024], P('wa'), may hold values from -0.1875 to 0.1875
- selfout: bfloat16 [1024, 896], P('wa'), may hold values from -1.5 to 1.5
- biastable: bfloat16 [32, 16], P('wa'), may hold values from -4 to 4
- crossnorm: bfloat16 [896], P('wa'), may hold values from 0.099609375 to 1.8984375
- crossquery: bfloat16 [896, 1024], P('wa'), may hold values from -0.1875 to 0.1875
- crosskey: bfloat16 [896, 1024], P('wa'), may hold values from -0.1875 to 0.1875
- crossvalue: bfloat16 [896, 1024], P('wa'), may hold values from -0.1875 to 0.1875
- crossout: bfloat16 [1024, 896], P('wa'), may hold values from -1.5 to 1.5
- feednorm: bfloat16 [896], P('wa'), may hold values from 0.099609375 to 1.8984375
- feedin: bfloat16 [896, 3584], P('wa'), may hold values from -0.1875 to 0.1875
- feedbias: bfloat16 [3584], P('wa'), may hold values from -3 to 3
- feedout: bfloat16 [3584, 896], P('wa'), may hold values from -0.09375 to 0.09375
- outbias: bfloat16 [896], P('wa'), may hold values from -3 to 3
Outputs:
- result: bfloat16 [4, 2048, 896], P('wa', 'ctx')
- grad_tokens: bfloat16 [4, 2048, 896], P('wa', 'ctx')
- grad_neighbours: bfloat16 [4, 32, 2, 128, 896], P('wa', 'ctx')
- grad_selfnorm: float32 [896], P('wa')
- grad_selfquery: float32 [896, 1024], P('wa')
- grad_selfkey: float32 [896, 1024], P('wa')
- grad_selfvalue: float32 [896, 1024], P('wa')
- grad_selfout: float32 [1024, 896], P('wa')
- grad_biastable: float32 [32, 16], P('wa')
- grad_crossnorm: float32 [896], P('wa')
- grad_crossquery: float32 [896, 1024], P('wa')
- grad_crosskey: float32 [896, 1024], P('wa')
- grad_crossvalue: float32 [896, 1024], P('wa')
- grad_crossout: float32 [1024, 896], P('wa')
- grad_feednorm: float32 [896], P('wa')
- grad_feedin: float32 [896, 3584], P('wa')
- grad_feedbias: float32 [3584], P('wa')
- grad_feedout: float32 [3584, 896], P('wa')
- grad_outbias: float32 [896], P('wa')
All inputs are finite; a program needn't handle non-finite values.
Results may differ from a plain program's by a relative error of at most 0.03.
Values may be sent and summed in bfloat16 or wider, within the bound.
A program may use at most 320 MiB of HBM per device.

v0:
```python
import math

import jax
import jax.numpy as jnp
from jax import lax
from jax.sharding import PartitionSpec as P

H = 16
HD = 64
NB = 32
MAXD = 128
BLOCK = 256
SPAN = 64


epsilon = 1e-06
negative = -1e30
strongest_precision = lax.Precision.HIGHEST


def passed_along(value, axis, by):
    peers = lax.axis_size(axis)
    pairs = [(i, i + by) for i in range(peers) if 0 <= i + by < peers]
    return lax.ppermute(value, axis, pairs)


def from_behind(block, axis, distance):
    devices = range(lax.axis_size(axis))
    route = [((i - distance) % len(devices), i) for i in devices]
    return lax.ppermute(block, axis, route)


def bucket_edges():
    half_count = NB // 2
    exact_part = half_count // 2
    edge_list = []
    for level_index in range(exact_part + 1, half_count):
        hits = [
            distance_now
            for distance_now in range(exact_part, MAXD + 1)
            if exact_part
            + int(
                math.log(distance_now / exact_part)
                / math.log(MAXD / exact_part)
                * (half_count - exact_part)
            )
            >= level_index
        ]
        edge_list.append(min(hits + [MAXD]))
    return (half_count, exact_part, edge_list)


def bucket_of(offset_value):
    half_count, exact_part, edge_list = bucket_edges()
    magnitude = jnp.abs(offset_value)
    far_part = exact_part + sum(
        [(magnitude >= edge_value).astype(magnitude.dtype) for edge_value in edge_list],
        jnp.zeros_like(magnitude),
    )
    return jnp.where(offset_value > 0, half_count, 0) + jnp.where(
        magnitude < exact_part, magnitude, far_part
    )


def root_norm(values, gain_vector):
    return (
        values
        * lax.rsqrt(jnp.mean(values * values, axis=-1, keepdims=True) + epsilon)
        * gain_vector
    )


def gelu_tanh(values):
    return jax.nn.gelu(values, approximate=True)


def forward_product(values, weight):
    return jnp.dot(values, weight, preferred_element_type=jnp.float32)


def outer_product(left_side, right_side):
    return lax.dot_general(
        left_side, right_side, (((0,), (0,)), ((), ())), preferred_element_type=jnp.float32
    )


def back_product(grad_low, weight):
    return lax.dot_general(
        grad_low, weight, (((1,), (1,)), ((), ())), preferred_element_type=jnp.float32
    )


def make_bias(bucket_bias_rows, row_count):
    query_place = jnp.arange(row_count)[:, None]
    key_place = jnp.arange(row_count)[None, :]
    levels = jnp.arange(NB)
    current_bucket_selector = (
        bucket_of(key_place - query_place)[None] == levels[:, None, None]
    ).astype(jnp.float32)
    previous_bucket_selector = (
        bucket_of(key_place - row_count - query_place)[None] == levels[:, None, None]
    ).astype(jnp.float32)
    onehot_far = (bucket_of(jnp.array(-MAXD, jnp.int32)) == levels).astype(jnp.float32)
    current_block_bias = jnp.einsum(
        "smz,sj->jmz", current_bucket_selector, bucket_bias_rows, precision=strongest_precision
    )
    previous_block_bias = jnp.einsum(
        "smz,sj->jmz", previous_bucket_selector, bucket_bias_rows, precision=strongest_precision
    )
    bias_far = jnp.dot(onehot_far, bucket_bias_rows, precision=strongest_precision)
    mask_same = key_place // BLOCK <= query_place // BLOCK
    return (
        (current_block_bias, previous_block_bias, bias_far, mask_same),
        (current_bucket_selector, previous_bucket_selector, onehot_far),
    )


def pair_scores(query_heads, key_heads, relation, bias_set, scale_factor):
    current_block_bias, previous_block_bias, bias_far, mask_same = bias_set
    raw_scores = jnp.einsum(
        "qhd,khd->hqk", query_heads, key_heads, preferred_element_type=jnp.float32
    )
    bias_rows = jnp.where(
        relation == 0,
        current_block_bias,
        jnp.where(relation == 1, previous_block_bias, bias_far[:, None, None]),
    )
    allowed = jnp.logical_or(relation > 0, mask_same)
    return jnp.where(allowed[None], raw_scores * scale_factor + bias_rows, negative)


def pair_core(
    query_heads,
    dout_heads,
    log_total,
    row_delta,
    key_heads,
    value_heads,
    relation,
    bias_set,
    scale_factor,
):
    scores = pair_scores(query_heads, key_heads, relation, bias_set, scale_factor)
    weights_now = jnp.exp(scores - log_total[:, :, None])
    grad_weights = jnp.einsum(
        "qhd,khd->hqk", dout_heads, value_heads, preferred_element_type=jnp.float32
    )
    dscores = weights_now * (grad_weights - row_delta[:, :, None])
    return (weights_now, dscores, (dscores * scale_factor).astype(jnp.bfloat16))


def add_tables(relative_bias_tables, dscores, relation):
    same_sum, prev_sum, far_sum = relative_bias_tables
    return (
        same_sum + jnp.where(relation == 0, dscores, 0.0),
        prev_sum + jnp.where(relation == 1, dscores, 0.0),
        far_sum + jnp.where(relation >= 2, jnp.sum(dscores, axis=(1, 2)), 0.0),
    )


def forward_fold(query_heads, position, row_count, bias_set, scale_factor, running, pieces):
    keys_all, values_all = pieces

    def one_shard(folded, shard_step):
        key_heads = lax.dynamic_slice_in_dim(
            keys_all, shard_step * row_count, row_count, 0
        ).reshape(row_count, H, HD)
        value_heads = lax.dynamic_slice_in_dim(
            values_all, shard_step * row_count, row_count, 0
        ).reshape(row_count, H, HD)
        relation = position - shard_step

        def one_compute(current):
            running_max, running_sum, running_acc = current
            scores = pair_scores(query_heads, key_heads, relation, bias_set, scale_factor)
            new_max = jnp.maximum(running_max, jnp.max(scores, axis=-1))
            factor = jnp.exp(running_max - new_max)
            weights_now = jnp.exp(scores - new_max[:, :, None])
            new_sum = running_sum * factor + jnp.sum(weights_now, axis=-1)
            update = jnp.einsum(
                "hqk,khd->qhd",
                weights_now.astype(jnp.bfloat16),
                value_heads,
                preferred_element_type=jnp.float32,
            )
            scaled = running_acc.reshape(row_count, H, HD) * factor.T[:, :, None]
            return (new_max, new_sum, (scaled + update).reshape(row_count, H * HD))

        return (lax.cond(relation >= 0, one_compute, lambda unchanged: unchanged, folded), None)

    running, unused = lax.scan(one_shard, running, jnp.arange(keys_all.shape[0] // row_count))
    return running


def per_device(
    tokens,
    neighbours,
    cotangent,
    selfnorm,
    selfquery,
    selfkey,
    selfvalue,
    selfout,
    biastable,
    crossnorm,
    crossquery,
    crosskey,
    crossvalue,
    crossout,
    feednorm,
    feedin,
    feedbias,
    feedout,
    outbias,
):
    gathered = (
        lax.all_gather(selfnorm, "wa", axis=0, tiled=True),
        lax.all_gather(selfquery, "wa", axis=0, tiled=True),
        lax.all_gather(selfkey, "wa", axis=0, tiled=True),
        lax.all_gather(selfvalue, "wa", axis=0, tiled=True),
        lax.all_gather(selfout, "wa", axis=0, tiled=True),
        lax.all_gather(biastable, "wa", axis=0, tiled=True),
        lax.all_gather(crossnorm, "wa", axis=0, tiled=True),
        lax.all_gather(crossquery, "wa", axis=0, tiled=True),
        lax.all_gather(crosskey, "wa", axis=0, tiled=True),
        lax.all_gather(crossvalue, "wa", axis=0, tiled=True),
        lax.all_gather(crossout, "wa", axis=0, tiled=True),
        lax.all_gather(feednorm, "wa", axis=0, tiled=True),
        lax.all_gather(feedin, "wa", axis=0, tiled=True),
        lax.all_gather(feedbias, "wa", axis=0, tiled=True),
        lax.all_gather(feedout, "wa", axis=0, tiled=True),
        lax.all_gather(outbias, "wa", axis=0, tiled=True),
    )
    (
        gain_self,
        proj_query,
        proj_key,
        proj_value,
        proj_out,
        bucket_table,
        gain_cross,
        cross_query,
        cross_key,
        cross_value,
        cross_out,
        gain_feed,
        feed_in,
        feed_bias,
        feed_out,
        out_bias,
    ) = gathered
    row_count = tokens.shape[1]
    model_width = tokens.shape[2]
    attn_width = proj_query.shape[1]
    cycle_size = lax.axis_size("ctx")
    position = lax.axis_index("ctx")
    scale_factor = HD ** (-0.5)
    inputs = tokens[0].astype(jnp.float32)
    bias_set, onehots = make_bias(bucket_table.astype(jnp.float32), row_count)
    normed_self, back_self = jax.vjp(root_norm, inputs, gain_self.astype(jnp.float32))
    normed_low = normed_self.astype(jnp.bfloat16)
    query_low = forward_product(normed_low, proj_query).astype(jnp.bfloat16)
    key_low = forward_product(normed_low, proj_key).astype(jnp.bfloat16)
    value_low = forward_product(normed_low, proj_value).astype(jnp.bfloat16)
    query_heads = query_low.reshape(row_count, H, HD)
    start_state = (
        jnp.full((H, row_count), negative, jnp.float32),
        jnp.zeros((H, row_count), jnp.float32),
        jnp.zeros((row_count, attn_width), jnp.float32),
    )
    running_max, running_sum, running_acc = forward_fold(
        query_heads,
        position,
        row_count,
        bias_set,
        scale_factor,
        start_state,
        (
            lax.all_gather(key_low, "ctx", axis=0, tiled=True),
            lax.all_gather(value_low, "ctx", axis=0, tiled=True),
        ),
    )
    attended = (running_acc.reshape(row_count, H, HD) / running_sum.T[:, :, None]).reshape(
        row_count, attn_width
    )
    log_total = running_max + jnp.log(running_sum)
    attended_low = attended.astype(jnp.bfloat16)
    hidden = inputs + forward_product(attended_low, proj_out)
    normed_cross, back_cross = jax.vjp(root_norm, hidden, gain_cross.astype(jnp.float32))
    cross_in = normed_cross.astype(jnp.bfloat16)
    query_cross = forward_product(cross_in, cross_query).astype(jnp.bfloat16)
    spans = neighbours.shape[1]
    neighbour_rows = neighbours.shape[2] * neighbours.shape[3]
    flat_neigh = neighbours[0].reshape(spans * neighbour_rows, model_width)
    keys_cross = (
        forward_product(flat_neigh, cross_key)
        .astype(jnp.bfloat16)
        .reshape(spans, neighbour_rows, attn_width)
    )
    values_cross = (
        forward_product(flat_neigh, cross_value)
        .astype(jnp.bfloat16)
        .reshape(spans, neighbour_rows, attn_width)
    )
    prev_key, prev_value = passed_along((keys_cross[spans - 1], values_cross[spans - 1]), "ctx", 1)
    group_keys = jnp.concatenate([prev_key[None], keys_cross], 0).reshape(
        spans + 1, neighbour_rows, H, HD
    )
    group_values = jnp.concatenate([prev_value[None], values_cross], 0).reshape(
        spans + 1, neighbour_rows, H, HD
    )
    padded = jnp.concatenate(
        [
            jnp.zeros((1, attn_width), jnp.bfloat16),
            query_cross,
            jnp.zeros((SPAN - 1, attn_width), jnp.bfloat16),
        ],
        0,
    ).reshape(spans + 1, SPAN, H, HD)
    cross_scores = (
        jnp.einsum("gqhd,gkhd->ghqk", padded, group_keys, preferred_element_type=jnp.float32)
        * scale_factor
    )
    cross_weights = jax.nn.softmax(cross_scores, axis=-1)
    cross_low = cross_weights.astype(jnp.bfloat16)
    mixed_rows = jnp.einsum(
        "ghqk,gkhd->gqhd", cross_low, group_values, preferred_element_type=jnp.float32
    ).reshape((spans + 1) * SPAN, attn_width)[1 : row_count + 1]
    keep_mask = jnp.logical_or(position > 0, jnp.arange(row_count) >= SPAN - 1).astype(jnp.float32)[
        :, None
    ]
    mixed_low = (mixed_rows * keep_mask).astype(jnp.bfloat16)
    hidden_two = hidden + forward_product(mixed_low, cross_out)
    normed_feed, back_feed = jax.vjp(root_norm, hidden_two, gain_feed.astype(jnp.float32))
    feed_low = normed_feed.astype(jnp.bfloat16)
    pre_act = forward_product(feed_low, feed_in) + feed_bias.astype(jnp.float32)
    activated, back_gelu = jax.vjp(gelu_tanh, pre_act)
    act_low = activated.astype(jnp.bfloat16)
    result = hidden_two + forward_product(act_low, feed_out) + out_bias.astype(jnp.float32)
    upstream_low = cotangent[0]
    upstream = upstream_low.astype(jnp.float32)
    grad_outbias = jnp.sum(upstream, axis=0)
    grad_feedout = outer_product(act_low, upstream_low)
    (grad_pre,) = back_gelu(back_product(upstream_low, feed_out))
    grad_feedbias = jnp.sum(grad_pre, axis=0)
    pre_low = grad_pre.astype(jnp.bfloat16)
    grad_feedin = outer_product(feed_low, pre_low)
    grad_two_part, grad_feednorm = back_feed(back_product(pre_low, feed_in))
    grad_two = upstream + grad_two_part
    two_low = grad_two.astype(jnp.bfloat16)
    grad_crossout = outer_product(mixed_low, two_low)
    grad_mixed = (back_product(two_low, cross_out) * keep_mask).astype(jnp.bfloat16)
    mixed_pad = jnp.concatenate(
        [
            jnp.zeros((1, attn_width), jnp.bfloat16),
            grad_mixed,
            jnp.zeros((SPAN - 1, attn_width), jnp.bfloat16),
        ],
        0,
    ).reshape(spans + 1, SPAN, H, HD)
    grad_cross_weights = jnp.einsum(
        "gqhd,gkhd->ghqk", mixed_pad, group_values, preferred_element_type=jnp.float32
    )
    cross_dscores = cross_weights * (
        grad_cross_weights - jnp.sum(cross_weights * grad_cross_weights, axis=-1, keepdims=True)
    )
    cross_ds_low = (cross_dscores * scale_factor).astype(jnp.bfloat16)
    grad_query_cross = (
        jnp.einsum("ghqk,gkhd->gqhd", cross_ds_low, group_keys, preferred_element_type=jnp.float32)
        .reshape((spans + 1) * SPAN, attn_width)[1 : row_count + 1]
        .astype(jnp.bfloat16)
    )
    grad_group_keys = jnp.einsum(
        "ghqk,gqhd->gkhd", cross_ds_low, padded, preferred_element_type=jnp.float32
    ).reshape(spans + 1, neighbour_rows, attn_width)
    grad_group_values = jnp.einsum(
        "ghqk,gqhd->gkhd", cross_low, mixed_pad, preferred_element_type=jnp.float32
    ).reshape(spans + 1, neighbour_rows, attn_width)
    back_key, back_value = (
        passed_along(grad_group_keys[0].astype(jnp.bfloat16), "ctx", -1).astype(jnp.float32),
        passed_along(grad_group_values[0].astype(jnp.bfloat16), "ctx", -1).astype(jnp.float32),
    )
    key_grads_low = (
        jnp.concatenate([grad_group_keys[1:spans], (grad_group_keys[spans] + back_key)[None]], 0)
        .astype(jnp.bfloat16)
        .reshape(spans * neighbour_rows, attn_width)
    )
    value_grads_low = (
        jnp.concatenate(
            [grad_group_values[1:spans], (grad_group_values[spans] + back_value)[None]], 0
        )
        .astype(jnp.bfloat16)
        .reshape(spans * neighbour_rows, attn_width)
    )
    grad_crosskey = outer_product(flat_neigh, key_grads_low)
    grad_crossvalue = outer_product(flat_neigh, value_grads_low)
    grad_neigh = (
        (back_product(key_grads_low, cross_key) + back_product(value_grads_low, cross_value))
        .astype(jnp.bfloat16)
        .reshape(neighbours.shape)
    )
    grad_crossquery = outer_product(cross_in, grad_query_cross)
    grad_hidden_part, grad_crossnorm = back_cross(back_product(grad_query_cross, cross_query))
    grad_hidden = grad_two + grad_hidden_part
    hidden_low = grad_hidden.astype(jnp.bfloat16)
    grad_selfout = outer_product(attended_low, hidden_low)
    dout_low = back_product(hidden_low, proj_out).astype(jnp.bfloat16)
    dout_heads = dout_low.reshape(row_count, H, HD)
    row_delta = jnp.sum(
        (dout_low.astype(jnp.float32) * attended).reshape(row_count, H, HD), axis=-1
    ).T
    zero_rows = jnp.zeros((row_count, attn_width), jnp.float32)
    zero_tables = (
        jnp.zeros((H, row_count, row_count), jnp.float32),
        jnp.zeros((H, row_count, row_count), jnp.float32),
        jnp.zeros((H,), jnp.float32),
    )

    def visit(folded, key_now, value_now, relation):

        def visit_compute(current):
            dquery_acc, dkey_acc, dvalue_acc, relative_bias_tables = current
            key_heads = key_now.reshape(row_count, H, HD)
            weights_now, dscores, ds_low = pair_core(
                query_heads,
                dout_heads,
                log_total,
                row_delta,
                key_heads,
                value_now.reshape(row_count, H, HD),
                relation,
                bias_set,
                scale_factor,
            )
            dquery = jnp.einsum(
                "hqk,khd->qhd", ds_low, key_heads, preferred_element_type=jnp.float32
            ).reshape(row_count, attn_width)
            dkey = jnp.einsum(
                "hqk,qhd->khd", ds_low, query_heads, preferred_element_type=jnp.float32
            ).reshape(row_count, attn_width)
            dvalue = jnp.einsum(
                "hqk,qhd->khd",
                weights_now.astype(jnp.bfloat16),
                dout_heads,
                preferred_element_type=jnp.float32,
            ).reshape(row_count, attn_width)
            return (
                dquery_acc + dquery,
                dkey_acc + dkey,
                dvalue_acc + dvalue,
                add_tables(relative_bias_tables, dscores, relation),
            )

        return lax.cond(relation >= 0, visit_compute, lambda unchanged: unchanged, folded)

    first_state = visit(
        (zero_rows, zero_rows, zero_rows, zero_tables), key_low, value_low, jnp.array(0, jnp.int32)
    )

    def cycle_step(carried, cycle_index):
        key_now, value_now, (dquery_acc, dkey_acc, dvalue_acc, relative_bias_tables) = carried
        key_next, value_next = passed_along((key_now, value_now), "ctx", 1)
        dkey_next, dvalue_next = (
            from_behind(dkey_acc.astype(jnp.bfloat16), "ctx", 1).astype(dkey_acc.dtype),
            from_behind(dvalue_acc.astype(jnp.bfloat16), "ctx", 1).astype(dvalue_acc.dtype),
        )
        relation = jnp.where(position >= cycle_index, cycle_index, -1)
        updated = visit(
            (dquery_acc, dkey_next, dvalue_next, relative_bias_tables),
            key_next,
            value_next,
            relation,
        )
        return ((key_next, value_next, updated), None)

    (
        unused_key,
        unused_value,
        (dquery_total, dkey_part, dvalue_part, relative_bias_tables),
    ), unused = lax.scan(cycle_step, (key_low, value_low, first_state), jnp.arange(1, cycle_size))
    dkey_total, dvalue_total = (
        from_behind(dkey_part.astype(jnp.bfloat16), "ctx", 1).astype(dkey_part.dtype),
        from_behind(dvalue_part.astype(jnp.bfloat16), "ctx", 1).astype(dvalue_part.dtype),
    )
    dquery_low = dquery_total.astype(jnp.bfloat16)
    dkey_low = dkey_total.astype(jnp.bfloat16)
    dvalue_low = dvalue_total.astype(jnp.bfloat16)
    grad_selfquery = outer_product(normed_low, dquery_low)
    grad_selfkey = outer_product(normed_low, dkey_low)
    grad_selfvalue = outer_product(normed_low, dvalue_low)
    grad_normed = (
        back_product(dquery_low, proj_query)
        + back_product(dkey_low, proj_key)
        + back_product(dvalue_low, proj_value)
    )
    grad_input_part, grad_selfnorm = back_self(grad_normed)
    grad_inputs = (grad_hidden + grad_input_part).astype(jnp.bfloat16)
    current_bucket_selector, previous_bucket_selector, onehot_far = onehots
    grad_biastable = (
        jnp.einsum(
            "afw,mfw->am",
            current_bucket_selector,
            relative_bias_tables[0],
            precision=strongest_precision,
        )
        + jnp.einsum(
            "afw,mfw->am",
            previous_bucket_selector,
            relative_bias_tables[1],
            precision=strongest_precision,
        )
        + onehot_far[:, None] * relative_bias_tables[2][None, :]
    )
    shares = (
        lax.psum_scatter(
            grad_selfnorm.astype(jnp.bfloat16), "wa", scatter_dimension=0, tiled=True
        ).astype(jnp.float32),
        lax.psum_scatter(
            grad_selfquery.astype(jnp.bfloat16), "wa", scatter_dimension=0, tiled=True
        ).astype(jnp.float32),
        lax.psum_scatter(
            grad_selfkey.astype(jnp.bfloat16), "wa", scatter_dimension=0, tiled=True
        ).astype(jnp.float32),
        lax.psum_scatter(
            grad_selfvalue.astype(jnp.bfloat16), "wa", scatter_dimension=0, tiled=True
        ).astype(jnp.float32),
        lax.psum_scatter(
            grad_selfout.astype(jnp.bfloat16), "wa", scatter_dimension=0, tiled=True
        ).astype(jnp.float32),
        lax.psum_scatter(
            grad_biastable.astype(jnp.bfloat16), "wa", scatter_dimension=0, tiled=True
        ).astype(jnp.float32),
        lax.psum_scatter(
            grad_crossnorm.astype(jnp.bfloat16), "wa", scatter_dimension=0, tiled=True
        ).astype(jnp.float32),
        lax.psum_scatter(
            grad_crossquery.astype(jnp.bfloat16), "wa", scatter_dimension=0, tiled=True
        ).astype(jnp.float32),
        lax.psum_scatter(
            grad_crosskey.astype(jnp.bfloat16), "wa", scatter_dimension=0, tiled=True
        ).astype(jnp.float32),
        lax.psum_scatter(
            grad_crossvalue.astype(jnp.bfloat16), "wa", scatter_dimension=0, tiled=True
        ).astype(jnp.float32),
        lax.psum_scatter(
            grad_crossout.astype(jnp.bfloat16), "wa", scatter_dimension=0, tiled=True
        ).astype(jnp.float32),
        lax.psum_scatter(
            grad_feednorm.astype(jnp.bfloat16), "wa", scatter_dimension=0, tiled=True
        ).astype(jnp.float32),
        lax.psum_scatter(
            grad_feedin.astype(jnp.bfloat16), "wa", scatter_dimension=0, tiled=True
        ).astype(jnp.float32),
        lax.psum_scatter(
            grad_feedbias.astype(jnp.bfloat16), "wa", scatter_dimension=0, tiled=True
        ).astype(jnp.float32),
        lax.psum_scatter(
            grad_feedout.astype(jnp.bfloat16), "wa", scatter_dimension=0, tiled=True
        ).astype(jnp.float32),
        lax.psum_scatter(
            grad_outbias.astype(jnp.bfloat16), "wa", scatter_dimension=0, tiled=True
        ).astype(jnp.float32),
    )
    totals = lax.psum(
        (
            shares[0],
            shares[1],
            shares[2],
            shares[3],
            shares[4],
            shares[5],
            shares[6],
            shares[7],
            shares[8],
            shares[9],
            shares[10],
            shares[11],
            shares[12],
            shares[13],
            shares[14],
            shares[15],
        ),
        "ctx",
    )
    return (
        result.astype(jnp.bfloat16)[None],
        grad_inputs[None],
        grad_neigh,
        totals[0],
        totals[1],
        totals[2],
        totals[3],
        totals[4],
        totals[5],
        totals[6],
        totals[7],
        totals[8],
        totals[9],
        totals[10],
        totals[11],
        totals[12],
        totals[13],
        totals[14],
        totals[15],
    )


def solution(mesh):
    return jax.shard_map(
        per_device,
        mesh=mesh,
        in_specs=(
            P("wa", "ctx", None),
            P("wa", "ctx", None, None, None),
            P("wa", "ctx", None),
            P("wa"),
            P("wa", None),
            P("wa", None),
            P("wa", None),
            P("wa", None),
            P("wa", None),
            P("wa"),
            P("wa", None),
            P("wa", None),
            P("wa", None),
            P("wa", None),
            P("wa"),
            P("wa", None),
            P("wa"),
            P("wa", None),
            P("wa"),
        ),
        out_specs=(
            P("wa", "ctx", None),
            P("wa", "ctx", None),
            P("wa", "ctx", None, None, None),
            P("wa"),
            P("wa", None),
            P("wa", None),
            P("wa", None),
            P("wa", None),
            P("wa", None),
            P("wa"),
            P("wa", None),
            P("wa", None),
            P("wa", None),
            P("wa", None),
            P("wa"),
            P("wa", None),
            P("wa"),
            P("wa", None),
            P("wa"),
        ),
        check_vma=False,
    )
```

profile of v0, /device:TPU:0, one launch (start us, length us, event | category | flops | bytes accessed | tf_op | source)
XLA Modules:
  0.0 1900.5 jit_solution(16746649579186559239)
XLA Ops:
  36.9 19.6 %all-gather.14.cloned.1.call-done = bf16[896,1024]{1,0:T(8,128)(2,1)} async-done(((bf16[224,1024]{1,0:T(8,128)(2,1)}), bf16[896,1024]{1,0:T(8,128)(2,1)}) %all-gather.14.cloned.1.call-update) | async-done | bytes 1835024 | tf_op jit(solution)/shard_map/all_gather | solution.py:219
  90.0 11.9 all-gather.30.cloned.1.call-done
  154.8 45.6 %all-gather.22.cloned.1.call-done = bf16[2048,1024]{1,0:T(8,128)(2,1)} async-done(((bf16[256,1024]{1,0:T(8,128)(2,1)}), bf16[2048,1024]{1,0:T(8,128)(2,1)}) %all-gather.22.cloned.1.call-update) | async-done | bytes 4194320 | tf_op jit(solution)/shard_map/all_gather | solution.py:280
  207.0 67.9 %all-gather.16.cloned.1.call-done = bf16[2048,1024]{1,0:T(8,128)(2,1)} async-done(((bf16[256,1024]{1,0:T(8,128)(2,1)}), bf16[2048,1024]{1,0:T(8,128)(2,1)}) %all-gather.16.cloned.1.call-update) | async-done | bytes 4194320 | tf_op jit(solution)/shard_map/all_gather | solution.py:279
  281.4 17.6 while.40
  309.0 9.5 all-gather.28.cloned.1.call-done
  334.4 15.4 convolution_bitcast_fusion.1
  360.4 29.4 %all-gather.34.cloned.1.call-done = bf16[896,3584]{1,0:T(8,128)(2,1)} async-done(((bf16[224,3584]{1,0:T(8,128)(2,1)}), bf16[896,3584]{1,0:T(8,128)(2,1)}) %all-gather.34.cloned.1.call-update) | async-done | bytes 6422544 | tf_op jit(solution)/shard_map/all_gather | solution.py:229
  396.9 41.5 %all-gather.36.cloned.1.call-done = bf16[3584,896]{1,0:T(8,128)(2,1)} async-done(((bf16[896,896]{1,0:T(8,128)(2,1)}), bf16[3584,896]{1,0:T(8,128)(2,1)}) %all-gather.36.cloned.1.call-update) | async-done | bytes 6422544 | tf_op jit(solution)/shard_map/all_gather | solution.py:231
  467.6 33.7 %fusion.78 = bf16[5,64,16,64]{1,3,2,0:T(8,128)(2,1)} fusion(f32[5,16,64,256]{3,2,1,0:T(8,128)} %fusion.74, bf16[4,256,16,64]{1,3,2,0:T(8,128)(2,1)} %copy.138, bf16[1,256,16,64]{1,3,2,0:T(8,128)(2,1)} %bitcast.222, f32[5,16,64,256]{3,2,1,0:T(8,128)} %get-tuple-element.793, f32[5,16,64]{2,1,0:T(8,128)S(1)} %get-tuple-element.792), kind=kOutput, calls=%fused_computation.114 | convolution fusion | flops 178590976 | bytes 13783040 | tf_op jit(solution)/shard_map/ghqk,gkhd->gqhd/dot_general | solution.py:369
  564.0 424.9 %while.41 = (s32[]{:T(128)}, bf16[256,1024]{0,1:T(8,128)(2,1)}, bf16[256,1024]{0,1:T(8,128)(2,1)}, f32[256,1024]{0,1:T(8,128)}, f32[256,1024]{0,1:T(8,128)S(1)},...) while((s32[]{:T(128)}, bf16[256,1024]{0,1:T(8,128)(2,1)}, ...), condition=%wide.region_19.20_spmd.clone, body=%wide.region_15.19_spmd.clone.sunk | while | flops 691929088 | bytes 169512192 | solution.py:480
  583.8 9.5 collective-permute-done.3
  601.3 10.6 collective-permute-done
  616.5 17.8 collective-permute-start.2
  669.4 9.7 collective-permute-done
  688.3 17.9 collective-permute-start.3
  758.1 16.9 collective-permute-start.1
  826.0 20.0 %collective-permute-start = (bf16[256,1024]{0,1:T(8,128)(2,1)}, bf16[256,1024]{0,1:T(8,128)(2,1)}, u32[]{:S(2)}, u32[]{:S(2)}) collective-permute-start(bf16[256,1024]{0,1:T(8,128)(2,1)} %get-tuple-element.1107), channel_id=1, source_target_pairs={{0,4},{4,8},{8,12},{12,16},{16,20},{20,24},{24,28},{1,5},{5,9},{9,... | collective-permute-start | bytes 1572872 | tf_op jit(solution)/shard_map/while/body/eval_jaxpr/ppermute | solution.py:24
  868.9 9.6 collective-permute-start.3
  878.6 12.1 collective-permute-start.1
  897.9 15.5 collective-permute-done.2
  933.8 11.0 collective-permute-start.1
  944.7 11.4 collective-permute-start
  958.0 19.3 %collective-permute-done.2 = bf16[256,1024]{0,1:T(8,128)(2,1)} collective-permute-done((bf16[256,1024]{0,1:T(8,128)(2,1)}, bf16[256,1024]{0,1:T(8,128)(2,1)}, u32[]{:S(2)}, u32[]{:S(2)}) %collective-permute-start.2) | collective-permute-done | bytes 524320 | tf_op jit(solution)/shard_map/while/body/eval_jaxpr/ppermute | solution.py:30
  992.4 15.8 convolution_bitcast_fusion
  1034.4 34.2 %fusion.62 = f32[5,256,16,64]{1,3,2,0:T(8,128)} fusion(bf16[5,64,16,64]{1,3,2,0:T(8,128)(2,1)} %copy.159, f32[5,16,64,256]{3,2,1,0:T(8,128)} %fusion.74, f32[5,16,64,256]{3,2,1,0:T(8,128)} %get-tuple-element.793, f32[5,16,64]{2,1,0:T(8,128)S(1)} %copy-done.58), kind=kOutput, calls=%fused_computation.86 | convolution fusion | flops 176952576 | bytes 16404480 | tf_op jit(solution)/shard_map/ghqk,gqhd->gkhd/dot_general | solution.py:373
  1099.5 41.1 %collective-permute-done.7 = bf16[256,1024]{0,1:T(8,128)(2,1)S(1)} collective-permute-done((bf16[256,1024]{0,1:T(8,128)(2,1)S(1)}, bf16[256,1024]{0,1:T(8,128)(2,1)S(1)}, u32[]{:S(2)}, u32[]{:S(2)}) %collective-permute-start.7) | collective-permute-done | bytes 524320 | tf_op jit(solution)/shard_map/ppermute | solution.py:30
  1143.6 11.9 collective-permute-done.6
  1194.9 10.9 all-reduce.11
  1222.5 61.9 %reduce-scatter.29.cloned.1.call-done = bf16[896,896]{1,0:T(8,128)(2,1)} async-done(((bf16[3584,896]{1,0:T(8,128)(2,1)}), bf16[896,896]{1,0:T(8,128)(2,1)}) %reduce-scatter.29.cloned.1.call-update) | async-done | bytes 1605648 | tf_op jit(solution)/shard_map/reduce_scatter | solution.py:557
  1284.4 62.0 %reduce-scatter.27.cloned.1.call-done = bf16[224,3584]{1,0:T(8,128)(2,1)} async-done(((bf16[896,3584]{1,0:T(8,128)(2,1)}), bf16[224,3584]{1,0:T(8,128)(2,1)}) %reduce-scatter.27.cloned.1.call-update) | async-done | bytes 1605648 | tf_op jit(solution)/shard_map/reduce_scatter | solution.py:551
  1346.4 542.1 %all-reduce.14 = (f32[224]{0:T(256)}, f32[224,1024]{1,0:T(8,128)}, f32[224,1024]{1,0:T(8,128)}, f32[224,1024]{1,0:T(8,128)}, f32[256,896]{1,0:T(8,128)}, /*index...) all-reduce(f32[224]{0:T(256)S(1)} %get-tuple-element.806, ...), channel_id=1, replica_groups=mesh['ctx'=8,'wa'=4] {'ctx'}, use_global_device_ids=true, to_apply=%region_23.24 | all-reduce | flops 3442560 | bytes 20659200 | tf_op jit(solution)/shard_map/psum | solution.py:564
  (482 shorter events, 638.8 us)
Async XLA Ops:
  8.0 48.5 %all-gather.14.cloned.1.call-start = ((), (), s32[]{:S(2)}) async-start(), calls=%async_computation.10 | async-start | bytes 2293760 | tf_op jit(solution)/shard_map/all_gather | solution.py:219
  8.7 72.7 %all-gather.26.cloned.1.call-start = ((), (), s32[]{:S(2)}) async-start(), calls=%async_computation.16 | async-start | bytes 2293760 | tf_op jit(solution)/shard_map/all_gather | solution.py:226
  9.4 92.4 %all-gather.30.cloned.1.call-start = ((), (), s32[]{:S(2)}) async-start(), calls=%async_computation.18 | async-start | bytes 2293760 | tf_op jit(solution)/shard_map/all_gather | solution.py:225
  10.0 125.8 %all-gather.18.cloned.1.call-start = ((), (), s32[]{:S(2)}) async-start(), calls=%async_computation.12 | async-start | bytes 2293760 | tf_op jit(solution)/shard_map/all_gather | solution.py:218
  10.6 189.8 %all-gather.22.cloned.1.call-start = ((), (), s32[]{:S(2)}) async-start(), calls=%async_computation.14 | async-start | bytes 4718592 | tf_op jit(solution)/shard_map/all_gather | solution.py:280
  36.8 238.0 %all-gather.16.cloned.1.call-start = ((), (), s32[]{:S(2)}) async-start(), calls=%async_computation.11 | async-start | bytes 4718592 | tf_op jit(solution)/shard_map/all_gather | solution.py:279
  59.6 246.7 %all-gather.24.cloned.1.call-start = ((), (), s32[]{:S(2)}) async-start(), calls=%async_computation.15 | async-start | bytes 2293760 | tf_op jit(solution)/shard_map/all_gather | solution.py:221
  60.3 258.2 %all-gather.28.cloned.1.call-start = ((), (), s32[]{:S(2)}) async-start(), calls=%async_computation.17 | async-start | bytes 2293760 | tf_op jit(solution)/shard_map/all_gather | solution.py:224
  61.1 295.8 %all-gather.32.cloned.1.call-start = ((), (), s32[]{:S(2)}) async-start(), calls=%async_computation.19 | async-start | bytes 2293760 | tf_op jit(solution)/shard_map/all_gather | solution.py:227
  61.7 328.2 %all-gather.34.cloned.1.call-start = ((), (), s32[]{:S(2)}) async-start(), calls=%async_computation.20 | async-start | bytes 8028160 | tf_op jit(solution)/shard_map/all_gather | solution.py:229
  62.4 376.0 %all-gather.36.cloned.1.call-start = ((), (), s32[]{:S(2)}) async-start(), calls=%async_computation.21 | async-start | bytes 8028160 | tf_op jit(solution)/shard_map/all_gather | solution.py:231
  63.0 1157.0 %reduce-scatter.25.cloned.1.call-start = ((), (), s32[]{:S(2)}) async-start(), calls=%async_computation.27 | async-start | bytes 2293760 | tf_op jit(solution)/shard_map/reduce_scatter | solution.py:545
  86.6 65.2 %collective-permute-start.4 = (bf16[256,1024]{1,0:T(8,128)(2,1)S(1)}, bf16[256,1024]{1,0:T(8,128)(2,1)S(1)}, u32[]{:S(2)}, u32[]{:S(2)}) collective-permute-start(bf16[256,1024]{1,0:T(8,128)(2,1)S(1)} %slice.57), channel_id=1, source_target_pairs={{0,4},{4,8},{8,12},{12,16},{16,20},{20,24},{24,28},{1,5},{5,9},{9,... | collective-permute-start | bytes 1572872 | tf_op jit(solution)/shard_map/ppermute | solution.py:24
  107.8 44.9 %collective-permute-start.5 = (bf16[256,1024]{1,0:T(8,128)(2,1)}, bf16[256,1024]{1,0:T(8,128)(2,1)}, u32[]{:S(2)}, u32[]{:S(2)}) collective-permute-start(bf16[256,1024]{1,0:T(8,128)(2,1)} %slice.58), channel_id=1, source_target_pairs={{0,4},{4,8},{8,12},{12,16},{16,20},{20,24},{24,28},{1,5},{5,9},{9,... | collective-permute-start | bytes 1572872 | tf_op jit(solution)/shard_map/ppermute | solution.py:24
  453.1 766.9 %reduce-scatter.23.cloned.1.call-start = ((), (), s32[]{:S(2)}) async-start(), calls=%async_computation.26 | async-start | bytes 2293760 | tf_op jit(solution)/shard_map/reduce_scatter | solution.py:536
  509.8 710.1 %reduce-scatter.21.cloned.1.call-start = ((), (), s32[]{:S(2)}) async-start(), calls=%async_computation.25 | async-start | bytes 2293760 | tf_op jit(solution)/shard_map/reduce_scatter | solution.py:527
  526.0 694.0 %reduce-scatter.15.cloned.1.call-start = ((), (), s32[]{:S(2)}) async-start(), calls=%async_computation.22 | async-start | bytes 2293760 | tf_op jit(solution)/shard_map/reduce_scatter | solution.py:518
  800.2 48.4 %collective-permute-start.2 = (bf16[256,1024]{0,1:T(8,128)(2,1)}, bf16[256,1024]{0,1:T(8,128)(2,1)}, u32[]{:S(2)}, u32[]{:S(2)}) collective-permute-start(bf16[256,1024]{0,1:T(8,128)(2,1)} %convert_element_type.668), channel_id=1, source_target_pairs={{28,0},{0,4},{4,8},{8,12},{12,16},{16,20},{20,24},{24,28},{29,1},{... | collective-permute-start | bytes 1572872 | tf_op jit(solution)/shard_map/while/body/eval_jaxpr/ppermute | solution.py:30
  810.6 45.6 %collective-permute-start.3 = (bf16[256,1024]{0,1:T(8,128)(2,1)}, bf16[256,1024]{0,1:T(8,128)(2,1)}, u32[]{:S(2)}, u32[]{:S(2)}) collective-permute-start(bf16[256,1024]{0,1:T(8,128)(2,1)} %convert_element_type.670), channel_id=1, source_target_pairs={{28,0},{0,4},{4,8},{8,12},{12,16},{16,20},{20,24},{24,28},{29,1},{... | collective-permute-start | bytes 1572872 | tf_op jit(solution)/shard_map/while/body/eval_jaxpr/ppermute | solution.py:30
  862.9 50.5 %collective-permute-start.2 = (bf16[256,1024]{0,1:T(8,128)(2,1)}, bf16[256,1024]{0,1:T(8,128)(2,1)}, u32[]{:S(2)}, u32[]{:S(2)}) collective-permute-start(bf16[256,1024]{0,1:T(8,128)(2,1)} %convert_element_type.668), channel_id=1, source_target_pairs={{28,0},{0,4},{4,8},{8,12},{12,16},{16,20},{20,24},{24,28},{29,1},{... | collective-permute-start | bytes 1572872 | tf_op jit(solution)/shard_map/while/body/eval_jaxpr/ppermute | solution.py:30
  868.9 51.1 %collective-permute-start.3 = (bf16[256,1024]{0,1:T(8,128)(2,1)}, bf16[256,1024]{0,1:T(8,128)(2,1)}, u32[]{:S(2)}, u32[]{:S(2)}) collective-permute-start(bf16[256,1024]{0,1:T(8,128)(2,1)} %convert_element_type.670), channel_id=1, source_target_pairs={{28,0},{0,4},{4,8},{8,12},{12,16},{16,20},{20,24},{24,28},{29,1},{... | collective-permute-start | bytes 1572872 | tf_op jit(solution)/shard_map/while/body/eval_jaxpr/ppermute | solution.py:30
  878.6 43.6 %collective-permute-start.1 = (bf16[256,1024]{0,1:T(8,128)(2,1)}, bf16[256,1024]{0,1:T(8,128)(2,1)}, u32[]{:S(2)}, u32[]{:S(2)}) collective-permute-start(bf16[256,1024]{0,1:T(8,128)(2,1)} %get-tuple-element.1108), channel_id=1, source_target_pairs={{0,4},{4,8},{8,12},{12,16},{16,20},{20,24},{24,28},{1,5},{5,9},{9,... | collective-permute-start | bytes 1572872 | tf_op jit(solution)/shard_map/while/body/eval_jaxpr/ppermute | solution.py:24
  926.7 50.5 %collective-permute-start.2 = (bf16[256,1024]{0,1:T(8,128)(2,1)}, bf16[256,1024]{0,1:T(8,128)(2,1)}, u32[]{:S(2)}, u32[]{:S(2)}) collective-permute-start(bf16[256,1024]{0,1:T(8,128)(2,1)} %convert_element_type.668), channel_id=1, source_target_pairs={{28,0},{0,4},{4,8},{8,12},{12,16},{16,20},{20,24},{24,28},{29,1},{... | collective-permute-start | bytes 1572872 | tf_op jit(solution)/shard_map/while/body/eval_jaxpr/ppermute | solution.py:30
  928.8 54.1 %collective-permute-start.3 = (bf16[256,1024]{0,1:T(8,128)(2,1)}, bf16[256,1024]{0,1:T(8,128)(2,1)}, u32[]{:S(2)}, u32[]{:S(2)}) collective-permute-start(bf16[256,1024]{0,1:T(8,128)(2,1)} %convert_element_type.670), channel_id=1, source_target_pairs={{28,0},{0,4},{4,8},{8,12},{12,16},{16,20},{20,24},{24,28},{29,1},{... | collective-permute-start | bytes 1572872 | tf_op jit(solution)/shard_map/while/body/eval_jaxpr/ppermute | solution.py:30
  933.8 51.3 %collective-permute-start.1 = (bf16[256,1024]{0,1:T(8,128)(2,1)}, bf16[256,1024]{0,1:T(8,128)(2,1)}, u32[]{:S(2)}, u32[]{:S(2)}) collective-permute-start(bf16[256,1024]{0,1:T(8,128)(2,1)} %get-tuple-element.1108), channel_id=1, source_target_pairs={{0,4},{4,8},{8,12},{12,16},{16,20},{20,24},{24,28},{1,5},{5,9},{9,... | collective-permute-start | bytes 1572872 | tf_op jit(solution)/shard_map/while/body/eval_jaxpr/ppermute | solution.py:24
  992.4 227.6 %reduce-scatter.33.cloned.1.call-start = ((), (), s32[]{:S(2)}) async-start(), calls=%async_computation.31 | async-start | bytes 2293760
  1034.3 186.9 %reduce-scatter.31.cloned.1.call-start = ((), (), s32[]{:S(2)}) async-start(), calls=%async_computation.30 | async-start | bytes 2293760
  1095.1 127.4 %reduce-scatter.19.cloned.1.call-start = ((), (), s32[]{:S(2)}) async-start(), calls=%async_computation.24 | async-start | bytes 2293760 | tf_op jit(solution)/shard_map/reduce_scatter | solution.py:524
  1096.4 44.1 %collective-permute-start.7 = (bf16[256,1024]{0,1:T(8,128)(2,1)S(1)}, bf16[256,1024]{0,1:T(8,128)(2,1)S(1)}, u32[]{:S(2)}, u32[]{:S(2)}) collective-permute-start(bf16[256,1024]{0,1:T(8,128)(2,1)S(1)} %convert_element_type.477), channel_id=1, source_target_pairs={{28,0},{0,4},{4,8},{8,12},{12,16},{16,20},{20,24},{24,28},{29,1},{... | collective-permute-start | bytes 1572872 | tf_op jit(solution)/shard_map/ppermute | solution.py:30
  1143.4 79.1 %reduce-scatter.17.cloned.1.call-start = ((), (), s32[]{:S(2)}) async-start(), calls=%async_computation.23 | async-start | bytes 2293760 | tf_op jit(solution)/shard_map/reduce_scatter | solution.py:521
  1158.3 126.1 %reduce-scatter.29.cloned.1.call-start = ((), (), s32[]{:S(2)}) async-start(), calls=%async_computation.29 | async-start | bytes 8028160 | tf_op jit(solution)/shard_map/reduce_scatter | solution.py:557
  1165.8 180.6 %reduce-scatter.27.cloned.1.call-start = ((), (), s32[]{:S(2)}) async-start(), calls=%async_computation.28 | async-start | bytes 8028160 | tf_op jit(solution)/shard_map/reduce_scatter | solution.py:551
  (91 other events, 2834.7 us)
Sparse Core Ops, SparseCore 0:
  9.6 23.8 all-gather.19
  35.1 21.3 all-gather.13
  58.0 21.1 all-gather.25
  80.7 21.1 all-gather.29
  103.3 21.1 all-gather.17
  127.0 73.4 all-gather.21
  203.1 71.6 all-gather.15
  276.4 19.3 all-gather.23
  297.4 21.1 all-gather.27
  319.9 21.1 all-gather.31
  342.7 47.1 all-gather.33
  391.3 47.1 all-gather.35
  453.2 29.8 reduce-scatter.24
  509.9 29.8 reduce-scatter.22
  542.2 29.8 reduce-scatter.20
  992.5 62.9 reduce-scatter.14
  1057.9 39.5 reduce-scatter.32
  1100.0 57.6 reduce-scatter.30
  1160.3 29.8 reduce-scatter.18
  1192.7 29.7 reduce-scatter.16
  1225.1 59.2 reduce-scatter.28
  1287.1 59.2 reduce-scatter.26
where the time goes:
time: 1910 us; the launch traced here: 1900 us
  blocking collectives  572 us (30%)
  waiting for transfers between devices  556 us (29%)
  matrix products  247 us (13%)
  starting transfers between devices  218 us (11%)
  local copies, waits for them, and re-layouts  201 us (11%)
  other arithmetic  73.1 us (4%)
    psum x1, blocking collectives, per_device(): lax.psum((shares[0], shares[1], shares[2], shares[3], shares[4], shares[5...  542 us
    ppermute x16, waiting for transfers between devices, from_behind(): return lax.ppermute(block, axis, route)  146 us
    ppermute x18, starting transfers between devices, passed_along(): return lax.ppermute(value, axis, pairs)  121 us
    ppermute x16, starting transfers between devices, from_behind(): return lax.ppermute(block, axis, route)  95.6 us
    unnamed x159, local copies, waits for them, and re-layouts  73.7 us
    all_gather x1, waiting for transfers between devices, per_device(): lax.all_gather(key_low, 'ctx', axis=0, tiled=True)  67.9 us
    reduce_scatter x1, waiting for transfers between devices, per_device(): lax.psum_scatter(grad_feedin.astype(jnp.bfloat16), 'wa', scatter_dimensio...  62 us
    reduce_scatter x1, waiting for transfers between devices, per_device(): lax.psum_scatter(grad_feedout.astype(jnp.bfloat16), 'wa', scatter_dimensi...  61.9 us
  transfers between devices with their start and end apart: 56, of which 33 were waited for; matrix products, arithmetic and copies ran while one was open for 26% of the time, Pallas kernels for 0%

commit v1 on v0

--- a/solution.py
+++ b/solution.py
@@ -1,8 +1,11 @@
+import functools
 import math
 
 import jax
 import jax.numpy as jnp
 from jax import lax
+from jax.experimental import pallas as pl
+from jax.experimental.pallas import tpu as pltpu
 from jax.sharding import PartitionSpec as P
 
 H = 16
@@ -11,6 +14,11 @@
 MAXD = 128
 BLOCK = 256
 SPAN = 64
+MESH = pl.DeviceIdType.MESH
+WIDE = 128
+LINE = 1024
+BF = jnp.bfloat16
+F32 = jnp.float32
 
 
 epsilon = 1e-06
@@ -190,6 +198,531 @@
 
     running, unused = lax.scan(one_shard, running, jnp.arange(keys_all.shape[0] // row_count))
     return running
+
+
+def nt_dot(left, right):
+    return lax.dot_general(left, right, (((1,), (1,)), ((), ())), preferred_element_type=F32)
+
+
+def nn_dot(left, right):
+    return jnp.dot(left, right, preferred_element_type=F32)
+
+
+def greet(axis, count):
+    me = lax.axis_index(axis)
+    barrier = pltpu.get_barrier_semaphore()
+    for d in range(1, count):
+        pl.semaphore_signal(
+            barrier, inc=1, device_id={axis: lax.rem(me + d, count)}, device_id_type=MESH
+        )
+    pl.semaphore_wait(barrier, count - 1)
+    return me
+
+
+def lanes_of(index):
+    return pl.ds(pl.multiple_of(index * WIDE, WIDE), WIDE)
+
+
+def rows_of(index, rows):
+    return pl.ds(pl.multiple_of(index * rows, rows), rows)
+
+
+def to_ctx(src, dst, send_sem, recv_sem, target):
+    return pltpu.make_async_remote_copy(
+        src_ref=src,
+        dst_ref=dst,
+        send_sem=send_sem,
+        recv_sem=recv_sem,
+        device_id={"ctx": target},
+        device_id_type=MESH,
+    )
+
+
+def head_mask(h, rows):
+    lane = lax.broadcasted_iota(jnp.int32, (rows, WIDE), 1)
+    return (lane < HD) if h == 0 else (lane >= HD)
+
+
+def bias_tiles(bias_ref, me, tiles):
+    for h in range(2):
+        line = bias_ref[pl.ds(2 * me + h, 1), :]
+        rolled = pltpu.roll(
+            jnp.broadcast_to(line, (BLOCK, LINE)), 0, 1, stride=1, stride_axis=0
+        )
+        tiles[h, 0] = rolled[:, :BLOCK]
+        tiles[h, 1] = rolled[:, BLOCK : 2 * BLOCK]
+
+
+def spread(n, me, pairs, send, recv):
+    for d in range(1, n):
+        peer = lax.rem(me + d, n)
+        for t, (src, dst) in enumerate(pairs):
+            to_ctx(
+                src.at[:, lanes_of(peer)],
+                dst.at[rows_of(me, BLOCK)],
+                send.at[t, d],
+                recv.at[t, d],
+                peer,
+            ).start()
+    for src, dst in pairs:
+        dst[rows_of(me, BLOCK), :] = src[:, lanes_of(me)]
+
+
+def attn_forward_kernel(
+    n, q_ref, k_ref, v_ref, bias_ref, o_ref, qh_out, kh_out, vh_out, ot_out, lse_out,
+    qh, kh, vh, vt, oh, land, tiles, acc, stat, send, recv, osend, orecv,
+):
+    me = greet("ctx", n)
+    pairs = ((q_ref, qh), (k_ref, kh), (v_ref, vh))
+    spread(n, me, pairs, send, recv)
+    bias_tiles(bias_ref, me, tiles)
+
+    def arrive(i):
+        @pl.when(i != me)
+        def _():
+            d = lax.rem(me - i + n, n)
+            for t, (src, dst) in enumerate(pairs):
+                to_ctx(
+                    src.at[:, lanes_of(i)], dst.at[rows_of(i, BLOCK)], send.at[t, d], recv.at[t, d], i
+                ).wait_recv()
+
+    def query_block(i, unused):
+        arrive(i)
+        rows = rows_of(i, BLOCK)
+        vt[:, rows] = vh[rows, :].astype(F32).T.astype(BF)
+        q_now = qh[rows, :] * BF(HD**-0.5)
+        masked = [jnp.where(head_mask(h, BLOCK), q_now, BF(0)) for h in range(2)]
+
+        def fold(j, which, first):
+            keys = kh[rows_of(j, BLOCK), :]
+            for h in range(2):
+                scores = nt_dot(keys, masked[h])
+                if which is None:
+                    scores = scores + bias_ref[pl.ds(2 * me + h, 1), WIDE : WIDE + BLOCK]
+                else:
+                    scores = scores + tiles[h, which]
+                top = jnp.max(scores, axis=0, keepdims=True)
+                if not first:
+                    old = stat[h : h + 1, :]
+                    top = jnp.maximum(old, top)
+                weights = jnp.exp(scores - top)
+                total = jnp.sum(weights, axis=0, keepdims=True)
+                vals = vt[h * HD : (h + 1) * HD, rows_of(j, BLOCK)]
+                mixed = nn_dot(vals, weights.astype(BF))
+                if not first:
+                    factor = jnp.exp(old - top)
+                    total = total + stat[2 + h : 3 + h, :] * factor
+                    mixed = mixed + acc[h * HD : (h + 1) * HD, :] * factor
+                stat[h : h + 1, :] = top
+                stat[2 + h : 3 + h, :] = total
+                acc[h * HD : (h + 1) * HD, :] = mixed
+
+        fold(i, 0, True)
+
+        @pl.when(i >= 1)
+        def _():
+            fold(i - 1, 1, False)
+
+        def far(j, unused):
+            fold(j, None, False)
+            return unused
+
+        lax.fori_loop(0, i - 1, far, 0)
+        for h in range(2):
+            total = stat[2 + h : 3 + h, :]
+            part = acc[h * HD : (h + 1) * HD, :] / total
+            acc[h * HD : (h + 1) * HD, :] = part
+            lse_out[h : h + 1, rows] = stat[h : h + 1, :] + jnp.log(total)
+        done = acc[...]
+        ot_out[:, rows] = done
+        oh[rows, :] = done.T.astype(BF)
+
+        @pl.when(i != me)
+        def _():
+            d = lax.rem(i - me + n, n)
+            to_ctx(oh.at[rows], land.at[:, lanes_of(me)], osend.at[d], orecv.at[d], i).start()
+
+        @pl.when(i == me)
+        def _():
+            land[:, lanes_of(me)] = oh[rows, :]
+
+        return unused
+
+    lax.fori_loop(0, n, query_block, 0)
+    qh_out[...] = qh[...]
+    kh_out[...] = kh[...]
+    vh_out[...] = vh[...]
+    for d in range(1, n):
+        peer = lax.rem(me + d, n)
+        for t, (src, dst) in enumerate(pairs):
+            to_ctx(
+                src.at[:, lanes_of(peer)], dst.at[rows_of(me, BLOCK)], send.at[t, d], recv.at[t, d], peer
+            ).wait_send()
+        back = to_ctx(
+            oh.at[rows_of(peer, BLOCK)], land.at[:, lanes_of(me)], osend.at[d], orecv.at[d], peer
+        )
+        back.wait_send()
+        back.wait_recv()
+    o_ref[...] = land[...]
+
+
+def vmem(count):
+    return [pl.BlockSpec(memory_space=pltpu.VMEM)] * count
+
+
+def attn_forward(n, query, key, value, bias_lines):
+    rows, seq = query.shape[0], n * query.shape[0]
+    heads = jax.ShapeDtypeStruct((seq, WIDE), BF)
+    return pl.pallas_call(
+        functools.partial(attn_forward_kernel, n),
+        out_shape=(
+            jax.ShapeDtypeStruct(query.shape, BF),
+            heads,
+            heads,
+            heads,
+            jax.ShapeDtypeStruct((WIDE, seq), F32),
+            jax.ShapeDtypeStruct((8, seq), F32),
+        ),
+        in_specs=vmem(4),
+        out_specs=tuple(vmem(6)),
+        scratch_shapes=[
+            pltpu.VMEM((seq, WIDE), BF),
+            pltpu.VMEM((seq, WIDE), BF),
+            pltpu.VMEM((seq, WIDE), BF),
+            pltpu.VMEM((WIDE, seq), BF),
+            pltpu.VMEM((seq, WIDE), BF),
+            pltpu.VMEM(query.shape, BF),
+            pltpu.VMEM((2, 2, BLOCK, BLOCK), F32),
+            pltpu.VMEM((WIDE, BLOCK), F32),
+            pltpu.VMEM((8, BLOCK), F32),
+            pltpu.SemaphoreType.DMA((3, n)),
+            pltpu.SemaphoreType.DMA((3, n)),
+            pltpu.SemaphoreType.DMA((n,)),
+            pltpu.SemaphoreType.DMA((n,)),
+        ],
+        compiler_params=pltpu.CompilerParams(
+            collective_id=1, has_side_effects=True, vmem_limit_bytes=40 << 20
+        ),
+        name="attn_forward",
+    )(query, key, value, bias_lines)
+
+
+def attn_backward_kernel(
+    n, do_ref, qh, kh, vh, ot_ref, lse_ref, bias_ref, dq_ref, dk_ref, dv_ref, line_ref,
+    doh, kt, stage, land, dk_acc, dv_acc, dqt, tiles, dtiles, far_sum, send, recv, gsend, grecv,
+):
+    me = greet("ctx", n)
+    pairs = ((do_ref, doh),)
+    spread(n, me, pairs, send, recv)
+    bias_tiles(bias_ref, me, tiles)
+    for j in range(n):
+        part = slice(j * BLOCK, (j + 1) * BLOCK)
+        kt[:, part] = (kh[part, :].astype(F32) * HD**-0.5).T.astype(BF)
+    dk_acc[...] = jnp.zeros_like(dk_acc)
+    dv_acc[...] = jnp.zeros_like(dv_acc)
+    dtiles[...] = jnp.zeros_like(dtiles)
+    far_sum[...] = jnp.zeros_like(far_sum)
+
+    def query_block(step, unused):
+        i = n - 1 - step
+
+        @pl.when(i != me)
+        def _():
+            d = lax.rem(me - i + n, n)
+            to_ctx(
+                do_ref.at[:, lanes_of(i)], doh.at[rows_of(i, BLOCK)], send.at[0, d], recv.at[0, d], i
+            ).wait_recv()
+
+        rows = rows_of(i, BLOCK)
+        q_now = qh[rows, :] * BF(HD**-0.5)
+        do_now = doh[rows, :]
+        q_masked = [jnp.where(head_mask(h, BLOCK), q_now, BF(0)) for h in range(2)]
+        do_masked = [jnp.where(head_mask(h, BLOCK), do_now, BF(0)) for h in range(2)]
+        products = do_now.astype(F32).T * ot_ref[:, rows]
+        delta = [
+            jnp.sum(products[h * HD : (h + 1) * HD], axis=0, keepdims=True) for h in range(2)
+        ]
+        lse = [lse_ref[h : h + 1, rows] for h in range(2)]
+        dqt[...] = jnp.zeros_like(dqt)
+
+        def fold(j, which):
+            there = rows_of(j, BLOCK)
+            keys, vals = kh[there, :], vh[there, :]
+            dk_part, dv_part = None, None
+            for h in range(2):
+                scores = nt_dot(keys, q_masked[h])
+                if which is None:
+                    bias = bias_ref[pl.ds(2 * me + h, 1), WIDE : WIDE + BLOCK]
+                    weights = jnp.exp(scores - (lse[h] - bias))
+                else:
+                    weights = jnp.exp(scores + tiles[h, which] - lse[h])
+                dweights = nt_dot(vals, do_masked[h])
+                dscores = weights * (dweights - delta[h])
+                if which is None:
+                    far_sum[h : h + 1, :] += jnp.sum(dscores, axis=0, keepdims=True)
+                else:
+                    dtiles[h, which] += dscores
+                low = dscores.astype(BF)
+                dv_now = nn_dot(weights.astype(BF), do_masked[h])
+                dk_now = nn_dot(low, q_masked[h])
+                dv_part = dv_now if dv_part is None else dv_part + dv_now
+                dk_part = dk_now if dk_part is None else dk_part + dk_now
+                half = slice(h * HD, (h + 1) * HD)
+                dqt[half, :] += nn_dot(kt[half, there], low)
+            dk_acc[there, :] += dk_part
+            dv_acc[there, :] += dv_part
+
+        fold(i, 0)
+
+        @pl.when(i >= 1)
+        def _():
+            fold(i - 1, 1)
+
+        def far(j, unused):
+            fold(j, None)
+            return unused
+
+        lax.fori_loop(0, i - 1, far, 0)
+        stage[0, rows, :] = dqt[...].T.astype(BF)
+        stage[1, rows, :] = dk_acc[rows, :].astype(BF)
+        stage[2, rows, :] = dv_acc[rows, :].astype(BF)
+
+        @pl.when(i != me)
+        def _():
+            d = lax.rem(i - me + n, n)
+            for t in range(3):
+                to_ctx(
+                    stage.at[t, rows], land.at[t, :, lanes_of(me)], gsend.at[t, d], grecv.at[t, d], i
+                ).start()
+
+        @pl.when(i == me)
+        def _():
+            for t in range(3):
+                land[t, :, lanes_of(me)] = stage[t, rows, :]
+
+        return unused
+
+    lax.fori_loop(0, n, query_block, 0)
+    for h in range(2):
+        line = jnp.concatenate(
+            [dtiles[h, 0], dtiles[h, 1], jnp.zeros((BLOCK, LINE - 2 * BLOCK), F32)], axis=1
+        )
+        row = lax.broadcasted_iota(jnp.int32, (BLOCK, LINE), 0)
+        for bit in range(8):
+            moved = pltpu.roll(line, LINE - (1 << bit), 1)
+            line = jnp.where((row >> bit) & 1 == 1, moved, line)
+        line_ref[h : h + 1, :] = jnp.sum(line, axis=0, keepdims=True)
+    line_ref[2:4, :BLOCK] = far_sum[0:2, :]
+    line_ref[2:4, BLOCK:] = jnp.zeros((2, LINE - BLOCK), F32)
+    line_ref[4:8, :] = jnp.zeros((4, LINE), F32)
+    for d in range(1, n):
+        peer = lax.rem(me + d, n)
+        to_ctx(
+            do_ref.at[:, lanes_of(peer)], doh.at[rows_of(me, BLOCK)], send.at[0, d], recv.at[0, d], peer
+        ).wait_send()
+        for t in range(3):
+            back = to_ctx(
+                stage.at[t, rows_of(peer, BLOCK)], land.at[t, :, lanes_of(me)], gsend.at[t, d], grecv.at[t, d], peer
+            )
+            back.wait_send()
+            back.wait_recv()
+    dq_ref[...] = land[0]
+    dk_ref[...] = land[1]
+    dv_ref[...] = land[2]
+
+
+def attn_backward(n, dout, qh, kh, vh, ot, lse, bias_lines):
+    rows, seq = dout.shape[0], n * dout.shape[0]
+    grads = jax.ShapeDtypeStruct(dout.shape, BF)
+    return pl.pallas_call(
+        functools.partial(attn_backward_kernel, n),
+        out_shape=(grads, grads, grads, jax.ShapeDtypeStruct((8, LINE), F32)),
+        in_specs=vmem(7),
+        out_specs=tuple(vmem(4)),
+        scratch_shapes=[
+            pltpu.VMEM((seq, WIDE), BF),
+            pltpu.VMEM((WIDE, seq), BF),
+            pltpu.VMEM((3, seq, WIDE), BF),
+            pltpu.VMEM((3, *dout.shape), BF),
+            pltpu.VMEM((seq, WIDE), F32),
+            pltpu.VMEM((seq, WIDE), F32),
+            pltpu.VMEM((WIDE, BLOCK), F32),
+            pltpu.VMEM((2, 2, BLOCK, BLOCK), F32),
+            pltpu.VMEM((2, 2, BLOCK, BLOCK), F32),
+            pltpu.VMEM((8, BLOCK), F32),
+            pltpu.SemaphoreType.DMA((1, n)),
+            pltpu.SemaphoreType.DMA((1, n)),
+            pltpu.SemaphoreType.DMA((3, n)),
+            pltpu.SemaphoreType.DMA((3, n)),
+        ],
+        compiler_params=pltpu.CompilerParams(
+            collective_id=2, has_side_effects=True, vmem_limit_bytes=40 << 20
+        ),
+        name="attn_backward",
+    )(dout, qh, kh, vh, ot, lse, bias_lines)
+
+
+def line_selector():
+    place = jnp.arange(LINE)
+    offset = jnp.where(place < LINE // 2, -place, LINE - place)
+    return (bucket_of(offset)[None, :] == jnp.arange(NB)[:, None]).astype(jnp.float32)
+
+
+def ring_forward(query_low, key_low, value_low, bucket_table):
+    row_count, attn_width = query_low.shape
+    position = lax.axis_index("ctx")
+    scale_factor = HD ** (-0.5)
+    bias_set, onehots = make_bias(bucket_table.astype(jnp.float32), row_count)
+    query_heads = query_low.reshape(row_count, H, HD)
+    start_state = (
+        jnp.full((H, row_count), negative, jnp.float32),
+        jnp.zeros((H, row_count), jnp.float32),
+        jnp.zeros((row_count, attn_width), jnp.float32),
+    )
+    running_max, running_sum, running_acc = forward_fold(
+        query_heads,
+        position,
+        row_count,
+        bias_set,
+        scale_factor,
+        start_state,
+        (
+            lax.all_gather(key_low, "ctx", axis=0, tiled=True),
+            lax.all_gather(value_low, "ctx", axis=0, tiled=True),
+        ),
+    )
+    attended = (running_acc.reshape(row_count, H, HD) / running_sum.T[:, :, None]).reshape(
+        row_count, attn_width
+    )
+    log_total = running_max + jnp.log(running_sum)
+    state = (query_heads, key_low, value_low, attended, log_total, bias_set, onehots)
+    return attended.astype(jnp.bfloat16), state
+
+
+def ring_backward(state, dout_low):
+    query_heads, key_low, value_low, attended, log_total, bias_set, onehots = state
+    row_count, attn_width = dout_low.shape
+    cycle_size = lax.axis_size("ctx")
+    position = lax.axis_index("ctx")
+    scale_factor = HD ** (-0.5)
+    dout_heads = dout_low.reshape(row_count, H, HD)
+    row_delta = jnp.sum(
+        (dout_low.astype(jnp.float32) * attended).reshape(row_count, H, HD), axis=-1
+    ).T
+    zero_rows = jnp.zeros((row_count, attn_width), jnp.float32)
+    zero_tables = (
+        jnp.zeros((H, row_count, row_count), jnp.float32),
+        jnp.zeros((H, row_count, row_count), jnp.float32),
+        jnp.zeros((H,), jnp.float32),
+    )
+
+    def visit(folded, key_now, value_now, relation):
+
+        def visit_compute(current):
+            dquery_acc, dkey_acc, dvalue_acc, relative_bias_tables = current
+            key_heads = key_now.reshape(row_count, H, HD)
+            weights_now, dscores, ds_low = pair_core(
+                query_heads,
+                dout_heads,
+                log_total,
+                row_delta,
+                key_heads,
+                value_now.reshape(row_count, H, HD),
+                relation,
+                bias_set,
+                scale_factor,
+            )
+            dquery = jnp.einsum(
+                "hqk,khd->qhd", ds_low, key_heads, preferred_element_type=jnp.float32
+            ).reshape(row_count, attn_width)
+            dkey = jnp.einsum(
+                "hqk,qhd->khd", ds_low, query_heads, preferred_element_type=jnp.float32
+            ).reshape(row_count, attn_width)
+            dvalue = jnp.einsum(
+                "hqk,qhd->khd",
+                weights_now.astype(jnp.bfloat16),
+                dout_heads,
+                preferred_element_type=jnp.float32,
+            ).reshape(row_count, attn_width)
+            return (
+                dquery_acc + dquery,
+                dkey_acc + dkey,
+                dvalue_acc + dvalue,
+                add_tables(relative_bias_tables, dscores, relation),
+            )
+
+        return lax.cond(relation >= 0, visit_compute, lambda unchanged: unchanged, folded)
+
+    first_state = visit(
+        (zero_rows, zero_rows, zero_rows, zero_tables), key_low, value_low, jnp.array(0, jnp.int32)
+    )
+
+    def cycle_step(carried, cycle_index):
+        key_now, value_now, (dquery_acc, dkey_acc, dvalue_acc, relative_bias_tables) = carried
+        key_next, value_next = passed_along((key_now, value_now), "ctx", 1)
+        dkey_next, dvalue_next = (
+            from_behind(dkey_acc.astype(jnp.bfloat16), "ctx", 1).astype(dkey_acc.dtype),
+            from_behind(dvalue_acc.astype(jnp.bfloat16), "ctx", 1).astype(dvalue_acc.dtype),
+        )
+        relation = jnp.where(position >= cycle_index, cycle_index, -1)
+        updated = visit(
+            (dquery_acc, dkey_next, dvalue_next, relative_bias_tables),
+            key_next,
+            value_next,
+            relation,
+        )
+        return ((key_next, value_next, updated), None)
+
+    (
+        unused_key,
+        unused_value,
+        (dquery_total, dkey_part, dvalue_part, relative_bias_tables),
+    ), unused = lax.scan(cycle_step, (key_low, value_low, first_state), jnp.arange(1, cycle_size))
+    dkey_total, dvalue_total = (
+        from_behind(dkey_part.astype(jnp.bfloat16), "ctx", 1).astype(dkey_part.dtype),
+        from_behind(dvalue_part.astype(jnp.bfloat16), "ctx", 1).astype(dvalue_part.dtype),
+    )
+    dquery_low = dquery_total.astype(jnp.bfloat16)
+    dkey_low = dkey_total.astype(jnp.bfloat16)
+    dvalue_low = dvalue_total.astype(jnp.bfloat16)
+    current_bucket_selector, previous_bucket_selector, onehot_far = onehots
+    grad_biastable = (
+        jnp.einsum(
+            "afw,mfw->am",
+            current_bucket_selector,
+            relative_bias_tables[0],
+            precision=strongest_precision,
+        )
+        + jnp.einsum(
+            "afw,mfw->am",
+            previous_bucket_selector,
+            relative_bias_tables[1],
+            precision=strongest_precision,
+        )
+        + onehot_far[:, None] * relative_bias_tables[2][None, :]
+    )
+    return dquery_low, dkey_low, dvalue_low, grad_biastable
+
+
+def heads_forward(query_low, key_low, value_low, bucket_table):
+    lines = jnp.dot(
+        bucket_table.astype(jnp.float32).T, line_selector(), precision=strongest_precision
+    )
+    peers = lax.axis_size("ctx")
+    attended_low, *saved = attn_forward(peers, query_low, key_low, value_low, lines)
+    return attended_low, (*saved, lines)
+
+
+def heads_backward(state, dout_low):
+    peers = lax.axis_size("ctx")
+    dquery_low, dkey_low, dvalue_low, sums = attn_backward(peers, dout_low, *state)
+    selector = line_selector()
+    table = jnp.dot(selector, sums[:2].T, precision=strongest_precision)
+    far = jnp.sum(sums[2:4], axis=1)
+    table = table + selector[:, WIDE : WIDE + 1] * far[None, :]
+    whole = jnp.zeros((NB, H), jnp.float32)
+    whole = lax.dynamic_update_slice(whole, table, (0, 2 * lax.axis_index("ctx")))
+    return dquery_low, dkey_low, dvalue_low, whole
 
 
 def per_device(
@@ -252,39 +785,18 @@
     row_count = tokens.shape[1]
     model_width = tokens.shape[2]
     attn_width = proj_query.shape[1]
-    cycle_size = lax.axis_size("ctx")
+    split_heads = lax.axis_size("ctx") * 2 == H and row_count == BLOCK
+    self_forward = heads_forward if split_heads else ring_forward
+    self_backward = heads_backward if split_heads else ring_backward
     position = lax.axis_index("ctx")
     scale_factor = HD ** (-0.5)
     inputs = tokens[0].astype(jnp.float32)
-    bias_set, onehots = make_bias(bucket_table.astype(jnp.float32), row_count)
     normed_self, back_self = jax.vjp(root_norm, inputs, gain_self.astype(jnp.float32))
     normed_low = normed_self.astype(jnp.bfloat16)
     query_low = forward_product(normed_low, proj_query).astype(jnp.bfloat16)
     key_low = forward_product(normed_low, proj_key).astype(jnp.bfloat16)
     value_low = forward_product(normed_low, proj_value).astype(jnp.bfloat16)
-    query_heads = query_low.reshape(row_count, H, HD)
-    start_state = (
-        jnp.full((H, row_count), negative, jnp.float32),
-        jnp.zeros((H, row_count), jnp.float32),
-        jnp.zeros((row_count, attn_width), jnp.float32),
-    )
-    running_max, running_sum, running_acc = forward_fold(
-        query_heads,
-        position,
-        row_count,
-        bias_set,
-        scale_factor,
-        start_state,
-        (
-            lax.all_gather(key_low, "ctx", axis=0, tiled=True),
-            lax.all_gather(value_low, "ctx", axis=0, tiled=True),
-        ),
-    )
-    attended = (running_acc.reshape(row_count, H, HD) / running_sum.T[:, :, None]).reshape(
-        row_count, attn_width
-    )
-    log_total = running_max + jnp.log(running_sum)
-    attended_low = attended.astype(jnp.bfloat16)
+    attended_low, attention_state = self_forward(query_low, key_low, value_low, bucket_table)
     hidden = inputs + forward_product(attended_low, proj_out)
     normed_cross, back_cross = jax.vjp(root_norm, hidden, gain_cross.astype(jnp.float32))
     cross_in = normed_cross.astype(jnp.bfloat16)
@@ -405,86 +917,9 @@
     hidden_low = grad_hidden.astype(jnp.bfloat16)
     grad_selfout = outer_product(attended_low, hidden_low)
     dout_low = back_product(hidden_low, proj_out).astype(jnp.bfloat16)
-    dout_heads = dout_low.reshape(row_count, H, HD)
-    row_delta = jnp.sum(
-        (dout_low.astype(jnp.float32) * attended).reshape(row_count, H, HD), axis=-1
-    ).T
-    zero_rows = jnp.zeros((row_count, attn_width), jnp.float32)
-    zero_tables = (
-        jnp.zeros((H, row_count, row_count), jnp.float32),
-        jnp.zeros((H, row_count, row_count), jnp.float32),
-        jnp.zeros((H,), jnp.float32),
-    )
-
-    def visit(folded, key_now, value_now, relation):
-
-        def visit_compute(current):
-            dquery_acc, dkey_acc, dvalue_acc, relative_bias_tables = current
-            key_heads = key_now.reshape(row_count, H, HD)
-            weights_now, dscores, ds_low = pair_core(
-                query_heads,
-                dout_heads,
-                log_total,
-                row_delta,
-                key_heads,
-                value_now.reshape(row_count, H, HD),
-                relation,
-                bias_set,
-                scale_factor,
-            )
-            dquery = jnp.einsum(
-                "hqk,khd->qhd", ds_low, key_heads, preferred_element_type=jnp.float32
-            ).reshape(row_count, attn_width)
-            dkey = jnp.einsum(
-                "hqk,qhd->khd", ds_low, query_heads, preferred_element_type=jnp.float32
-            ).reshape(row_count, attn_width)
-            dvalue = jnp.einsum(
-                "hqk,qhd->khd",
-                weights_now.astype(jnp.bfloat16),
-                dout_heads,
-                preferred_element_type=jnp.float32,
-            ).reshape(row_count, attn_width)
-            return (
-                dquery_acc + dquery,
-                dkey_acc + dkey,
-                dvalue_acc + dvalue,
-                add_tables(relative_bias_tables, dscores, relation),
-            )
-
-        return lax.cond(relation >= 0, visit_compute, lambda unchanged: unchanged, folded)
-
-    first_state = visit(
-        (zero_rows, zero_rows, zero_rows, zero_tables), key_low, value_low, jnp.array(0, jnp.int32)
-    )
-
-    def cycle_step(carried, cycle_index):
-        key_now, value_now, (dquery_acc, dkey_acc, dvalue_acc, relative_bias_tables) = carried
-        key_next, value_next = passed_along((key_now, value_now), "ctx", 1)
-        dkey_next, dvalue_next = (
-            from_behind(dkey_acc.astype(jnp.bfloat16), "ctx", 1).astype(dkey_acc.dtype),
-            from_behind(dvalue_acc.astype(jnp.bfloat16), "ctx", 1).astype(dvalue_acc.dtype),
-        )
-        relation = jnp.where(position >= cycle_index, cycle_index, -1)
-        updated = visit(
-            (dquery_acc, dkey_next, dvalue_next, relative_bias_tables),
-            key_next,
-            value_next,
-            relation,
-        )
-        return ((key_next, value_next, updated), None)
-
-    (
-        unused_key,
-        unused_value,
-        (dquery_total, dkey_part, dvalue_part, relative_bias_tables),
-    ), unused = lax.scan(cycle_step, (key_low, value_low, first_state), jnp.arange(1, cycle_size))
-    dkey_total, dvalue_total = (
-        from_behind(dkey_part.astype(jnp.bfloat16), "ctx", 1).astype(dkey_part.dtype),
-        from_behind(dvalue_part.astype(jnp.bfloat16), "ctx", 1).astype(dvalue_part.dtype),
-    )
-    dquery_low = dquery_total.astype(jnp.bfloat16)
-    dkey_low = dkey_total.astype(jnp.bfloat16)
-    dvalue_low = dvalue_total.astype(jnp.bfloat16)
+    dquery_low, dkey_low, dvalue_low, grad_biastable = self_backward(
+        attention_state, dout_low
+    )
     grad_selfquery = outer_product(normed_low, dquery_low)
     grad_selfkey = outer_product(normed_low, dkey_low)
     grad_selfvalue = outer_product(normed_low, dvalue_low)
@@ -495,22 +930,6 @@
     )
     grad_input_part, grad_selfnorm = back_self(grad_normed)
     grad_inputs = (grad_hidden + grad_input_part).astype(jnp.bfloat16)
-    current_bucket_selector, previous_bucket_selector, onehot_far = onehots
-    grad_biastable = (
-        jnp.einsum(
-            "afw,mfw->am",
-            current_bucket_selector,
-            relative_bias_tables[0],
-            precision=strongest_precision,
-        )
-        + jnp.einsum(
-            "afw,mfw->am",
-            previous_bucket_selector,
-            relative_bias_tables[1],
-            precision=strongest_precision,
-        )
-        + onehot_far[:, None] * relative_bias_tables[2][None, :]
-    )
     shares = (
         lax.psum_scatter(
             grad_selfnorm.astype(jnp.bfloat16), "wa", scatter_dimension=0, tiled=True

time: 1910 us -> 1370 us (0.72)
  waiting for transfers between devices: 556 us -> 300 us
  starting transfers between devices: 218 us -> 11.7 us
  Pallas kernels: 0 us -> 117 us
  local copies, waits for them, and re-layouts: 201 us -> 114 us
  other arithmetic: 73.1 us -> 14.5 us
  matrix products: 247 us -> 215 us
    ppermute x16 -> x0, waiting for transfers between devices: 146 us -> none  [from_behind(): return lax.ppermute(block, axis, route)]
    pallas_call x0 -> x2, Pallas kernels: none -> 117 us  [the longest x1 68.9 us: attn_backward(): pl.pallas_call(functools.partial(attn_backward_kernel, n), out_shape=(gra...]
    all_gather x2 -> x0, waiting for transfers between devices: 113 us -> none  [the longest x1 67.9 us: per_device(): lax.all_gather(key_low, 'ctx', axis=0, tiled=True)]
    ppermute x18 -> x4, starting transfers between devices: 121 us -> 10.9 us  [passed_along(): return lax.ppermute(value, axis, pairs)]
    ppermute x16 -> x0, starting transfers between devices: 95.6 us -> none  [from_behind(): return lax.ppermute(block, axis, route)]
    unnamed x24 -> x22, waiting for transfers between devices: 6.46 us -> 69.8 us
    convert_element_type x32 -> x0, other arithmetic: 53 us -> none  [the longest x7 15 us: cycle_step(): from_behind(dvalue_acc.astype(jnp.bfloat16), 'ctx', 1)]
    unnamed x159 -> x144, local copies, waits for them, and re-layouts: 73.7 us -> 29.9 us
  transfers between devices with their start and end apart: 56 -> 24, of which waited for: 33 -> 12; matrix products, arithmetic and copies ran while one was open for 26% -> 19% of each run, Pallas kernels for 0% -> 4%
where the time goes in v1:
time: 1370 us; the launch traced here: 1360 us
  blocking collectives  572 us (42%)
  waiting for transfers between devices  300 us (22%)
  matrix products  215 us (16%)
  Pallas kernels  117 us (9%)
  local copies, waits for them, and re-layouts  114 us (8%)
  between operations  18.4 us (1%)
  other arithmetic  14.5 us (1%)
    psum x1, blocking collectives, per_device(): lax.psum((shares[0], shares[1], shares[2], shares[3], shares[4], shares[5...  542 us
    unnamed x22, waiting for transfers between devices  69.8 us
    pallas_call x1, Pallas kernels, attn_backward(): pl.pallas_call(functools.partial(attn_backward_kernel, n), out_shape=(gra...  68.9 us
    reduce_scatter x1, waiting for transfers between devices, per_device(): lax.psum_scatter(grad_feedout.astype(jnp.bfloat16), 'wa', scatter_dimensi...  61.8 us
    reduce_scatter x1, waiting for transfers between devices, per_device(): lax.psum_scatter(grad_feedin.astype(jnp.bfloat16), 'wa', scatter_dimensio...  60.6 us
    pallas_call x1, Pallas kernels, attn_forward(): pl.pallas_call(functools.partial(attn_forward_kernel, n), out_shape=(jax....  48 us
    all_gather x1, waiting for transfers between devices, per_device(): lax.all_gather(feedout, 'wa', axis=0, tiled=True)  41.5 us
    dot_general x10, matrix products, forward_product(): return jnp.dot(values, weight, preferred_element_type=jnp.float32)  40.5 us
  transfers between devices with their start and end apart: 24, of which 12 were waited for; matrix products, arithmetic and copies ran while one was open for 19% of the time, Pallas kernels for 4%

profile of v1, /device:TPU:0, one launch (start us, length us, event | category | flops | bytes accessed | tf_op | source)
XLA Modules:
  0.0 1362.4 jit_solution(15802632731930532669)
XLA Ops:
  16.2 8.7 all-reduce.12
  26.1 5.2 all-gather
  32.0 5.2 all_gather.52
  38.3 5.2 convolution_convert_fusion.3
  43.5 6.4 reshape.244
  56.5 5.1 convolution_convert_fusion.2
  61.7 6.5 reshape.245
  70.0 5.8 copy.72
  86.1 15.8 %all-gather.14.cloned.1.call-done = bf16[896,1024]{1,0:T(8,128)(2,1)} async-done(((bf16[224,1024]{1,0:T(8,128)(2,1)}), bf16[896,1024]{1,0:T(8,128)(2,1)}) %all-gather.14.cloned.1.call-update) | async-done | bytes 1835024 | tf_op jit(solution)/shard_map/all_gather | solution.py:752
  104.1 20.3 %all-gather.16.cloned.1.call-done = bf16[896,1024]{1,0:T(8,128)(2,1)} async-done(((bf16[224,1024]{1,0:T(8,128)(2,1)}), bf16[896,1024]{1,0:T(8,128)(2,1)}) %all-gather.16.cloned.1.call-update) | async-done | bytes 1835024 | tf_op jit(solution)/shard_map/all_gather | solution.py:753
  126.7 48.0 %attn_forward.1 = (bf16[256,1024]{1,0:T(8,128)(2,1)S(1)}, bf16[2048,128]{1,0:T(8,128)(2,1)S(1)}, bf16[2048,128]{1,0:T(8,128)(2,1)S(1)}, bf16[2048,128]{1,0:T(8,1...) custom-call(bf16[256,1024]{1,0:T(8,128)(2,1)S(1)} %convolution_convert_fusion.14.q_ref, ...), custom_call_target="tpu_custom_call" | custom-call | tf_op jit(solution)/shard_map/attn_forward/pallas_call | solution.py:376
  189.9 6.3 copy.75
  209.6 15.4 %convolution_bitcast_fusion.1 = f32[5,64,16,64]{1,3,2,0:T(8,128)} fusion(bf16[4,256,16,64]{1,3,2,0:T(8,128)(2,1)} %copy.72, bf16[1,256,16,64]{1,3,2,0:T(8,128)(2,1)} %bitcast.120, f32[5,16,64]{2,1,0:T(8,128)S(1)} %get-tuple-element.132, f32[5,16,64,256]{3,2,1,0:T(8,128)} %copy-done.17), kind=kOutput, calls=%fused_computation.48 | convolution fusion | flops 175641856 | bytes 9195520 | tf_op jit(solution)/shard_map/ghqk,gkhd->gqhd/dot_general | solution.py:838
  235.0 6.3 all-gather.28.cloned.1.call-done
  241.3 7.0 convolution_add_fusion
  248.3 41.5 %all-gather.30.cloned.1.call-done = bf16[3584,896]{1,0:T(8,128)(2,1)} async-done(((bf16[896,896]{1,0:T(8,128)(2,1)}), bf16[3584,896]{1,0:T(8,128)(2,1)}) %all-gather.30.cloned.1.call-update) | async-done | bytes 6422544 | tf_op jit(solution)/shard_map/all_gather | solution.py:764
  289.9 8.4 fusion.112
  310.0 5.2 fusion.27
  315.2 33.6 %fusion.31 = bf16[5,64,16,64]{1,3,2,0:T(8,128)(2,1)} fusion(f32[5,16,64,256]{3,2,1,0:T(8,128)} %fusion.27, bf16[4,256,16,64]{1,3,2,0:T(8,128)(2,1)} %copy.75, bf16[1,256,16,64]{1,3,2,0:T(8,128)(2,1)} %bitcast.123, f32[5,16,64,256]{3,2,1,0:T(8,128)} %get-tuple-element.133, f32[5,16,64]{2,1,0:T(8,128)S(1)} %get-tuple-element.132), kind=kOutput, calls=%fused_computation.52 | convolution fusion | flops 178590976 | bytes 13783040 | tf_op jit(solution)/shard_map/ghqk,gkhd->gqhd/dot_general | solution.py:881
  359.8 68.9 %attn_backward.1 = (bf16[256,1024]{1,0:T(8,128)(2,1)S(1)}, bf16[256,1024]{1,0:T(8,128)(2,1)S(1)}, bf16[256,1024]{1,0:T(8,128)(2,1)S(1)}, f32[8,1024]{1,0:T(8,128)S(1)}) custom-call(bf16[256,1024]{1,0:T(8,128)(2,1)S(1)} %convolution_convert_fusion.10.do_ref, bf16[2048,128]{1,0:T(8,128)(2,1)S(1)} %copy-done.6, bf16[2048,128]{1,0:T(8,128)(2,1)S(1)} %copy-done.8, ...), custom_call_target="tpu_custom_call" | custom-call | tf_op jit(solution)/shard_map/attn_backward/pallas_call | solution.py:537
  449.1 34.0 %fusion.23 = f32[5,256,16,64]{1,3,2,0:T(8,128)} fusion(bf16[5,64,16,64]{1,3,2,0:T(8,128)(2,1)} %copy.80, f32[5,16,64,256]{3,2,1,0:T(8,128)} %fusion.27, f32[5,16,64,256]{3,2,1,0:T(8,128)} %get-tuple-element.133, f32[5,16,64]{2,1,0:T(8,128)S(1)} %copy-done.37), kind=kOutput, calls=%fused_computation.32 | convolution fusion | flops 176952576 | bytes 16404480 | tf_op jit(solution)/shard_map/ghqk,gqhd->gkhd/dot_general | solution.py:885
  510.6 15.9 %convolution_bitcast_fusion = f32[5,256,16,64]{1,3,2,0:T(8,128)} fusion(bf16[5,64,16,64]{1,3,2,0:T(8,128)(2,1)} %copy.84, f32[5,16,64]{2,1,0:T(8,128)S(1)} %copy-done.37, f32[5,16,64,256]{3,2,1,0:T(8,128)} %copy-done.17), kind=kOutput, calls=%fused_computation.31 | convolution fusion | flops 174331136 | bytes 11161600 | tf_op jit(solution)/shard_map/ghqk,gqhd->gkhd/dot_general | solution.py:888
  553.4 6.4 convolution_convert_fusion.1
  560.8 7.3 convolution_convert_fusion
  578.6 11.2 all-reduce.11
  592.6 7.6 fusion.39
  606.3 14.5 %reduce-scatter.25.cloned.1.call-done = bf16[256,896]{1,0:T(8,128)(2,1)} async-done(((bf16[1024,896]{1,0:T(8,128)(2,1)}), bf16[256,896]{1,0:T(8,128)(2,1)}) %reduce-scatter.25.cloned.1.call-update) | async-done | bytes 458768 | tf_op jit(solution)/shard_map/reduce_scatter | solution.py:964
  620.8 32.2 %reduce-scatter.31.cloned.1.call-done = bf16[224,1024]{1,0:T(8,128)(2,1)} async-done(((bf16[896,1024]{1,0:T(8,128)(2,1)}), bf16[224,1024]{1,0:T(8,128)(2,1)}) %reduce-scatter.31.cloned.1.call-update) | async-done | bytes 458768
  654.3 31.2 %reduce-scatter.33.cloned.1.call-done = bf16[224,1024]{1,0:T(8,128)(2,1)} async-done(((bf16[896,1024]{1,0:T(8,128)(2,1)}), bf16[224,1024]{1,0:T(8,128)(2,1)}) %reduce-scatter.33.cloned.1.call-update) | async-done | bytes 458768
  686.7 60.6 %reduce-scatter.27.cloned.1.call-done = bf16[224,3584]{1,0:T(8,128)(2,1)} async-done(((bf16[896,3584]{1,0:T(8,128)(2,1)}), bf16[224,3584]{1,0:T(8,128)(2,1)}) %reduce-scatter.27.cloned.1.call-update) | async-done | bytes 1605648 | tf_op jit(solution)/shard_map/reduce_scatter | solution.py:970
  747.3 61.8 %reduce-scatter.29.cloned.1.call-done = bf16[896,896]{1,0:T(8,128)(2,1)} async-done(((bf16[3584,896]{1,0:T(8,128)(2,1)}), bf16[896,896]{1,0:T(8,128)(2,1)}) %reduce-scatter.29.cloned.1.call-update) | async-done | bytes 1605648 | tf_op jit(solution)/shard_map/reduce_scatter | solution.py:976
  809.2 542.1 %all-reduce.14 = (f32[224]{0:T(256)}, f32[224,1024]{1,0:T(8,128)}, f32[224,1024]{1,0:T(8,128)}, f32[224,1024]{1,0:T(8,128)}, f32[256,896]{1,0:T(8,128)}, /*index...) all-reduce(f32[224]{0:T(256)S(1)} %get-tuple-element.144, ...), channel_id=1, replica_groups=mesh['ctx'=8,'wa'=4] {'ctx'}, use_global_device_ids=true, to_apply=%region_11.12 | all-reduce | flops 3442560 | bytes 20659200 | tf_op jit(solution)/shard_map/psum | solution.py:983
  (292 shorter events, 194.2 us)
Async XLA Ops:
  7.2 31.1 %copy-start = (bf16[1,4,2,128,896]{4,3,2,1,0:T(8,128)(2,1)S(1)}, bf16[1,4,2,128,896]{4,3,2,1,0:T(8,128)(2,1)}, u32[]{:S(2)}) copy-start(bf16[1,4,2,128,896]{4,3,2,1,0:T(8,128)(2,1)} %param.20) | copy-start | bytes 5505028
  7.2 31.1 %all-gather.20.cloned.1.call-start = ((), (), s32[]{:S(2)}) async-start(), calls=%async_computation.14 | async-start | bytes 2293760 | tf_op jit(solution)/shard_map/all_gather | solution.py:759
  7.9 48.6 %all-gather.24.cloned.1.call-start = ((), (), s32[]{:S(2)}) async-start(), calls=%async_computation.16 | async-start | bytes 2293760 | tf_op jit(solution)/shard_map/all_gather | solution.py:758
  8.7 75.1 %all-gather.12.cloned.1.call-start = ((), (), s32[]{:S(2)}) async-start(), calls=%async_computation.10 | async-start | bytes 2293760 | tf_op jit(solution)/shard_map/all_gather | solution.py:751
  9.4 92.4 %all-gather.14.cloned.1.call-start = ((), (), s32[]{:S(2)}) async-start(), calls=%async_computation.11 | async-start | bytes 2293760 | tf_op jit(solution)/shard_map/all_gather | solution.py:752
  10.1 27.7 %copy-start.14 = (bf16[1,256,896]{2,1,0:T(8,128)(2,1)S(1)}, bf16[1,256,896]{2,1,0:T(8,128)(2,1)}, u32[]{:S(2)}) copy-start(bf16[1,256,896]{2,1,0:T(8,128)(2,1)} %param.19) | copy-start | bytes 1376260
  10.1 114.4 %all-gather.16.cloned.1.call-start = ((), (), s32[]{:S(2)}) async-start(), calls=%async_computation.12 | async-start | bytes 2293760 | tf_op jit(solution)/shard_map/all_gather | solution.py:753
  10.7 167.5 %all-gather.18.cloned.1.call-start = ((), (), s32[]{:S(2)}) async-start(), calls=%async_computation.13 | async-start | bytes 2293760 | tf_op jit(solution)/shard_map/all_gather | solution.py:754
  11.2 169.6 %all-gather.22.cloned.1.call-start = ((), (), s32[]{:S(2)}) async-start(), calls=%async_computation.15 | async-start | bytes 2293760 | tf_op jit(solution)/shard_map/all_gather | solution.py:757
  12.0 219.4 %all-gather.26.cloned.1.call-start = ((), (), s32[]{:S(2)}) async-start(), calls=%async_computation.17 | async-start | bytes 2293760 | tf_op jit(solution)/shard_map/all_gather | solution.py:760
  12.7 228.5 %all-gather.28.cloned.1.call-start = ((), (), s32[]{:S(2)}) async-start(), calls=%async_computation.18 | async-start | bytes 8028160 | tf_op jit(solution)/shard_map/all_gather | solution.py:762
  13.5 276.4 %all-gather.30.cloned.1.call-start = ((), (), s32[]{:S(2)}) async-start(), calls=%async_computation.19 | async-start | bytes 8028160 | tf_op jit(solution)/shard_map/all_gather | solution.py:764
  14.1 592.2 %reduce-scatter.15.cloned.1.call-start = ((), (), s32[]{:S(2)}) async-start(), calls=%async_computation.20 | async-start | bytes 2293760 | tf_op jit(solution)/shard_map/reduce_scatter | solution.py:937
  75.8 120.4 %collective-permute-start = (bf16[256,1024]{1,0:T(8,128)(2,1)}, bf16[256,1024]{1,0:T(8,128)(2,1)}, u32[]{:S(2)}, u32[]{:S(2)}) collective-permute-start(bf16[256,1024]{1,0:T(8,128)(2,1)} %slice.70), channel_id=1, source_target_pairs={{0,4},{4,8},{8,12},{12,16},{16,20},{20,24},{24,28},{1,5},{5,9},{9,... | collective-permute-start | bytes 1572872 | tf_op jit(solution)/shard_map/ppermute | solution.py:32
  80.1 118.2 %collective-permute-start.1 = (bf16[256,1024]{1,0:T(8,128)(2,1)}, bf16[256,1024]{1,0:T(8,128)(2,1)}, u32[]{:S(2)}, u32[]{:S(2)}) collective-permute-start(bf16[256,1024]{1,0:T(8,128)(2,1)} %slice.71), channel_id=1, source_target_pairs={{0,4},{4,8},{8,12},{12,16},{16,20},{20,24},{24,28},{1,5},{5,9},{9,... | collective-permute-start | bytes 1572872 | tf_op jit(solution)/shard_map/ppermute | solution.py:32
  180.8 176.7 %copy-start.13 = (f32[256,896]{1,0:T(8,128)}, f32[256,896]{1,0:T(8,128)S(1)}, u32[]{:S(2)}) copy-start(f32[256,896]{1,0:T(8,128)S(1)} %get-tuple-element.131) | copy-start | bytes 2752516
  180.8 176.7 %copy-start.41 = (f32[256]{0:T(256)}, f32[256]{0:T(256)S(1)}, u32[]{:S(2)}) copy-start(f32[256]{0:T(256)S(1)} %fusion.82) | copy-start | bytes 3076
  209.6 105.6 %copy-start.36 = (f32[5,16,64]{2,1,0:T(8,128)}, f32[5,16,64]{2,1,0:T(8,128)S(1)}, u32[]{:S(2)}) copy-start(f32[5,16,64]{2,1,0:T(8,128)S(1)} %get-tuple-element.132) | copy-start | bytes 61444
  235.0 66.0 %copy-start.43 = (f32[256]{0:T(256)}, f32[256]{0:T(256)S(1)}, u32[]{:S(2)}) copy-start(f32[256]{0:T(256)S(1)} %fusion.83) | copy-start | bytes 3076
  359.0 69.7 %copy-start.18 = (f32[256,896]{1,0:T(8,128)}, f32[256,896]{1,0:T(8,128)S(1)}, u32[]{:S(2)}) copy-start(f32[256,896]{1,0:T(8,128)S(1)} %fusion.46) | copy-start | bytes 2752516
  359.0 71.1 %copy-start.15 = (bf16[1,256,896]{2,1,0:T(8,128)(2,1)S(1)}, bf16[1,256,896]{2,1,0:T(8,128)(2,1)}, u32[]{:S(2)}) copy-start(bf16[1,256,896]{2,1,0:T(8,128)(2,1)} %param.19) | copy-start | bytes 1376260
  432.2 174.1 %reduce-scatter.17.cloned.1.call-start = ((), (), s32[]{:S(2)}) async-start(), calls=%async_computation.21 | async-start | bytes 2293760 | tf_op jit(solution)/shard_map/reduce_scatter | solution.py:940
  435.5 170.8 %reduce-scatter.19.cloned.1.call-start = ((), (), s32[]{:S(2)}) async-start(), calls=%async_computation.22 | async-start | bytes 2293760 | tf_op jit(solution)/shard_map/reduce_scatter | solution.py:943
  438.7 167.6 %reduce-scatter.21.cloned.1.call-start = ((), (), s32[]{:S(2)}) async-start(), calls=%async_computation.23 | async-start | bytes 2293760 | tf_op jit(solution)/shard_map/reduce_scatter | solution.py:946
  441.9 164.4 %reduce-scatter.23.cloned.1.call-start = ((), (), s32[]{:S(2)}) async-start(), calls=%async_computation.24 | async-start | bytes 2293760 | tf_op jit(solution)/shard_map/reduce_scatter | solution.py:955
  445.3 175.5 %reduce-scatter.25.cloned.1.call-start = ((), (), s32[]{:S(2)}) async-start(), calls=%async_computation.25 | async-start | bytes 2293760 | tf_op jit(solution)/shard_map/reduce_scatter | solution.py:964
  449.0 204.1 %reduce-scatter.31.cloned.1.call-start = ((), (), s32[]{:S(2)}) async-start(), calls=%async_computation.28 | async-start | bytes 2293760
  485.3 14.7 %collective-permute-start.2 = (bf16[256,1024]{1,0:T(8,128)(2,1)}, bf16[256,1024]{1,0:T(8,128)(2,1)S(1)}, u32[]{:S(2)}, u32[]{:S(2)}) collective-permute-start(bf16[256,1024]{1,0:T(8,128)(2,1)} %copy.81), channel_id=1, source_target_pairs={{4,0},{8,4},{12,8},{16,12},{20,16},{24,20},{28,24},{5,1},{9,5},{13... | collective-permute-start | bytes 1572872 | tf_op jit(solution)/shard_map/ppermute | solution.py:32
  510.6 174.9 %reduce-scatter.33.cloned.1.call-start = ((), (), s32[]{:S(2)}) async-start(), calls=%async_computation.29 | async-start | bytes 2293760
  528.8 14.1 %collective-permute-start.3 = (bf16[256,1024]{1,0:T(8,128)(2,1)}, bf16[256,1024]{1,0:T(8,128)(2,1)S(1)}, u32[]{:S(2)}, u32[]{:S(2)}) collective-permute-start(bf16[256,1024]{1,0:T(8,128)(2,1)} %copy.85), channel_id=1, source_target_pairs={{4,0},{8,4},{12,8},{16,12},{20,16},{24,20},{28,24},{5,1},{9,5},{13... | collective-permute-start | bytes 1572872 | tf_op jit(solution)/shard_map/ppermute | solution.py:32
  553.3 194.0 %reduce-scatter.27.cloned.1.call-start = ((), (), s32[]{:S(2)}) async-start(), calls=%async_computation.26 | async-start | bytes 8028160 | tf_op jit(solution)/shard_map/reduce_scatter | solution.py:970
  559.8 249.4 %reduce-scatter.29.cloned.1.call-start = ((), (), s32[]{:S(2)}) async-start(), calls=%async_computation.27 | async-start | bytes 8028160 | tf_op jit(solution)/shard_map/reduce_scatter | solution.py:976
  (56 other events, 229.0 us)
Sparse Core Ops, SparseCore 0:
  9.6 23.9 all-gather.19
  35.2 21.3 all-gather.23
  58.1 21.1 all-gather.11
  80.7 21.1 all-gather.13
  103.3 21.1 all-gather.15
  125.9 21.1 all-gather.17
  148.6 21.1 all-gather.21
  171.4 21.0 all-gather.25
  194.1 47.1 all-gather.27
  242.7 47.1 all-gather.29
  432.3 25.9 reduce-scatter.14
  460.8 30.0 reduce-scatter.16
  493.4 29.7 reduce-scatter.18
  525.8 29.8 reduce-scatter.20
  558.0 30.1 reduce-scatter.22
  590.8 30.0 reduce-scatter.24
  623.2 29.8 reduce-scatter.30
  655.6 29.8 reduce-scatter.32
  688.1 59.2 reduce-scatter.26
  749.9 59.2 reduce-scatter.28

commit v2 on v1

--- a/solution.py
+++ b/solution.py
@@ -725,302 +725,653 @@
     return dquery_low, dkey_low, dvalue_low, whole
 
 
-def per_device(
-    tokens,
-    neighbours,
-    cotangent,
-    selfnorm,
-    selfquery,
-    selfkey,
-    selfvalue,
-    selfout,
-    biastable,
-    crossnorm,
-    crossquery,
-    crosskey,
-    crossvalue,
-    crossout,
-    feednorm,
-    feedin,
-    feedbias,
-    feedout,
-    outbias,
+RING = 8
+HOPS = RING - 1
+
+
+def ring_place(n):
+    me = lax.axis_index("ctx")
+    half = n // 2
+
+    def at(place):
+        return jnp.where(place < half, 2 * place, 2 * (n - 1 - place) + 1)
+
+    place = jnp.where(lax.rem(me, 2) == 0, me // 2, n - 1 - me // 2)
+    return place, at(lax.rem(place + 1, n)), at(lax.rem(place + n - 1, n))
+
+
+def other_wa(me, bit):
+    flipped = lax.rem(me // bit, 2)
+    return me + bit - 2 * bit * flipped
+
+
+def remote(src, dst, send_sem, recv_sem, **device):
+    return pltpu.make_async_remote_copy(
+        src_ref=src,
+        dst_ref=dst,
+        send_sem=send_sem,
+        recv_sem=recv_sem,
+        device_id=device,
+        device_id_type=MESH,
+    )
+
+
+TALL, FLAT = (224, 1024), (256, 896)
+UNITS = ("cq", "ck", "cv", "co", "q", "k", "v", "so")
+LANES = (
+    (1, ("fin",), 0),
+    (-1, ("fout",), 0),
+    (1, ("cA",), 9),
+    (-1, ("cB", "co"), 9),
+    (1, ("sA",), 15),
+    (-1, ("sB", "so"), 15),
+)
+MEMBERS = {"cA": ("cq", "ck"), "cB": ("cv",), "sA": ("q", "k"), "sB": ("v",)}
+BUFFERS = {
+    "fin": (112, 896),
+    "fout": (112, 896),
+    "cA": (448, 128),
+    "cB": (224, 128),
+    "co": (32, 896),
+    "sA": (448, 128),
+    "sB": (224, 128),
+    "so": (32, 896),
+}
+NAMES = tuple(BUFFERS)
+
+
+def reduce_kernel(*refs):
+    parts = dict(zip(UNITS, refs[:8], strict=True))
+    fin_ref, fout_ref = refs[8:10]
+    full = dict(zip(NAMES, refs[10:18], strict=True))
+    rest = refs[18:]
+    share = dict(zip(NAMES, rest[:8], strict=True))
+    hold = dict(zip(NAMES, rest[8:16], strict=True))
+    rest = rest[16:]
+    tall_own, tall_in, tall_out, tall_x, flat_own, flat_in, flat_out, flat_x = rest[:8]
+    (own_sem, core_send, core_recv, x_send, x_recv, a_send, a_recv, ring_send, ring_recv, f_sem) = rest[8:]
+
+    wa = lax.axis_index("wa")
+    place, after, before = ring_place(RING)
+    mate, across = other_wa(wa, 1), other_wa(wa, 2)
+    core, half = lax.rem(wa, 2), wa // 2
+    barrier = pltpu.get_barrier_semaphore()
+    neighbours = [{"wa": mate}, {"wa": across}, {"wa": other_wa(across, 1)}, {"ctx": after}, {"ctx": before}]
+    for who in neighbours:
+        pl.semaphore_signal(barrier, inc=1, device_id=who, device_id_type=MESH)
+    pl.semaphore_wait(barrier, len(neighbours))
+
+    load_out = pltpu.make_async_copy(fout_ref, share["fout"], f_sem.at[0])
+    load_out.start()
+    own_fin = pltpu.make_async_copy(
+        fin_ref.at[pl.ds(2 * wa, 2)], share["fin"].at[pl.ds(2 * wa, 2)], f_sem.at[1]
+    )
+    own_fin.start()
+    fin_copies = []
+    for d, peer in enumerate((across, other_wa(across, 1), mate)):
+        copy = remote(
+            fin_ref.at[pl.ds(2 * peer, 2)],
+            share["fin"].at[pl.ds(2 * wa, 2)],
+            a_send.at[d],
+            a_recv.at[d],
+            wa=peer,
+        )
+        copy.start()
+        fin_copies.append(copy)
+
+    own_copies, core_copies, x_copies = {}, {}, {}
+    place_of = {}
+    counts = {TALL: 0, FLAT: 0}
+    for u, name in enumerate(UNITS):
+        shape = FLAT if name in ("co", "so") else TALL
+        slot = counts[shape]
+        counts[shape] += 1
+        own, inn = (tall_own, tall_in) if shape == TALL else (flat_own, flat_in)
+        place_of[name] = (shape, slot)
+        rows = shape[0]
+        for x in range(2):
+            mine = pl.ds(pl.multiple_of((2 * x + core) * rows, 16), rows)
+            theirs = pl.ds(pl.multiple_of((2 * x + 1 - core) * rows, 16), rows)
+            copy = pltpu.make_async_copy(parts[name].at[mine], own.at[slot, x], own_sem.at[u, x])
+            copy.start()
+            own_copies[name, x] = copy
+            copy = remote(
+                parts[name].at[theirs], inn.at[slot, x], core_send.at[u, x], core_recv.at[u, x], wa=mate
+            )
+            copy.start()
+            core_copies[name, x] = copy
+
+    def send_across(name):
+        u = UNITS.index(name)
+        shape, slot = place_of[name]
+        own, inn, out, land = (
+            (tall_own, tall_in, tall_out, tall_x) if shape == TALL else (flat_own, flat_in, flat_out, flat_x)
+        )
+        for x in range(2):
+            own_copies[name, x].wait()
+            core_copies[name, x].wait_recv()
+        out[slot] = (own[slot, 1 - half].astype(F32) + inn[slot, 1 - half].astype(F32)).astype(BF)
+        copy = remote(out.at[slot], land.at[slot], x_send.at[u], x_recv.at[u], wa=across)
+        copy.start()
+        x_copies[name] = copy
+
+    def gather_share(name):
+        shape, slot = place_of[name]
+        own, inn, land = (tall_own, tall_in, tall_x) if shape == TALL else (flat_own, flat_in, flat_x)
+        x_copies[name].wait_recv()
+        total = (
+            own[slot, half].astype(F32) + inn[slot, half].astype(F32) + land[slot].astype(F32)
+        ).astype(BF)
+        if shape == FLAT:
+            for c in range(RING):
+                share[name][c] = total[c * 32 : (c + 1) * 32, :]
+        else:
+            [(target, at)] = [(b, m.index(name)) for b, m in MEMBERS.items() if name in m]
+            for c in range(RING):
+                share[target][c, at * 224 : (at + 1) * 224, :] = total[:, c * 128 : (c + 1) * 128]
+
+    copies = {}
+
+    def ring_step(lane, step):
+        way, buffers, unused = LANES[lane]
+        here = place if way == 1 else lax.rem(RING - place, RING)
+        target = after if way == 1 else before
+        for name in buffers:
+            b = NAMES.index(name)
+
+            def chunk(offset):
+                return lax.rem(here + offset + 2 * RING, RING)
+
+            if step < HOPS:
+                now = chunk(-step)
+                if step > 0:
+                    copies[name, step - 1].wait_recv()
+                    share[name][now] = (
+                        share[name][now].astype(F32) + hold[name][step - 1].astype(F32)
+                    ).astype(BF)
+                src, dst = share[name].at[now], hold[name].at[step]
+            elif step == HOPS:
+                now = chunk(1)
+                copies[name, step - 1].wait_recv()
+                full[name][now] = (
+                    share[name][now].astype(F32) + hold[name][step - 1].astype(F32)
+                ).astype(BF)
+                src = dst = full[name].at[now]
+            else:
+                copies[name, step - 1].wait_recv()
+                now = chunk(1 - (step - HOPS))
+                if step == 2 * HOPS:
+                    continue
+                src = dst = full[name].at[now]
+            copy = remote(src, dst, ring_send.at[b, step], ring_recv.at[b, step], ctx=target)
+            copy.start()
+            copies[name, step] = copy
+
+    load_out.wait()
+    ring_step(1, 0)
+    for name in UNITS[:4]:
+        send_across(name)
+    own_fin.wait()
+    for copy in fin_copies:
+        copy.wait_recv()
+    ring_step(0, 0)
+    for name in UNITS[4:]:
+        send_across(name)
+    last = max(start for _, _, start in LANES) + 2 * HOPS
+    for tick in range(1, last + 1):
+        for lane, (_, buffers, start) in enumerate(LANES):
+            step = tick - start
+            if step == 0:
+                for name in buffers:
+                    for member in MEMBERS.get(name, (name,)):
+                        gather_share(member)
+            if 0 <= step <= 2 * HOPS:
+                ring_step(lane, step)
+    for copy in fin_copies:
+        copy.wait_send()
+    for name in UNITS:
+        for x in range(2):
+            core_copies[name, x].wait_send()
+        x_copies[name].wait_send()
+    for copy in copies.values():
+        copy.wait_send()
+
+
+def reduce_grads(parts, fin, fout):
+    any_spec = pl.BlockSpec(memory_space=pl.ANY)
+    dma = pltpu.SemaphoreType.DMA
+    return pl.pallas_call(
+        reduce_kernel,
+        out_shape=tuple(jax.ShapeDtypeStruct((RING, *BUFFERS[b]), BF) for b in NAMES),
+        in_specs=[any_spec] * 10,
+        out_specs=tuple(vmem(len(NAMES))),
+        scratch_shapes=[
+            *(pltpu.VMEM((RING, *BUFFERS[b]), BF) for b in NAMES),
+            *(pltpu.VMEM((HOPS, *BUFFERS[b]), BF) for b in NAMES),
+            pltpu.VMEM((6, 2, *TALL), BF),
+            pltpu.VMEM((6, 2, *TALL), BF),
+            pltpu.VMEM((6, *TALL), BF),
+            pltpu.VMEM((6, *TALL), BF),
+            pltpu.VMEM((2, 2, *FLAT), BF),
+            pltpu.VMEM((2, 2, *FLAT), BF),
+            pltpu.VMEM((2, *FLAT), BF),
+            pltpu.VMEM((2, *FLAT), BF),
+            dma((8, 2)),
+            dma((8, 2)),
+            dma((8, 2)),
+            dma((8,)),
+            dma((8,)),
+            dma((3,)),
+            dma((3,)),
+            dma((8, 2 * HOPS)),
+            dma((8, 2 * HOPS)),
+            dma((2,)),
+        ],
+        compiler_params=pltpu.CompilerParams(
+            collective_id=3, has_side_effects=True, vmem_limit_bytes=60 << 20
+        ),
+        name="reduce_grads",
+    )(*parts, *(part.reshape(RING, *BUFFERS["fin"]) for part in (fin, fout)))
+
+
+def unfold(full):
+    def tall(name, at):
+        piece = full[name][:, at * 224 : (at + 1) * 224, :].astype(F32)
+        return jnp.transpose(piece, (1, 0, 2)).reshape(TALL)
+
+    out = {m: tall(b, at) for b, members in MEMBERS.items() for at, m in enumerate(members)}
+    for name in ("co", "so"):
+        out[name] = full[name].reshape(FLAT).astype(F32)
+    out["fout"] = full["fout"].reshape(896, 896).astype(F32)
+    out["fin"] = jnp.transpose(full["fin"].reshape(4, 224, 896).astype(F32), (1, 0, 2)).reshape(224, 3584)
+    return out
+
+
+GELU = (2.0 / math.pi) ** 0.5
+
+
+def ffn_kernel(
+    f_ref, cot_ref, win_ref, wout_ref, bias_ref, res_ref, df_ref, dwin_ref, dwout_ref, dbias_ref,
+    f_all, g_all, dul_all, own, kept, out_mate, out_cross, in_mate, in_cross, x_out, x_in,
+    f_send, f_recv, p_send, p_recv,
 ):
-    gathered = (
-        lax.all_gather(selfnorm, "wa", axis=0, tiled=True),
-        lax.all_gather(selfquery, "wa", axis=0, tiled=True),
-        lax.all_gather(selfkey, "wa", axis=0, tiled=True),
-        lax.all_gather(selfvalue, "wa", axis=0, tiled=True),
-        lax.all_gather(selfout, "wa", axis=0, tiled=True),
-        lax.all_gather(biastable, "wa", axis=0, tiled=True),
-        lax.all_gather(crossnorm, "wa", axis=0, tiled=True),
-        lax.all_gather(crossquery, "wa", axis=0, tiled=True),
-        lax.all_gather(crosskey, "wa", axis=0, tiled=True),
-        lax.all_gather(crossvalue, "wa", axis=0, tiled=True),
-        lax.all_gather(crossout, "wa", axis=0, tiled=True),
-        lax.all_gather(feednorm, "wa", axis=0, tiled=True),
-        lax.all_gather(feedin, "wa", axis=0, tiled=True),
-        lax.all_gather(feedbias, "wa", axis=0, tiled=True),
-        lax.all_gather(feedout, "wa", axis=0, tiled=True),
-        lax.all_gather(outbias, "wa", axis=0, tiled=True),
-    )
-    (
-        gain_self,
-        proj_query,
-        proj_key,
-        proj_value,
-        proj_out,
-        bucket_table,
-        gain_cross,
-        cross_query,
-        cross_key,
-        cross_value,
-        cross_out,
-        gain_feed,
-        feed_in,
-        feed_bias,
-        feed_out,
-        out_bias,
-    ) = gathered
-    row_count = tokens.shape[1]
-    model_width = tokens.shape[2]
-    attn_width = proj_query.shape[1]
-    split_heads = lax.axis_size("ctx") * 2 == H and row_count == BLOCK
+    me = lax.axis_index("wa")
+    mate, across = other_wa(me, 1), other_wa(me, 2)
+    both = other_wa(across, 1)
+    barrier = pltpu.get_barrier_semaphore()
+    for peer in (mate, across):
+        pl.semaphore_signal(barrier, inc=1, device_id={"wa": peer}, device_id_type=MESH)
+    pl.semaphore_wait(barrier, 2)
+    to_across = remote(f_ref, f_all.at[me], f_send.at[1], f_recv.at[1], wa=across)
+    to_across.start()
+    to_mate = remote(f_ref, f_all.at[me], f_send.at[0], f_recv.at[0], wa=mate)
+    to_mate.start()
+    forward = remote(f_all.at[across], f_all.at[across], f_send.at[2], f_recv.at[2], wa=mate)
+    f_all[me] = f_ref[...]
+    order = (me, mate, across, both)
+    dbias_ref[...] = jnp.zeros_like(dbias_ref)
+    for k, s in enumerate(order):
+        if k == 1:
+            to_mate.wait_recv()
+        if k == 2:
+            to_across.wait_recv()
+            forward.start()
+        if k == 3:
+            forward.wait_recv()
+        u = nn_dot(f_all[s], win_ref[...]) + bias_ref[...]
+        square = u * u
+        t = jnp.tanh(GELU * (u + 0.044715 * (square * u)))
+        g_all[s] = (0.5 * u * (1.0 + t)).astype(BF)
+        slope = 0.5 * (1.0 + t) + 0.5 * u * (1.0 - t * t) * (GELU * (1.0 + 3 * 0.044715 * square))
+        du = nt_dot(cot_ref[s], wout_ref[...]) * slope
+        dbias_ref[...] += jnp.sum(du.reshape(32, 8, du.shape[1]), axis=0)
+        dul_all[s] = du.astype(BF)
+
+    def scatter(which, product):
+        out_cross[which] = product(both).astype(BF)
+        cross = remote(
+            out_cross.at[which], in_cross.at[which], p_send.at[which, 0], p_recv.at[which, 0], wa=mate
+        )
+        cross.start()
+        kept[...] = product(across)
+        cross.wait_recv()
+        x_out[which] = (kept[...] + in_cross[which].astype(F32)).astype(BF)
+        over = remote(
+            x_out.at[which], x_in.at[which], p_send.at[which, 1], p_recv.at[which, 1], wa=across
+        )
+        over.start()
+        out_mate[which] = product(mate).astype(BF)
+        near = remote(
+            out_mate.at[which], in_mate.at[which], p_send.at[which, 2], p_recv.at[which, 2], wa=mate
+        )
+        near.start()
+        own[which] = product(me)
+        return cross, over, near
+
+    def finish(which, copies, out_ref):
+        cross, over, near = copies
+        near.wait_recv()
+        over.wait_recv()
+        out_ref[...] = own[which] + in_mate[which].astype(F32) + x_in[which].astype(F32)
+        for copy in copies:
+            copy.wait_send()
+
+    df_copies = scatter(0, lambda s: nt_dot(dul_all[s], win_ref[...]))
+    res_copies = scatter(1, lambda s: nn_dot(g_all[s], wout_ref[...]))
+    width = f_ref.shape[1]
+
+    def outer(left_all, right, out_ref):
+        for c in range(width // WIDE):
+            lanes = slice(c * WIDE, (c + 1) * WIDE)
+            total = None
+            for s in range(4):
+                left = left_all[s, :, lanes].astype(F32).T.astype(BF)
+                now = nn_dot(left, right[s])
+                total = now if total is None else total + now
+            out_ref[lanes, :] = total.astype(BF)
+
+    outer(f_all, dul_all, dwin_ref)
+    outer(g_all, cot_ref, dwout_ref)
+    finish(0, df_copies, df_ref)
+    finish(1, res_copies, res_ref)
+    for copy in (to_mate, to_across, forward):
+        copy.wait_send()
+
+
+def ffn(f_low, cot_all, win, wout, bias):
+    rows, width = f_low.shape
+    hidden = win.shape[1]
+    dma = pltpu.SemaphoreType.DMA
+    block = (rows, width)
+    return pl.pallas_call(
+        ffn_kernel,
+        out_shape=(
+            jax.ShapeDtypeStruct(block, F32),
+            jax.ShapeDtypeStruct(block, F32),
+            jax.ShapeDtypeStruct(win.shape, BF),
+            jax.ShapeDtypeStruct(wout.shape, BF),
+            jax.ShapeDtypeStruct((8, hidden), F32),
+        ),
+        in_specs=vmem(5),
+        out_specs=tuple(vmem(5)),
+        scratch_shapes=[
+            pltpu.VMEM((4, *block), BF),
+            pltpu.VMEM((4, rows, hidden), BF),
+            pltpu.VMEM((4, rows, hidden), BF),
+            pltpu.VMEM((2, *block), F32),
+            pltpu.VMEM(block, F32),
+            *[pltpu.VMEM((2, *block), BF)] * 6,
+            dma((3,)),
+            dma((3,)),
+            dma((2, 3)),
+            dma((2, 3)),
+        ],
+        compiler_params=pltpu.CompilerParams(
+            collective_id=4, has_side_effects=True, vmem_limit_bytes=56 << 20
+        ),
+        name="feed_forward",
+    )(f_low, cot_all, win, wout, bias)
+
+
+def padded_rows(pad, values):
+    rows = values.shape[0]
+    pad[...] = jnp.zeros_like(pad)
+    pad[1 : rows + 1, :] = values.astype(F32)
+
+
+def both_heads(pad, g):
+    here = pad[g * SPAN : (g + 1) * SPAN, :]
+    left = head_mask(0, SPAN)
+    return jnp.concatenate([jnp.where(left, here, 0.0), jnp.where(left, 0.0, here)], 0).astype(BF)
+
+
+def join_heads(stacked):
+    return jnp.where(head_mask(0, SPAN), stacked[:SPAN], stacked[SPAN:])
+
+
+def cross_forward_kernel(groups, keep_ref, q_ref, k_ref, v_ref, x_ref, q_pad, x_pad):
+    padded_rows(q_pad, q_ref[...])
+    for g in range(groups):
+        rows = slice(g * 256, (g + 1) * 256)
+        query = both_heads(q_pad, g) * BF(HD**-0.5)
+        scores = nt_dot(query, k_ref[rows, :])
+        weights = jnp.exp(scores - jnp.max(scores, axis=1, keepdims=True))
+        weights = weights / jnp.sum(weights, axis=1, keepdims=True)
+        mixed = join_heads(nn_dot(weights.astype(BF), v_ref[rows, :]))
+        if g == 0:
+            mixed = mixed * keep_ref[0:1, :]
+        x_pad[g * SPAN : (g + 1) * SPAN, :] = mixed
+    x_ref[...] = x_pad[1 : x_ref.shape[0] + 1, :].astype(BF)
+
+
+def pair_specs(*rows):
+    return [pl.BlockSpec((r, WIDE), lambda p: (0, p)) for r in rows]
+
+
+def cross_forward(keep, query, keys, values):
+    rows, width = query.shape
+    many = keys.shape[0]
+    groups = many // 256
+    return pl.pallas_call(
+        functools.partial(cross_forward_kernel, groups),
+        grid=(width // WIDE,),
+        out_shape=jax.ShapeDtypeStruct(query.shape, BF),
+        in_specs=[pl.BlockSpec((8, WIDE), lambda p: (0, 0)), *pair_specs(rows, many, many)],
+        out_specs=pair_specs(rows)[0],
+        scratch_shapes=[pltpu.VMEM((groups * SPAN, WIDE), F32)] * 2,
+        compiler_params=pltpu.CompilerParams(vmem_limit_bytes=16 << 20),
+        name="cross_forward",
+    )(keep, query, keys, values)
+
+
+def cross_backward_kernel(
+    groups, keep_ref, q_ref, dx_ref, k_ref, v_ref, dq_ref, dk_ref, dv_ref, q_pad, dx_pad, dq_pad
+):
+    padded_rows(q_pad, q_ref[...])
+    padded_rows(dx_pad, dx_ref[...])
+    dx_pad[:SPAN, :] = dx_pad[:SPAN, :] * keep_ref[0:1, :]
+    for g in range(groups):
+        rows = slice(g * 256, (g + 1) * 256)
+        query = both_heads(q_pad, g) * BF(HD**-0.5)
+        dmixed = both_heads(dx_pad, g)
+        keys, values = k_ref[rows, :], v_ref[rows, :]
+        scores = nt_dot(keys, query)
+        weights = jnp.exp(scores - jnp.max(scores, axis=0, keepdims=True))
+        weights = weights / jnp.sum(weights, axis=0, keepdims=True)
+        dweights = nt_dot(values, dmixed)
+        dscores = weights * (dweights - jnp.sum(weights * dweights, axis=0, keepdims=True))
+        dk_ref[rows, :] = nn_dot(dscores.astype(BF), query).astype(BF)
+        dv_ref[rows, :] = nn_dot(weights.astype(BF), dmixed).astype(BF)
+        back = (dscores * HD**-0.5).T.astype(BF)
+        dq_pad[g * SPAN : (g + 1) * SPAN, :] = join_heads(nn_dot(back, keys))
+    dq_ref[...] = dq_pad[1 : dq_ref.shape[0] + 1, :].astype(BF)
+
+
+def cross_backward(keep, query, dmixed, keys, values):
+    rows, width = query.shape
+    many = keys.shape[0]
+    groups = many // 256
+    return pl.pallas_call(
+        functools.partial(cross_backward_kernel, groups),
+        grid=(width // WIDE,),
+        out_shape=(
+            jax.ShapeDtypeStruct(query.shape, BF),
+            jax.ShapeDtypeStruct(keys.shape, BF),
+            jax.ShapeDtypeStruct(keys.shape, BF),
+        ),
+        in_specs=[
+            pl.BlockSpec((8, WIDE), lambda p: (0, 0)),
+            *pair_specs(rows, rows, many, many),
+        ],
+        out_specs=tuple(pair_specs(rows, many, many)),
+        scratch_shapes=[pltpu.VMEM((groups * SPAN, WIDE), F32)] * 3,
+        compiler_params=pltpu.CompilerParams(vmem_limit_bytes=16 << 20),
+        name="cross_backward",
+    )(keep, query, dmixed, keys, values)
+
+
+NAMES_OF_WEIGHTS = (
+    "selfnorm", "selfquery", "selfkey", "selfvalue", "selfout", "biastable", "crossnorm", "crossquery",
+    "crosskey", "crossvalue", "crossout", "feednorm", "feedin", "feedbias", "feedout", "outbias",
+)
+UNIT_WEIGHTS = (
+    "crossquery", "crosskey", "crossvalue", "crossout", "selfquery", "selfkey", "selfvalue", "selfout",
+)
+
+
+def whole_over_wa(shard):
+    return lax.all_gather(shard, "wa", axis=0, tiled=True)
+
+
+def reduce_plain(parts, fin, fout):
+    shares = [
+        lax.psum_scatter(part, "wa", scatter_dimension=0, tiled=True).astype(F32) for part in parts
+    ]
+    own_rows = lax.all_to_all(fin, "wa", 0, 1, tiled=True).astype(F32)
+    totals = lax.psum((*shares, own_rows, fout.astype(F32)), "ctx")
+    return dict(zip((*UNITS, "fin", "fout"), totals, strict=True))
+
+
+def per_device(tokens, neighbours, cotangent, *shards):
+    given = dict(zip(NAMES_OF_WEIGHTS, shards, strict=True))
+    peers = lax.axis_size("ctx")
+    position = lax.axis_index("ctx")
+    row_count, model_width = tokens.shape[1:]
+    split_heads = peers * 2 == H and row_count == BLOCK
     self_forward = heads_forward if split_heads else ring_forward
     self_backward = heads_backward if split_heads else ring_backward
-    position = lax.axis_index("ctx")
-    scale_factor = HD ** (-0.5)
-    inputs = tokens[0].astype(jnp.float32)
-    normed_self, back_self = jax.vjp(root_norm, inputs, gain_self.astype(jnp.float32))
-    normed_low = normed_self.astype(jnp.bfloat16)
-    query_low = forward_product(normed_low, proj_query).astype(jnp.bfloat16)
-    key_low = forward_product(normed_low, proj_key).astype(jnp.bfloat16)
-    value_low = forward_product(normed_low, proj_value).astype(jnp.bfloat16)
+
+    small_names = ("selfnorm", "crossnorm", "feednorm", "outbias", "biastable")
+    small = jnp.concatenate([given[name].reshape(-1) for name in small_names])
+    small = lax.all_gather(small, "wa", axis=0)
+    small_of, start = {}, 0
+    for name in small_names:
+        size = given[name].size
+        small_of[name] = small[:, start : start + size].reshape(-1).astype(F32)
+        start += size
+    bucket_table = small_of["biastable"].reshape(NB, H)
+    full = {name: whole_over_wa(given[name]) for name in UNIT_WEIGHTS}
+    upstream_low = cotangent[0]
+    upstream = upstream_low.astype(F32)
+    upstream_all = lax.all_gather(upstream_low, "wa", axis=0)
+    feed_in = lax.all_to_all(given["feedin"], "wa", 1, 0, tiled=True)
+
+    inputs = tokens[0].astype(F32)
+    normed_self, back_self = jax.vjp(root_norm, inputs, small_of["selfnorm"])
+    normed_low = normed_self.astype(BF)
+    query_low = forward_product(normed_low, full["selfquery"]).astype(BF)
+    key_low = forward_product(normed_low, full["selfkey"]).astype(BF)
+    value_low = forward_product(normed_low, full["selfvalue"]).astype(BF)
     attended_low, attention_state = self_forward(query_low, key_low, value_low, bucket_table)
-    hidden = inputs + forward_product(attended_low, proj_out)
-    normed_cross, back_cross = jax.vjp(root_norm, hidden, gain_cross.astype(jnp.float32))
-    cross_in = normed_cross.astype(jnp.bfloat16)
-    query_cross = forward_product(cross_in, cross_query).astype(jnp.bfloat16)
+    hidden = inputs + forward_product(attended_low, full["selfout"])
+
     spans = neighbours.shape[1]
-    neighbour_rows = neighbours.shape[2] * neighbours.shape[3]
-    flat_neigh = neighbours[0].reshape(spans * neighbour_rows, model_width)
-    keys_cross = (
-        forward_product(flat_neigh, cross_key)
-        .astype(jnp.bfloat16)
-        .reshape(spans, neighbour_rows, attn_width)
-    )
-    values_cross = (
-        forward_product(flat_neigh, cross_value)
-        .astype(jnp.bfloat16)
-        .reshape(spans, neighbour_rows, attn_width)
-    )
-    prev_key, prev_value = passed_along((keys_cross[spans - 1], values_cross[spans - 1]), "ctx", 1)
-    group_keys = jnp.concatenate([prev_key[None], keys_cross], 0).reshape(
-        spans + 1, neighbour_rows, H, HD
-    )
-    group_values = jnp.concatenate([prev_value[None], values_cross], 0).reshape(
-        spans + 1, neighbour_rows, H, HD
-    )
-    padded = jnp.concatenate(
-        [
-            jnp.zeros((1, attn_width), jnp.bfloat16),
-            query_cross,
-            jnp.zeros((SPAN - 1, attn_width), jnp.bfloat16),
-        ],
-        0,
-    ).reshape(spans + 1, SPAN, H, HD)
-    cross_scores = (
-        jnp.einsum("gqhd,gkhd->ghqk", padded, group_keys, preferred_element_type=jnp.float32)
-        * scale_factor
-    )
-    cross_weights = jax.nn.softmax(cross_scores, axis=-1)
-    cross_low = cross_weights.astype(jnp.bfloat16)
-    mixed_rows = jnp.einsum(
-        "ghqk,gkhd->gqhd", cross_low, group_values, preferred_element_type=jnp.float32
-    ).reshape((spans + 1) * SPAN, attn_width)[1 : row_count + 1]
-    keep_mask = jnp.logical_or(position > 0, jnp.arange(row_count) >= SPAN - 1).astype(jnp.float32)[
-        :, None
-    ]
-    mixed_low = (mixed_rows * keep_mask).astype(jnp.bfloat16)
-    hidden_two = hidden + forward_product(mixed_low, cross_out)
-    normed_feed, back_feed = jax.vjp(root_norm, hidden_two, gain_feed.astype(jnp.float32))
-    feed_low = normed_feed.astype(jnp.bfloat16)
-    pre_act = forward_product(feed_low, feed_in) + feed_bias.astype(jnp.float32)
-    activated, back_gelu = jax.vjp(gelu_tanh, pre_act)
-    act_low = activated.astype(jnp.bfloat16)
-    result = hidden_two + forward_product(act_low, feed_out) + out_bias.astype(jnp.float32)
-    upstream_low = cotangent[0]
-    upstream = upstream_low.astype(jnp.float32)
-    grad_outbias = jnp.sum(upstream, axis=0)
-    grad_feedout = outer_product(act_low, upstream_low)
-    (grad_pre,) = back_gelu(back_product(upstream_low, feed_out))
-    grad_feedbias = jnp.sum(grad_pre, axis=0)
-    pre_low = grad_pre.astype(jnp.bfloat16)
-    grad_feedin = outer_product(feed_low, pre_low)
-    grad_two_part, grad_feednorm = back_feed(back_product(pre_low, feed_in))
+    span_rows = neighbours.shape[2] * neighbours.shape[3]
+    own_rows = neighbours[0].reshape(spans * span_rows, model_width)
+    before = passed_along(own_rows[-span_rows:], "ctx", 1)
+    near_rows = jnp.concatenate([before, own_rows], 0)
+    keys_cross = forward_product(near_rows, full["crosskey"]).astype(BF)
+    values_cross = forward_product(near_rows, full["crossvalue"]).astype(BF)
+    normed_cross, back_cross = jax.vjp(root_norm, hidden, small_of["crossnorm"])
+    cross_in = normed_cross.astype(BF)
+    query_cross = forward_product(cross_in, full["crossquery"]).astype(BF)
+    keep = jnp.full((8, WIDE), jnp.where(position > 0, 1.0, 0.0), F32)
+    mixed_low = cross_forward(keep, query_cross, keys_cross, values_cross)
+    hidden_two = hidden + forward_product(mixed_low, full["crossout"])
+
+    normed_feed, back_feed = jax.vjp(root_norm, hidden_two, small_of["feednorm"])
+    feed_low = normed_feed.astype(BF)
+    bias_row = given["feedbias"].astype(F32)[None]
+    fed, grad_feed, fin, fout, bias_sums = ffn(
+        feed_low, upstream_all, feed_in, given["feedout"], bias_row
+    )
+    result = (hidden_two + fed + small_of["outbias"]).astype(BF)
+    grad_two_part, grad_feednorm = back_feed(grad_feed)
     grad_two = upstream + grad_two_part
-    two_low = grad_two.astype(jnp.bfloat16)
-    grad_crossout = outer_product(mixed_low, two_low)
-    grad_mixed = (back_product(two_low, cross_out) * keep_mask).astype(jnp.bfloat16)
-    mixed_pad = jnp.concatenate(
-        [
-            jnp.zeros((1, attn_width), jnp.bfloat16),
-            grad_mixed,
-            jnp.zeros((SPAN - 1, attn_width), jnp.bfloat16),
-        ],
-        0,
-    ).reshape(spans + 1, SPAN, H, HD)
-    grad_cross_weights = jnp.einsum(
-        "gqhd,gkhd->ghqk", mixed_pad, group_values, preferred_element_type=jnp.float32
-    )
-    cross_dscores = cross_weights * (
-        grad_cross_weights - jnp.sum(cross_weights * grad_cross_weights, axis=-1, keepdims=True)
-    )
-    cross_ds_low = (cross_dscores * scale_factor).astype(jnp.bfloat16)
-    grad_query_cross = (
-        jnp.einsum("ghqk,gkhd->gqhd", cross_ds_low, group_keys, preferred_element_type=jnp.float32)
-        .reshape((spans + 1) * SPAN, attn_width)[1 : row_count + 1]
-        .astype(jnp.bfloat16)
-    )
-    grad_group_keys = jnp.einsum(
-        "ghqk,gqhd->gkhd", cross_ds_low, padded, preferred_element_type=jnp.float32
-    ).reshape(spans + 1, neighbour_rows, attn_width)
-    grad_group_values = jnp.einsum(
-        "ghqk,gqhd->gkhd", cross_low, mixed_pad, preferred_element_type=jnp.float32
-    ).reshape(spans + 1, neighbour_rows, attn_width)
-    back_key, back_value = (
-        passed_along(grad_group_keys[0].astype(jnp.bfloat16), "ctx", -1).astype(jnp.float32),
-        passed_along(grad_group_values[0].astype(jnp.bfloat16), "ctx", -1).astype(jnp.float32),
-    )
-    key_grads_low = (
-        jnp.concatenate([grad_group_keys[1:spans], (grad_group_keys[spans] + back_key)[None]], 0)
-        .astype(jnp.bfloat16)
-        .reshape(spans * neighbour_rows, attn_width)
-    )
-    value_grads_low = (
-        jnp.concatenate(
-            [grad_group_values[1:spans], (grad_group_values[spans] + back_value)[None]], 0
-        )
-        .astype(jnp.bfloat16)
-        .reshape(spans * neighbour_rows, attn_width)
-    )
-    grad_crosskey = outer_product(flat_neigh, key_grads_low)
-    grad_crossvalue = outer_product(flat_neigh, value_grads_low)
+    two_low = grad_two.astype(BF)
+
+    grad_mixed = back_product(two_low, full["crossout"]).astype(BF)
+    grad_query_cross, dkeys, dvalues = cross_backward(
+        keep, query_cross, grad_mixed, keys_cross, values_cross
+    )
+    edge = span_rows * spans
+
+    def owned(grads):
+        back = passed_along(grads[:span_rows], "ctx", -1).astype(F32)
+        last = (grads[edge:].astype(F32) + back).astype(BF)
+        return jnp.concatenate([grads[span_rows:edge], last], 0)
+
+    key_grads, value_grads = owned(dkeys), owned(dvalues)
     grad_neigh = (
-        (back_product(key_grads_low, cross_key) + back_product(value_grads_low, cross_value))
-        .astype(jnp.bfloat16)
+        (back_product(key_grads, full["crosskey"]) + back_product(value_grads, full["crossvalue"]))
+        .astype(BF)
         .reshape(neighbours.shape)
     )
-    grad_crossquery = outer_product(cross_in, grad_query_cross)
-    grad_hidden_part, grad_crossnorm = back_cross(back_product(grad_query_cross, cross_query))
+    grad_hidden_part, grad_crossnorm = back_cross(
+        back_product(grad_query_cross, full["crossquery"])
+    )
     grad_hidden = grad_two + grad_hidden_part
-    hidden_low = grad_hidden.astype(jnp.bfloat16)
-    grad_selfout = outer_product(attended_low, hidden_low)
-    dout_low = back_product(hidden_low, proj_out).astype(jnp.bfloat16)
-    dquery_low, dkey_low, dvalue_low, grad_biastable = self_backward(
-        attention_state, dout_low
-    )
-    grad_selfquery = outer_product(normed_low, dquery_low)
-    grad_selfkey = outer_product(normed_low, dkey_low)
-    grad_selfvalue = outer_product(normed_low, dvalue_low)
+    hidden_low = grad_hidden.astype(BF)
+    dout_low = back_product(hidden_low, full["selfout"]).astype(BF)
+    dquery_low, dkey_low, dvalue_low, grad_biastable = self_backward(attention_state, dout_low)
     grad_normed = (
-        back_product(dquery_low, proj_query)
-        + back_product(dkey_low, proj_key)
-        + back_product(dvalue_low, proj_value)
+        back_product(dquery_low, full["selfquery"])
+        + back_product(dkey_low, full["selfkey"])
+        + back_product(dvalue_low, full["selfvalue"])
     )
     grad_input_part, grad_selfnorm = back_self(grad_normed)
-    grad_inputs = (grad_hidden + grad_input_part).astype(jnp.bfloat16)
-    shares = (
-        lax.psum_scatter(
-            grad_selfnorm.astype(jnp.bfloat16), "wa", scatter_dimension=0, tiled=True
-        ).astype(jnp.float32),
-        lax.psum_scatter(
-            grad_selfquery.astype(jnp.bfloat16), "wa", scatter_dimension=0, tiled=True
-        ).astype(jnp.float32),
-        lax.psum_scatter(
-            grad_selfkey.astype(jnp.bfloat16), "wa", scatter_dimension=0, tiled=True
-        ).astype(jnp.float32),
-        lax.psum_scatter(
-            grad_selfvalue.astype(jnp.bfloat16), "wa", scatter_dimension=0, tiled=True
-        ).astype(jnp.float32),
-        lax.psum_scatter(
-            grad_selfout.astype(jnp.bfloat16), "wa", scatter_dimension=0, tiled=True
-        ).astype(jnp.float32),
-        lax.psum_scatter(
-            grad_biastable.astype(jnp.bfloat16), "wa", scatter_dimension=0, tiled=True
-        ).astype(jnp.float32),
-        lax.psum_scatter(
-            grad_crossnorm.astype(jnp.bfloat16), "wa", scatter_dimension=0, tiled=True
-        ).astype(jnp.float32),
-        lax.psum_scatter(
-            grad_crossquery.astype(jnp.bfloat16), "wa", scatter_dimension=0, tiled=True
-        ).astype(jnp.float32),
-        lax.psum_scatter(
-            grad_crosskey.astype(jnp.bfloat16), "wa", scatter_dimension=0, tiled=True
-        ).astype(jnp.float32),
-        lax.psum_scatter(
-            grad_crossvalue.astype(jnp.bfloat16), "wa", scatter_dimension=0, tiled=True
-        ).astype(jnp.float32),
-        lax.psum_scatter(
-            grad_crossout.astype(jnp.bfloat16), "wa", scatter_dimension=0, tiled=True
-        ).astype(jnp.float32),
-        lax.psum_scatter(
-            grad_feednorm.astype(jnp.bfloat16), "wa", scatter_dimension=0, tiled=True
-        ).astype(jnp.float32),
-        lax.psum_scatter(
-            grad_feedin.astype(jnp.bfloat16), "wa", scatter_dimension=0, tiled=True
-        ).astype(jnp.float32),
-        lax.psum_scatter(
-            grad_feedbias.astype(jnp.bfloat16), "wa", scatter_dimension=0, tiled=True
-        ).astype(jnp.float32),
-        lax.psum_scatter(
-            grad_feedout.astype(jnp.bfloat16), "wa", scatter_dimension=0, tiled=True
-        ).astype(jnp.float32),
-        lax.psum_scatter(
-            grad_outbias.astype(jnp.bfloat16), "wa", scatter_dimension=0, tiled=True
-        ).astype(jnp.float32),
-    )
-    totals = lax.psum(
-        (
-            shares[0],
-            shares[1],
-            shares[2],
-            shares[3],
-            shares[4],
-            shares[5],
-            shares[6],
-            shares[7],
-            shares[8],
-            shares[9],
-            shares[10],
-            shares[11],
-            shares[12],
-            shares[13],
-            shares[14],
-            shares[15],
-        ),
-        "ctx",
-    )
+    grad_inputs = (grad_hidden + grad_input_part).astype(BF)
+
+    pairs = {
+        "cq": (cross_in, grad_query_cross),
+        "ck": (own_rows, key_grads),
+        "cv": (own_rows, value_grads),
+        "co": (mixed_low, two_low),
+        "q": (normed_low, dquery_low),
+        "k": (normed_low, dkey_low),
+        "v": (normed_low, dvalue_low),
+        "so": (attended_low, hidden_low),
+    }
+    parts = [outer_product(*pairs[name]).astype(BF) for name in UNITS]
+    if peers == RING:
+        grads = unfold(dict(zip(NAMES, reduce_grads(parts, fin, fout), strict=True)))
+    else:
+        grads = reduce_plain(parts, fin, fout)
+
+    wa, owners = lax.axis_index("wa"), lax.axis_size("wa")
+    bias_grad = jnp.sum(bias_sums, axis=0)
+    placed = lax.dynamic_update_slice(
+        jnp.zeros((owners, bias_grad.size), F32), bias_grad[None], (wa, 0)
+    )
+    sums = [grad_selfnorm, grad_crossnorm, grad_feednorm, jnp.sum(upstream, axis=0), grad_biastable]
+    packed = jnp.concatenate([*(v.reshape(owners, -1) for v in sums), placed], axis=1)
+    packed = lax.psum(packed, ("ctx", "wa"))
+    mine = lax.dynamic_index_in_dim(packed, wa, 0, keepdims=False)
+    cuts, start = [], 0
+    for v in (*sums, placed):
+        cuts.append(mine[start : start + v.size // owners])
+        start += v.size // owners
+    own_selfnorm, own_crossnorm, own_feednorm, own_outbias, own_table, own_feedbias = cuts
     return (
-        result.astype(jnp.bfloat16)[None],
+        result[None],
         grad_inputs[None],
         grad_neigh,
-        totals[0],
-        totals[1],
-        totals[2],
-        totals[3],
-        totals[4],
-        totals[5],
-        totals[6],
-        totals[7],
-        totals[8],
-        totals[9],
-        totals[10],
-        totals[11],
-        totals[12],
-        totals[13],
-        totals[14],
-        totals[15],
+        own_selfnorm,
+        grads["q"],
+        grads["k"],
+        grads["v"],
+        grads["so"],
+        own_table.reshape(-1, H),
+        own_crossnorm,
+        grads["cq"],
+        grads["ck"],
+        grads["cv"],
+        grads["co"],
+        own_feednorm,
+        grads["fin"],
+        own_feedbias,
+        grads["fout"],
+        own_outbias,
     )
 
 

time: 1370 us -> 678 us (0.49)
  blocking collectives: 572 us -> 80.8 us
  Pallas kernels: 117 us -> 371 us
  waiting for transfers between devices: 300 us -> 84.5 us
  matrix products: 215 us -> 58.1 us
  local copies, waits for them, and re-layouts: 114 us -> 30.3 us
    psum x1, blocking collectives: 542 us -> 56.2 us  [per_device(): packed = lax.psum(packed, ('ctx', 'wa'))]
    pallas_call x0 -> x4, Pallas kernels: none -> 258 us  [the longest x1 187 us: reduce_grads(): pl.pallas_call(reduce_kernel, out_shape=tuple((jax.ShapeDtypeStruct((RING...]
    reduce_scatter x8 -> x0, waiting for transfers between devices: 137 us -> none  [the longest x1 61.8 us: per_device(): lax.psum_scatter(grad_feedout.astype(jnp.bfloat16), 'wa', scatter_dimensi...]
    dot_general x6 -> x0, matrix products: 107 us -> none  [the longest x1 34 us: per_device(): jnp.einsum('ghqk,gqhd->gkhd', cross_ds_low, padded, preferred_element_typ...]
    unnamed x22 -> x9, waiting for transfers between devices: 69.8 us -> 5.71 us
    concatenate x6 -> x2, local copies, waits for them, and re-layouts: 26.2 us -> 0.19 us  [the longest x1 0.1 us: per_device(): jnp.concatenate([*(v.reshape(owners, -1) for v in sums), placed], axis=1)]
    dot_general x10 -> x8, matrix products: 39.5 us -> 18.7 us  [outer_product(): lax.dot_general(left_side, right_side, (((0,), (0,)), ((), ())), preferre...]
    unnamed x2 -> x0, blocking collectives: 20 us -> none
  transfers between devices with their start and end apart: 24 -> 13, of which waited for: 12 -> 6; matrix products, arithmetic and copies ran while one was open for 19% -> 7% of each run, Pallas kernels for 4% -> 9%
where the time goes in v2:
time: 678 us; the launch traced here: 669 us
  Pallas kernels  371 us (55%)
  waiting for transfers between devices  84.5 us (12%)
  blocking collectives  80.8 us (12%)
  matrix products  58.1 us (9%)
  local copies, waits for them, and re-layouts  30.3 us (4%)
  other arithmetic  16.5 us (2%)
  between operations  15 us (2%)
  starting transfers between devices  12.5 us (2%)
    pallas_call x1, Pallas kernels, reduce_grads(): pl.pallas_call(reduce_kernel, out_shape=tuple((jax.ShapeDtypeStruct((RING...  187 us
    pallas_call x1, Pallas kernels, attn_backward(): pl.pallas_call(functools.partial(attn_backward_kernel, n), out_shape=(gra...  64.8 us
    all_gather x8, waiting for transfers between devices, whole_over_wa(): return lax.all_gather(shard, 'wa', axis=0, tiled=True)  60.4 us
    psum x1, blocking collectives, per_device(): packed = lax.psum(packed, ('ctx', 'wa'))  56.2 us
    pallas_call x1, Pallas kernels, attn_forward(): pl.pallas_call(functools.partial(attn_forward_kernel, n), out_shape=(jax....  48 us
    pallas_call x1, Pallas kernels, ffn(): pl.pallas_call(ffn_kernel, out_shape=(jax.ShapeDtypeStruct(block, F32), j...  44.1 us
    dot_general x8, matrix products, forward_product(): return jnp.dot(values, weight, preferred_element_type=jnp.float32)  26.9 us
    all_gather x1, blocking collectives, per_device(): small = lax.all_gather(small, 'wa', axis=0)  24.7 us
  transfers between devices with their start and end apart: 13, of which 6 were waited for; matrix products, arithmetic and copies ran while one was open for 7% of the time, Pallas kernels for 9%

profile of v2, /device:TPU:0, one launch (start us, length us, event | category | flops | bytes accessed | tf_op | source)
XLA Modules:
  0.0 668.7 jit_solution(13700277143628353661)
XLA Ops:
  13.7 4.9 collective-permute-start
  20.0 4.5 all-to-all-start
  25.4 24.7 %all-gather = bf16[4096]{0:T(1024)(128)(2,1)S(1)} all-gather(bf16[1024]{0:T(1024)(128)(2,1)S(1)} %concatenate.15), channel_id=2, replica_groups=mesh['ctx'=8,'wa'=4] {'wa'}, dimensions={0}, use_global_device_ids=true | all-gather | bytes 10240 | tf_op jit(solution)/shard_map/all_gather | solution.py:1246
  52.2 2.3 convolution_convert_fusion.13.q_ref
  54.4 8.1 %all-gather.13.cloned.1.call-done = bf16[896,1024]{1,0:T(8,128)(2,1)} async-done(((bf16[224,1024]{1,0:T(8,128)(2,1)}), bf16[896,1024]{1,0:T(8,128)(2,1)}) %all-gather.13.cloned.1.call-update) | async-done | bytes 1835024 | tf_op jit(solution)/shard_map/all_gather | solution.py:1223
  62.6 2.3 convolution_convert_fusion.12.k_ref
  64.8 20.5 %all-gather.15.cloned.1.call-done = bf16[896,1024]{1,0:T(8,128)(2,1)} async-done(((bf16[224,1024]{1,0:T(8,128)(2,1)}), bf16[896,1024]{1,0:T(8,128)(2,1)}) %all-gather.15.cloned.1.call-update) | async-done | bytes 1835024 | tf_op jit(solution)/shard_map/all_gather | solution.py:1223
  85.3 2.3 convolution_convert_fusion.11.v_ref
  87.6 48.0 %attn_forward.1 = (bf16[256,1024]{1,0:T(8,128)(2,1)S(1)}, bf16[2048,128]{1,0:T(8,128)(2,1)S(1)}, bf16[2048,128]{1,0:T(8,128)(2,1)S(1)}, bf16[2048,128]{1,0:T(8,1...) custom-call(bf16[256,1024]{1,0:T(8,128)(2,1)S(1)} %convolution_convert_fusion.13.q_ref, ...), custom_call_target="tpu_custom_call" | custom-call | tf_op jit(solution)/shard_map/attn_forward/pallas_call | solution.py:376
  138.9 3.6 multiply_reduce_fusion.5
  142.5 5.0 convolution_convert_fusion.1.k_ref
  147.5 5.6 all-gather.23.cloned.1.call-done
  153.1 6.4 convolution_convert_fusion.v_ref
  159.5 16.4 %all-gather.19.cloned.1.call-done = bf16[896,1024]{1,0:T(8,128)(2,1)} async-done(((bf16[224,1024]{1,0:T(8,128)(2,1)}), bf16[896,1024]{1,0:T(8,128)(2,1)}) %all-gather.19.cloned.1.call-update) | async-done | bytes 1835024 | tf_op jit(solution)/shard_map/all_gather | solution.py:1223
  175.9 2.7 convolution_convert_fusion.10.q_ref
  178.6 9.5 %cross_forward.1 = bf16[256,1024]{1,0:T(8,128)(2,1)S(1)} custom-call(f32[8,128]{1,0:T(8,128)S(1)} %broadcast_in_dim.53.keep_ref, bf16[256,1024]{1,0:T(8,128)(2,1)S(1)} %convolution_convert_fusion.10.q_ref, bf16[1280,1024]{1,0:T(8,128)(2,1)S(1)} %convolution_convert_fusion.1.k_ref, bf16[1280,1024]{1,0:T(8,128)(2,1)S(1)} %copy-done), custom_call_target="tpu_custom_call" | custom-call | tf_op jit(solution)/shard_map/cross_forward/pallas_call | solution.py:1155
  188.9 9.8 %all-gather.25.cloned.1.call-done = bf16[1024,896]{1,0:T(8,128)(2,1)} async-done(((bf16[256,896]{1,0:T(8,128)(2,1)}), bf16[1024,896]{1,0:T(8,128)(2,1)}) %all-gather.25.cloned.1.call-update) | async-done | bytes 1835024 | tf_op jit(solution)/shard_map/all_gather | solution.py:1223
  198.7 2.5 multiply_reduce_fusion.4
  203.1 18.3 %all-gather.27.cloned.1.call-done.cot_ref = bf16[4,256,896]{2,1,0:T(8,128)(2,1)} async-done(((bf16[1,256,896]{2,1,0:T(8,128)(2,1)}), bf16[4,256,896]{2,1,0:T(8,128)(2,1)}) %all-gather.27.cloned.1.call-update) | async-done | bytes 1835024 | tf_op jit(solution)/shard_map/all_gather | solution.py:1256
  221.4 44.1 %feed_forward.1 = (f32[256,896]{1,0:T(8,128)}, f32[256,896]{1,0:T(8,128)}, bf16[896,896]{1,0:T(8,128)(2,1)}, bf16[896,896]{1,0:T(8,128)(2,1)}, f32[8,896]{1,0:T(8,128)}) custom-call(bf16[256,896]{1,0:T(8,128)(2,1)} %multiply_convert_fusion.f_ref, bf16[4,256,896]{2,1,0:T(8,128)(2,1)} %all-gather.27.cloned.1.call-done.cot_ref, ...), custom_call_target="tpu_custom_call" | custom-call | tf_op jit(solution)/shard_map/feed_forward/pallas_call | solution.py:1086
  267.1 2.4 fusion.5
  271.4 17.3 %cross_backward.1 = (bf16[256,1024]{1,0:T(8,128)(2,1)S(1)}, bf16[1280,1024]{1,0:T(8,128)(2,1)S(1)}, bf16[1280,1024]{1,0:T(8,128)(2,1)S(1)}) custom-call(f32[8,128]{1,0:T(8,128)S(1)} %broadcast_in_dim.53.keep_ref, bf16[256,1024]{1,0:T(8,128)(2,1)S(1)} %copy-done.3, bf16[256,1024]{1,0:T(8,128)(2,1)S(1)} %convolution_convert_fusion.9.dx_ref, ...), custom_call_target="tpu_custom_call" | custom-call | tf_op jit(solution)/shard_map/cross_backward/pallas_call | solution.py:1194
  301.3 64.8 %attn_backward.1 = (bf16[256,1024]{1,0:T(8,128)(2,1)S(1)}, bf16[256,1024]{1,0:T(8,128)(2,1)S(1)}, bf16[256,1024]{1,0:T(8,128)(2,1)S(1)}, f32[8,1024]{1,0:T(8,128)S(1)}) custom-call(bf16[256,1024]{1,0:T(8,128)(2,1)S(1)} %convolution_convert_fusion.8.do_ref, bf16[2048,128]{1,0:T(8,128)(2,1)S(1)} %copy-done.13, bf16[2048,128]{1,0:T(8,128)(2,1)S(1)} %copy-done.15, ...), custom_call_target="tpu_custom_call" | custom-call | tf_op jit(solution)/shard_map/attn_backward/pallas_call | solution.py:537
  366.0 2.0 convolution_convert_fusion.5.refs_4_
  381.0 56.2 %psum.7 = f32[4,1920]{1,0:T(4,128)S(1)} all-reduce(f32[4,1920]{1,0:T(4,128)S(1)} %concatenate.19), channel_id=1, replica_groups=mesh['ctx'=8,'wa'=4] {'ctx','wa'}, use_global_device_ids=true, to_apply=%region_12.13 | all-reduce | flops 7680 | bytes 61440 | tf_op jit(solution)/shard_map/psum | solution.py:1348
  439.3 2.2 fusion.12
  445.0 3.3 convert_bitcast_fusion.2.refs_1_
  449.7 3.3 convert_bitcast_fusion.1.refs_2_
  453.1 187.4 %reduce_grads.1 = (bf16[8,112,896]{2,1,0:T(8,128)(2,1)}, bf16[8,112,896]{2,1,0:T(8,128)(2,1)}, bf16[8,448,128]{2,1,0:T(8,128)(2,1)}, bf16[8,224,128]{2,1,0:T(8,1...) custom-call(bf16[896,1024]{1,0:T(8,128)(2,1)} %convolution_convert_f, ...), custom_call_target="tpu_custom_call" | custom-call | tf_op jit(solution)/shard_map/reduce_grads/pallas_call | solution.py:943
  649.0 2.3 copy.74
  655.7 2.4 fusion
  658.0 3.7 add_convert_fusion
  (213 shorter events, 65.1 us)
Async XLA Ops:
  7.2 45.0 %all-gather.11.cloned.1.call-start = ((), (), s32[]{:S(2)}) async-start(), calls=%async_computation.1 | async-start | bytes 2293760 | tf_op jit(solution)/shard_map/all_gather | solution.py:1223
  7.9 54.7 %all-gather.13.cloned.1.call-start = ((), (), s32[]{:S(2)}) async-start(), calls=%async_computation.2 | async-start | bytes 2293760 | tf_op jit(solution)/shard_map/all_gather | solution.py:1223
  8.7 10.0 %copy-start.32 = (bf16[224,3584]{1,0:T(8,128)(2,1)S(1)}, bf16[224,3584]{1,0:T(8,128)(2,1)}, u32[]{:S(2)}) copy-start(bf16[224,3584]{1,0:T(8,128)(2,1)} %param.34) | copy-start | bytes 4816900
  8.7 76.6 %all-gather.15.cloned.1.call-start = ((), (), s32[]{:S(2)}) async-start(), calls=%async_computation.3 | async-start | bytes 2293760 | tf_op jit(solution)/shard_map/all_gather | solution.py:1223
  9.4 129.5 %all-gather.17.cloned.1.call-start = ((), (), s32[]{:S(2)}) async-start(), calls=%async_computation.4 | async-start | bytes 2293760 | tf_op jit(solution)/shard_map/all_gather | solution.py:1223
  10.0 132.5 %all-gather.21.cloned.1.call-start = ((), (), s32[]{:S(2)}) async-start(), calls=%async_computation.6 | async-start | bytes 2293760 | tf_op jit(solution)/shard_map/all_gather | solution.py:1223
  10.6 142.5 %all-gather.23.cloned.1.call-start = ((), (), s32[]{:S(2)}) async-start(), calls=%async_computation.7 | async-start | bytes 2293760 | tf_op jit(solution)/shard_map/all_gather | solution.py:1223
  11.2 164.7 %all-gather.19.cloned.1.call-start = ((), (), s32[]{:S(2)}) async-start(), calls=%async_computation.5 | async-start | bytes 2293760 | tf_op jit(solution)/shard_map/all_gather | solution.py:1223
  11.9 186.8 %all-gather.25.cloned.1.call-start = ((), (), s32[]{:S(2)}) async-start(), calls=%async_computation.8 | async-start | bytes 2293760 | tf_op jit(solution)/shard_map/all_gather | solution.py:1223
  13.7 128.8 %collective-permute-start = (bf16[256,896]{1,0:T(8,128)(2,1)S(1)}, bf16[256,896]{1,0:T(8,128)(2,1)S(1)}, u32[]{:S(2)}, u32[]{:S(2)}) collective-permute-start(bf16[256,896]{1,0:T(8,128)(2,1)S(1)} %bitcast.139), channel_id=1, source_target_pairs={{0,4},{4,8},{8,12},{12,16},{16,20},{20,24},{24,28},{1,5},{5,9},{9,... | collective-permute-start | bytes 1376264 | tf_op jit(solution)/shard_map/ppermute | solution.py:32
  19.9 5.3 copy-start.47
  19.9 5.4 copy-start.49
  19.9 5.4 copy-start.50
  19.9 5.4 copy-start.51
  19.9 5.4 copy-start.52
  19.9 30.3 %copy-start.26 = (bf16[1,256,896]{2,1,0:T(8,128)(2,1)S(1)}, bf16[1,256,896]{2,1,0:T(8,128)(2,1)}, u32[]{:S(2)}) copy-start(bf16[1,256,896]{2,1,0:T(8,128)(2,1)} %param.21) | copy-start | bytes 1376260
  20.0 30.4 %copy-start.19 = (bf16[1,256,896]{2,1,0:T(8,128)(2,1)S(1)}, bf16[1,256,896]{2,1,0:T(8,128)(2,1)}, u32[]{:S(2)}) copy-start(bf16[1,256,896]{2,1,0:T(8,128)(2,1)} %param.19) | copy-start | bytes 1376260
  20.0 31.4 %copy-start.48 = (bf16[896]{0:T(1024)(128)(2,1)S(1)}, bf16[896]{0:T(1024)(128)(2,1)}, u32[]{:S(2)}) copy-start(bf16[896]{0:T(1024)(128)(2,1)} %param.35) | copy-start | bytes 5380
  20.0 183.1 %all-to-all-start = ((bf16[224,4,896]{2,0,1:T(8,128)(2,1)}), bf16[224,4,896]{2,0,1:T(8,128)(2,1)}, u32[]{:S(2)}, u32[]{:S(2)}) async-start(bf16[224,4,896]{2,0,1:T(8,128)(2,1)} %bitcast.120), calls=%async_computation | async-start | bytes 3211264 | tf_op jit(solution)/shard_map/all_to_all | solution.py:1257
  24.5 197.0 %all-gather.27.cloned.1.call-start = ((), (), s32[]{:S(2)}) async-start(), calls=%async_computation.9 | async-start | bytes 2293760 | tf_op jit(solution)/shard_map/all_gather | solution.py:1256
  138.9 3.6 copy-start.6
  221.4 44.1 %copy-start.22 = (f32[256,896]{1,0:T(8,128)S(1)}, f32[256,896]{1,0:T(8,128)}, u32[]{:S(2)}) copy-start(f32[256,896]{1,0:T(8,128)} %copy-done.21) | copy-start | bytes 2752516
  288.7 3.5 copy-start.5
  288.7 6.8 %copy-start.8 = (bf16[256,1024]{1,0:T(8,128)(2,1)}, bf16[256,1024]{1,0:T(8,128)(2,1)S(1)}, u32[]{:S(2)}) copy-start(bf16[256,1024]{1,0:T(8,128)(2,1)S(1)} %get-tuple-element.48) | copy-start | bytes 1572868
  300.4 65.7 %copy-start.20 = (bf16[1,256,896]{2,1,0:T(8,128)(2,1)S(1)}, bf16[1,256,896]{2,1,0:T(8,128)(2,1)}, u32[]{:S(2)}) copy-start(bf16[1,256,896]{2,1,0:T(8,128)(2,1)} %param.19) | copy-start | bytes 1376260
  375.1 5.7 copy-start.46
  376.9 64.6 %copy-start.9 = (bf16[256,1024]{1,0:T(8,128)(2,1)S(1)}, bf16[256,1024]{1,0:T(8,128)(2,1)}, u32[]{:S(2)}) copy-start(bf16[256,1024]{1,0:T(8,128)(2,1)} %copy-done.8) | copy-start | bytes 1572868
  376.9 71.4 %collective-permute-start.2 = (bf16[256,1024]{1,0:T(8,128)(2,1)}, bf16[256,1024]{1,0:T(8,128)(2,1)}, u32[]{:S(2)}, u32[]{:S(2)}) collective-permute-start(bf16[256,1024]{1,0:T(8,128)(2,1)} %slice.107), channel_id=1, source_target_pairs={{4,0},{8,4},{12,8},{16,12},{20,16},{24,20},{28,24},{5,1},{9,5},{13... | collective-permute-start | bytes 1572872 | tf_op jit(solution)/shard_map/ppermute | solution.py:32
  378.4 65.2 %collective-permute-start.1 = (bf16[256,1024]{1,0:T(8,128)(2,1)}, bf16[256,1024]{1,0:T(8,128)(2,1)}, u32[]{:S(2)}, u32[]{:S(2)}) collective-permute-start(bf16[256,1024]{1,0:T(8,128)(2,1)} %slice.104), channel_id=1, source_target_pairs={{4,0},{8,4},{12,8},{16,12},{20,16},{24,20},{28,24},{5,1},{9,5},{13... | collective-permute-start | bytes 1572872 | tf_op jit(solution)/shard_map/ppermute | solution.py:32
  441.5 3.4 copy-start.35
  441.5 3.4 copy-start.45
  445.0 4.8 copy-start.36
  (36 other events, 65.4 us)
Sparse Core Ops, SparseCore 0:
  9.6 28.1 all-gather.10
  39.3 23.2 all-gather.12
  64.1 21.1 all-gather.14
  86.7 21.1 all-gather.16
  109.3 21.0 all-gather.20
  131.9 21.1 all-gather.22
  154.6 21.2 all-gather.18
  177.4 21.2 all-gather.24
  200.3 21.1 all-gather.26

commit v3 on v1

v3 whole, which is shorter than its diff:
```python
import functools
import math

import jax
import jax.numpy as jnp
from jax import lax
from jax.experimental import pallas as pl
from jax.experimental.pallas import tpu as pltpu
from jax.sharding import PartitionSpec as P

H = 16
HD = 64
NB = 32
MAXD = 128
BLOCK = 256
SPAN = 64
MESH = pl.DeviceIdType.MESH
WIDE = 128
LINE = 1024
BF = jnp.bfloat16
F32 = jnp.float32


epsilon = 1e-06
negative = -1e30
strongest_precision = lax.Precision.HIGHEST


def passed_along(value, axis, by):
    peers = lax.axis_size(axis)
    pairs = [(i, i + by) for i in range(peers) if 0 <= i + by < peers]
    return lax.ppermute(value, axis, pairs)


def from_behind(block, axis, distance):
    devices = range(lax.axis_size(axis))
    route = [((i - distance) % len(devices), i) for i in devices]
    return lax.ppermute(block, axis, route)


def bucket_edges():
    half_count = NB // 2
    exact_part = half_count // 2
    edge_list = []
    for level_index in range(exact_part + 1, half_count):
        hits = [
            distance_now
            for distance_now in range(exact_part, MAXD + 1)
            if exact_part
            + int(
                math.log(distance_now / exact_part)
                / math.log(MAXD / exact_part)
                * (half_count - exact_part)
            )
            >= level_index
        ]
        edge_list.append(min(hits + [MAXD]))
    return (half_count, exact_part, edge_list)


def bucket_of(offset_value):
    half_count, exact_part, edge_list = bucket_edges()
    magnitude = jnp.abs(offset_value)
    far_part = exact_part + sum(
        [(magnitude >= edge_value).astype(magnitude.dtype) for edge_value in edge_list],
        jnp.zeros_like(magnitude),
    )
    return jnp.where(offset_value > 0, half_count, 0) + jnp.where(
        magnitude < exact_part, magnitude, far_part
    )


def root_norm(values, gain_vector):
    return (
        values
        * lax.rsqrt(jnp.mean(values * values, axis=-1, keepdims=True) + epsilon)
        * gain_vector
    )


def gelu_tanh(values):
    return jax.nn.gelu(values, approximate=True)


def forward_product(values, weight):
    return jnp.dot(values, weight, preferred_element_type=jnp.float32)


def outer_product(left_side, right_side):
    return lax.dot_general(
        left_side, right_side, (((0,), (0,)), ((), ())), preferred_element_type=jnp.float32
    )


def back_product(grad_low, weight):
    return lax.dot_general(
        grad_low, weight, (((1,), (1,)), ((), ())), preferred_element_type=jnp.float32
    )


def make_bias(bucket_bias_rows, row_count):
    query_place = jnp.arange(row_count)[:, None]
    key_place = jnp.arange(row_count)[None, :]
    levels = jnp.arange(NB)
    current_bucket_selector = (
        bucket_of(key_place - query_place)[None] == levels[:, None, None]
    ).astype(jnp.float32)
    previous_bucket_selector = (
        bucket_of(key_place - row_count - query_place)[None] == levels[:, None, None]
    ).astype(jnp.float32)
    onehot_far = (bucket_of(jnp.array(-MAXD, jnp.int32)) == levels).astype(jnp.float32)
    current_block_bias = jnp.einsum(
        "smz,sj->jmz", current_bucket_selector, bucket_bias_rows, precision=strongest_precision
    )
    previous_block_bias = jnp.einsum(
        "smz,sj->jmz", previous_bucket_selector, bucket_bias_rows, precision=strongest_precision
    )
    bias_far = jnp.dot(onehot_far, bucket_bias_rows, precision=strongest_precision)
    mask_same = key_place // BLOCK <= query_place // BLOCK
    return (
        (current_block_bias, previous_block_bias, bias_far, mask_same),
        (current_bucket_selector, previous_bucket_selector, onehot_far),
    )


def pair_scores(query_heads, key_heads, relation, bias_set, scale_factor):
    current_block_bias, previous_block_bias, bias_far, mask_same = bias_set
    raw_scores = jnp.einsum(
        "qhd,khd->hqk", query_heads, key_heads, preferred_element_type=jnp.float32
    )
    bias_rows = jnp.where(
        relation == 0,
        current_block_bias,
        jnp.where(relation == 1, previous_block_bias, bias_far[:, None, None]),
    )
    allowed = jnp.logical_or(relation > 0, mask_same)
    return jnp.where(allowed[None], raw_scores * scale_factor + bias_rows, negative)


def pair_core(
    query_heads,
    dout_heads,
    log_total,
    row_delta,
    key_heads,
    value_heads,
    relation,
    bias_set,
    scale_factor,
):
    scores = pair_scores(query_heads, key_heads, relation, bias_set, scale_factor)
    weights_now = jnp.exp(scores - log_total[:, :, None])
    grad_weights = jnp.einsum(
        "qhd,khd->hqk", dout_heads, value_heads, preferred_element_type=jnp.float32
    )
    dscores = weights_now * (grad_weights - row_delta[:, :, None])
    return (weights_now, dscores, (dscores * scale_factor).astype(jnp.bfloat16))


def add_tables(relative_bias_tables, dscores, relation):
    same_sum, prev_sum, far_sum = relative_bias_tables
    return (
        same_sum + jnp.where(relation == 0, dscores, 0.0),
        prev_sum + jnp.where(relation == 1, dscores, 0.0),
        far_sum + jnp.where(relation >= 2, jnp.sum(dscores, axis=(1, 2)), 0.0),
    )


def forward_fold(query_heads, position, row_count, bias_set, scale_factor, running, pieces):
    keys_all, values_all = pieces

    def one_shard(folded, shard_step):
        key_heads = lax.dynamic_slice_in_dim(
            keys_all, shard_step * row_count, row_count, 0
        ).reshape(row_count, H, HD)
        value_heads = lax.dynamic_slice_in_dim(
            values_all, shard_step * row_count, row_count, 0
        ).reshape(row_count, H, HD)
        relation = position - shard_step

        def one_compute(current):
            running_max, running_sum, running_acc = current
            scores = pair_scores(query_heads, key_heads, relation, bias_set, scale_factor)
            new_max = jnp.maximum(running_max, jnp.max(scores, axis=-1))
            factor = jnp.exp(running_max - new_max)
            weights_now = jnp.exp(scores - new_max[:, :, None])
            new_sum = running_sum * factor + jnp.sum(weights_now, axis=-1)
            update = jnp.einsum(
                "hqk,khd->qhd",
                weights_now.astype(jnp.bfloat16),
                value_heads,
                preferred_element_type=jnp.float32,
            )
            scaled = running_acc.reshape(row_count, H, HD) * factor.T[:, :, None]
            return (new_max, new_sum, (scaled + update).reshape(row_count, H * HD))

        return (lax.cond(relation >= 0, one_compute, lambda unchanged: unchanged, folded), None)

    running, unused = lax.scan(one_shard, running, jnp.arange(keys_all.shape[0] // row_count))
    return running


def nt_dot(left, right):
    return lax.dot_general(left, right, (((1,), (1,)), ((), ())), preferred_element_type=F32)


def nn_dot(left, right):
    return jnp.dot(left, right, preferred_element_type=F32)


def meet(neighbours):
    barrier = pltpu.get_barrier_semaphore()
    for who in neighbours:
        pl.semaphore_signal(barrier, inc=1, device_id=who, device_id_type=MESH)
    pl.semaphore_wait(barrier, len(neighbours))


def ctx_peers(n):
    me = lax.axis_index("ctx")
    return [{"ctx": lax.rem(me + d, n)} for d in range(1, n)]


def other_wa(me, bit):
    flipped = lax.rem(me // bit, 2)
    return me + bit - 2 * bit * flipped


def remote(src, dst, send_sem, recv_sem, **device):
    return pltpu.make_async_remote_copy(
        src_ref=src,
        dst_ref=dst,
        send_sem=send_sem,
        recv_sem=recv_sem,
        device_id=device,
        device_id_type=MESH,
    )


RING = 8
HOPS = RING - 1


def ring_place(n):
    me = lax.axis_index("ctx")
    half = n // 2

    def at(place):
        return jnp.where(place < half, 2 * place, 2 * (n - 1 - place) + 1)

    place = jnp.where(lax.rem(me, 2) == 0, me // 2, n - 1 - me // 2)
    return place, at(lax.rem(place + 1, n)), at(lax.rem(place + n - 1, n))


class Ring:
    def __init__(self, lanes, send, recv, share=None, hold=None, full=None):
        self.lanes, self.share, self.hold, self.full = lanes, share, hold, full
        self.sems = send, recv
        self.place, self.after, self.before = ring_place(RING)

    def copy(self, lane, src, dst, step):
        send, recv = self.sems
        way = self.lanes[lane][1]
        return remote(
            src, dst, send.at[lane, step], recv.at[lane, step], ctx=self.after if way == 1 else self.before
        )

    def chunk(self, lane, offset):
        here = self.place if self.lanes[lane][1] == 1 else RING - self.place
        return lax.rem(here + offset + 2 * RING, RING)

    def scatter(self, step, which):
        for lane in which:
            b, _, rows = self.lanes[lane]
            share = self.share.at[b, self.chunk(lane, -step), rows]

            @pl.when(step > 0)
            def _():
                there = self.hold.at[b, jnp.maximum(step - 1, 0), rows]
                self.copy(lane, share, there, jnp.maximum(step - 1, 0)).wait_recv()
                share[...] = (share[...].astype(F32) + there[...].astype(F32)).astype(BF)

            @pl.when(step < HOPS)
            def _():
                there = jnp.minimum(step, HOPS - 1)
                self.copy(lane, share, self.hold.at[b, there, rows], there).start()

    def gather(self, step, which):
        for lane in which:
            b, _, rows = self.lanes[lane]
            full = self.full[b].at[self.chunk(lane, 1 - step), rows]

            @pl.when(step > 0)
            def _():
                self.copy(lane, full, full, jnp.maximum(step - 1, 0)).wait_recv()

            @pl.when(step < HOPS)
            def _():
                self.copy(lane, full, full, jnp.minimum(step, HOPS - 1)).start()

    def finish(self, part):
        def one(step, unused):
            for lane in range(len(self.lanes)):
                self.copy(lane, part(lane), part(lane), step).wait_send()
            return unused

        lax.fori_loop(0, HOPS, one, 0)


TALL, FLAT = (224, 1024), (256, 896)
EARLY = ("cq", "ck", "cv", "co", "so")
LATE = ("q", "k", "v")
FEED = (8, 112, 896)
FEED_LANES = (
    (0, 1, slice(0, 64)),
    (1, -1, slice(0, 64)),
    (0, 1, slice(64, 112)),
    (1, -1, slice(64, 112)),
)
FEED_TURNS = ((0, 1), (2, 3))


class Folding:
    def __init__(self, names, parts, scratch):
        self.names = names
        self.parts = parts
        tall, flat, sems = scratch
        self.sets = {TALL: tall, FLAT: flat}
        self.own_sem, self.core_send, self.core_recv, self.x_send, self.x_recv = sems
        self.wa = lax.axis_index("wa")
        self.mate, self.across = other_wa(self.wa, 1), other_wa(self.wa, 2)
        self.core, self.half = lax.rem(self.wa, 2), self.wa // 2
        self.slots, count = {}, {TALL: 0, FLAT: 0}
        for name in names:
            shape = self.shape_of(name)
            self.slots[name] = (count[shape], self.sets[shape])
            count[shape] += 1
        self.own_copies, self.core_copies, self.x_copies = {}, {}, {}

    @staticmethod
    def shape_of(name):
        return FLAT if name in ("co", "so") else TALL

    @classmethod
    def scratch(cls, names):
        shapes = []
        for shape in (TALL, FLAT):
            many = sum(cls.shape_of(name) == shape for name in names)
            if many:
                shapes += [pltpu.VMEM((many, 2, *shape), BF)] * 2 + [pltpu.VMEM((many, *shape), BF)] * 2
        dma = pltpu.SemaphoreType.DMA
        many = len(names)
        return shapes + [dma((many, 2))] * 3 + [dma((many,))] * 2

    def start(self):
        for u, name in enumerate(self.names):
            slot, (own, inn, _, _) = self.slots[name]
            rows = self.shape_of(name)[0]
            for x in range(2):
                mine = pl.ds(pl.multiple_of((2 * x + self.core) * rows, 16), rows)
                theirs = pl.ds(pl.multiple_of((2 * x + 1 - self.core) * rows, 16), rows)
                copy = remote(
                    self.parts[name].at[theirs],
                    inn.at[slot, x],
                    self.core_send.at[u, x],
                    self.core_recv.at[u, x],
                    wa=self.mate,
                )
                copy.start()
                self.core_copies[name, x] = copy
                copy = pltpu.make_async_copy(
                    self.parts[name].at[mine], own.at[slot, x], self.own_sem.at[u, x]
                )
                copy.start()
                self.own_copies[name, x] = copy
            slot, (_, _, out, land) = self.slots[name]
            self.x_copies[name] = remote(
                out.at[slot], land.at[slot], self.x_send.at[u], self.x_recv.at[u], wa=self.across
            )

    def send(self, name):
        slot, (own, inn, out, _) = self.slots[name]
        for x in range(2):
            self.own_copies[name, x].wait()
            self.core_copies[name, x].wait_recv()
        away = 1 - self.half
        out[slot] = (own[slot, away].astype(F32) + inn[slot, away].astype(F32)).astype(BF)
        self.x_copies[name].start()

    def total(self, name):
        slot, (own, inn, _, land) = self.slots[name]
        self.x_copies[name].wait_recv()
        here = self.half
        return (
            own[slot, here].astype(F32) + inn[slot, here].astype(F32) + land[slot].astype(F32)
        ).astype(BF)

    def finish(self):
        for name in self.names:
            for x in range(2):
                self.core_copies[name, x].wait_send()
            self.x_copies[name].wait_send()


def lasting(microseconds):
    return pl.CostEstimate(
        flops=0, bytes_accessed=int(microseconds * 3.0e6), transcendentals=0
    )


def lanes_of(index):
    return pl.ds(pl.multiple_of(index * WIDE, WIDE), WIDE)


def rows_of(index, rows):
    return pl.ds(pl.multiple_of(index * rows, rows), rows)


def to_ctx(src, dst, send_sem, recv_sem, target):
    return pltpu.make_async_remote_copy(
        src_ref=src,
        dst_ref=dst,
        send_sem=send_sem,
        recv_sem=recv_sem,
        device_id={"ctx": target},
        device_id_type=MESH,
    )


def head_mask(h, rows):
    lane = lax.broadcasted_iota(jnp.int32, (rows, WIDE), 1)
    return (lane < HD) if h == 0 else (lane >= HD)


def bias_tiles(bias_ref, me, tiles):
    for h in range(2):
        line = bias_ref[pl.ds(2 * me + h, 1), :]
        rolled = pltpu.roll(
            jnp.broadcast_to(line, (BLOCK, LINE)), 0, 1, stride=1, stride_axis=0
        )
        tiles[h, 0] = rolled[:, :BLOCK]
        tiles[h, 1] = rolled[:, BLOCK : 2 * BLOCK]
        tiles[h, 2] = jnp.broadcast_to(line[:, WIDE : WIDE + BLOCK], (BLOCK, BLOCK))


def spread(n, me, pairs, send, recv, t):
    src, dst = pairs[t]
    for d in range(1, n):
        peer = lax.rem(me + d, n)
        to_ctx(
            src.at[:, lanes_of(peer)], dst.at[rows_of(me, BLOCK)], send.at[t, d], recv.at[t, d], peer
        ).start()
    dst[rows_of(me, BLOCK), :] = src[:, lanes_of(me)]


GATHERED = ("q", "k", "v", "so", "ck", "cv", "cq", "co")
GAINS = ("selfnorm", "crossnorm", "feednorm", "outbias")


class Gathering:
    def __init__(self, names, shards, whole, own_sem, send, recv):
        self.names, self.shards, self.whole = names, shards, whole
        self.sems = own_sem, send, recv
        self.wa = lax.axis_index("wa")
        self.mate, self.across = other_wa(self.wa, 1), other_wa(self.wa, 2)
        self.copies = {}

    def start(self):
        own_sem, send, recv = self.sems
        for u, name in enumerate(self.names):
            rows = self.shards[name].shape[0]
            shard, whole = self.shards[name], self.whole[name]
            mine = whole.at[pl.ds(pl.multiple_of(self.wa * rows, 16), rows)]
            theirs = whole.at[pl.ds(pl.multiple_of(self.across * rows, 16), rows)]
            over = remote(shard, mine, send.at[u, 0], recv.at[u, 0], wa=self.across)
            near = remote(shard, mine, send.at[u, 1], recv.at[u, 1], wa=self.mate)
            near.start()
            own = pltpu.make_async_copy(shard, mine, own_sem.at[u])
            own.start()
            pass_on = remote(theirs, theirs, send.at[u, 2], recv.at[u, 2], wa=self.mate)
            self.copies[name] = (over, near, pass_on, own)

    def cross(self, *names):
        for name in names:
            self.copies[name][0].start()

    def forward(self, *names):
        for name in names:
            over, _, pass_on, _ = self.copies[name]
            over.wait_recv()
            pass_on.start()

    def arrive(self, name):
        _, near, pass_on, own = self.copies[name]
        near.wait_recv()
        pass_on.wait_recv()
        own.wait()

    def finish(self):
        for copies in self.copies.values():
            for copy in copies[:3]:
                copy.wait_send()


def attn_forward_kernel(n, tokens_ref, small_ref, *refs):
    shards = dict(zip(GATHERED, refs[:8], strict=True))
    wholes = dict(zip(GATHERED, refs[8:16], strict=True))
    o_ref, low_ref, qh_out, kh_out, vh_out, ot_out, lse_out, small_out = refs[16:24]
    (
        held_q, held_k, held_v, proj, small_in, small_mid, qh, kh, vh, vt, oh, land, tiles, acc, stat,
        send, recv, osend, orecv, small_sem, own_sem, out_sem, gather_send, gather_recv,
    ) = refs[24:]
    held = {"q": held_q, "k": held_k, "v": held_v}
    gathering = Gathering(GATHERED, shards, wholes | held, own_sem, gather_send, gather_recv)
    meet([*ctx_peers(n), {"wa": gathering.mate}, {"wa": gathering.across}])
    me = lax.axis_index("ctx")
    near = remote(small_ref, small_in.at[0], small_sem.at[0], small_sem.at[1], wa=gathering.mate)
    near.start()
    gathering.start()
    gathering.cross("q")
    over = remote(small_mid, small_in.at[1], small_sem.at[2], small_sem.at[3], wa=gathering.across)
    near.wait_recv()
    small_mid[...] = (small_ref[...].astype(F32) + small_in[0].astype(F32)).astype(BF)
    over.start()
    over.wait_recv()
    small_out[...] = small_mid[...].astype(F32) + small_in[1].astype(F32)
    bias_ref = small_out
    values = tokens_ref[...].astype(F32)
    width = values.shape[1]
    norm = lax.rsqrt(jnp.mean(values * values, axis=1, keepdims=True) + epsilon)
    low_ref[...] = (values * norm * small_out[H : H + 1, :width]).astype(BF)
    bias_tiles(bias_ref, me, tiles)
    pairs = tuple((proj.at[t], dst) for t, dst in enumerate((qh, kh, vh)))
    saving = []
    for t, name in enumerate(("q", "k", "v")):
        gathering.forward(name)
        gathering.cross(*(("k",), ("v",), ("so", "ck"))[t])
        gathering.arrive(name)
        proj[t] = nn_dot(low_ref[...], held[name][...]).astype(BF)
        spread(n, me, pairs, send, recv, t)
        copy = pltpu.make_async_copy(held[name], wholes[name], out_sem.at[t])
        copy.start()
        saving.append(copy)

    def arrive(i):
        @pl.when(i != me)
        def _():
            d = lax.rem(me - i + n, n)
            for t, (src, dst) in enumerate(pairs):
                to_ctx(
                    src.at[:, lanes_of(i)], dst.at[rows_of(i, BLOCK)], send.at[t, d], recv.at[t, d], i
                ).wait_recv()

    def query_block(i, unused):
        @pl.when(i == 5)
        def _():
            gathering.forward("so", "ck")
            gathering.cross("cv", "cq")

        @pl.when(i == 7)
        def _():
            gathering.forward("cv", "cq")
            gathering.cross("co")

        arrive(i)
        rows = rows_of(i, BLOCK)
        vt[:, rows] = vh[rows, :].astype(F32).T.astype(BF)
        q_now = qh[rows, :] * BF(HD**-0.5)
        masked = [jnp.where(head_mask(h, BLOCK), q_now, BF(0)) for h in range(2)]

        def fold(j, which, first):
            keys = kh[rows_of(j, BLOCK), :]
            for h in range(2):
                scores = nt_dot(keys, masked[h])
                if which is None:
                    scores = scores + bias_ref[pl.ds(2 * me + h, 1), WIDE : WIDE + BLOCK]
                else:
                    scores = scores + tiles[h, which]
                top = jnp.max(scores, axis=0, keepdims=True)
                if not first:
                    old = stat[h : h + 1, :]
                    top = jnp.maximum(old, top)
                weights = jnp.exp(scores - top)
                total = jnp.sum(weights, axis=0, keepdims=True)
                vals = vt[h * HD : (h + 1) * HD, rows_of(j, BLOCK)]
                mixed = nn_dot(vals, weights.astype(BF))
                if not first:
                    factor = jnp.exp(old - top)
                    total = total + stat[2 + h : 3 + h, :] * factor
                    mixed = mixed + acc[h * HD : (h + 1) * HD, :] * factor
                stat[h : h + 1, :] = top
                stat[2 + h : 3 + h, :] = total
                acc[h * HD : (h + 1) * HD, :] = mixed

        fold(i, 0, True)

        @pl.when(i >= 1)
        def _():
            fold(i - 1, 1, False)

        def far(j, unused):
            fold(j, None, False)
            return unused

        lax.fori_loop(0, i - 1, far, 0)
        for h in range(2):
            total = stat[2 + h : 3 + h, :]
            part = acc[h * HD : (h + 1) * HD, :] / total
            acc[h * HD : (h + 1) * HD, :] = part
            lse_out[h : h + 1, rows] = stat[h : h + 1, :] + jnp.log(total)
        done = acc[...]
        ot_out[:, rows] = done
        oh[rows, :] = done.T.astype(BF)

        @pl.when(i != me)
        def _():
            d = lax.rem(i - me + n, n)
            to_ctx(oh.at[rows], land.at[:, lanes_of(me)], osend.at[d], orecv.at[d], i).start()

        @pl.when(i == me)
        def _():
            land[:, lanes_of(me)] = oh[rows, :]

        return unused

    lax.fori_loop(0, n, query_block, 0)
    qh_out[...] = qh[...]
    kh_out[...] = kh[...]
    vh_out[...] = vh[...]
    gathering.forward("co")
    for d in range(1, n):
        peer = lax.rem(me + d, n)
        for t, (src, dst) in enumerate(pairs):
            to_ctx(
                src.at[:, lanes_of(peer)], dst.at[rows_of(me, BLOCK)], send.at[t, d], recv.at[t, d], peer
            ).wait_send()
        back = to_ctx(
            oh.at[rows_of(peer, BLOCK)], land.at[:, lanes_of(me)], osend.at[d], orecv.at[d], peer
        )
        back.wait_send()
        back.wait_recv()
    o_ref[...] = land[...]
    for name in GATHERED[3:]:
        gathering.arrive(name)
    gathering.finish()
    near.wait_send()
    over.wait_send()
    for copy in saving:
        copy.wait()


def vmem(count):
    return [pl.BlockSpec(memory_space=pltpu.VMEM)] * count


def attn_forward(n, tokens, small, shards):
    rows, seq = tokens.shape[0], n * tokens.shape[0]
    owners = lax.axis_size("wa")
    heads = jax.ShapeDtypeStruct((seq, WIDE), BF)
    wholes = [jax.ShapeDtypeStruct((owners * s.shape[0], s.shape[1]), BF) for s in shards]
    width = wholes[0].shape[1]
    dma = pltpu.SemaphoreType.DMA
    return pl.pallas_call(
        functools.partial(attn_forward_kernel, n),
        out_shape=(
            *wholes,
            jax.ShapeDtypeStruct((rows, width), BF),
            jax.ShapeDtypeStruct(tokens.shape, BF),
            heads,
            heads,
            heads,
            jax.ShapeDtypeStruct((WIDE, seq), F32),
            jax.ShapeDtypeStruct((8, seq), F32),
            jax.ShapeDtypeStruct(small.shape, F32),
        ),
        in_specs=vmem(2) + [pl.BlockSpec(memory_space=pl.ANY)] * 8,
        out_specs=tuple([pl.BlockSpec(memory_space=pl.ANY)] * 8 + vmem(8)),
        scratch_shapes=[
            *(pltpu.VMEM(w.shape, BF) for w in wholes[:3]),
            pltpu.VMEM((3, rows, width), BF),
            pltpu.VMEM((2, *small.shape), BF),
            pltpu.VMEM(small.shape, BF),
            pltpu.VMEM((seq, WIDE), BF),
            pltpu.VMEM((seq, WIDE), BF),
            pltpu.VMEM((seq, WIDE), BF),
            pltpu.VMEM((WIDE, seq), BF),
            pltpu.VMEM((seq, WIDE), BF),
            pltpu.VMEM((rows, width), BF),
            pltpu.VMEM((2, 3, BLOCK, BLOCK), F32),
            pltpu.VMEM((WIDE, BLOCK), F32),
            pltpu.VMEM((8, BLOCK), F32),
            dma((3, n)),
            dma((3, n)),
            dma((n,)),
            dma((n,)),
            dma((4,)),
            dma((8,)),
            dma((3,)),
            dma((8, 3)),
            dma((8, 3)),
        ],
        compiler_params=pltpu.CompilerParams(
            collective_id=1, has_side_effects=True, vmem_limit_bytes=44 << 20
        ),
        cost_estimate=lasting(85),
        name="attn_forward",
    )(tokens, small, *shards)


def attn_backward_kernel(
    n, do_ref, qh, kh, vh, ot_ref, lse_ref, bias_ref, *rest
):
    parts = dict(zip(EARLY, rest[:5], strict=True))
    feed_part = rest[5]
    dq_ref, dk_ref, dv_ref, line_ref, tall_pair, tall_one, flat_out = rest[6:13]
    feed_full = rest[13:15]
    (
        doh, kt, stage, land, dk_acc, dv_acc, dqt, q_masked, do_masked, rowstat, tiles, dtiles,
        send, recv, gsend, grecv, ring_send, ring_recv,
    ) = rest[15:33]
    extra = rest[33:]
    fold_wa = Folding(EARLY, parts, (extra[0:4], extra[4:8], extra[8:13]))
    ring = Ring(FEED_LANES, ring_send, ring_recv, full=feed_full)
    for lane in range(2):
        feed_full[lane][ring.chunk(lane, 1)] = feed_part[lane]
    meet([*ctx_peers(n), {"wa": fold_wa.mate}, {"wa": fold_wa.across}])
    me = lax.axis_index("ctx")
    pairs = ((do_ref, doh),)
    spread(n, me, pairs, send, recv, 0)
    fold_wa.start()
    bias_tiles(bias_ref, me, tiles)
    for j in range(n):
        part = slice(j * BLOCK, (j + 1) * BLOCK)
        kt[:, part] = (kh[part, :].astype(F32) * HD**-0.5).T.astype(BF)
    dk_acc[...] = jnp.zeros_like(dk_acc)
    dv_acc[...] = jnp.zeros_like(dv_acc)
    dtiles[...] = jnp.zeros_like(dtiles)
    for name in EARLY[:2]:
        fold_wa.send(name)

    def pair(t, now):
        i, j = now
        rows, there = rows_of(i, BLOCK), rows_of(j, BLOCK)

        @pl.when(t == n)
        def _():
            for name in EARLY[2:]:
                fold_wa.send(name)

        for turn, lanes in enumerate(FEED_TURNS):

            @pl.when((lax.rem(t, 4) == 2 * turn) & (t <= 4 * HOPS + 2))
            def _():
                ring.gather(t // 4, lanes)

        @pl.when(j == i)
        def _():
            @pl.when(i != me)
            def _():
                d = lax.rem(me - i + n, n)
                to_ctx(
                    do_ref.at[:, lanes_of(i)], doh.at[rows], send.at[0, d], recv.at[0, d], i
                ).wait_recv()

            q_now = qh[rows, :] * BF(HD**-0.5)
            do_now = doh[rows, :]
            products = do_now.astype(F32).T * ot_ref[:, rows]
            for h in range(2):
                mask = head_mask(h, BLOCK)
                q_masked[h] = jnp.where(mask, q_now, BF(0))
                do_masked[h] = jnp.where(mask, do_now, BF(0))
                rowstat[h : h + 1, :] = lse_ref[h : h + 1, rows]
                rowstat[2 + h : 3 + h, :] = jnp.sum(
                    products[h * HD : (h + 1) * HD], axis=0, keepdims=True
                )
            dqt[...] = jnp.zeros_like(dqt)

        which = jnp.minimum(i - j, 2)
        keys, vals = kh[there, :], vh[there, :]
        dk_part, dv_part = None, None
        for h in range(2):
            scores = nt_dot(keys, q_masked[h])
            weights = jnp.exp(scores + tiles[h, which] - rowstat[h : h + 1, :])
            dweights = nt_dot(vals, do_masked[h])
            dscores = weights * (dweights - rowstat[2 + h : 3 + h, :])
            dtiles[h, which] += dscores
            low = dscores.astype(BF)
            dv_now = nn_dot(weights.astype(BF), do_masked[h])
            dk_now = nn_dot(low, q_masked[h])
            dv_part = dv_now if dv_part is None else dv_part + dv_now
            dk_part = dk_now if dk_part is None else dk_part + dk_now
            half = slice(h * HD, (h + 1) * HD)
            dqt[half, :] += nn_dot(kt[half, there], low)
        dk_acc[there, :] += dk_part
        dv_acc[there, :] += dv_part
        last = j == 0

        @pl.when(last)
        def _():
            stage[0, rows, :] = dqt[...].T.astype(BF)
            stage[1, rows, :] = dk_acc[rows, :].astype(BF)
            stage[2, rows, :] = dv_acc[rows, :].astype(BF)

            @pl.when(i != me)
            def _():
                d = lax.rem(i - me + n, n)
                for t in range(3):
                    to_ctx(
                        stage.at[t, rows],
                        land.at[t, :, lanes_of(me)],
                        gsend.at[t, d],
                        grecv.at[t, d],
                        i,
                    ).start()

            @pl.when(i == me)
            def _():
                for t in range(3):
                    land[t, :, lanes_of(me)] = stage[t, rows, :]

        return jnp.where(last, i - 1, i), jnp.where(last, i - 1, j - 1)

    lax.fori_loop(0, n * (n + 1) // 2, pair, (jnp.int32(n - 1), jnp.int32(n - 1)))
    ring.finish(lambda lane: feed_full[FEED_LANES[lane][0]].at[0, FEED_LANES[lane][2]])
    tall_pair[:224, :] = fold_wa.total("cq")
    tall_pair[224:, :] = fold_wa.total("ck")
    tall_one[...] = fold_wa.total("cv")
    for at, name in ((0, "co"), (32, "so")):
        flat_out[:, at : at + 32, :] = fold_wa.total(name).reshape(8, 32, 896)
    fold_wa.finish()
    for h in range(2):
        line = jnp.concatenate(
            [dtiles[h, 0], dtiles[h, 1], jnp.zeros((BLOCK, LINE - 2 * BLOCK), F32)], axis=1
        )
        row = lax.broadcasted_iota(jnp.int32, (BLOCK, LINE), 0)
        for bit in range(8):
            moved = pltpu.roll(line, LINE - (1 << bit), 1)
            line = jnp.where((row >> bit) & 1 == 1, moved, line)
        line_ref[h : h + 1, :] = jnp.sum(line, axis=0, keepdims=True)
        line_ref[2 + h : 3 + h, :BLOCK] = jnp.sum(dtiles[h, 2], axis=0, keepdims=True)
    line_ref[2:4, BLOCK:] = jnp.zeros((2, LINE - BLOCK), F32)
    line_ref[4:8, :] = jnp.zeros((4, LINE), F32)
    for d in range(1, n):
        peer = lax.rem(me + d, n)
        to_ctx(
            do_ref.at[:, lanes_of(peer)], doh.at[rows_of(me, BLOCK)], send.at[0, d], recv.at[0, d], peer
        ).wait_send()
        for t in range(3):
            back = to_ctx(
                stage.at[t, rows_of(peer, BLOCK)], land.at[t, :, lanes_of(me)], gsend.at[t, d], grecv.at[t, d], peer
            )
            back.wait_send()
            back.wait_recv()
    dq_ref[...] = land[0]
    dk_ref[...] = land[1]
    dv_ref[...] = land[2]


def attn_backward(n, dout, qh, kh, vh, ot, lse, bias_lines, parts, feed_part):
    rows, seq = dout.shape[0], n * dout.shape[0]
    grads = jax.ShapeDtypeStruct(dout.shape, BF)
    feed = jax.ShapeDtypeStruct(FEED, BF)
    return pl.pallas_call(
        functools.partial(attn_backward_kernel, n),
        out_shape=(
            grads,
            grads,
            grads,
            jax.ShapeDtypeStruct((8, LINE), F32),
            jax.ShapeDtypeStruct((448, 1024), BF),
            jax.ShapeDtypeStruct((224, 1024), BF),
            jax.ShapeDtypeStruct((8, 64, 896), BF),
            feed,
            feed,
        ),
        in_specs=vmem(7) + [pl.BlockSpec(memory_space=pl.ANY)] * 5 + vmem(1),
        out_specs=tuple(vmem(9)),
        scratch_shapes=[
            pltpu.VMEM((seq, WIDE), BF),
            pltpu.VMEM((WIDE, seq), BF),
            pltpu.VMEM((3, seq, WIDE), BF),
            pltpu.VMEM((3, *dout.shape), BF),
            pltpu.VMEM((seq, WIDE), F32),
            pltpu.VMEM((seq, WIDE), F32),
            pltpu.VMEM((WIDE, BLOCK), F32),
            pltpu.VMEM((2, BLOCK, WIDE), BF),
            pltpu.VMEM((2, BLOCK, WIDE), BF),
            pltpu.VMEM((8, BLOCK), F32),
            pltpu.VMEM((2, 3, BLOCK, BLOCK), F32),
            pltpu.VMEM((2, 3, BLOCK, BLOCK), F32),
            pltpu.SemaphoreType.DMA((1, n)),
            pltpu.SemaphoreType.DMA((1, n)),
            pltpu.SemaphoreType.DMA((3, n)),
            pltpu.SemaphoreType.DMA((3, n)),
            pltpu.SemaphoreType.DMA((len(FEED_LANES), HOPS)),
            pltpu.SemaphoreType.DMA((len(FEED_LANES), HOPS)),
            *Folding.scratch(EARLY),
        ],
        compiler_params=pltpu.CompilerParams(
            collective_id=2, has_side_effects=True, vmem_limit_bytes=58 << 20
        ),
        cost_estimate=lasting(100),
        name="attn_backward",
    )(dout, qh, kh, vh, ot, lse, bias_lines, *parts, feed_part)


LANES = (
    (1, ("cA",), 0),
    (-1, ("cB", "out"), 0),
    (1, ("sA",), 5),
    (-1, ("sB", "small"), 5),
)
BUFFERS = {
    "cA": (448, 1024),
    "cB": (224, 1024),
    "out": (8, 64, 896),
    "sA": (448, 1024),
    "sB": (224, 1024),
    "small": (8, 8, 128),
}
NAMES = tuple(BUFFERS)


def kind_of(name):
    return F32 if name == "small" else BF


def chunk_shape(name):
    shape = BUFFERS[name]
    return (shape[0], WIDE) if len(shape) == 2 else shape[1:]


def chunk_of(ref, name, c):
    return ref.at[:, lanes_of(c)] if len(BUFFERS[name]) == 2 else ref.at[c]


def reduce_kernel(*refs):
    ca_ref, cb_ref, out_ref, small_ref = refs[:4]
    parts = dict(zip(LATE, refs[4:7], strict=True))
    fin_ref, fin_out = refs[7], refs[14]
    full = dict(zip(NAMES, refs[8:14], strict=True))
    share = dict(zip(NAMES, refs[15:21], strict=True))
    hold = dict(zip(NAMES, refs[21:27], strict=True))
    small_in, small_mid, small_sem = refs[27:30]
    ring_send, ring_recv, fin_send, fin_recv = refs[30:34]
    extra = refs[34:]
    fold_wa = Folding(LATE, parts, (extra[0:4], None, extra[4:9]))
    place, after, before = ring_place(RING)
    wa, both = fold_wa.wa, other_wa(fold_wa.across, 1)
    meet(
        [{"wa": peer} for peer in (fold_wa.mate, fold_wa.across, both)]
        + [{"ctx": after}, {"ctx": before}]
    )
    own_fin = pltpu.make_async_copy(fin_ref.at[wa], fin_out.at[wa], fin_send.at[3])
    own_fin.start()
    fin_copies = [
        remote(fin_ref.at[peer], fin_out.at[wa], fin_send.at[d], fin_recv.at[d], wa=peer)
        for d, peer in enumerate((fold_wa.across, both, fold_wa.mate))
    ]
    fold_wa.start()
    near = remote(small_ref, small_in.at[0], small_sem.at[0], small_sem.at[1], wa=fold_wa.mate)
    near.start()
    over = remote(small_mid, small_in.at[1], small_sem.at[2], small_sem.at[3], wa=fold_wa.across)
    share["cA"][...] = ca_ref[...]
    share["cB"][...] = cb_ref[...]
    share["out"][...] = out_ref[...]
    copies = {}

    def ring_step(lane, step):
        way, buffers, unused = LANES[lane]
        here = place if way == 1 else lax.rem(RING - place, RING)
        target = after if way == 1 else before

        def number(offset):
            return lax.rem(here + offset + 2 * RING, RING)

        for name in buffers:
            b = NAMES.index(name)
            if step > 0:
                copies[name, step - 1].wait_recv()
            if step == 2 * HOPS:
                continue
            if step <= HOPS:
                now = number(-step) if step < HOPS else number(1)
                mine = chunk_of(share[name], name, now)
                if step > 0:
                    total = mine[...].astype(F32) + hold[name][step - 1].astype(F32)
                    if step == HOPS:
                        mine = chunk_of(full[name], name, now)
                    mine[...] = total.astype(kind_of(name))
                src, dst = (mine, hold[name].at[step]) if step < HOPS else (mine, mine)
            else:
                src = dst = chunk_of(full[name], name, number(1 - (step - HOPS)))
            copy = remote(src, dst, ring_send.at[b, step], ring_recv.at[b, step], ctx=target)
            copy.start()
            copies[name, step] = copy

    ring_step(0, 0)
    ring_step(1, 0)
    for name in LATE:
        fold_wa.send(name)
    near.wait_recv()
    small_mid[...] = small_ref[...] + small_in[0]
    over.start()
    last = max(start for _, _, start in LANES) + 2 * HOPS
    for tick in range(1, last + 1):
        if tick == 8:
            for copy in fin_copies:
                copy.start()
        for lane, (_, buffers, start) in enumerate(LANES):
            step = tick - start
            if step == 0 and buffers[0] == "sA":
                share["sA"][:224, :] = fold_wa.total("q")
                share["sA"][224:, :] = fold_wa.total("k")
            if step == 0 and buffers[0] == "sB":
                share["sB"][...] = fold_wa.total("v")
                over.wait_recv()
                share["small"][...] = (small_mid[...] + small_in[1]).reshape(8, 8, 128)
            if 0 <= step <= 2 * HOPS:
                ring_step(lane, step)
    fold_wa.finish()
    near.wait_send()
    over.wait_send()
    for copy in copies.values():
        copy.wait_send()
    own_fin.wait()
    for copy in fin_copies:
        copy.wait()


def reduce_grads(pair, one, flat, small, parts, fin):
    dma = pltpu.SemaphoreType.DMA
    return pl.pallas_call(
        reduce_kernel,
        out_shape=(
            *(jax.ShapeDtypeStruct(BUFFERS[b], kind_of(b)) for b in NAMES),
            jax.ShapeDtypeStruct((4, 224, 896), BF),
        ),
        in_specs=vmem(4) + [pl.BlockSpec(memory_space=pl.ANY)] * 4,
        out_specs=(*vmem(len(NAMES)), pl.BlockSpec(memory_space=pl.ANY)),
        scratch_shapes=[
            *(pltpu.VMEM(BUFFERS[b], kind_of(b)) for b in NAMES),
            *(pltpu.VMEM((HOPS, *chunk_shape(b)), kind_of(b)) for b in NAMES),
            pltpu.VMEM((2, 64, 128), F32),
            pltpu.VMEM((64, 128), F32),
            dma((4,)),
            dma((len(NAMES), 2 * HOPS)),
            dma((len(NAMES), 2 * HOPS)),
            dma((4,)),
            dma((3,)),
            *Folding.scratch(LATE),
        ],
        compiler_params=pltpu.CompilerParams(
            collective_id=3, has_side_effects=True, vmem_limit_bytes=56 << 20
        ),
        cost_estimate=lasting(90),
        name="reduce_grads",
    )(pair, one, flat, small, *parts, fin.reshape(4, 224, 896))


def unfold(full):
    wide = {name: value.astype(F32) for name, value in full.items()}
    return {
        "cq": wide["cA"][:224],
        "ck": wide["cA"][224:],
        "cv": wide["cB"],
        "co": wide["out"][:, :32].reshape(FLAT),
        "so": wide["out"][:, 32:].reshape(FLAT),
        "q": wide["sA"][:224],
        "k": wide["sA"][224:],
        "v": wide["sB"],
    }


GELU = (2.0 / math.pi) ** 0.5


def ffn_kernel(
    f_ref, cot_ref, win_ref, wout_ref, bias_ref, res_ref, df_ref, dwin_ref, dwout_ref, dbias_ref,
    f_all, g_all, dul_all, own, kept, out_mate, out_cross, in_mate, in_cross, x_out, x_in,
    f_send, f_recv, p_send, p_recv,
):
    me = lax.axis_index("wa")
    mate, across = other_wa(me, 1), other_wa(me, 2)
    both = other_wa(across, 1)
    barrier = pltpu.get_barrier_semaphore()
    for peer in (mate, across):
        pl.semaphore_signal(barrier, inc=1, device_id={"wa": peer}, device_id_type=MESH)
    pl.semaphore_wait(barrier, 2)
    to_across = remote(f_ref, f_all.at[me], f_send.at[1], f_recv.at[1], wa=across)
    to_across.start()
    to_mate = remote(f_ref, f_all.at[me], f_send.at[0], f_recv.at[0], wa=mate)
    to_mate.start()
    forward = remote(f_all.at[across], f_all.at[across], f_send.at[2], f_recv.at[2], wa=mate)
    f_all[me] = f_ref[...]
    order = (me, mate, across, both)
    dbias_ref[...] = jnp.zeros_like(dbias_ref)
    for k, s in enumerate(order):
        if k == 1:
            to_mate.wait_recv()
        if k == 2:
            to_across.wait_recv()
            forward.start()
        if k == 3:
            forward.wait_recv()
        u = nn_dot(f_all[s], win_ref[...]) + bias_ref[...]
        square = u * u
        t = jnp.tanh(GELU * (u + 0.044715 * (square * u)))
        g_all[s] = (0.5 * u * (1.0 + t)).astype(BF)
        slope = 0.5 * (1.0 + t) + 0.5 * u * (1.0 - t * t) * (GELU * (1.0 + 3 * 0.044715 * square))
        du = nt_dot(cot_ref[s], wout_ref[...]) * slope
        dbias_ref[...] += jnp.sum(du.reshape(32, 8, du.shape[1]), axis=0)
        dul_all[s] = du.astype(BF)

    def scatter(which, product):
        out_cross[which] = product(both).astype(BF)
        cross = remote(
            out_cross.at[which], in_cross.at[which], p_send.at[which, 0], p_recv.at[which, 0], wa=mate
        )
        cross.start()
        kept[...] = product(across)
        cross.wait_recv()
        x_out[which] = (kept[...] + in_cross[which].astype(F32)).astype(BF)
        over = remote(
            x_out.at[which], x_in.at[which], p_send.at[which, 1], p_recv.at[which, 1], wa=across
        )
        over.start()
        out_mate[which] = product(mate).astype(BF)
        near = remote(
            out_mate.at[which], in_mate.at[which], p_send.at[which, 2], p_recv.at[which, 2], wa=mate
        )
        near.start()
        own[which] = product(me)
        return cross, over, near

    def finish(which, copies, out_ref):
        cross, over, near = copies
        near.wait_recv()
        over.wait_recv()
        out_ref[...] = own[which] + in_mate[which].astype(F32) + x_in[which].astype(F32)
        for copy in copies:
            copy.wait_send()

    df_copies = scatter(0, lambda s: nt_dot(dul_all[s], win_ref[...]))
    res_copies = scatter(1, lambda s: nn_dot(g_all[s], wout_ref[...]))
    width = f_ref.shape[1]

    def outer(left_all, right, out_ref):
        for c in range(width // WIDE):
            lanes = slice(c * WIDE, (c + 1) * WIDE)
            total = None
            for s in range(4):
                left = left_all[s, :, lanes].astype(F32).T.astype(BF)
                now = nn_dot(left, right[s])
                total = now if total is None else total + now
            out_ref[lanes, :] = total.astype(BF)

    outer(f_all, dul_all, dwin_ref)
    outer(g_all, cot_ref, dwout_ref)
    finish(0, df_copies, df_ref)
    finish(1, res_copies, res_ref)
    for copy in (to_mate, to_across, forward):
        copy.wait_send()


def ffn(f_low, cot_all, win, wout, bias):
    rows, width = f_low.shape
    hidden = win.shape[1]
    dma = pltpu.SemaphoreType.DMA
    block = (rows, width)
    return pl.pallas_call(
        ffn_kernel,
        out_shape=(
            jax.ShapeDtypeStruct(block, F32),
            jax.ShapeDtypeStruct(block, F32),
            jax.ShapeDtypeStruct(win.shape, BF),
            jax.ShapeDtypeStruct(wout.shape, BF),
            jax.ShapeDtypeStruct((8, hidden), F32),
        ),
        in_specs=vmem(5),
        out_specs=tuple(vmem(5)),
        scratch_shapes=[
            pltpu.VMEM((4, *block), BF),
            pltpu.VMEM((4, rows, hidden), BF),
            pltpu.VMEM((4, rows, hidden), BF),
            pltpu.VMEM((2, *block), F32),
            pltpu.VMEM(block, F32),
            *[pltpu.VMEM((2, *block), BF)] * 6,
            dma((3,)),
            dma((3,)),
            dma((2, 3)),
            dma((2, 3)),
        ],
        compiler_params=pltpu.CompilerParams(
            collective_id=4, has_side_effects=True, vmem_limit_bytes=56 << 20
        ),
        cost_estimate=lasting(44),
        name="feed_forward",
    )(f_low, cot_all, win, wout, bias)


def padded_rows(pad, values):
    rows = values.shape[0]
    pad[...] = jnp.zeros_like(pad)
    pad[1 : rows + 1, :] = values.astype(F32)


def both_heads(pad, g):
    here = pad[g * SPAN : (g + 1) * SPAN, :]
    left = head_mask(0, SPAN)
    return jnp.concatenate([jnp.where(left, here, 0.0), jnp.where(left, 0.0, here)], 0).astype(BF)


def join_heads(stacked):
    return jnp.where(head_mask(0, SPAN), stacked[:SPAN], stacked[SPAN:])


def cross_forward_kernel(groups, keep_ref, q_ref, k_ref, v_ref, x_ref, q_pad, x_pad):
    padded_rows(q_pad, q_ref[...])
    for g in range(groups):
        rows = slice(g * 256, (g + 1) * 256)
        query = both_heads(q_pad, g) * BF(HD**-0.5)
        scores = nt_dot(query, k_ref[rows, :])
        weights = jnp.exp(scores - jnp.max(scores, axis=1, keepdims=True))
        weights = weights / jnp.sum(weights, axis=1, keepdims=True)
        mixed = join_heads(nn_dot(weights.astype(BF), v_ref[rows, :]))
        if g == 0:
            mixed = mixed * keep_ref[0:1, :]
        x_pad[g * SPAN : (g + 1) * SPAN, :] = mixed
    x_ref[...] = x_pad[1 : x_ref.shape[0] + 1, :].astype(BF)


def pair_specs(*rows):
    return [pl.BlockSpec((r, WIDE), lambda p: (0, p)) for r in rows]


def cross_forward(keep, query, keys, values):
    rows, width = query.shape
    many = keys.shape[0]
    groups = many // 256
    return pl.pallas_call(
        functools.partial(cross_forward_kernel, groups),
        grid=(width // WIDE,),
        out_shape=jax.ShapeDtypeStruct(query.shape, BF),
        in_specs=[pl.BlockSpec((8, WIDE), lambda p: (0, 0)), *pair_specs(rows, many, many)],
        out_specs=pair_specs(rows)[0],
        scratch_shapes=[pltpu.VMEM((groups * SPAN, WIDE), F32)] * 2,
        compiler_params=pltpu.CompilerParams(vmem_limit_bytes=16 << 20),
        cost_estimate=lasting(9),
        name="cross_forward",
    )(keep, query, keys, values)


def cross_backward_kernel(
    groups, keep_ref, q_ref, dx_ref, k_ref, v_ref, dq_ref, dk_ref, dv_ref, q_pad, dx_pad, dq_pad
):
    padded_rows(q_pad, q_ref[...])
    padded_rows(dx_pad, dx_ref[...])
    dx_pad[:SPAN, :] = dx_pad[:SPAN, :] * keep_ref[0:1, :]
    for g in range(groups):
        rows = slice(g * 256, (g + 1) * 256)
        query = both_heads(q_pad, g) * BF(HD**-0.5)
        dmixed = both_heads(dx_pad, g)
        keys, values = k_ref[rows, :], v_ref[rows, :]
        scores = nt_dot(keys, query)
        weights = jnp.exp(scores - jnp.max(scores, axis=0, keepdims=True))
        weights = weights / jnp.sum(weights, axis=0, keepdims=True)
        dweights = nt_dot(values, dmixed)
        dscores = weights * (dweights - jnp.sum(weights * dweights, axis=0, keepdims=True))
        dk_ref[rows, :] = nn_dot(dscores.astype(BF), query).astype(BF)
        dv_ref[rows, :] = nn_dot(weights.astype(BF), dmixed).astype(BF)
        back = (dscores * HD**-0.5).T.astype(BF)
        dq_pad[g * SPAN : (g + 1) * SPAN, :] = join_heads(nn_dot(back, keys))
    dq_ref[...] = dq_pad[1 : dq_ref.shape[0] + 1, :].astype(BF)


def cross_backward(keep, query, dmixed, keys, values):
    rows, width = query.shape
    many = keys.shape[0]
    groups = many // 256
    return pl.pallas_call(
        functools.partial(cross_backward_kernel, groups),
        grid=(width // WIDE,),
        out_shape=(
            jax.ShapeDtypeStruct(query.shape, BF),
            jax.ShapeDtypeStruct(keys.shape, BF),
            jax.ShapeDtypeStruct(keys.shape, BF),
        ),
        in_specs=[
            pl.BlockSpec((8, WIDE), lambda p: (0, 0)),
            *pair_specs(rows, rows, many, many),
        ],
        out_specs=tuple(pair_specs(rows, many, many)),
        scratch_shapes=[pltpu.VMEM((groups * SPAN, WIDE), F32)] * 3,
        compiler_params=pltpu.CompilerParams(vmem_limit_bytes=16 << 20),
        cost_estimate=lasting(17),
        name="cross_backward",
    )(keep, query, dmixed, keys, values)


def line_selector():
    place = jnp.arange(LINE)
    offset = jnp.where(place < LINE // 2, -place, LINE - place)
    return (bucket_of(offset)[None, :] == jnp.arange(NB)[:, None]).astype(jnp.float32)


def ring_forward(query_low, key_low, value_low, bucket_table):
    row_count, attn_width = query_low.shape
    position = lax.axis_index("ctx")
    scale_factor = HD ** (-0.5)
    bias_set, onehots = make_bias(bucket_table.astype(jnp.float32), row_count)
    query_heads = query_low.reshape(row_count, H, HD)
    start_state = (
        jnp.full((H, row_count), negative, jnp.float32),
        jnp.zeros((H, row_count), jnp.float32),
        jnp.zeros((row_count, attn_width), jnp.float32),
    )
    running_max, running_sum, running_acc = forward_fold(
        query_heads,
        position,
        row_count,
        bias_set,
        scale_factor,
        start_state,
        (
            lax.all_gather(key_low, "ctx", axis=0, tiled=True),
            lax.all_gather(value_low, "ctx", axis=0, tiled=True),
        ),
    )
    attended = (running_acc.reshape(row_count, H, HD) / running_sum.T[:, :, None]).reshape(
        row_count, attn_width
    )
    log_total = running_max + jnp.log(running_sum)
    state = (query_heads, key_low, value_low, attended, log_total, bias_set, onehots)
    return attended.astype(jnp.bfloat16), state


def ring_backward(state, dout_low):
    query_heads, key_low, value_low, attended, log_total, bias_set, onehots = state
    row_count, attn_width = dout_low.shape
    cycle_size = lax.axis_size("ctx")
    position = lax.axis_index("ctx")
    scale_factor = HD ** (-0.5)
    dout_heads = dout_low.reshape(row_count, H, HD)
    row_delta = jnp.sum(
        (dout_low.astype(jnp.float32) * attended).reshape(row_count, H, HD), axis=-1
    ).T
    zero_rows = jnp.zeros((row_count, attn_width), jnp.float32)
    zero_tables = (
        jnp.zeros((H, row_count, row_count), jnp.float32),
        jnp.zeros((H, row_count, row_count), jnp.float32),
        jnp.zeros((H,), jnp.float32),
    )

    def visit(folded, key_now, value_now, relation):

        def visit_compute(current):
            dquery_acc, dkey_acc, dvalue_acc, relative_bias_tables = current
            key_heads = key_now.reshape(row_count, H, HD)
            weights_now, dscores, ds_low = pair_core(
                query_heads,
                dout_heads,
                log_total,
                row_delta,
                key_heads,
                value_now.reshape(row_count, H, HD),
                relation,
                bias_set,
                scale_factor,
            )
            dquery = jnp.einsum(
                "hqk,khd->qhd", ds_low, key_heads, preferred_element_type=jnp.float32
            ).reshape(row_count, attn_width)
            dkey = jnp.einsum(
                "hqk,qhd->khd", ds_low, query_heads, preferred_element_type=jnp.float32
            ).reshape(row_count, attn_width)
            dvalue = jnp.einsum(
                "hqk,qhd->khd",
                weights_now.astype(jnp.bfloat16),
                dout_heads,
                preferred_element_type=jnp.float32,
            ).reshape(row_count, attn_width)
            return (
                dquery_acc + dquery,
                dkey_acc + dkey,
                dvalue_acc + dvalue,
                add_tables(relative_bias_tables, dscores, relation),
            )

        return lax.cond(relation >= 0, visit_compute, lambda unchanged: unchanged, folded)

    first_state = visit(
        (zero_rows, zero_rows, zero_rows, zero_tables), key_low, value_low, jnp.array(0, jnp.int32)
    )

    def cycle_step(carried, cycle_index):
        key_now, value_now, (dquery_acc, dkey_acc, dvalue_acc, relative_bias_tables) = carried
        key_next, value_next = passed_along((key_now, value_now), "ctx", 1)
        dkey_next, dvalue_next = (
            from_behind(dkey_acc.astype(jnp.bfloat16), "ctx", 1).astype(dkey_acc.dtype),
            from_behind(dvalue_acc.astype(jnp.bfloat16), "ctx", 1).astype(dvalue_acc.dtype),
        )
        relation = jnp.where(position >= cycle_index, cycle_index, -1)
        updated = visit(
            (dquery_acc, dkey_next, dvalue_next, relative_bias_tables),
            key_next,
            value_next,
            relation,
        )
        return ((key_next, value_next, updated), None)

    (
        unused_key,
        unused_value,
        (dquery_total, dkey_part, dvalue_part, relative_bias_tables),
    ), unused = lax.scan(cycle_step, (key_low, value_low, first_state), jnp.arange(1, cycle_size))
    dkey_total, dvalue_total = (
        from_behind(dkey_part.astype(jnp.bfloat16), "ctx", 1).astype(dkey_part.dtype),
        from_behind(dvalue_part.astype(jnp.bfloat16), "ctx", 1).astype(dvalue_part.dtype),
    )
    dquery_low = dquery_total.astype(jnp.bfloat16)
    dkey_low = dkey_total.astype(jnp.bfloat16)
    dvalue_low = dvalue_total.astype(jnp.bfloat16)
    current_bucket_selector, previous_bucket_selector, onehot_far = onehots
    grad_biastable = (
        jnp.einsum(
            "afw,mfw->am",
            current_bucket_selector,
            relative_bias_tables[0],
            precision=strongest_precision,
        )
        + jnp.einsum(
            "afw,mfw->am",
            previous_bucket_selector,
            relative_bias_tables[1],
            precision=strongest_precision,
        )
        + onehot_far[:, None] * relative_bias_tables[2][None, :]
    )
    return dquery_low, dkey_low, dvalue_low, grad_biastable


def heads_forward(tokens, given):
    wa, owners = lax.axis_index("wa"), lax.axis_size("wa")
    table = given["biastable"].astype(F32)
    selector = lax.dynamic_slice_in_dim(line_selector(), wa * table.shape[0], table.shape[0], 0)
    lines = jnp.dot(table.T, selector, precision=strongest_precision).astype(BF)

    def placed(gain):
        row = jnp.zeros((LINE,), BF)
        return lax.dynamic_update_slice(row, gain, (wa * gain.shape[0],))

    gains = jnp.stack([placed(given[name]) for name in GAINS])
    small = jnp.concatenate([lines, gains, jnp.zeros((H - len(GAINS), LINE), BF)], 0)
    shards = [given[LONG_NAMES[name]] for name in GATHERED]
    *wholes, attended_low, low, qh, kh, vh, ot, lse, small = attn_forward(
        lax.axis_size("ctx"), tokens, small, shards
    )
    width = tokens.shape[1]
    gain_of = {name: small[H + g, :width] for g, name in enumerate(GAINS)}
    full = {LONG_NAMES[name]: whole for name, whole in zip(GATHERED, wholes, strict=True)}
    return attended_low, low, full, gain_of, (qh, kh, vh, ot, lse, small[:H])


def heads_backward(state, dout_low, parts, feed_part):
    peers = lax.axis_size("ctx")
    dquery_low, dkey_low, dvalue_low, sums, *shares = attn_backward(
        peers, dout_low, *state, parts, feed_part
    )
    selector = line_selector()
    table = jnp.dot(selector, sums[:2].T, precision=strongest_precision)
    far = jnp.sum(sums[2:4], axis=1)
    table = table + selector[:, WIDE : WIDE + 1] * far[None, :]
    whole = jnp.zeros((NB, H), jnp.float32)
    whole = lax.dynamic_update_slice(whole, table, (0, 2 * lax.axis_index("ctx")))
    return dquery_low, dkey_low, dvalue_low, whole, shares


def cross_pair(groups, keep_ref, q_ref, dx_ref, k_ref, v_ref, dq_ref, dk_ref, dv_ref, q_pad, dx_pad, dq_pad, p):
    lanes = lanes_of(p)
    padded_rows(q_pad, q_ref[:, lanes])
    padded_rows(dx_pad, dx_ref[:, lanes])
    dx_pad[:SPAN, :] = dx_pad[:SPAN, :] * keep_ref[0:1, :]
    for g in range(groups):
        rows = slice(g * 256, (g + 1) * 256)
        query = both_heads(q_pad, g) * BF(HD**-0.5)
        dmixed = both_heads(dx_pad, g)
        keys, values = k_ref[rows, lanes], v_ref[rows, lanes]
        scores = nt_dot(keys, query)
        weights = jnp.exp(scores - jnp.max(scores, axis=0, keepdims=True))
        weights = weights / jnp.sum(weights, axis=0, keepdims=True)
        dweights = nt_dot(values, dmixed)
        dscores = weights * (dweights - jnp.sum(weights * dweights, axis=0, keepdims=True))
        dk_ref[rows, lanes] = nn_dot(dscores.astype(BF), query).astype(BF)
        dv_ref[rows, lanes] = nn_dot(weights.astype(BF), dmixed).astype(BF)
        back = (dscores * HD**-0.5).T.astype(BF)
        dq_pad[g * SPAN : (g + 1) * SPAN, :] = join_heads(nn_dot(back, keys))
    dq_ref[:, lanes] = dq_pad[1 : dq_ref.shape[0] + 1, :].astype(BF)


def middle_kernel(
    keep_ref, q_ref, dx_ref, k_ref, v_ref, near_ref, wk_ref, wv_ref, fin_ref, fout_ref,
    dq_ref, dwk_ref, dwv_ref, near_out, last_out, feed_out,
    dk, dv, q_pad, dx_pad, dq_pad, share, hold, load_sem, ring_send, ring_recv,
):
    ring = Ring(FEED_LANES, ring_send, ring_recv, share=share, hold=hold)
    loads = [
        pltpu.make_async_copy(part, share.at[b], load_sem.at[b])
        for b, part in enumerate((fin_ref, fout_ref))
    ]
    for load in loads:
        load.start()
    meet([{"ctx": ring.after}, {"ctx": ring.before}])
    for load in loads:
        load.wait()
    for lanes in FEED_TURNS:
        ring.scatter(jnp.int32(0), lanes)
    groups = k_ref.shape[0] // 256

    def two_pairs(m, unused):
        for turn, lanes in enumerate(FEED_TURNS):
            cross_pair(
                groups, keep_ref, q_ref, dx_ref, k_ref, v_ref, dq_ref, dk, dv, q_pad, dx_pad, dq_pad,
                2 * m + turn,
            )
            ring.scatter(m + 1, lanes)
        return unused

    pairs = q_ref.shape[1] // (2 * WIDE)
    lax.fori_loop(0, pairs, two_pairs, 0)
    calls = [(step, lanes) for step in range(pairs + 1, HOPS + 1) for lanes in FEED_TURNS]

    def turn():
        if calls:
            step, lanes = calls.pop(0)
            ring.scatter(jnp.int32(step), lanes)

    for g in range(groups):
        rows = slice(g * 256, (g + 1) * 256)
        total = nt_dot(dk[rows, :], wk_ref[...]) + nt_dot(dv[rows, :], wv_ref[...])
        near_out[rows, :] = total.astype(BF)
        if g == groups - 1:
            last_out[...] = total
        if g % 2 == 1:
            turn()
    for c in range(near_ref.shape[1] // WIDE):
        lanes = slice(c * WIDE, (c + 1) * WIDE)
        left = near_ref[:, lanes].astype(F32).T.astype(BF)
        dwk_ref[lanes, :] = nn_dot(left, dk[...]).astype(BF)
        dwv_ref[lanes, :] = nn_dot(left, dv[...]).astype(BF)
        if c % 2 == 1:
            turn()
    while calls:
        turn()
    for lane in range(2):
        feed_out[lane] = share[lane, ring.chunk(lane, 1)]
    ring.finish(lambda lane: share.at[FEED_LANES[lane][0], 0, FEED_LANES[lane][2]])


def middle(keep, query, dmixed, keys, values, near, wk, wv, fin, fout):
    many, width = keys.shape
    wide = near.shape[1]
    low = functools.partial(jax.ShapeDtypeStruct, dtype=BF)
    dma = pltpu.SemaphoreType.DMA
    pad = pltpu.VMEM((many // 256 * SPAN, WIDE), F32)
    return pl.pallas_call(
        middle_kernel,
        out_shape=(
            low(query.shape),
            low(wk.shape),
            low(wv.shape),
            low(near.shape),
            jax.ShapeDtypeStruct((256, wide), F32),
            low((2, *FEED[1:])),
        ),
        in_specs=vmem(8) + [pl.BlockSpec(memory_space=pl.ANY)] * 2,
        out_specs=tuple(vmem(6)),
        scratch_shapes=[
            pltpu.VMEM((many, width), BF),
            pltpu.VMEM((many, width), BF),
            pad,
            pad,
            pad,
            pltpu.VMEM((2, *FEED), BF),
            pltpu.VMEM((2, HOPS, *FEED[1:]), BF),
            dma((2,)),
            dma((len(FEED_LANES), HOPS)),
            dma((len(FEED_LANES), HOPS)),
        ],
        compiler_params=pltpu.CompilerParams(
            collective_id=5, has_side_effects=True, vmem_limit_bytes=56 << 20
        ),
        cost_estimate=lasting(38),
        name="middle",
    )(keep, query, dmixed, keys, values, near, wk, wv, fin.reshape(FEED), fout.reshape(FEED))


NAMES_OF_WEIGHTS = (
    "selfnorm", "selfquery", "selfkey", "selfvalue", "selfout", "biastable", "crossnorm", "crossquery",
    "crosskey", "crossvalue", "crossout", "feednorm", "feedin", "feedbias", "feedout", "outbias",
)
LONG_NAMES = {
    "q": "selfquery",
    "k": "selfkey",
    "v": "selfvalue",
    "so": "selfout",
    "ck": "crosskey",
    "cv": "crossvalue",
    "cq": "crossquery",
    "co": "crossout",
}


def whole_over_wa(shard):
    return lax.all_gather(shard, "wa", axis=0, tiled=True)


def reduce_plain(parts, smalls):
    shares = [
        lax.psum_scatter(part, "wa", scatter_dimension=0, tiled=True).astype(F32)
        for part in parts.values()
    ]
    totals = lax.psum(shares, "ctx")
    return dict(zip(parts, totals, strict=True)), lax.psum(smalls, ("ctx", "wa"))


def per_device(tokens, neighbours, cotangent, *shards):
    given = dict(zip(NAMES_OF_WEIGHTS, shards, strict=True))
    peers = lax.axis_size("ctx")
    position = lax.axis_index("ctx")
    row_count, model_width = tokens.shape[1:]
    split_heads = peers * 2 == H and row_count == BLOCK
    inputs = tokens[0].astype(F32)
    upstream_low = cotangent[0]
    upstream = upstream_low.astype(F32)
    if split_heads:
        attended_low, normed_low, full, small_of, attention_state = heads_forward(tokens[0], given)
        normed_self, back_self = jax.vjp(root_norm, inputs, small_of["selfnorm"])
    else:
        small_of = {name: whole_over_wa(given[name]).astype(F32) for name in GAINS}
        full = {name: whole_over_wa(given[name]) for name in LONG_NAMES.values()}
        normed_self, back_self = jax.vjp(root_norm, inputs, small_of["selfnorm"])
        normed_low = normed_self.astype(BF)
        attended_low, attention_state = ring_forward(
            *(
                forward_product(normed_low, full[name]).astype(BF)
                for name in ("selfquery", "selfkey", "selfvalue")
            ),
            whole_over_wa(given["biastable"]),
        )
    attended_low, feed_in, upstream_low = lax.optimization_barrier(
        (attended_low, given["feedin"], upstream_low)
    )
    upstream_all = lax.all_gather(upstream_low, "wa", axis=0)
    feed_in = lax.all_to_all(feed_in, "wa", 1, 0, tiled=True)
    hidden = inputs + forward_product(attended_low, full["selfout"])

    spans = neighbours.shape[1]
    span_rows = neighbours.shape[2] * neighbours.shape[3]
    own_rows = neighbours[0].reshape(spans * span_rows, model_width)
    before = passed_along(own_rows[-span_rows:], "ctx", 1)
    near_rows = jnp.concatenate([before, own_rows], 0)
    keys_cross = forward_product(near_rows, full["crosskey"]).astype(BF)
    values_cross = forward_product(near_rows, full["crossvalue"]).astype(BF)
    normed_cross, back_cross = jax.vjp(root_norm, hidden, small_of["crossnorm"])
    cross_in = normed_cross.astype(BF)
    query_cross = forward_product(cross_in, full["crossquery"]).astype(BF)
    keep = jnp.full((8, WIDE), jnp.where(position > 0, 1.0, 0.0), F32)
    mixed_low = cross_forward(keep, query_cross, keys_cross, values_cross)
    hidden_two = hidden + forward_product(mixed_low, full["crossout"])

    normed_feed, back_feed = jax.vjp(root_norm, hidden_two, small_of["feednorm"])
    feed_low = normed_feed.astype(BF)
    bias_row = given["feedbias"].astype(F32)[None]
    fed, grad_feed, fin, fout, bias_sums = ffn(
        feed_low, upstream_all, feed_in, given["feedout"], bias_row
    )
    result = (hidden_two + fed + small_of["outbias"]).astype(BF)
    grad_two_part, grad_feednorm = back_feed(grad_feed)
    grad_two = upstream + grad_two_part
    two_low = grad_two.astype(BF)

    grad_mixed = back_product(two_low, full["crossout"]).astype(BF)
    early = {}
    if split_heads:
        grad_query_cross, early["ck"], early["cv"], near_low, near_last, feed_part = middle(
            keep,
            query_cross,
            grad_mixed,
            keys_cross,
            values_cross,
            near_rows,
            full["crosskey"],
            full["crossvalue"],
            fin,
            fout,
        )
    else:
        grad_query_cross, dkeys, dvalues = cross_backward(
            keep, query_cross, grad_mixed, keys_cross, values_cross
        )
        near_grads = back_product(dkeys, full["crosskey"]) + back_product(
            dvalues, full["crossvalue"]
        )
        near_low, near_last = near_grads.astype(BF), near_grads[-span_rows:]
        early["ck"] = outer_product(near_rows, dkeys).astype(BF)
        early["cv"] = outer_product(near_rows, dvalues).astype(BF)
    back = passed_along(near_low[:span_rows], "ctx", -1).astype(F32)
    grad_hidden_part, grad_crossnorm = back_cross(
        back_product(grad_query_cross, full["crossquery"])
    )
    grad_hidden = grad_two + grad_hidden_part
    hidden_low = grad_hidden.astype(BF)
    dout_low = back_product(hidden_low, full["selfout"]).astype(BF)
    early["cq"] = outer_product(cross_in, grad_query_cross).astype(BF)
    early["co"] = outer_product(mixed_low, two_low).astype(BF)
    early["so"] = outer_product(attended_low, hidden_low).astype(BF)
    if split_heads:
        dquery_low, dkey_low, dvalue_low, grad_biastable, shares = heads_backward(
            attention_state, dout_low, [early[name] for name in EARLY], feed_part
        )
        *shares, fin, fout = shares
    else:
        dquery_low, dkey_low, dvalue_low, grad_biastable = ring_backward(attention_state, dout_low)
    grad_normed = (
        back_product(dquery_low, full["selfquery"])
        + back_product(dkey_low, full["selfkey"])
        + back_product(dvalue_low, full["selfvalue"])
    )
    grad_input_part, grad_selfnorm = back_self(grad_normed)
    grad_inputs = (grad_hidden + grad_input_part).astype(BF)

    edge = span_rows * spans
    grad_neigh = (
        jnp.concatenate([near_low[span_rows:edge], (near_last + back).astype(BF)], 0)
        .reshape(neighbours.shape)
    )
    late = {
        "q": outer_product(normed_low, dquery_low).astype(BF),
        "k": outer_product(normed_low, dkey_low).astype(BF),
        "v": outer_product(normed_low, dvalue_low).astype(BF),
    }
    wa, owners = lax.axis_index("wa"), lax.axis_size("wa")
    bias_grad = jnp.sum(bias_sums, axis=0)
    placed = lax.dynamic_update_slice(
        jnp.zeros((owners, bias_grad.size), F32), bias_grad[None], (wa, 0)
    )
    sums = [grad_selfnorm, grad_crossnorm, grad_feednorm, jnp.sum(upstream, axis=0), grad_biastable]
    packed = jnp.concatenate([*(v.reshape(owners, -1) for v in sums), placed], axis=1)
    packed = jnp.pad(packed, ((0, 0), (0, LINE * 2 - packed.shape[1]))).reshape(-1, WIDE)
    if split_heads:
        *reduced, fin = reduce_grads(*shares, packed, [late[name] for name in LATE], fin)
        reduced = dict(zip(NAMES, reduced, strict=True))
        grads, packed = unfold(reduced), reduced["small"]
        fin = jnp.transpose(fin, (1, 0, 2)).reshape(given["feedin"].shape)
        fout = fout.reshape(given["feedout"].shape)
    else:
        grads, packed = reduce_plain(early | late, packed)
        fin, fout = lax.psum((fin, fout), "ctx")
        fin = lax.all_to_all(fin, "wa", 0, 1, tiled=True)
    grads["fin"], grads["fout"] = fin.astype(F32), fout.astype(F32)
    mine = lax.dynamic_index_in_dim(packed.reshape(owners, -1), wa, 0, keepdims=False)
    cuts, start = [], 0
    for v in (*sums, placed):
        cuts.append(mine[start : start + v.size // owners])
        start += v.size // owners
    own_selfnorm, own_crossnorm, own_feednorm, own_outbias, own_table, own_feedbias = cuts
    return (
        result[None],
        grad_inputs[None],
        grad_neigh,
        own_selfnorm,
        grads["q"],
        grads["k"],
        grads["v"],
        grads["so"],
        own_table.reshape(-1, H),
        own_crossnorm,
        grads["cq"],
        grads["ck"],
        grads["cv"],
        grads["co"],
        own_feednorm,
        grads["fin"],
        own_feedbias,
        grads["fout"],
        own_outbias,
    )


def solution(mesh):
    return jax.shard_map(
        per_device,
        mesh=mesh,
        in_specs=(
            P("wa", "ctx", None),
            P("wa", "ctx", None, None, None),
            P("wa", "ctx", None),
            P("wa"),
            P("wa", None),
            P("wa", None),
            P("wa", None),
            P("wa", None),
            P("wa", None),
            P("wa"),
            P("wa", None),
            P("wa", None),
            P("wa", None),
            P("wa", None),
            P("wa"),
            P("wa", None),
            P("wa"),
            P("wa", None),
            P("wa"),
        ),
        out_specs=(
            P("wa", "ctx", None),
            P("wa", "ctx", None),
            P("wa", "ctx", None, None, None),
            P("wa"),
            P("wa", None),
            P("wa", None),
            P("wa", None),
            P("wa", None),
            P("wa", None),
            P("wa"),
            P("wa", None),
            P("wa", None),
            P("wa", None),
            P("wa", None),
            P("wa"),
            P("wa", None),
            P("wa"),
            P("wa", None),
            P("wa"),
        ),
        check_vma=False,
    )
```

time: 1370 us -> 550 us (0.40)
  blocking collectives: 572 us -> 0 us
  Pallas kernels: 117 us -> 418 us
  waiting for transfers between devices: 300 us -> 0.03 us
  matrix products: 215 us -> 35 us
  local copies, waits for them, and re-layouts: 114 us -> 43.2 us
    psum x1 -> x0, blocking collectives: 542 us -> none  [per_device(): lax.psum((shares[0], shares[1], shares[2], shares[3], shares[4], shares[5...]
    pallas_call x1 -> x5, Pallas kernels: 48 us -> 301 us  [the longest x1 103 us: reduce_grads(): pl.pallas_call(reduce_kernel, out_shape=(*(jax.ShapeDtypeStruct(BUFFERS[b...]
    reduce_scatter x8 -> x0, waiting for transfers between devices: 137 us -> none  [the longest x1 61.8 us: per_device(): lax.psum_scatter(grad_feedout.astype(jnp.bfloat16), 'wa', scatter_dimensi...]
    dot_general x7 -> x1, matrix products: 108 us -> 0.34 us  [heads_forward(): lines = jnp.dot(table.T, selector, precision=strongest_precision).astype(BF)]
    all_gather x10 -> x1, waiting for transfers between devices: 88.9 us -> 0.01 us  [per_device(): upstream_all = lax.all_gather(upstream_low, 'wa', axis=0)]
    unnamed x22 -> x1, waiting for transfers between devices: 69.8 us -> 0.02 us
    pallas_call x1, Pallas kernels: 68.9 us -> 117 us  [attn_backward(): pl.pallas_call(functools.partial(attn_backward_kernel, n), out_shape=(gra...]
    dot_general x10 -> x6, matrix products: 39.5 us -> 11.7 us  [outer_product(): lax.dot_general(left_side, right_side, (((0,), (0,)), ((), ())), preferre...]
  transfers between devices with their start and end apart: 24 -> 4, of which waited for: 12 -> 0; matrix products, arithmetic and copies ran while one was open for 19% -> 10% of each run, Pallas kernels for 4% -> 59%
where the time goes in v3:
time: 550 us; the launch traced here: 540 us
  Pallas kernels  418 us (76%)
  local copies, waits for them, and re-layouts  43.2 us (8%)
  matrix products  35 us (6%)
  other arithmetic  18.1 us (3%)
  between operations  15.1 us (3%)
  starting transfers between devices  11.5 us (2%)
    pallas_call x1, Pallas kernels, attn_backward(): pl.pallas_call(functools.partial(attn_backward_kernel, n), out_shape=(gra...  117 us
    pallas_call x1, Pallas kernels, reduce_grads(): pl.pallas_call(reduce_kernel, out_shape=(*(jax.ShapeDtypeStruct(BUFFERS[b...  103 us
    pallas_call x1, Pallas kernels, attn_forward(): pl.pallas_call(functools.partial(attn_forward_kernel, n), out_shape=(*who...  91.9 us
    pallas_call x1, Pallas kernels, middle(): pl.pallas_call(middle_kernel, out_shape=(low(query.shape), low(wk.shape),...  50.7 us
    pallas_call x1, Pallas kernels, ffn(): pl.pallas_call(ffn_kernel, out_shape=(jax.ShapeDtypeStruct(block, F32), j...  45.4 us
    unnamed x138, local copies, waits for them, and re-layouts  16.5 us
    dot_general x5, matrix products, forward_product(): return jnp.dot(values, weight, preferred_element_type=jnp.float32)  14.8 us
    dot_general x6, matrix products, outer_product(): lax.dot_general(left_side, right_side, (((0,), (0,)), ((), ())), preferre...  11.7 us
  transfers between devices with their start and end apart: 4, of which 0 were waited for; matrix products, arithmetic and copies ran while one was open for 10% of the time, Pallas kernels for 59%

profile of v3, /device:TPU:0, one launch (start us, length us, event | category | flops | bytes accessed | tf_op | source)
XLA Modules:
  0.0 540.4 jit_solution(2987813938554371831)
XLA Ops:
  7.3 1.8 slice.90
  9.1 5.7 %collective-permute-start = (bf16[256,896]{1,0:T(8,128)(2,1)}, bf16[256,896]{1,0:T(8,128)(2,1)}, u32[]{:S(2)}, u32[]{:S(2)}) collective-permute-start(bf16[256,896]{1,0:T(8,128)(2,1)} %bitcast.3), channel_id=1, source_target_pairs={{0,4},{4,8},{8,12},{12,16},{16,20},{20,24},{24,28},{1,5},{5,9},{9,... | collective-permute-start | bytes 1376264 | tf_op jit(solution)/shard_map/ppermute | solution.py:32
  28.1 91.9 %attn_forward.1 = (bf16[896,1024]{1,0:T(8,128)(2,1)S(1)}, bf16[896,1024]{1,0:T(8,128)(2,1)}, bf16[896,1024]{1,0:T(8,128)(2,1)}, bf16[1024,896]{1,0:T(8,128)(2,1)...) custom-call(bf16[256,896]{1,0:T(8,128)(2,1)S(1)} %bitcast.71, ...), custom_call_target="tpu_custom_call" | custom-call | bytes 255000000 | tf_op jit(solution)/shard_map/attn_forward/pallas_call | solution.py:662
  124.1 3.5 copy.46
  127.6 4.5 all-to-all-start
  132.9 2.3 multiply_reduce_fusion.5
  138.4 2.5 convolution_convert_fusion.10.q_ref
  140.9 4.7 convolution_convert_fusion.1.k_ref
  145.7 4.5 convolution_convert_fusion.v_ref
  150.3 9.7 %cross_forward.1 = bf16[256,1024]{1,0:T(8,128)(2,1)S(1)} custom-call(f32[8,128]{1,0:T(8,128)S(1)} %broadcast_in_dim.53.keep_ref, bf16[256,1024]{1,0:T(8,128)(2,1)S(1)} %convolution_convert_fusion.10.q_ref, bf16[1280,1024]{1,0:T(8,128)(2,1)S(1)} %convolution_convert_fusion.1.k_ref, bf16[1280,1024]{1,0:T(8,128)(2,1)S(1)} %convolution_convert_fusion.v_ref), custom_call_target="tpu_custom_call" | custom-call | bytes 27000000 | tf_op jit(solution)/shard_map/cross_forward/pallas_call | solution.py:1240
  161.8 2.6 pad_maximum_fusion.near_ref
  164.4 45.4 %feed_forward.1 = (f32[256,896]{1,0:T(8,128)}, f32[256,896]{1,0:T(8,128)}, bf16[896,896]{1,0:T(8,128)(2,1)}, bf16[896,896]{1,0:T(8,128)(2,1)}, f32[8,896]{1,0:T(8,128)}) custom-call(bf16[256,896]{1,0:T(8,128)(2,1)} %multiply_convert_fusion.f_ref, bf16[4,256,896]{2,1,0:T(8,128)(2,1)} %bitcast.79, bf16[896,896]{1,0:T(8,128)(2,1)} %bitcast.7.win_ref, ...), custom_call_target="tpu_custom_call" | custom-call | bytes 132000000 | tf_op jit(solution)/shard_map/feed_forward/pallas_call | solution.py:1170
  209.8 1.5 multiply_reduce_fusion
  211.4 2.5 convert_add_fusion.1
  213.8 1.5 convolution_convert_fusion.9.dx_ref
  215.4 50.7 %middle.1 = (bf16[256,1024]{1,0:T(8,128)(2,1)}, bf16[896,1024]{1,0:T(8,128)(2,1)}, bf16[896,1024]{1,0:T(8,128)(2,1)}, bf16[1280,896]{1,0:T(8,128)(2,1)}, f32[256...) custom-call(f32[8,128]{1,0:T(8,128)} %copy-done.26, bf16[256,1024]{1,0:T(8,128)(2,1)} %copy-done.8, ...), custom_call_target="tpu_custom_call" | custom-call | bytes 114000000 | tf_op jit(solution)/shard_map/middle/pallas_call | solution.py:1565
  266.1 2.0 slice.97
  268.1 2.5 slice.96
  271.7 2.0 convolution_convert_fusion.7.rest_0_
  275.2 1.5 convolution_convert_fusion.8.do_ref
  276.7 2.0 convolution_convert_fusion.5.rest_4_
  278.7 2.0 convolution_convert_fusion.6.rest_3_
  282.3 116.6 %attn_backward.1 = (bf16[256,1024]{1,0:T(8,128)(2,1)}, bf16[256,1024]{1,0:T(8,128)(2,1)}, bf16[256,1024]{1,0:T(8,128)(2,1)}, f32[8,1024]{1,0:T(8,128)}, bf16[448...) custom-call(bf16[256,1024]{1,0:T(8,128)(2,1)} %convolution_convert_f, ...), custom_call_target="tpu_custom_call" | custom-call | bytes 300000000 | tf_op jit(solution)/shard_map/attn_backward/pallas_call | solution.py:862
  398.9 1.8 fusion.36
  400.8 1.9 convolution_convert_fusion.4.refs_4_
  402.7 1.9 convolution_convert_fusion.3.refs_5_
  404.6 1.9 convolution_convert_fusion.2.refs_6_
  411.1 103.3 %reduce_grads.1 = (bf16[448,1024]{1,0:T(8,128)(2,1)}, bf16[224,1024]{1,0:T(8,128)(2,1)}, bf16[8,64,896]{2,1,0:T(8,128)(2,1)}, bf16[448,1024]{1,0:T(8,128)(2,1)},...) custom-call(bf16[448,1024]{1,0:T(8,128)(2,1)} %get-tuple-element.96.refs_0_, ...), custom_call_target="tpu_custom_call" | custom-call | bytes 270000000 | tf_op jit(solution)/shard_map/reduce_grads/pallas_call | solution.py:1032
  516.0 2.7 fusion.32
  521.0 2.0 fusion.33
  525.0 2.1 copy.44
  528.5 2.0 bitcast_convert_fusion
  (208 shorter events, 41.7 us)
Async XLA Ops:
  7.2 11.2 %copy-start = (bf16[8,16]{1,0:T(8,128)(2,1)S(1)}, bf16[8,16]{1,0:T(8,128)(2,1)}, u32[]{:S(2)}) copy-start(bf16[8,16]{1,0:T(8,128)(2,1)} %param.27) | copy-start | bytes 772
  7.2 157.2 %all-gather.3.cloned.1.call-start = ((), (), s32[]{:S(2)}) async-start(), calls=%async_computation.1 | async-start | bytes 2293760 | tf_op jit(solution)/shard_map/all_gather | solution.py:1653
  9.1 131.8 %collective-permute-start = (bf16[256,896]{1,0:T(8,128)(2,1)}, bf16[256,896]{1,0:T(8,128)(2,1)}, u32[]{:S(2)}, u32[]{:S(2)}) collective-permute-start(bf16[256,896]{1,0:T(8,128)(2,1)} %bitcast.3), channel_id=1, source_target_pairs={{0,4},{4,8},{8,12},{12,16},{16,20},{20,24},{24,28},{1,5},{5,9},{9,... | collective-permute-start | bytes 1376264 | tf_op jit(solution)/shard_map/ppermute | solution.py:32
  14.8 3.6 copy-start.59
  17.6 102.4 %copy-start.52 = (pred[32,1024]{0,1:T(8,128)(4,1)}, pred[32,1024]{0,1:T(8,128)(4,1)S(1)}, u32[]{:S(2)}) copy-start(pred[32,1024]{0,1:T(8,128)(4,1)S(1)} %iota_compare_fusion) | copy-start | bytes 98308
  124.0 3.6 copy-start.11
  124.0 8.8 %copy-start.9 = (bf16[256,1024]{1,0:T(8,128)(2,1)}, bf16[256,1024]{1,0:T(8,128)(2,1)S(1)}, u32[]{:S(2)}) copy-start(bf16[256,1024]{1,0:T(8,128)(2,1)S(1)} %get-tuple-element.66) | copy-start | bytes 1572868
  127.6 4.5 copy-start.3
  127.6 36.8 %all-to-all-start = ((bf16[224,4,896]{2,0,1:T(8,128)(2,1)}), bf16[224,4,896]{2,0,1:T(8,128)(2,1)}, u32[]{:S(2)}, u32[]{:S(2)}) async-start(bf16[224,4,896]{2,0,1:T(8,128)(2,1)} %bitcast.72), calls=%async_computation | async-start | bytes 3211264 | tf_op jit(solution)/shard_map/all_to_all | solution.py:1654
  132.3 2.9 copy-start.61
  132.9 3.7 copy-start.67
  135.2 5.7 %copy-start.27 = (f32[256,896]{1,0:T(8,128)}, f32[256,896]{1,0:T(8,128)S(1)}, u32[]{:S(2)}) copy-start(f32[256,896]{1,0:T(8,128)S(1)} %get-tuple-element.135) | copy-start | bytes 2752516
  135.2 5.7 %copy-start.64 = (f32[256]{0:T(256)}, f32[256]{0:T(256)S(1)}, u32[]{:S(2)}) copy-start(f32[256]{0:T(256)S(1)} %get-tuple-element.134) | copy-start | bytes 3076
  135.2 10.4 %copy-start.56 = (f32[256]{0:T(256)}, f32[256]{0:T(256)S(1)}, u32[]{:S(2)}) copy-start(f32[256]{0:T(256)S(1)} %fusion.27) | copy-start | bytes 3076
  137.7 3.2 copy-start.40
  140.9 9.3 %copy-start.8 = (bf16[256,1024]{1,0:T(8,128)(2,1)}, bf16[256,1024]{1,0:T(8,128)(2,1)S(1)}, u32[]{:S(2)}) copy-start(bf16[256,1024]{1,0:T(8,128)(2,1)S(1)} %convolution_convert_fusion.10.q_ref) | copy-start | bytes 1572868
  140.9 4.8 copy-start.48
  145.7 4.5 copy-start.4
  150.2 9.8 %copy-start.5 = (bf16[1280,1024]{1,0:T(8,128)(2,1)}, bf16[1280,1024]{1,0:T(8,128)(2,1)S(1)}, u32[]{:S(2)}) copy-start(bf16[1280,1024]{1,0:T(8,128)(2,1)S(1)} %convolution_convert_fusion.v_ref) | copy-start | bytes 7864324
  150.2 9.8 %copy-start.26 = (f32[8,128]{1,0:T(8,128)}, f32[8,128]{1,0:T(8,128)S(1)}, u32[]{:S(2)}) copy-start(f32[8,128]{1,0:T(8,128)S(1)} %broadcast_in_dim.53.keep_ref) | copy-start | bytes 12292
  150.2 9.8 %copy-start.28 = (f32[256,896]{1,0:T(8,128)S(1)}, f32[256,896]{1,0:T(8,128)}, u32[]{:S(2)}) copy-start(f32[256,896]{1,0:T(8,128)} %copy-done.27) | copy-start | bytes 2752516
  150.2 9.8 %copy-start.32 = (bf16[1024,896]{1,0:T(8,128)(2,1)S(1)}, bf16[1024,896]{1,0:T(8,128)(2,1)}, u32[]{:S(2)}) copy-start(bf16[1024,896]{1,0:T(8,128)(2,1)} %get-tuple-element.72) | copy-start | bytes 5505028
  266.1 4.6 copy-start.29
  266.1 4.6 copy-start.35
  266.1 4.6 copy-start.44
  266.1 4.6 copy-start.57
  275.2 3.5 copy-start.30
  281.0 249.5 %collective-permute-start.1 = (bf16[256,896]{1,0:T(8,128)(2,1)}, bf16[256,896]{1,0:T(8,128)(2,1)}, u32[]{:S(2)}, u32[]{:S(2)}) collective-permute-start(bf16[256,896]{1,0:T(8,128)(2,1)} %slice.97), channel_id=1, source_target_pairs={{4,0},{8,4},{12,8},{16,12},{20,16},{24,20},{28,24},{5,1},{9,5},{13... | collective-permute-start | bytes 1376264 | tf_op jit(solution)/shard_map/ppermute | solution.py:32
  282.3 116.6 %copy-start.12 = (bf16[896,1024]{1,0:T(8,128)(2,1)S(1)}, bf16[896,1024]{1,0:T(8,128)(2,1)}, u32[]{:S(2)}) copy-start(bf16[896,1024]{1,0:T(8,128)(2,1)} %copy-done.11) | copy-start | bytes 5505028
  521.0 3.0 copy-start.53
  525.0 3.4 copy-start.49
  530.5 2.8 copy-start.1
  (41 other events, 59.4 us)
Sparse Core Ops, SparseCore 0:
  124.2 37.5 all-gather.2

commit v4 on v3

--- a/solution.py
+++ b/solution.py
@@ -378,13 +378,16 @@
             )
 
     def send(self, name):
+        self.prepare(name)
+        self.x_copies[name].start()
+
+    def prepare(self, name):
         slot, (own, inn, out, _) = self.slots[name]
         for x in range(2):
             self.own_copies[name, x].wait()
             self.core_copies[name, x].wait_recv()
         away = 1 - self.half
         out[slot] = (own[slot, away].astype(F32) + inn[slot, away].astype(F32)).astype(BF)
-        self.x_copies[name].start()
 
     def total(self, name):
         slot, (own, inn, _, land) = self.slots[name]
@@ -453,70 +456,150 @@
 
 
 GATHERED = ("q", "k", "v", "so", "ck", "cv", "cq", "co")
+SINGLE = ("cot",)
 GAINS = ("selfnorm", "crossnorm", "feednorm", "outbias")
 
 
 class Gathering:
-    def __init__(self, names, shards, whole, own_sem, send, recv):
-        self.names, self.shards, self.whole = names, shards, whole
+    def __init__(self, shards, whole, own_sem, send, recv):
+        self.names, self.shards, self.whole = tuple(shards), shards, whole
         self.sems = own_sem, send, recv
-        self.wa = lax.axis_index("wa")
+        self.wa, me = lax.axis_index("wa"), lax.axis_index("ctx")
         self.mate, self.across = other_wa(self.wa, 1), other_wa(self.wa, 2)
+        self.y = lax.rem(me, 2)
+        self.beside = me + 1 - 2 * self.y
         self.copies = {}
 
     def start(self):
         own_sem, send, recv = self.sems
         for u, name in enumerate(self.names):
-            rows = self.shards[name].shape[0]
             shard, whole = self.shards[name], self.whole[name]
-            mine = whole.at[pl.ds(pl.multiple_of(self.wa * rows, 16), rows)]
-            theirs = whole.at[pl.ds(pl.multiple_of(self.across * rows, 16), rows)]
-            over = remote(shard, mine, send.at[u, 0], recv.at[u, 0], wa=self.across)
-            near = remote(shard, mine, send.at[u, 1], recv.at[u, 1], wa=self.mate)
-            near.start()
-            own = pltpu.make_async_copy(shard, mine, own_sem.at[u])
-            own.start()
-            pass_on = remote(theirs, theirs, send.at[u, 2], recv.at[u, 2], wa=self.mate)
-            self.copies[name] = (over, near, pass_on, own)
+            rows = shard.shape[0]
+            parts = 1 if name in SINGLE else 2
+            some = rows // parts
+            shift = 0 if parts == 1 else self.y * some
+
+            def at(start, count, ref=whole):
+                return ref.at[pl.ds(pl.multiple_of(start, 16), count)]
+
+            mine = at(self.wa * rows, rows)
+            theirs = at(self.across * rows, rows)
+            theirs_some = at(self.across * rows + shift, some)
+            self.copies[name] = {
+                "over": remote(
+                    at(shift, some, shard), at(self.wa * rows + shift, some), send.at[u, 0], recv.at[u, 0], wa=self.across
+                ),
+                "near": remote(shard, mine, send.at[u, 1], recv.at[u, 1], wa=self.mate),
+                "pass": remote(theirs, theirs, send.at[u, 2], recv.at[u, 2], wa=self.mate),
+                "side": remote(theirs_some, theirs_some, send.at[u, 3], recv.at[u, 3], ctx=self.beside),
+                "own": pltpu.make_async_copy(shard, mine, own_sem.at[u]),
+            }
+            self.copies[name]["near"].start()
+            self.copies[name]["own"].start()
 
     def cross(self, *names):
         for name in names:
-            self.copies[name][0].start()
+            self.copies[name]["over"].start()
 
     def forward(self, *names):
         for name in names:
-            over, _, pass_on, _ = self.copies[name]
+            self.copies[name]["over"].wait_recv()
+            self.copies[name]["pass" if name in SINGLE else "side"].start()
+
+    def land(self, *names):
+        for name in names:
+            self.copies[name]["side"].wait_recv()
+            self.copies[name]["pass"].start()
+
+    def arrive(self, *names):
+        for name in names:
+            self.copies[name]["near"].wait_recv()
+            self.copies[name]["pass"].wait_recv()
+            self.copies[name]["own"].wait()
+
+    def finish(self):
+        for name, copies in self.copies.items():
+            for which in ("over", "near", "pass") + (() if name in SINGLE else ("side",)):
+                copies[which].wait_send()
+
+
+class Columns:
+    def __init__(self, gathering, shard, whole, send, recv):
+        wa, mate, across, y = gathering.wa, gathering.mate, gathering.across, gathering.y
+        both = other_wa(across, 1)
+        rows, width = shard.shape[0], whole.shape[1]
+        some = rows // 2
+
+        def block(owner, columns):
+            return shard.at[owner, pl.ds(pl.multiple_of(columns * width, WIDE), width)]
+
+        def at(start, count):
+            return whole.at[pl.ds(pl.multiple_of(start, 16), count)]
+
+        everything = slice(0, rows)
+        mine = pl.ds(pl.multiple_of(y * some, 16), some)
+        self.own = pltpu.make_async_copy(block(everything, wa), at(wa * rows, rows), send.at[5])
+        self.near = remote(block(everything, mate), at(wa * rows, rows), send.at[0], recv.at[0], wa=mate)
+        self.over = [
+            remote(block(mine, peer), at(wa * rows + y * some, some), send.at[1 + d], recv.at[1 + d], wa=peer)
+            for d, peer in enumerate((across, both))
+        ]
+        self.side = []
+        for d, peer in enumerate((across, both)):
+            got = at(peer * rows + y * some, some)
+            self.side.append(remote(got, got, send.at[3 + d], recv.at[3 + d], ctx=gathering.beside))
+
+    def start(self):
+        self.own.start()
+        self.near.start()
+
+    def cross(self):
+        for copy in self.over:
+            copy.start()
+
+    def forward(self):
+        for over, side in zip(self.over, self.side, strict=True):
             over.wait_recv()
-            pass_on.start()
-
-    def arrive(self, name):
-        _, near, pass_on, own = self.copies[name]
-        near.wait_recv()
-        pass_on.wait_recv()
-        own.wait()
+            side.start()
 
     def finish(self):
-        for copies in self.copies.values():
-            for copy in copies[:3]:
-                copy.wait_send()
-
-
-def attn_forward_kernel(n, tokens_ref, small_ref, *refs):
-    shards = dict(zip(GATHERED, refs[:8], strict=True))
-    wholes = dict(zip(GATHERED, refs[8:16], strict=True))
-    o_ref, low_ref, qh_out, kh_out, vh_out, ot_out, lse_out, small_out = refs[16:24]
+        self.own.wait()
+        self.near.wait()
+        for over, side in zip(self.over, self.side, strict=True):
+            side.wait()
+            over.wait_send()
+
+
+def attn_forward_kernel(n, tokens_ref, small_ref, near_ref, *refs):
+    shards = dict(zip((*GATHERED, "cot"), refs[:9], strict=True))
+    feed_ref = refs[9]
+    wholes = dict(zip((*GATHERED, "cot"), refs[10:19], strict=True))
+    feed_whole = refs[19]
+    o_ref, low_ref, qh_out, kh_out, vh_out, ot_out, lse_out, small_out, before_ref, keys_ref, values_ref = refs[20:31]
     (
-        held_q, held_k, held_v, proj, small_in, small_mid, qh, kh, vh, vt, oh, land, tiles, acc, stat,
-        send, recv, osend, orecv, small_sem, own_sem, out_sem, gather_send, gather_recv,
-    ) = refs[24:]
-    held = {"q": held_q, "k": held_k, "v": held_v}
-    gathering = Gathering(GATHERED, shards, wholes | held, own_sem, gather_send, gather_recv)
-    meet([*ctx_peers(n), {"wa": gathering.mate}, {"wa": gathering.across}])
+        held_q, held_k, held_v, held_ck, held_cv, proj, small_in, small_mid, qh, kh, vh, vt, oh, land, tiles,
+        acc, stat, send, recv, osend, orecv, small_sem, own_sem, out_sem, gather_send, gather_recv, feed_send,
+        feed_recv, span_sem,
+    ) = refs[31:]
+    held = {"q": held_q, "k": held_k, "v": held_v, "ck": held_ck, "cv": held_cv}
+    gathering = Gathering(shards, wholes | held, own_sem, gather_send, gather_recv)
+    columns = Columns(gathering, feed_ref, feed_whole, feed_send, feed_recv)
+    both = other_wa(gathering.across, 1)
+    meet([*ctx_peers(n), *({"wa": peer} for peer in (gathering.mate, gathering.across, both))])
     me = lax.axis_index("ctx")
     near = remote(small_ref, small_in.at[0], small_sem.at[0], small_sem.at[1], wa=gathering.mate)
     near.start()
     gathering.start()
     gathering.cross("q")
+    columns.start()
+    span_rows = before_ref.shape[0]
+    span = remote(
+        near_ref.at[near_ref.shape[0] - span_rows :],
+        before_ref,
+        span_sem.at[0],
+        span_sem.at[1],
+        ctx=lax.rem(me + 1, n),
+    )
     over = remote(small_mid, small_in.at[1], small_sem.at[2], small_sem.at[3], wa=gathering.across)
     near.wait_recv()
     small_mid[...] = (small_ref[...].astype(F32) + small_in[0].astype(F32)).astype(BF)
@@ -531,39 +614,63 @@
     bias_tiles(bias_ref, me, tiles)
     pairs = tuple((proj.at[t], dst) for t, dst in enumerate((qh, kh, vh)))
     saving = []
-    for t, name in enumerate(("q", "k", "v")):
-        gathering.forward(name)
-        gathering.cross(*(("k",), ("v",), ("so", "ck"))[t])
+
+    def save(name):
+        copy = pltpu.make_async_copy(held[name], wholes[name], out_sem.at[len(saving)])
+        copy.start()
+        saving.append(copy)
+
+    def project(t, name):
+        gathering.land(name)
         gathering.arrive(name)
         proj[t] = nn_dot(low_ref[...], held[name][...]).astype(BF)
         spread(n, me, pairs, send, recv, t)
-        copy = pltpu.make_async_copy(held[name], wholes[name], out_sem.at[t])
-        copy.start()
-        saving.append(copy)
-
-    def arrive(i):
-        @pl.when(i != me)
-        def _():
-            d = lax.rem(me - i + n, n)
-            for t, (src, dst) in enumerate(pairs):
-                to_ctx(
-                    src.at[:, lanes_of(i)], dst.at[rows_of(i, BLOCK)], send.at[t, d], recv.at[t, d], i
-                ).wait_recv()
-
-    def query_block(i, unused):
-        @pl.when(i == 5)
-        def _():
-            gathering.forward("so", "ck")
-            gathering.cross("cv", "cq")
-
-        @pl.when(i == 7)
+        save(name)
+
+    gathering.forward("q")
+    gathering.cross("k")
+    gathering.forward("k")
+    gathering.cross("v")
+    project(0, "q")
+    gathering.forward("v")
+    gathering.cross("so", "ck")
+    project(1, "k")
+    project(2, "v")
+
+    @pl.when(me < n - 1)
+    def _():
+        span.start()
+
+    gathering.forward("so", "ck")
+    gathering.cross("cv", "cq")
+
+    for d in range(1, n):
+        peer = lax.rem(me + n - d, n)
+        for t, (src, dst) in enumerate(pairs):
+            to_ctx(
+                src.at[:, lanes_of(peer)], dst.at[rows_of(peer, BLOCK)], send.at[t, d], recv.at[t, d], peer
+            ).wait_recv()
+    for i in range(n):
+        part = slice(i * BLOCK, (i + 1) * BLOCK)
+        vt[:, part] = vh[part, :].astype(F32).T.astype(BF)
+
+    def query_block(step, unused):
+        @pl.when(step == 1)
         def _():
             gathering.forward("cv", "cq")
+            gathering.land("so", "ck")
             gathering.cross("co")
-
-        arrive(i)
+            columns.cross()
+
+        @pl.when(step == 6)
+        def _():
+            gathering.land("cv", "cq")
+            gathering.forward("co")
+            columns.forward()
+            gathering.cross("cot")
+
+        i = lax.rem(me + 1 + step, n)
         rows = rows_of(i, BLOCK)
-        vt[:, rows] = vh[rows, :].astype(F32).T.astype(BF)
         q_now = qh[rows, :] * BF(HD**-0.5)
         masked = [jnp.where(head_mask(h, BLOCK), q_now, BF(0)) for h in range(2)]
 
@@ -626,7 +733,25 @@
     qh_out[...] = qh[...]
     kh_out[...] = kh[...]
     vh_out[...] = vh[...]
-    gathering.forward("co")
+
+    @pl.when(me > 0)
+    def _():
+        span.wait_recv()
+
+    @pl.when(me == 0)
+    def _():
+        before_ref[...] = jnp.zeros_like(before_ref)
+
+    for name, out_ref in (("ck", keys_ref), ("cv", values_ref)):
+        gathering.arrive(name)
+        save(name)
+        out_ref[:span_rows, :] = nn_dot(before_ref[...], held[name][...]).astype(BF)
+        for g in range(near_ref.shape[0] // span_rows):
+            rows = slice(g * span_rows, (g + 1) * span_rows)
+            there = slice((g + 1) * span_rows, (g + 2) * span_rows)
+            out_ref[there, :] = nn_dot(near_ref[rows, :], held[name][...]).astype(BF)
+    gathering.land("co")
+    gathering.forward("cot")
     for d in range(1, n):
         peer = lax.rem(me + d, n)
         for t, (src, dst) in enumerate(pairs):
@@ -639,9 +764,14 @@
         back.wait_send()
         back.wait_recv()
     o_ref[...] = land[...]
-    for name in GATHERED[3:]:
-        gathering.arrive(name)
+    gathering.arrive("so", "cq", "co", "cot")
     gathering.finish()
+    columns.finish()
+
+    @pl.when(me < n - 1)
+    def _():
+        span.wait_send()
+
     near.wait_send()
     over.wait_send()
     for copy in saving:
@@ -652,30 +782,38 @@
     return [pl.BlockSpec(memory_space=pltpu.VMEM)] * count
 
 
-def attn_forward(n, tokens, small, shards):
+def attn_forward(n, tokens, small, near, shards, feed):
     rows, seq = tokens.shape[0], n * tokens.shape[0]
     owners = lax.axis_size("wa")
-    heads = jax.ShapeDtypeStruct((seq, WIDE), BF)
-    wholes = [jax.ShapeDtypeStruct((owners * s.shape[0], s.shape[1]), BF) for s in shards]
+    low = functools.partial(jax.ShapeDtypeStruct, dtype=BF)
+    heads = low((seq, WIDE))
+    wholes = [low((owners * s.shape[0], s.shape[1])) for s in shards]
     width = wholes[0].shape[1]
     dma = pltpu.SemaphoreType.DMA
+    span_rows = 256
+    keys = low((span_rows + near.shape[0], width))
+    any_spec = pl.BlockSpec(memory_space=pl.ANY)
     return pl.pallas_call(
         functools.partial(attn_forward_kernel, n),
         out_shape=(
             *wholes,
-            jax.ShapeDtypeStruct((rows, width), BF),
-            jax.ShapeDtypeStruct(tokens.shape, BF),
+            low((owners * feed.shape[0], feed.shape[1] // owners)),
+            low((rows, width)),
+            low(tokens.shape),
             heads,
             heads,
             heads,
             jax.ShapeDtypeStruct((WIDE, seq), F32),
             jax.ShapeDtypeStruct((8, seq), F32),
             jax.ShapeDtypeStruct(small.shape, F32),
+            low((span_rows, near.shape[1])),
+            keys,
+            keys,
         ),
-        in_specs=vmem(2) + [pl.BlockSpec(memory_space=pl.ANY)] * 8,
-        out_specs=tuple([pl.BlockSpec(memory_space=pl.ANY)] * 8 + vmem(8)),
+        in_specs=vmem(3) + [any_spec] * 10,
+        out_specs=tuple([any_spec] * 10 + vmem(11)),
         scratch_shapes=[
-            *(pltpu.VMEM(w.shape, BF) for w in wholes[:3]),
+            *[pltpu.VMEM(wholes[0].shape, BF)] * 5,
             pltpu.VMEM((3, rows, width), BF),
             pltpu.VMEM((2, *small.shape), BF),
             pltpu.VMEM(small.shape, BF),
@@ -693,17 +831,20 @@
             dma((n,)),
             dma((n,)),
             dma((4,)),
-            dma((8,)),
-            dma((3,)),
-            dma((8, 3)),
-            dma((8, 3)),
+            dma((9,)),
+            dma((5,)),
+            dma((9, 4)),
+            dma((9, 4)),
+            dma((6,)),
+            dma((5,)),
+            dma((2,)),
         ],
         compiler_params=pltpu.CompilerParams(
-            collective_id=1, has_side_effects=True, vmem_limit_bytes=44 << 20
+            collective_id=1, has_side_effects=True, vmem_limit_bytes=60 << 20
         ),
         cost_estimate=lasting(85),
         name="attn_forward",
-    )(tokens, small, *shards)
+    )(tokens, small, near, *shards, feed)
 
 
 def attn_backward_kernel(
@@ -714,7 +855,7 @@
     dq_ref, dk_ref, dv_ref, line_ref, tall_pair, tall_one, flat_out = rest[6:13]
     feed_full = rest[13:15]
     (
-        doh, kt, stage, land, dk_acc, dv_acc, dqt, q_masked, do_masked, rowstat, tiles, dtiles,
+        doh, kt, stage, land, dk_acc, dv_acc, dq_acc, q_masked, do_masked, delta, tiles, dtiles,
         send, recv, gsend, grecv, ring_send, ring_recv,
     ) = rest[15:33]
     extra = rest[33:]
@@ -731,95 +872,112 @@
     for j in range(n):
         part = slice(j * BLOCK, (j + 1) * BLOCK)
         kt[:, part] = (kh[part, :].astype(F32) * HD**-0.5).T.astype(BF)
-    dk_acc[...] = jnp.zeros_like(dk_acc)
-    dv_acc[...] = jnp.zeros_like(dv_acc)
     dtiles[...] = jnp.zeros_like(dtiles)
     for name in EARLY[:2]:
         fold_wa.send(name)
+    ring.gather(jnp.int32(0), FEED_TURNS[0])
+    ring.gather(jnp.int32(0), FEED_TURNS[1])
+    dq_acc[...] = jnp.zeros_like(dq_acc)
+    for d in range(1, n):
+        peer = lax.rem(me + n - d, n)
+        to_ctx(
+            do_ref.at[:, lanes_of(peer)], doh.at[rows_of(peer, BLOCK)], send.at[0, d], recv.at[0, d], peer
+        ).wait_recv()
+    for i in range(n):
+        rows = slice(i * BLOCK, (i + 1) * BLOCK)
+        q_now = qh[rows, :] * BF(HD**-0.5)
+        do_now = doh[rows, :]
+        products = do_now.astype(F32).T * ot_ref[:, rows]
+        for h in range(2):
+            mask = head_mask(h, BLOCK)
+            q_masked[h, rows, :] = jnp.where(mask, q_now, BF(0))
+            do_masked[h, rows, :] = jnp.where(mask, do_now, BF(0))
+            delta[h : h + 1, rows] = jnp.sum(
+                products[h * HD : (h + 1) * HD], axis=0, keepdims=True
+            )
 
     def pair(t, now):
         i, j = now
         rows, there = rows_of(i, BLOCK), rows_of(j, BLOCK)
 
-        @pl.when(t == n)
+        @pl.when(t == 6)
         def _():
             for name in EARLY[2:]:
                 fold_wa.send(name)
 
         for turn, lanes in enumerate(FEED_TURNS):
 
-            @pl.when((lax.rem(t, 4) == 2 * turn) & (t <= 4 * HOPS + 2))
+            @pl.when((lax.rem(t, 4) == 2 * turn + 1) & (t <= 4 * HOPS))
             def _():
-                ring.gather(t // 4, lanes)
-
-        @pl.when(j == i)
-        def _():
-            @pl.when(i != me)
-            def _():
-                d = lax.rem(me - i + n, n)
-                to_ctx(
-                    do_ref.at[:, lanes_of(i)], doh.at[rows], send.at[0, d], recv.at[0, d], i
-                ).wait_recv()
-
-            q_now = qh[rows, :] * BF(HD**-0.5)
-            do_now = doh[rows, :]
-            products = do_now.astype(F32).T * ot_ref[:, rows]
-            for h in range(2):
-                mask = head_mask(h, BLOCK)
-                q_masked[h] = jnp.where(mask, q_now, BF(0))
-                do_masked[h] = jnp.where(mask, do_now, BF(0))
-                rowstat[h : h + 1, :] = lse_ref[h : h + 1, rows]
-                rowstat[2 + h : 3 + h, :] = jnp.sum(
-                    products[h * HD : (h + 1) * HD], axis=0, keepdims=True
-                )
-            dqt[...] = jnp.zeros_like(dqt)
-
+                ring.gather(t // 4 + 1, lanes)
+
+        first = i == j
         which = jnp.minimum(i - j, 2)
         keys, vals = kh[there, :], vh[there, :]
         dk_part, dv_part = None, None
         for h in range(2):
-            scores = nt_dot(keys, q_masked[h])
-            weights = jnp.exp(scores + tiles[h, which] - rowstat[h : h + 1, :])
-            dweights = nt_dot(vals, do_masked[h])
-            dscores = weights * (dweights - rowstat[2 + h : 3 + h, :])
+            query, dout = q_masked[h, rows, :], do_masked[h, rows, :]
+            scores = nt_dot(keys, query)
+            weights = jnp.exp(scores + tiles[h, which] - lse_ref[h : h + 1, rows])
+            dweights = nt_dot(vals, dout)
+            dscores = weights * (dweights - delta[h : h + 1, rows])
             dtiles[h, which] += dscores
             low = dscores.astype(BF)
-            dv_now = nn_dot(weights.astype(BF), do_masked[h])
-            dk_now = nn_dot(low, q_masked[h])
+            dv_now = nn_dot(weights.astype(BF), dout)
+            dk_now = nn_dot(low, query)
             dv_part = dv_now if dv_part is None else dv_part + dv_now
             dk_part = dk_now if dk_part is None else dk_part + dk_now
             half = slice(h * HD, (h + 1) * HD)
-            dqt[half, :] += nn_dot(kt[half, there], low)
-        dk_acc[there, :] += dk_part
-        dv_acc[there, :] += dv_part
-        last = j == 0
+            dq_acc[half, rows] += nn_dot(kt[half, there], low)
+
+        @pl.when(first)
+        def _():
+            dk_acc[...] = dk_part
+            dv_acc[...] = dv_part
+
+        @pl.when(jnp.logical_not(first))
+        def _():
+            dk_acc[...] += dk_part
+            dv_acc[...] += dv_part
+
+        last = i == n - 1
 
         @pl.when(last)
         def _():
-            stage[0, rows, :] = dqt[...].T.astype(BF)
-            stage[1, rows, :] = dk_acc[rows, :].astype(BF)
-            stage[2, rows, :] = dv_acc[rows, :].astype(BF)
-
-            @pl.when(i != me)
-            def _():
-                d = lax.rem(i - me + n, n)
-                for t in range(3):
-                    to_ctx(
-                        stage.at[t, rows],
-                        land.at[t, :, lanes_of(me)],
-                        gsend.at[t, d],
-                        grecv.at[t, d],
-                        i,
-                    ).start()
-
-            @pl.when(i == me)
-            def _():
-                for t in range(3):
-                    land[t, :, lanes_of(me)] = stage[t, rows, :]
-
-        return jnp.where(last, i - 1, i), jnp.where(last, i - 1, j - 1)
-
-    lax.fori_loop(0, n * (n + 1) // 2, pair, (jnp.int32(n - 1), jnp.int32(n - 1)))
+            stage[1, there, :] = dk_acc[...].astype(BF)
+            stage[2, there, :] = dv_acc[...].astype(BF)
+            deliver(j, (1, 2))
+
+        after = lax.rem(j + 1, n)
+        return jnp.where(last, after, i + 1), jnp.where(last, after, j)
+
+    def deliver(i, arrays):
+        rows = rows_of(i, BLOCK)
+
+        @pl.when(i != me)
+        def _():
+            d = lax.rem(i - me + n, n)
+            for t in arrays:
+                to_ctx(
+                    stage.at[t, rows], land.at[t, :, lanes_of(me)], gsend.at[t, d], grecv.at[t, d], i
+                ).start()
+
+        @pl.when(i == me)
+        def _():
+            for t in arrays:
+                land[t, :, lanes_of(me)] = stage[t, rows, :]
+
+    begin = lax.rem(me + 1, n)
+    lax.fori_loop(0, n * (n + 1) // 2, pair, (begin, begin))
+
+    def dq_block(step, unused):
+        i = lax.rem(me + 1 + step, n)
+        rows = rows_of(i, BLOCK)
+        stage[0, rows, :] = dq_acc[:, rows].T.astype(BF)
+        deliver(i, (0,))
+        return unused
+
+    lax.fori_loop(0, n, dq_block, 0)
     ring.finish(lambda lane: feed_full[FEED_LANES[lane][0]].at[0, FEED_LANES[lane][2]])
     tall_pair[:224, :] = fold_wa.total("cq")
     tall_pair[224:, :] = fold_wa.total("ck")
@@ -879,12 +1037,12 @@
             pltpu.VMEM((WIDE, seq), BF),
             pltpu.VMEM((3, seq, WIDE), BF),
             pltpu.VMEM((3, *dout.shape), BF),
-            pltpu.VMEM((seq, WIDE), F32),
-            pltpu.VMEM((seq, WIDE), F32),
-            pltpu.VMEM((WIDE, BLOCK), F32),
-            pltpu.VMEM((2, BLOCK, WIDE), BF),
-            pltpu.VMEM((2, BLOCK, WIDE), BF),
-            pltpu.VMEM((8, BLOCK), F32),
+            pltpu.VMEM((BLOCK, WIDE), F32),
+            pltpu.VMEM((BLOCK, WIDE), F32),
+            pltpu.VMEM((WIDE, seq), F32),
+            pltpu.VMEM((2, seq, WIDE), BF),
+            pltpu.VMEM((2, seq, WIDE), BF),
+            pltpu.VMEM((8, seq), F32),
             pltpu.VMEM((2, 3, BLOCK, BLOCK), F32),
             pltpu.VMEM((2, 3, BLOCK, BLOCK), F32),
             pltpu.SemaphoreType.DMA((1, n)),
@@ -903,148 +1061,261 @@
     )(dout, qh, kh, vh, ot, lse, bias_lines, *parts, feed_part)
 
 
-LANES = (
-    (1, ("cA",), 0),
-    (-1, ("cB", "out"), 0),
-    (1, ("sA",), 5),
-    (-1, ("sB", "small"), 5),
-)
 BUFFERS = {
-    "cA": (448, 1024),
-    "cB": (224, 1024),
-    "out": (8, 64, 896),
-    "sA": (448, 1024),
-    "sB": (224, 1024),
-    "small": (8, 8, 128),
+    "cq": (1, (224, 1024)),
+    "cv": (-1, (224, 1024)),
+    "ck": (1, (224, 1024)),
+    "co": (-1, (8, 32, 896)),
+    "so0": (1, (8, 16, 896)),
+    "so1": (-1, (8, 16, 896)),
 }
 NAMES = tuple(BUFFERS)
 
 
-def kind_of(name):
-    return F32 if name == "small" else BF
-
-
 def chunk_shape(name):
-    shape = BUFFERS[name]
+    shape = BUFFERS[name][1]
     return (shape[0], WIDE) if len(shape) == 2 else shape[1:]
 
 
 def chunk_of(ref, name, c):
-    return ref.at[:, lanes_of(c)] if len(BUFFERS[name]) == 2 else ref.at[c]
+    return ref.at[:, lanes_of(c)] if len(BUFFERS[name][1]) == 2 else ref.at[c]
+
+
+class Grid:
+    def __init__(self, u, share, half_in, half, quarters, whole, send, recv):
+        self.u, self.share, self.half_in, self.half = u, share, half_in, half
+        self.quarters, self.whole, self.sems = quarters, whole, (send, recv)
+        me = lax.axis_index("ctx")
+        self.y, self.z = lax.rem(me, 2), me // 2
+        self.beside = me + 1 - 2 * self.y
+        self.column = [lax.rem(self.z + d, 4) for d in range(1, 4)]
+
+    def half_of(self, y):
+        return pl.ds(pl.multiple_of(y * 4 * WIDE, WIDE), 4 * WIDE)
+
+    def piece_of(self, z, y=None):
+        start = z * WIDE if y is None else (4 * y + z) * WIDE
+        return pl.ds(pl.multiple_of(start, WIDE), WIDE)
+
+    def copy(self, number, src, dst, target):
+        send, recv = self.sems
+        return remote(src, dst, send.at[self.u, number], recv.at[self.u, number], ctx=target)
+
+    def start(self, total):
+        self.share[...] = total
+        self.first = self.copy(
+            0, self.share.at[:, self.half_of(1 - self.y)], self.half_in, self.beside
+        )
+        self.first.start()
+
+    def spread(self):
+        self.first.wait_recv()
+        mine = self.share[:, self.half_of(self.y)]
+        self.half[...] = (mine.astype(F32) + self.half_in[...].astype(F32)).astype(BF)
+        self.out = []
+        for d, z in enumerate(self.column):
+            copy = self.copy(
+                1 + d, self.half.at[:, self.piece_of(z)], self.quarters.at[self.z], 2 * z + self.y
+            )
+            copy.start()
+            self.out.append(copy)
+        self.quarters[self.z] = self.half[:, self.piece_of(self.z)]
+
+    def total(self):
+        for copy in self.out:
+            copy.wait_recv()
+        done = self.quarters[0].astype(F32)
+        for z in range(1, 4):
+            done = done + self.quarters[z].astype(F32)
+        piece = self.whole.at[:, self.piece_of(self.z, self.y)]
+        piece[...] = done.astype(BF)
+        self.back = []
+        for d, z in enumerate(self.column):
+            copy = self.copy(4 + d, piece, piece, 2 * z + self.y)
+            copy.start()
+            self.back.append(copy)
+
+    def join(self):
+        for copy in self.back:
+            copy.wait_recv()
+        mine = self.whole.at[:, self.half_of(self.y)]
+        self.last = self.copy(7, mine, mine, self.beside)
+        self.last.start()
+
+    def finish(self):
+        self.last.wait_recv()
+        for copy in (self.first, *self.out, *self.back, self.last):
+            copy.wait_send()
 
 
 def reduce_kernel(*refs):
     ca_ref, cb_ref, out_ref, small_ref = refs[:4]
     parts = dict(zip(LATE, refs[4:7], strict=True))
-    fin_ref, fin_out = refs[7], refs[14]
-    full = dict(zip(NAMES, refs[8:14], strict=True))
-    share = dict(zip(NAMES, refs[15:21], strict=True))
-    hold = dict(zip(NAMES, refs[21:27], strict=True))
-    small_in, small_mid, small_sem = refs[27:30]
-    ring_send, ring_recv, fin_send, fin_recv = refs[30:34]
-    extra = refs[34:]
+    fin_ref = refs[7]
+    count = len(NAMES)
+    full = dict(zip(NAMES, refs[8 : 8 + count], strict=True))
+    refs = refs[8 + count :]
+    late_full = dict(zip(LATE, refs[:3], strict=True))
+    small_out, fin_out = refs[3:5]
+    refs = refs[5:]
+    share = dict(zip(NAMES, refs[:count], strict=True))
+    hold = dict(zip(NAMES, refs[count : 2 * count], strict=True))
+    refs = refs[2 * count :]
+    grid_share, half_in, half, quarters, small_in, small_mid, small_beside, small_column = refs[:8]
+    small_send, small_recv, ring_send, ring_recv, grid_send, grid_recv, fin_send, fin_recv = refs[8:16]
+    extra = refs[16:]
     fold_wa = Folding(LATE, parts, (extra[0:4], None, extra[4:9]))
     place, after, before = ring_place(RING)
+    grids = {
+        name: Grid(
+            u, grid_share.at[u], half_in.at[u], half.at[u], quarters.at[u], late_full[name], grid_send, grid_recv
+        )
+        for u, name in enumerate(LATE)
+    }
     wa, both = fold_wa.wa, other_wa(fold_wa.across, 1)
+    some = grids["q"]
+    in_column = [2 * z + some.y for z in some.column]
     meet(
         [{"wa": peer} for peer in (fold_wa.mate, fold_wa.across, both)]
-        + [{"ctx": after}, {"ctx": before}]
-    )
-    own_fin = pltpu.make_async_copy(fin_ref.at[wa], fin_out.at[wa], fin_send.at[3])
+        + [{"ctx": peer} for peer in (after, before, some.beside, *in_column)]
+    )
+    fold_wa.start()
+    near = remote(small_ref, small_in.at[0], small_send.at[0], small_recv.at[0], wa=fold_wa.mate)
+    near.start()
+    over = remote(small_mid.at[0], small_in.at[1], small_send.at[1], small_recv.at[1], wa=fold_wa.across)
+    beside = remote(small_mid.at[1], small_beside, small_send.at[2], small_recv.at[2], ctx=some.beside)
+    columns = [
+        remote(small_mid.at[2], small_column.at[some.z], small_send.at[3 + d], small_recv.at[3 + d], ctx=peer)
+        for d, peer in enumerate(in_column)
+    ]
+    own_fin = pltpu.make_async_copy(fin_ref.at[wa], fin_out.at[:, columns_of(wa)], fin_send.at[3])
     own_fin.start()
     fin_copies = [
-        remote(fin_ref.at[peer], fin_out.at[wa], fin_send.at[d], fin_recv.at[d], wa=peer)
+        remote(fin_ref.at[peer], fin_out.at[:, columns_of(wa)], fin_send.at[d], fin_recv.at[d], wa=peer)
         for d, peer in enumerate((fold_wa.across, both, fold_wa.mate))
     ]
-    fold_wa.start()
-    near = remote(small_ref, small_in.at[0], small_sem.at[0], small_sem.at[1], wa=fold_wa.mate)
-    near.start()
-    over = remote(small_mid, small_in.at[1], small_sem.at[2], small_sem.at[3], wa=fold_wa.across)
-    share["cA"][...] = ca_ref[...]
-    share["cB"][...] = cb_ref[...]
-    share["out"][...] = out_ref[...]
+    share["cq"][...] = ca_ref[:224]
+    share["ck"][...] = ca_ref[224:]
+    share["cv"][...] = cb_ref[...]
+    share["co"][...] = out_ref[:, :32]
+    share["so0"][...] = out_ref[:, 32:48]
+    share["so1"][...] = out_ref[:, 48:]
     copies = {}
 
-    def ring_step(lane, step):
-        way, buffers, unused = LANES[lane]
-        here = place if way == 1 else lax.rem(RING - place, RING)
+    def ring_step(b, name, step):
+        way = BUFFERS[name][0]
+        here = place if way == 1 else RING - place
         target = after if way == 1 else before
-
-        def number(offset):
-            return lax.rem(here + offset + 2 * RING, RING)
-
-        for name in buffers:
-            b = NAMES.index(name)
-            if step > 0:
-                copies[name, step - 1].wait_recv()
-            if step == 2 * HOPS:
-                continue
-            if step <= HOPS:
-                now = number(-step) if step < HOPS else number(1)
-                mine = chunk_of(share[name], name, now)
-                if step > 0:
-                    total = mine[...].astype(F32) + hold[name][step - 1].astype(F32)
-                    if step == HOPS:
-                        mine = chunk_of(full[name], name, now)
-                    mine[...] = total.astype(kind_of(name))
-                src, dst = (mine, hold[name].at[step]) if step < HOPS else (mine, mine)
-            else:
-                src = dst = chunk_of(full[name], name, number(1 - (step - HOPS)))
-            copy = remote(src, dst, ring_send.at[b, step], ring_recv.at[b, step], ctx=target)
+        if step > 0:
+            copies[name, step - 1].wait_recv()
+        if step == 2 * HOPS:
+            return
+        now = lax.rem(here - step + 3 * RING, RING)
+        mine = chunk_of(share[name], name, now)
+        done = chunk_of(full[name], name, now)
+        if 0 < step <= HOPS:
+            total = mine[...].astype(F32) + hold[name][step - 1].astype(F32)
+            (mine if step < HOPS else done)[...] = total.astype(BF)
+        src, dst = (mine, hold[name].at[step]) if step < HOPS else (done, done)
+        copy = remote(src, dst, ring_send.at[b, step], ring_recv.at[b, step], ctx=target)
+        copy.start()
+        copies[name, step] = copy
+
+    def small_over():
+        near.wait_recv()
+        small_mid[0] = small_ref[...] + small_in[0]
+        over.start()
+
+    def small_next():
+        over.wait_recv()
+        small_mid[1] = small_mid[0] + small_in[1]
+        beside.start()
+
+    def small_last():
+        beside.wait_recv()
+        small_mid[2] = small_mid[1] + small_beside[...]
+        small_column[some.z] = small_mid[2]
+        for copy in columns:
             copy.start()
-            copies[name, step] = copy
-
-    ring_step(0, 0)
-    ring_step(1, 0)
+
+    def begin(name, following=None):
+        total = fold_wa.total(name)
+        if following:
+            fold_wa.x_copies[following].start()
+        grids[name].start(total)
+
+    events = {
+        0: [
+            lambda: fold_wa.send("q"),
+            lambda: fold_wa.prepare("k"),
+            lambda: fold_wa.prepare("v"),
+            small_over,
+        ],
+        4: [lambda: begin("q", "k"), small_next],
+        6: [grids["q"].spread, lambda: begin("k", "v"), small_last],
+        8: [grids["q"].total, grids["k"].spread],
+        9: [lambda: begin("v"), grids["q"].join, *(copy.start for copy in fin_copies)],
+        10: [grids["k"].total],
+        11: [grids["v"].spread, grids["k"].join],
+        12: [grids["v"].total],
+        14: [grids["v"].join],
+    }
+    for tick in range(2 * HOPS + 1):
+        for b, name in enumerate(NAMES):
+            ring_step(b, name, tick)
+        for event in events.get(tick, ()):
+            event()
+    for copy in columns:
+        copy.wait_recv()
+    total = small_column[0]
+    for z in range(1, 4):
+        total = total + small_column[z]
+    small_out[...] = total
     for name in LATE:
-        fold_wa.send(name)
-    near.wait_recv()
-    small_mid[...] = small_ref[...] + small_in[0]
-    over.start()
-    last = max(start for _, _, start in LANES) + 2 * HOPS
-    for tick in range(1, last + 1):
-        if tick == 8:
-            for copy in fin_copies:
-                copy.start()
-        for lane, (_, buffers, start) in enumerate(LANES):
-            step = tick - start
-            if step == 0 and buffers[0] == "sA":
-                share["sA"][:224, :] = fold_wa.total("q")
-                share["sA"][224:, :] = fold_wa.total("k")
-            if step == 0 and buffers[0] == "sB":
-                share["sB"][...] = fold_wa.total("v")
-                over.wait_recv()
-                share["small"][...] = (small_mid[...] + small_in[1]).reshape(8, 8, 128)
-            if 0 <= step <= 2 * HOPS:
-                ring_step(lane, step)
+        grids[name].finish()
     fold_wa.finish()
-    near.wait_send()
-    over.wait_send()
-    for copy in copies.values():
+    for copy in (near, over, beside, *columns, *copies.values()):
         copy.wait_send()
     own_fin.wait()
     for copy in fin_copies:
         copy.wait()
 
 
+def columns_of(owner):
+    return pl.ds(pl.multiple_of(owner * 896, WIDE), 896)
+
+
 def reduce_grads(pair, one, flat, small, parts, fin):
     dma = pltpu.SemaphoreType.DMA
+    any_spec = pl.BlockSpec(memory_space=pl.ANY)
+    late = len(LATE)
     return pl.pallas_call(
         reduce_kernel,
         out_shape=(
-            *(jax.ShapeDtypeStruct(BUFFERS[b], kind_of(b)) for b in NAMES),
-            jax.ShapeDtypeStruct((4, 224, 896), BF),
+            *(jax.ShapeDtypeStruct(BUFFERS[b][1], BF) for b in NAMES),
+            *[jax.ShapeDtypeStruct(TALL, BF)] * late,
+            jax.ShapeDtypeStruct(small.shape, F32),
+            jax.ShapeDtypeStruct((224, 3584), BF),
         ),
-        in_specs=vmem(4) + [pl.BlockSpec(memory_space=pl.ANY)] * 4,
-        out_specs=(*vmem(len(NAMES)), pl.BlockSpec(memory_space=pl.ANY)),
+        in_specs=vmem(4) + [any_spec] * 4,
+        out_specs=(*vmem(len(NAMES) + late + 1), any_spec),
         scratch_shapes=[
-            *(pltpu.VMEM(BUFFERS[b], kind_of(b)) for b in NAMES),
-            *(pltpu.VMEM((HOPS, *chunk_shape(b)), kind_of(b)) for b in NAMES),
-            pltpu.VMEM((2, 64, 128), F32),
-            pltpu.VMEM((64, 128), F32),
-            dma((4,)),
+            *(pltpu.VMEM(BUFFERS[b][1], BF) for b in NAMES),
+            *(pltpu.VMEM((HOPS, *chunk_shape(b)), BF) for b in NAMES),
+            pltpu.VMEM((late, *TALL), BF),
+            pltpu.VMEM((late, 224, 4 * WIDE), BF),
+            pltpu.VMEM((late, 224, 4 * WIDE), BF),
+            pltpu.VMEM((late, 4, 224, WIDE), BF),
+            pltpu.VMEM((2, *small.shape), F32),
+            pltpu.VMEM((3, *small.shape), F32),
+            pltpu.VMEM(small.shape, F32),
+            pltpu.VMEM((4, *small.shape), F32),
+            dma((6,)),
+            dma((6,)),
             dma((len(NAMES), 2 * HOPS)),
             dma((len(NAMES), 2 * HOPS)),
+            dma((late, 8)),
+            dma((late, 8)),
             dma((4,)),
             dma((3,)),
             *Folding.scratch(LATE),
@@ -1060,14 +1331,9 @@
 def unfold(full):
     wide = {name: value.astype(F32) for name, value in full.items()}
     return {
-        "cq": wide["cA"][:224],
-        "ck": wide["cA"][224:],
-        "cv": wide["cB"],
-        "co": wide["out"][:, :32].reshape(FLAT),
-        "so": wide["out"][:, 32:].reshape(FLAT),
-        "q": wide["sA"][:224],
-        "k": wide["sA"][224:],
-        "v": wide["sB"],
+        "co": wide["co"].reshape(FLAT),
+        "so": jnp.concatenate([wide["so0"], wide["so1"]], 1).reshape(FLAT),
+        **{name: wide[name] for name in ("cq", "ck", "cv", *LATE)},
     }
 
 
@@ -1439,26 +1705,26 @@
     return dquery_low, dkey_low, dvalue_low, grad_biastable
 
 
-def heads_forward(tokens, given):
+def heads_forward(tokens, near, cotangent, given):
     wa, owners = lax.axis_index("wa"), lax.axis_size("wa")
     table = given["biastable"].astype(F32)
     selector = lax.dynamic_slice_in_dim(line_selector(), wa * table.shape[0], table.shape[0], 0)
     lines = jnp.dot(table.T, selector, precision=strongest_precision).astype(BF)
-
-    def placed(gain):
-        row = jnp.zeros((LINE,), BF)
-        return lax.dynamic_update_slice(row, gain, (wa * gain.shape[0],))
-
-    gains = jnp.stack([placed(given[name]) for name in GAINS])
-    small = jnp.concatenate([lines, gains, jnp.zeros((H - len(GAINS), LINE), BF)], 0)
+    gains = jnp.concatenate([given[name] for name in GAINS]).reshape(len(GAINS), -1)
+    small = jnp.zeros((H, LINE), BF)
+    small = lax.dynamic_update_slice(small, gains, (0, wa * gains.shape[1]))
+    small = jnp.concatenate([lines, small], 0)
     shards = [given[LONG_NAMES[name]] for name in GATHERED]
-    *wholes, attended_low, low, qh, kh, vh, ot, lse, small = attn_forward(
-        lax.axis_size("ctx"), tokens, small, shards
+    *wholes, upstream_all, feed_in, attended_low, low, qh, kh, vh, ot, lse, small, before, keys, values = attn_forward(
+        lax.axis_size("ctx"), tokens, small, near, [*shards, cotangent], given["feedin"]
     )
     width = tokens.shape[1]
     gain_of = {name: small[H + g, :width] for g, name in enumerate(GAINS)}
     full = {LONG_NAMES[name]: whole for name, whole in zip(GATHERED, wholes, strict=True)}
-    return attended_low, low, full, gain_of, (qh, kh, vh, ot, lse, small[:H])
+    full["feedin"] = feed_in
+    upstream_all = upstream_all.reshape(owners, *tokens.shape)
+    saved = (qh, kh, vh, ot, lse, small[:H])
+    return attended_low, low, full, gain_of, upstream_all, (before, keys, values), saved
 
 
 def heads_backward(state, dout_low, parts, feed_part):
@@ -1498,8 +1764,8 @@
 
 
 def middle_kernel(
-    keep_ref, q_ref, dx_ref, k_ref, v_ref, near_ref, wk_ref, wv_ref, fin_ref, fout_ref,
-    dq_ref, dwk_ref, dwv_ref, near_out, last_out, feed_out,
+    keep_ref, q_ref, dx_ref, k_ref, v_ref, before_ref, near_ref, wk_ref, wv_ref, fin_ref, fout_ref,
+    dq_ref, dwk_ref, dwv_ref, first_out, near_out, last_out, feed_out,
     dk, dv, q_pad, dx_pad, dq_pad, share, hold, load_sem, ring_send, ring_recv,
 ):
     ring = Ring(FEED_LANES, ring_send, ring_recv, share=share, hold=hold)
@@ -1537,16 +1803,21 @@
     for g in range(groups):
         rows = slice(g * 256, (g + 1) * 256)
         total = nt_dot(dk[rows, :], wk_ref[...]) + nt_dot(dv[rows, :], wv_ref[...])
-        near_out[rows, :] = total.astype(BF)
-        if g == groups - 1:
+        if g == 0:
+            first_out[...] = total.astype(BF)
+        elif g == groups - 1:
             last_out[...] = total
+        else:
+            near_out[(g - 1) * 256 : g * 256, :] = total.astype(BF)
         if g % 2 == 1:
             turn()
     for c in range(near_ref.shape[1] // WIDE):
         lanes = slice(c * WIDE, (c + 1) * WIDE)
+        first = before_ref[:, lanes].astype(F32).T.astype(BF)
         left = near_ref[:, lanes].astype(F32).T.astype(BF)
-        dwk_ref[lanes, :] = nn_dot(left, dk[...]).astype(BF)
-        dwv_ref[lanes, :] = nn_dot(left, dv[...]).astype(BF)
+        for grads, out_ref in ((dk, dwk_ref), (dv, dwv_ref)):
+            total = nn_dot(first, grads[:256, :]) + nn_dot(left, grads[256:, :])
+            out_ref[lanes, :] = total.astype(BF)
         if c % 2 == 1:
             turn()
     while calls:
@@ -1556,7 +1827,7 @@
     ring.finish(lambda lane: share.at[FEED_LANES[lane][0], 0, FEED_LANES[lane][2]])
 
 
-def middle(keep, query, dmixed, keys, values, near, wk, wv, fin, fout):
+def middle(keep, query, dmixed, keys, values, before, near, wk, wv, fin, fout):
     many, width = keys.shape
     wide = near.shape[1]
     low = functools.partial(jax.ShapeDtypeStruct, dtype=BF)
@@ -1568,12 +1839,13 @@
             low(query.shape),
             low(wk.shape),
             low(wv.shape),
-            low(near.shape),
+            low((256, wide)),
+            low((many - 512, wide)),
             jax.ShapeDtypeStruct((256, wide), F32),
             low((2, *FEED[1:])),
         ),
-        in_specs=vmem(8) + [pl.BlockSpec(memory_space=pl.ANY)] * 2,
-        out_specs=tuple(vmem(6)),
+        in_specs=vmem(9) + [pl.BlockSpec(memory_space=pl.ANY)] * 2,
+        out_specs=tuple(vmem(7)),
         scratch_shapes=[
             pltpu.VMEM((many, width), BF),
             pltpu.VMEM((many, width), BF),
@@ -1591,7 +1863,7 @@
         ),
         cost_estimate=lasting(38),
         name="middle",
-    )(keep, query, dmixed, keys, values, near, wk, wv, fin.reshape(FEED), fout.reshape(FEED))
+    )(keep, query, dmixed, keys, values, before, near, wk, wv, fin.reshape(FEED), fout.reshape(FEED))
 
 
 NAMES_OF_WEIGHTS = (
@@ -1632,8 +1904,15 @@
     inputs = tokens[0].astype(F32)
     upstream_low = cotangent[0]
     upstream = upstream_low.astype(F32)
-    if split_heads:
-        attended_low, normed_low, full, small_of, attention_state = heads_forward(tokens[0], given)
+    spans = neighbours.shape[1]
+    span_rows = neighbours.shape[2] * neighbours.shape[3]
+    own_rows = neighbours[0].reshape(spans * span_rows, model_width)
+    if split_heads and span_rows == BLOCK:
+        attended_low, normed_low, full, small_of, upstream_all, projected, attention_state = (
+            heads_forward(tokens[0], own_rows, upstream_low, given)
+        )
+        before, keys_cross, values_cross = projected
+        feed_in = full["feedin"]
         normed_self, back_self = jax.vjp(root_norm, inputs, small_of["selfnorm"])
     else:
         small_of = {name: whole_over_wa(given[name]).astype(F32) for name in GAINS}
@@ -1647,20 +1926,14 @@
             ),
             whole_over_wa(given["biastable"]),
         )
-    attended_low, feed_in, upstream_low = lax.optimization_barrier(
-        (attended_low, given["feedin"], upstream_low)
-    )
-    upstream_all = lax.all_gather(upstream_low, "wa", axis=0)
-    feed_in = lax.all_to_all(feed_in, "wa", 1, 0, tiled=True)
+        upstream_all = lax.all_gather(upstream_low, "wa", axis=0)
+        feed_in = lax.all_to_all(given["feedin"], "wa", 1, 0, tiled=True)
+        before = passed_along(own_rows[-span_rows:], "ctx", 1)
+        near_rows = jnp.concatenate([before, own_rows], 0)
+        keys_cross = forward_product(near_rows, full["crosskey"]).astype(BF)
+        values_cross = forward_product(near_rows, full["crossvalue"]).astype(BF)
     hidden = inputs + forward_product(attended_low, full["selfout"])
 
-    spans = neighbours.shape[1]
-    span_rows = neighbours.shape[2] * neighbours.shape[3]
-    own_rows = neighbours[0].reshape(spans * span_rows, model_width)
-    before = passed_along(own_rows[-span_rows:], "ctx", 1)
-    near_rows = jnp.concatenate([before, own_rows], 0)
-    keys_cross = forward_product(near_rows, full["crosskey"]).astype(BF)
-    values_cross = forward_product(near_rows, full["crossvalue"]).astype(BF)
     normed_cross, back_cross = jax.vjp(root_norm, hidden, small_of["crossnorm"])
     cross_in = normed_cross.astype(BF)
     query_cross = forward_product(cross_in, full["crossquery"]).astype(BF)
@@ -1682,13 +1955,14 @@
     grad_mixed = back_product(two_low, full["crossout"]).astype(BF)
     early = {}
     if split_heads:
-        grad_query_cross, early["ck"], early["cv"], near_low, near_last, feed_part = middle(
+        grad_query_cross, early["ck"], early["cv"], first, near_low, near_last, feed_part = middle(
             keep,
             query_cross,
             grad_mixed,
             keys_cross,
             values_cross,
-            near_rows,
+            before,
+            own_rows,
             full["crosskey"],
             full["crossvalue"],
             fin,
@@ -1701,10 +1975,11 @@
         near_grads = back_product(dkeys, full["crosskey"]) + back_product(
             dvalues, full["crossvalue"]
         )
-        near_low, near_last = near_grads.astype(BF), near_grads[-span_rows:]
+        first, near_last = near_grads[:span_rows].astype(BF), near_grads[-span_rows:]
+        near_low = near_grads[span_rows:-span_rows].astype(BF)
         early["ck"] = outer_product(near_rows, dkeys).astype(BF)
         early["cv"] = outer_product(near_rows, dvalues).astype(BF)
-    back = passed_along(near_low[:span_rows], "ctx", -1).astype(F32)
+    back = passed_along(first, "ctx", -1).astype(F32)
     grad_hidden_part, grad_crossnorm = back_cross(
         back_product(grad_query_cross, full["crossquery"])
     )
@@ -1729,9 +2004,8 @@
     grad_input_part, grad_selfnorm = back_self(grad_normed)
     grad_inputs = (grad_hidden + grad_input_part).astype(BF)
 
-    edge = span_rows * spans
     grad_neigh = (
-        jnp.concatenate([near_low[span_rows:edge], (near_last + back).astype(BF)], 0)
+        jnp.concatenate([near_low, (near_last + back).astype(BF)], 0)
         .reshape(neighbours.shape)
     )
     late = {
@@ -1748,10 +2022,10 @@
     packed = jnp.concatenate([*(v.reshape(owners, -1) for v in sums), placed], axis=1)
     packed = jnp.pad(packed, ((0, 0), (0, LINE * 2 - packed.shape[1]))).reshape(-1, WIDE)
     if split_heads:
-        *reduced, fin = reduce_grads(*shares, packed, [late[name] for name in LATE], fin)
-        reduced = dict(zip(NAMES, reduced, strict=True))
-        grads, packed = unfold(reduced), reduced["small"]
-        fin = jnp.transpose(fin, (1, 0, 2)).reshape(given["feedin"].shape)
+        *reduced, packed, fin = reduce_grads(
+            *shares, packed, [late[name] for name in LATE], fin
+        )
+        grads = unfold(dict(zip((*NAMES, *LATE), reduced, strict=True)))
         fout = fout.reshape(given["feedout"].shape)
     else:
         grads, packed = reduce_plain(early | late, packed)

time: 550 us -> 481 us (0.87)
  local copies, waits for them, and re-layouts: 43.2 us -> 13.4 us
  Pallas kernels: 418 us -> 402 us
  between operations: 15.1 us -> 1.39 us
  starting transfers between devices: 11.5 us -> 1.7 us
  matrix products: 35 us -> 27.8 us
  other arithmetic: 18.1 us -> 25.3 us
    pallas_call x1, Pallas kernels: 91.9 us -> 115 us  [attn_forward(): pl.pallas_call(functools.partial(attn_forward_kernel, n), out_shape=(*who...]
    pallas_call x1, Pallas kernels: 117 us -> 96.2 us  [attn_backward(): pl.pallas_call(functools.partial(attn_backward_kernel, n), out_shape=(gra...]
    unnamed x138 -> x92, local copies, waits for them, and re-layouts: 16.5 us -> 4.82 us
    slice x6 -> x1, local copies, waits for them, and re-layouts: 11.7 us -> 0.63 us  [heads_forward(): saved = (qh, kh, vh, ot, lse, small[:H])]
    pallas_call x1, Pallas kernels: 103 us -> 94.1 us  [reduce_grads(): pl.pallas_call(reduce_kernel, out_shape=(*(jax.ShapeDtypeStruct(BUFFERS[b...]
    dot_general x5 -> x3, matrix products: 14.8 us -> 6.09 us  [forward_product(): return jnp.dot(values, weight, preferred_element_type=jnp.float32)]
    pallas_call x1, Pallas kernels: 50.7 us -> 42.9 us  [middle(): pl.pallas_call(middle_kernel, out_shape=(low(query.shape), low(wk.shape),...]
    convert_element_type x2 -> x6, other arithmetic: 2.03 us -> 8.27 us  [unfold(): wide = {name: value.astype(F32) for name, value in full.items()}]
  transfers between devices with their start and end apart: 4 -> 1, of which waited for: 0 -> 0; matrix products, arithmetic and copies ran while one was open for 10% -> 9% of each run, Pallas kernels for 59% -> 40%
where the time goes in v4:
time: 481 us; the launch traced here: 471 us
  Pallas kernels  402 us (84%)
  matrix products  27.8 us (6%)
  other arithmetic  25.3 us (5%)
  local copies, waits for them, and re-layouts  13.4 us (3%)
    pallas_call x1, Pallas kernels, attn_forward(): pl.pallas_call(functools.partial(attn_forward_kernel, n), out_shape=(*who...  115 us
    pallas_call x1, Pallas kernels, attn_backward(): pl.pallas_call(functools.partial(attn_backward_kernel, n), out_shape=(gra...  96.2 us
    pallas_call x1, Pallas kernels, reduce_grads(): pl.pallas_call(reduce_kernel, out_shape=(*(jax.ShapeDtypeStruct(BUFFERS[b...  94.1 us
    pallas_call x1, Pallas kernels, ffn(): pl.pallas_call(ffn_kernel, out_shape=(jax.ShapeDtypeStruct(block, F32), j...  44 us
    pallas_call x1, Pallas kernels, middle(): pl.pallas_call(middle_kernel, out_shape=(low(query.shape), low(wk.shape),...  42.9 us
    dot_general x6, matrix products, outer_product(): lax.dot_general(left_side, right_side, (((0,), (0,)), ((), ())), preferre...  11.6 us
    pallas_call x1, Pallas kernels, cross_forward(): pl.pallas_call(functools.partial(cross_forward_kernel, groups), grid=(wid...  9.73 us
  transfers between devices with their start and end apart: 1, of which 0 were waited for; matrix products, arithmetic and copies ran while one was open for 9% of the time, Pallas kernels for 40%

profile of v4, /device:TPU:0, one launch (start us, length us, event | category | flops | bytes accessed | tf_op | source)
XLA Modules:
  0.0 471.3 jit_solution(16936368631460934216)
XLA Ops:
  1.6 1.3 reshape.217.bias_ref
  4.6 114.8 %attn_forward.1 = (bf16[896,1024]{1,0:T(8,128)(2,1)}, bf16[896,1024]{1,0:T(8,128)(2,1)}, bf16[896,1024]{1,0:T(8,128)(2,1)}, bf16[1024,896]{1,0:T(8,128)(2,1)}, b...) custom-call(bf16[256,896]{1,0:T(8,128)(2,1)} %bitcast.61, ...), custom_call_target="tpu_custom_call" | custom-call | bytes 255000000 | tf_op jit(solution)/shard_map/attn_forward/pallas_call | solution.py:796
  119.4 1.5 slice_reduce_fusion.1
  120.9 2.5 multiply_reduce_fusion.5
  124.0 2.8 convolution_convert_fusion.8.q_ref
  126.8 1.9 copy-done.3
  128.7 9.7 %cross_forward.1 = bf16[256,1024]{1,0:T(8,128)(2,1)S(1)} custom-call(f32[8,128]{1,0:T(8,128)S(1)} %broadcast_in_dim.53.keep_ref, bf16[256,1024]{1,0:T(8,128)(2,1)S(1)} %convolution_convert_fusion.8.q_ref, bf16[1280,1024]{1,0:T(8,128)(2,1)S(1)} %copy-done.2, bf16[1280,1024]{1,0:T(8,128)(2,1)S(1)} %copy-done.3), custom_call_target="tpu_custom_call" | custom-call | bytes 27000000 | tf_op jit(solution)/shard_map/cross_forward/pallas_call | solution.py:1506
  140.3 44.0 %feed_forward.1 = (f32[256,896]{1,0:T(8,128)}, f32[256,896]{1,0:T(8,128)}, bf16[896,896]{1,0:T(8,128)(2,1)}, bf16[896,896]{1,0:T(8,128)(2,1)}, f32[8,896]{1,0:T(8,128)}) custom-call(bf16[256,896]{1,0:T(8,128)(2,1)} %multiply_convert_fusion.f_ref, bf16[4,256,896]{2,1,0:T(8,128)(2,1)} %bitcast.66, bf16[896,896]{1,0:T(8,128)(2,1)} %get-tuple-element.80.win_ref, ...), custom_call_target="tpu_custom_call" | custom-call | bytes 132000000 | tf_op jit(solution)/shard_map/feed_forward/pallas_call | solution.py:1436
  184.3 1.6 multiply_reduce_fusion
  185.9 2.4 convert_add_fusion.1
  188.3 1.5 convolution_convert_fusion.7.dx_ref
  189.8 42.9 %middle.1 = (bf16[256,1024]{1,0:T(8,128)(2,1)}, bf16[896,1024]{1,0:T(8,128)(2,1)}, bf16[896,1024]{1,0:T(8,128)(2,1)}, bf16[256,896]{1,0:T(8,128)(2,1)}, bf16[768...) custom-call(f32[8,128]{1,0:T(8,128)} %copy-done.5, bf16[256,1024]{1,0:T(8,128)(2,1)} %copy-done.4, ...), custom_call_target="tpu_custom_call" | custom-call | bytes 114000000 | tf_op jit(solution)/shard_map/middle/pallas_call | solution.py:1836
  232.8 1.7 collective-permute-start
  236.0 2.6 multiply_reduce_fusion.1
  238.6 2.0 convolution_convert_fusion.5.rest_0_
  240.9 1.2 copy-done.14
  242.1 1.5 convolution_convert_fusion.6.do_ref
  243.7 2.0 convolution_convert_fusion.3.rest_4_
  245.6 2.0 convolution_convert_fusion.4.rest_3_
  247.9 96.2 %attn_backward.1 = (bf16[256,1024]{1,0:T(8,128)(2,1)}, bf16[256,1024]{1,0:T(8,128)(2,1)}, bf16[256,1024]{1,0:T(8,128)(2,1)}, f32[8,1024]{1,0:T(8,128)}, bf16[448...) custom-call(bf16[256,1024]{1,0:T(8,128)(2,1)} %convolution_convert_f, ...), custom_call_target="tpu_custom_call" | custom-call | bytes 300000000 | tf_op jit(solution)/shard_map/attn_backward/pallas_call | solution.py:1020
  344.1 1.9 fusion.33
  346.0 1.9 convolution_convert_fusion.2.refs_4_
  347.9 1.9 convolution_convert_fusion.1.refs_5_
  349.8 1.9 convolution_convert_fusion.refs_6_
  356.3 94.1 %reduce_grads.1 = (bf16[224,1024]{1,0:T(8,128)(2,1)}, bf16[224,1024]{1,0:T(8,128)(2,1)}, bf16[224,1024]{1,0:T(8,128)(2,1)}, bf16[8,32,896]{2,1,0:T(8,128)(2,1)},...) custom-call(bf16[448,1024]{1,0:T(8,128)(2,1)} %get-tuple-element.106, ...), custom_call_target="tpu_custom_call" | custom-call | bytes 270000000 | tf_op jit(solution)/shard_map/reduce_grads/pallas_call | solution.py:1292
  452.0 2.1 convert_element_type.211
  454.1 2.1 convert_element_type.212
  460.4 1.4 bitcast_convert_fusion.1
  462.9 2.1 convert_element_type.217
  466.3 2.0 bitcast_convert_fusion
  468.3 1.2 add_convert_fusion
  469.8 1.4 pad_maximum_fusion
  (142 shorter events, 19.9 us)
Async XLA Ops:
  0.7 2.9 copy-start
  0.7 2.4 copy-start.41
  3.1 116.3 %copy-start.30 = (pred[32,1024]{0,1:T(8,128)(4,1)}, pred[32,1024]{0,1:T(8,128)(4,1)S(1)}, u32[]{:S(2)}) copy-start(pred[32,1024]{0,1:T(8,128)(4,1)S(1)} %iota_compare_fusion) | copy-start | bytes 98308
  4.6 116.3 %copy-start.11 = (bf16[1,256,896]{2,1,0:T(8,128)(2,1)S(1)}, bf16[1,256,896]{2,1,0:T(8,128)(2,1)}, u32[]{:S(2)}) copy-start(bf16[1,256,896]{2,1,0:T(8,128)(2,1)} %param.19) | copy-start | bytes 1376260
  123.4 3.4 copy-start.6
  123.4 3.4 copy-start.2
  126.8 11.7 %copy-start.4 = (bf16[256,1024]{1,0:T(8,128)(2,1)}, bf16[256,1024]{1,0:T(8,128)(2,1)S(1)}, u32[]{:S(2)}) copy-start(bf16[256,1024]{1,0:T(8,128)(2,1)S(1)} %convolution_convert_fusion.8.q_ref) | copy-start | bytes 1572868
  126.8 11.7 %copy-start.5 = (f32[8,128]{1,0:T(8,128)}, f32[8,128]{1,0:T(8,128)S(1)}, u32[]{:S(2)}) copy-start(f32[8,128]{1,0:T(8,128)S(1)} %broadcast_in_dim.53.keep_ref) | copy-start | bytes 12292
  128.7 9.8 %copy-start.7 = (f32[256,896]{1,0:T(8,128)S(1)}, f32[256,896]{1,0:T(8,128)}, u32[]{:S(2)}) copy-start(f32[256,896]{1,0:T(8,128)} %copy-done.6) | copy-start | bytes 2752516
  128.7 9.8 %copy-start.13 = (bf16[1024,896]{1,0:T(8,128)(2,1)S(1)}, bf16[1024,896]{1,0:T(8,128)(2,1)}, u32[]{:S(2)}) copy-start(bf16[1024,896]{1,0:T(8,128)(2,1)} %get-tuple-element.78) | copy-start | bytes 5505028
  189.8 44.6 %copy-start.12 = (bf16[1,256,896]{2,1,0:T(8,128)(2,1)S(1)}, bf16[1,256,896]{2,1,0:T(8,128)(2,1)}, u32[]{:S(2)}) copy-start(bf16[1,256,896]{2,1,0:T(8,128)(2,1)} %param.19) | copy-start | bytes 1376260
  189.8 45.5 %copy-start.38 = (f32[32,1024]{1,0:T(8,128)S(1)}, f32[32,1024]{1,0:T(8,128)}, u32[]{:S(2)}) copy-start(f32[32,1024]{1,0:T(8,128)} %get-tuple-element.74) | copy-start | bytes 393220
  189.8 46.1 %copy-start.8 = (f32[256,896]{1,0:T(8,128)S(1)}, f32[256,896]{1,0:T(8,128)}, u32[]{:S(2)}) copy-start(f32[256,896]{1,0:T(8,128)} %copy-done.6) | copy-start | bytes 2752516
  232.8 235.5 %collective-permute-start = (bf16[256,896]{1,0:T(8,128)(2,1)}, bf16[256,896]{1,0:T(8,128)(2,1)}, u32[]{:S(2)}, u32[]{:S(2)}) collective-permute-start(bf16[256,896]{1,0:T(8,128)(2,1)} %get-tuple-element.105), channel_id=1, source_target_pairs={{4,0},{8,4},{12,8},{16,12},{20,16},{24,20},{28,24},{5,1},{9,5},{13... | collective-permute-start | bytes 1376264 | tf_op jit(solution)/shard_map/ppermute | solution.py:32
  236.0 2.6 copy-start.20
  238.6 2.0 copy-start.44
  242.1 3.5 copy-start.9
  245.6 2.0 copy-start.39
  247.9 96.2 %copy-start.23 = (bf16[896,1024]{1,0:T(8,128)(2,1)S(1)}, bf16[896,1024]{1,0:T(8,128)(2,1)}, u32[]{:S(2)}) copy-start(bf16[896,1024]{1,0:T(8,128)(2,1)} %get-tuple-element.98) | copy-start | bytes 5505028
  344.1 1.9 copy-start.15
  346.0 1.9 copy-start.21
  347.9 1.9 copy-start.19
  349.8 1.9 copy-start.25
  450.4 5.8 %copy-start.35 = (bf16[224,1024]{1,0:T(8,128)(2,1)S(1)}, bf16[224,1024]{1,0:T(8,128)(2,1)}, u32[]{:S(2)}) copy-start(bf16[224,1024]{1,0:T(8,128)(2,1)} %get-tuple-element.116) | copy-start | bytes 1376260
  452.0 5.2 %copy-start.34 = (bf16[224,1024]{1,0:T(8,128)(2,1)S(1)}, bf16[224,1024]{1,0:T(8,128)(2,1)}, u32[]{:S(2)}) copy-start(bf16[224,1024]{1,0:T(8,128)(2,1)} %get-tuple-element.119) | copy-start | bytes 1376260
  454.1 4.2 copy-start.33
  456.2 3.1 copy-start.10
  458.3 2.1 copy-start.36
  458.3 2.1 copy-start.37
  460.4 2.5 copy-start.27
  462.9 3.4 copy-start.26
  466.3 2.0 copy-start.29
  (15 other events, 21.8 us)

commit v5 on v4

--- a/solution.py
+++ b/solution.py
@@ -307,7 +307,8 @@
 
 
 TALL, FLAT = (224, 1024), (256, 896)
-EARLY = ("cq", "ck", "cv", "co", "so")
+EARLY = ("ck", "cv", "cq", "co", "so")
+MADE = ("cq", "co", "so")
 LATE = ("q", "k", "v")
 FEED = (8, 112, 896)
 FEED_LANES = (
@@ -317,6 +318,13 @@
     (1, -1, slice(64, 112)),
 )
 FEED_TURNS = ((0, 1), (2, 3))
+
+
+def product_into(out_ref, left, right):
+    for c in range(left.shape[1] // WIDE):
+        lanes = slice(c * WIDE, (c + 1) * WIDE)
+        turned = left[:, lanes].astype(F32).T.astype(BF)
+        out_ref[lanes, :] = nn_dot(turned, right[...]).astype(BF)
 
 
 class Folding:
@@ -351,8 +359,9 @@
         many = len(names)
         return shapes + [dma((many, 2))] * 3 + [dma((many,))] * 2
 
-    def start(self):
-        for u, name in enumerate(self.names):
+    def start(self, *names):
+        for name in names:
+            u = self.names.index(name)
             slot, (own, inn, _, _) = self.slots[name]
             rows = self.shape_of(name)[0]
             for x in range(2):
@@ -404,6 +413,22 @@
             self.x_copies[name].wait_send()
 
 
+class Moves:
+    def __init__(self, sem):
+        self.sem, self.count = sem, 0
+
+    def start(self, src, dst):
+        copy = pltpu.make_async_copy(src, dst, self.sem.at[self.count])
+        copy.start()
+        self.count += 1
+        return copy
+
+
+def wait_all(copies):
+    for copy in copies:
+        copy.wait()
+
+
 def lasting(microseconds):
     return pl.CostEstimate(
         flops=0, bytes_accessed=int(microseconds * 3.0e6), transcendentals=0
@@ -466,18 +491,19 @@
         self.sems = own_sem, send, recv
         self.wa, me = lax.axis_index("wa"), lax.axis_index("ctx")
         self.mate, self.across = other_wa(self.wa, 1), other_wa(self.wa, 2)
-        self.y = lax.rem(me, 2)
-        self.beside = me + 1 - 2 * self.y
+        y, z = lax.rem(me, 2), lax.rem(me // 2, 2)
+        self.pairs = ((y, me + 1 - 2 * y), (z, me + 2 - 4 * z))
         self.copies = {}
 
     def start(self):
         own_sem, send, recv = self.sems
         for u, name in enumerate(self.names):
+            part, beside = self.pairs[(u + 1) % 2]
             shard, whole = self.shards[name], self.whole[name]
             rows = shard.shape[0]
             parts = 1 if name in SINGLE else 2
             some = rows // parts
-            shift = 0 if parts == 1 else self.y * some
+            shift = 0 if parts == 1 else part * some
 
             def at(start, count, ref=whole):
                 return ref.at[pl.ds(pl.multiple_of(start, 16), count)]
@@ -491,7 +517,7 @@
                 ),
                 "near": remote(shard, mine, send.at[u, 1], recv.at[u, 1], wa=self.mate),
                 "pass": remote(theirs, theirs, send.at[u, 2], recv.at[u, 2], wa=self.mate),
-                "side": remote(theirs_some, theirs_some, send.at[u, 3], recv.at[u, 3], ctx=self.beside),
+                "side": remote(theirs_some, theirs_some, send.at[u, 3], recv.at[u, 3], ctx=beside),
                 "own": pltpu.make_async_copy(shard, mine, own_sem.at[u]),
             }
             self.copies[name]["near"].start()
@@ -525,7 +551,7 @@
 
 class Columns:
     def __init__(self, gathering, shard, whole, send, recv):
-        wa, mate, across, y = gathering.wa, gathering.mate, gathering.across, gathering.y
+        wa, mate, across = gathering.wa, gathering.mate, gathering.across
         both = other_wa(across, 1)
         rows, width = shard.shape[0], whole.shape[1]
         some = rows // 2
@@ -537,17 +563,15 @@
             return whole.at[pl.ds(pl.multiple_of(start, 16), count)]
 
         everything = slice(0, rows)
-        mine = pl.ds(pl.multiple_of(y * some, 16), some)
         self.own = pltpu.make_async_copy(block(everything, wa), at(wa * rows, rows), send.at[5])
         self.near = remote(block(everything, mate), at(wa * rows, rows), send.at[0], recv.at[0], wa=mate)
-        self.over = [
-            remote(block(mine, peer), at(wa * rows + y * some, some), send.at[1 + d], recv.at[1 + d], wa=peer)
-            for d, peer in enumerate((across, both))
-        ]
-        self.side = []
+        self.over, self.side = [], []
         for d, peer in enumerate((across, both)):
-            got = at(peer * rows + y * some, some)
-            self.side.append(remote(got, got, send.at[3 + d], recv.at[3 + d], ctx=gathering.beside))
+            part, beside = gathering.pairs[d]
+            mine = pl.ds(pl.multiple_of(part * some, 16), some)
+            gone, got = at(wa * rows + part * some, some), at(peer * rows + part * some, some)
+            self.over.append(remote(block(mine, peer), gone, send.at[1 + d], recv.at[1 + d], wa=peer))
+            self.side.append(remote(got, got, send.at[3 + d], recv.at[3 + d], ctx=beside))
 
     def start(self):
         self.own.start()
@@ -570,17 +594,19 @@
             over.wait_send()
 
 
-def attn_forward_kernel(n, tokens_ref, small_ref, near_ref, *refs):
+def attn_forward_kernel(n, tokens_ref, small_ref, near_far, *refs):
     shards = dict(zip((*GATHERED, "cot"), refs[:9], strict=True))
     feed_ref = refs[9]
     wholes = dict(zip((*GATHERED, "cot"), refs[10:19], strict=True))
     feed_whole = refs[19]
-    o_ref, low_ref, qh_out, kh_out, vh_out, ot_out, lse_out, small_out, before_ref, keys_ref, values_ref = refs[20:31]
+    o_ref, low_ref, ot_out, lse_out, small_out, before_ref, qh_out, kh_out, vh_out, keys_out, values_out = refs[20:31]
     (
         held_q, held_k, held_v, held_ck, held_cv, proj, small_in, small_mid, qh, kh, vh, vt, oh, land, tiles,
         acc, stat, send, recv, osend, orecv, small_sem, own_sem, out_sem, gather_send, gather_recv, feed_send,
-        feed_recv, span_sem,
+        feed_recv, span_sem, near_ref, keys_ref, values_ref, move_sem,
     ) = refs[31:]
+    moves = Moves(move_sem)
+    load_near = moves.start(near_far, near_ref)
     held = {"q": held_q, "k": held_k, "v": held_v, "ck": held_ck, "cv": held_cv}
     gathering = Gathering(shards, wholes | held, own_sem, gather_send, gather_recv)
     columns = Columns(gathering, feed_ref, feed_whole, feed_send, feed_recv)
@@ -594,7 +620,7 @@
     columns.start()
     span_rows = before_ref.shape[0]
     span = remote(
-        near_ref.at[near_ref.shape[0] - span_rows :],
+        near_far.at[near_far.shape[0] - span_rows :],
         before_ref,
         span_sem.at[0],
         span_sem.at[1],
@@ -637,10 +663,6 @@
     project(1, "k")
     project(2, "v")
 
-    @pl.when(me < n - 1)
-    def _():
-        span.start()
-
     gathering.forward("so", "ck")
     gathering.cross("cv", "cq")
 
@@ -650,11 +672,16 @@
             to_ctx(
                 src.at[:, lanes_of(peer)], dst.at[rows_of(peer, BLOCK)], send.at[t, d], recv.at[t, d], peer
             ).wait_recv()
+    stores = [moves.start(*pair) for pair in ((qh, qh_out), (kh, kh_out), (vh, vh_out))]
     for i in range(n):
         part = slice(i * BLOCK, (i + 1) * BLOCK)
         vt[:, part] = vh[part, :].astype(F32).T.astype(BF)
 
     def query_block(step, unused):
+        @pl.when((step == 0) & (me < n - 1))
+        def _():
+            span.start()
+
         @pl.when(step == 1)
         def _():
             gathering.forward("cv", "cq")
@@ -730,9 +757,7 @@
         return unused
 
     lax.fori_loop(0, n, query_block, 0)
-    qh_out[...] = qh[...]
-    kh_out[...] = kh[...]
-    vh_out[...] = vh[...]
+    load_near.wait()
 
     @pl.when(me > 0)
     def _():
@@ -742,7 +767,7 @@
     def _():
         before_ref[...] = jnp.zeros_like(before_ref)
 
-    for name, out_ref in (("ck", keys_ref), ("cv", values_ref)):
+    for name, out_ref, far_ref in (("ck", keys_ref, keys_out), ("cv", values_ref, values_out)):
         gathering.arrive(name)
         save(name)
         out_ref[:span_rows, :] = nn_dot(before_ref[...], held[name][...]).astype(BF)
@@ -750,6 +775,7 @@
             rows = slice(g * span_rows, (g + 1) * span_rows)
             there = slice((g + 1) * span_rows, (g + 2) * span_rows)
             out_ref[there, :] = nn_dot(near_ref[rows, :], held[name][...]).astype(BF)
+        stores.append(moves.start(out_ref, far_ref))
     gathering.land("co")
     gathering.forward("cot")
     for d in range(1, n):
@@ -774,8 +800,7 @@
 
     near.wait_send()
     over.wait_send()
-    for copy in saving:
-        copy.wait()
+    wait_all(saving + stores)
 
 
 def vmem(count):
@@ -800,18 +825,18 @@
             low((owners * feed.shape[0], feed.shape[1] // owners)),
             low((rows, width)),
             low(tokens.shape),
-            heads,
-            heads,
-            heads,
             jax.ShapeDtypeStruct((WIDE, seq), F32),
             jax.ShapeDtypeStruct((8, seq), F32),
             jax.ShapeDtypeStruct(small.shape, F32),
             low((span_rows, near.shape[1])),
+            heads,
+            heads,
+            heads,
             keys,
             keys,
         ),
-        in_specs=vmem(3) + [any_spec] * 10,
-        out_specs=tuple([any_spec] * 10 + vmem(11)),
+        in_specs=vmem(2) + [any_spec] * 11,
+        out_specs=tuple([any_spec] * 10 + vmem(6) + [any_spec] * 5),
         scratch_shapes=[
             *[pltpu.VMEM(wholes[0].shape, BF)] * 5,
             pltpu.VMEM((3, rows, width), BF),
@@ -838,6 +863,10 @@
             dma((6,)),
             dma((5,)),
             dma((2,)),
+            pltpu.VMEM(near.shape, BF),
+            pltpu.VMEM(keys.shape, BF),
+            pltpu.VMEM(keys.shape, BF),
+            dma((6,)),
         ],
         compiler_params=pltpu.CompilerParams(
             collective_id=1, has_side_effects=True, vmem_limit_bytes=60 << 20
@@ -850,15 +879,17 @@
 def attn_backward_kernel(
     n, do_ref, qh, kh, vh, ot_ref, lse_ref, bias_ref, *rest
 ):
-    parts = dict(zip(EARLY, rest[:5], strict=True))
-    feed_part = rest[5]
-    dq_ref, dk_ref, dv_ref, line_ref, tall_pair, tall_one, flat_out = rest[6:13]
-    feed_full = rest[13:15]
+    given = dict(zip(MADE, zip(rest[2:8:2], rest[3:8:2], strict=True), strict=True))
+    feed_part = rest[8]
+    dq_ref, dk_ref, dv_ref, line_ref, tall_pair, tall_one, flat_out = rest[9:16]
+    feed_full = rest[16:18]
     (
         doh, kt, stage, land, dk_acc, dv_acc, dq_acc, q_masked, do_masked, delta, tiles, dtiles,
         send, recv, gsend, grecv, ring_send, ring_recv,
-    ) = rest[15:33]
-    extra = rest[33:]
+    ) = rest[18:36]
+    made = dict(zip(MADE, rest[36:39], strict=True))
+    parts = dict(zip(EARLY, (rest[0], rest[1], *made.values()), strict=True))
+    extra = rest[39:]
     fold_wa = Folding(EARLY, parts, (extra[0:4], extra[4:8], extra[8:13]))
     ring = Ring(FEED_LANES, ring_send, ring_recv, full=feed_full)
     for lane in range(2):
@@ -867,7 +898,7 @@
     me = lax.axis_index("ctx")
     pairs = ((do_ref, doh),)
     spread(n, me, pairs, send, recv, 0)
-    fold_wa.start()
+    fold_wa.start("ck", "cv")
     bias_tiles(bias_ref, me, tiles)
     for j in range(n):
         part = slice(j * BLOCK, (j + 1) * BLOCK)
@@ -877,6 +908,9 @@
         fold_wa.send(name)
     ring.gather(jnp.int32(0), FEED_TURNS[0])
     ring.gather(jnp.int32(0), FEED_TURNS[1])
+    for name in MADE:
+        product_into(made[name], *given[name])
+        fold_wa.start(name)
     dq_acc[...] = jnp.zeros_like(dq_acc)
     for d in range(1, n):
         peer = lax.rem(me + n - d, n)
@@ -1030,7 +1064,7 @@
             feed,
             feed,
         ),
-        in_specs=vmem(7) + [pl.BlockSpec(memory_space=pl.ANY)] * 5 + vmem(1),
+        in_specs=vmem(7) + [pl.BlockSpec(memory_space=pl.ANY)] * 2 + vmem(7),
         out_specs=tuple(vmem(9)),
         scratch_shapes=[
             pltpu.VMEM((seq, WIDE), BF),
@@ -1051,10 +1085,13 @@
             pltpu.SemaphoreType.DMA((3, n)),
             pltpu.SemaphoreType.DMA((len(FEED_LANES), HOPS)),
             pltpu.SemaphoreType.DMA((len(FEED_LANES), HOPS)),
+            pltpu.VMEM((896, 1024), BF),
+            pltpu.VMEM((1024, 896), BF),
+            pltpu.VMEM((1024, 896), BF),
             *Folding.scratch(EARLY),
         ],
         compiler_params=pltpu.CompilerParams(
-            collective_id=2, has_side_effects=True, vmem_limit_bytes=58 << 20
+            collective_id=2, has_side_effects=True, vmem_limit_bytes=60 << 20
         ),
         cost_estimate=lasting(100),
         name="attn_backward",
@@ -1149,12 +1186,12 @@
 
 
 def reduce_kernel(*refs):
-    ca_ref, cb_ref, out_ref, small_ref = refs[:4]
-    parts = dict(zip(LATE, refs[4:7], strict=True))
-    fin_ref = refs[7]
+    ca_ref, cb_ref, out_ref, small_ref, low_ref = refs[:5]
+    given = dict(zip(LATE, refs[5:8], strict=True))
+    fin_ref = refs[8]
     count = len(NAMES)
-    full = dict(zip(NAMES, refs[8 : 8 + count], strict=True))
-    refs = refs[8 + count :]
+    full = dict(zip(NAMES, refs[9 : 9 + count], strict=True))
+    refs = refs[9 + count :]
     late_full = dict(zip(LATE, refs[:3], strict=True))
     small_out, fin_out = refs[3:5]
     refs = refs[5:]
@@ -1163,7 +1200,9 @@
     refs = refs[2 * count :]
     grid_share, half_in, half, quarters, small_in, small_mid, small_beside, small_column = refs[:8]
     small_send, small_recv, ring_send, ring_recv, grid_send, grid_recv, fin_send, fin_recv = refs[8:16]
-    extra = refs[16:]
+    made, turned = refs[16:18]
+    parts = {name: made.at[u] for u, name in enumerate(LATE)}
+    extra = refs[18:]
     fold_wa = Folding(LATE, parts, (extra[0:4], None, extra[4:9]))
     place, after, before = ring_place(RING)
     grids = {
@@ -1179,7 +1218,6 @@
         [{"wa": peer} for peer in (fold_wa.mate, fold_wa.across, both)]
         + [{"ctx": peer} for peer in (after, before, some.beside, *in_column)]
     )
-    fold_wa.start()
     near = remote(small_ref, small_in.at[0], small_send.at[0], small_recv.at[0], wa=fold_wa.mate)
     near.start()
     over = remote(small_mid.at[0], small_in.at[1], small_send.at[1], small_recv.at[1], wa=fold_wa.across)
@@ -1244,13 +1282,21 @@
             fold_wa.x_copies[following].start()
         grids[name].start(total)
 
+    def make(name):
+        parts[name][...] = nn_dot(turned[...], given[name][...]).astype(BF)
+        fold_wa.start(name)
+
+    def make_all():
+        turned[...] = low_ref[...].astype(F32).T.astype(BF)
+        make("q")
+        make("k")
+        fold_wa.send("q")
+        make("v")
+        fold_wa.prepare("k")
+        fold_wa.prepare("v")
+
     events = {
-        0: [
-            lambda: fold_wa.send("q"),
-            lambda: fold_wa.prepare("k"),
-            lambda: fold_wa.prepare("v"),
-            small_over,
-        ],
+        0: [make_all, small_over],
         4: [lambda: begin("q", "k"), small_next],
         6: [grids["q"].spread, lambda: begin("k", "v"), small_last],
         8: [grids["q"].total, grids["k"].spread],
@@ -1285,7 +1331,7 @@
     return pl.ds(pl.multiple_of(owner * 896, WIDE), 896)
 
 
-def reduce_grads(pair, one, flat, small, parts, fin):
+def reduce_grads(pair, one, flat, small, low, grads, fin):
     dma = pltpu.SemaphoreType.DMA
     any_spec = pl.BlockSpec(memory_space=pl.ANY)
     late = len(LATE)
@@ -1297,7 +1343,7 @@
             jax.ShapeDtypeStruct(small.shape, F32),
             jax.ShapeDtypeStruct((224, 3584), BF),
         ),
-        in_specs=vmem(4) + [any_spec] * 4,
+        in_specs=vmem(8) + [any_spec],
         out_specs=(*vmem(len(NAMES) + late + 1), any_spec),
         scratch_shapes=[
             *(pltpu.VMEM(BUFFERS[b][1], BF) for b in NAMES),
@@ -1318,6 +1364,8 @@
             dma((late, 8)),
             dma((4,)),
             dma((3,)),
+            pltpu.VMEM((late, 896, 1024), BF),
+            pltpu.VMEM((896, 256), BF),
             *Folding.scratch(LATE),
         ],
         compiler_params=pltpu.CompilerParams(
@@ -1325,7 +1373,7 @@
         ),
         cost_estimate=lasting(90),
         name="reduce_grads",
-    )(pair, one, flat, small, *parts, fin.reshape(4, 224, 896))
+    )(pair, one, flat, small, low, *grads, fin.reshape(4, 224, 896))
 
 
 def unfold(full):
@@ -1341,8 +1389,8 @@
 
 
 def ffn_kernel(
-    f_ref, cot_ref, win_ref, wout_ref, bias_ref, res_ref, df_ref, dwin_ref, dwout_ref, dbias_ref,
-    f_all, g_all, dul_all, own, kept, out_mate, out_cross, in_mate, in_cross, x_out, x_in,
+    late, f_ref, cot_ref, win_ref, wout_ref, bias_ref, res_ref, parts_ref, df_ref, dwin_ref, dwout_ref, dbias_ref,
+    f_all, g_all, dul_all, ahead, own, kept, out_mate, out_cross, in_mate, in_cross, x_out, x_in,
     f_send, f_recv, p_send, p_recv,
 ):
     me = lax.axis_index("wa")
@@ -1364,6 +1412,8 @@
         if k == 1:
             to_mate.wait_recv()
         if k == 2:
+            for d in range(2):
+                ahead[d] = nt_dot(cot_ref[order[2 + d]], wout_ref[...])
             to_across.wait_recv()
             forward.start()
         if k == 3:
@@ -1373,7 +1423,7 @@
         t = jnp.tanh(GELU * (u + 0.044715 * (square * u)))
         g_all[s] = (0.5 * u * (1.0 + t)).astype(BF)
         slope = 0.5 * (1.0 + t) + 0.5 * u * (1.0 - t * t) * (GELU * (1.0 + 3 * 0.044715 * square))
-        du = nt_dot(cot_ref[s], wout_ref[...]) * slope
+        du = (nt_dot(cot_ref[s], wout_ref[...]) if k < 2 else ahead[k - 2]) * slope
         dbias_ref[...] += jnp.sum(du.reshape(32, 8, du.shape[1]), axis=0)
         dul_all[s] = du.astype(BF)
 
@@ -1407,7 +1457,13 @@
             copy.wait_send()
 
     df_copies = scatter(0, lambda s: nt_dot(dul_all[s], win_ref[...]))
-    res_copies = scatter(1, lambda s: nn_dot(g_all[s], wout_ref[...]))
+    if late:
+        res_ref[...] = nn_dot(g_all[me], wout_ref[...])
+        for d, s in enumerate(order[1:]):
+            parts_ref[d] = nn_dot(g_all[s], wout_ref[...]).astype(BF)
+    else:
+        res_copies = scatter(1, lambda s: nn_dot(g_all[s], wout_ref[...]))
+        parts_ref[...] = jnp.zeros_like(parts_ref)
     width = f_ref.shape[1]
 
     def outer(left_all, right, out_ref):
@@ -1423,31 +1479,34 @@
     outer(f_all, dul_all, dwin_ref)
     outer(g_all, cot_ref, dwout_ref)
     finish(0, df_copies, df_ref)
-    finish(1, res_copies, res_ref)
+    if not late:
+        finish(1, res_copies, res_ref)
     for copy in (to_mate, to_across, forward):
         copy.wait_send()
 
 
-def ffn(f_low, cot_all, win, wout, bias):
+def ffn(late, f_low, cot_all, win, wout, bias):
     rows, width = f_low.shape
     hidden = win.shape[1]
     dma = pltpu.SemaphoreType.DMA
     block = (rows, width)
     return pl.pallas_call(
-        ffn_kernel,
+        functools.partial(ffn_kernel, late),
         out_shape=(
             jax.ShapeDtypeStruct(block, F32),
+            jax.ShapeDtypeStruct((3, *block), BF),
             jax.ShapeDtypeStruct(block, F32),
             jax.ShapeDtypeStruct(win.shape, BF),
             jax.ShapeDtypeStruct(wout.shape, BF),
             jax.ShapeDtypeStruct((8, hidden), F32),
         ),
         in_specs=vmem(5),
-        out_specs=tuple(vmem(5)),
+        out_specs=tuple(vmem(6)),
         scratch_shapes=[
             pltpu.VMEM((4, *block), BF),
             pltpu.VMEM((4, rows, hidden), BF),
             pltpu.VMEM((4, rows, hidden), BF),
+            pltpu.VMEM((2, rows, hidden), F32),
             pltpu.VMEM((2, *block), F32),
             pltpu.VMEM(block, F32),
             *[pltpu.VMEM((2, *block), BF)] * 6,
@@ -1715,7 +1774,7 @@
     small = lax.dynamic_update_slice(small, gains, (0, wa * gains.shape[1]))
     small = jnp.concatenate([lines, small], 0)
     shards = [given[LONG_NAMES[name]] for name in GATHERED]
-    *wholes, upstream_all, feed_in, attended_low, low, qh, kh, vh, ot, lse, small, before, keys, values = attn_forward(
+    *wholes, upstream_all, feed_in, attended_low, low, ot, lse, small, before, qh, kh, vh, keys, values = attn_forward(
         lax.axis_size("ctx"), tokens, small, near, [*shards, cotangent], given["feedin"]
     )
     width = tokens.shape[1]
@@ -1764,23 +1823,38 @@
 
 
 def middle_kernel(
-    keep_ref, q_ref, dx_ref, k_ref, v_ref, before_ref, near_ref, wk_ref, wv_ref, fin_ref, fout_ref,
-    dq_ref, dwk_ref, dwv_ref, first_out, near_out, last_out, feed_out,
-    dk, dv, q_pad, dx_pad, dq_pad, share, hold, load_sem, ring_send, ring_recv,
+    keep_ref, fed_ref, fed_parts, q_far, dx_far, k_far, v_far, before_far, near_far, wk_far, wv_far, fin_ref,
+    fout_ref, feed_out, fed_out, dq_out, dwk_out, dwv_out, first_out, near_out, last_out,
+    q_ref, dx_ref, k_ref, v_ref, before_ref, near_ref, wk_ref, wv_ref, dq_ref, dwk_ref, dwv_ref, near_low, near_last,
+    dk, dv, q_pad, dx_pad, dq_pad, share, hold, in_mate, in_cross, x_out, x_in, load_sem, ring_send, ring_recv,
+    fed_send, fed_recv,
 ):
     ring = Ring(FEED_LANES, ring_send, ring_recv, share=share, hold=hold)
-    loads = [
-        pltpu.make_async_copy(part, share.at[b], load_sem.at[b])
-        for b, part in enumerate((fin_ref, fout_ref))
+    moves = Moves(load_sem)
+    loads = [moves.start(part, share.at[b]) for b, part in enumerate((fin_ref, fout_ref))]
+    pair_loads = [
+        moves.start(*pair) for pair in ((q_far, q_ref), (dx_far, dx_ref), (k_far, k_ref), (v_far, v_ref))
     ]
-    for load in loads:
-        load.start()
-    meet([{"ctx": ring.after}, {"ctx": ring.before}])
-    for load in loads:
-        load.wait()
+    later_loads = [
+        moves.start(*pair)
+        for pair in ((wk_far, wk_ref), (wv_far, wv_ref), (before_far, before_ref), (near_far, near_ref))
+    ]
+    wa = lax.axis_index("wa")
+    mate, across = other_wa(wa, 1), other_wa(wa, 2)
+    meet([{"ctx": ring.after}, {"ctx": ring.before}, {"wa": mate}, {"wa": across}])
+    cross = remote(fed_parts.at[2], in_cross, fed_send.at[0], fed_recv.at[0], wa=mate)
+    cross.start()
+    near = remote(fed_parts.at[0], in_mate, fed_send.at[1], fed_recv.at[1], wa=mate)
+    near.start()
+    over = remote(x_out, x_in, fed_send.at[2], fed_recv.at[2], wa=across)
+    wait_all(loads)
     for lanes in FEED_TURNS:
         ring.scatter(jnp.int32(0), lanes)
+    cross.wait_recv()
+    x_out[...] = (fed_parts[1].astype(F32) + in_cross[...].astype(F32)).astype(BF)
+    over.start()
     groups = k_ref.shape[0] // 256
+    wait_all(pair_loads)
 
     def two_pairs(m, unused):
         for turn, lanes in enumerate(FEED_TURNS):
@@ -1793,6 +1867,8 @@
 
     pairs = q_ref.shape[1] // (2 * WIDE)
     lax.fori_loop(0, pairs, two_pairs, 0)
+    stores = [moves.start(dq_ref, dq_out)]
+    wait_all(later_loads)
     calls = [(step, lanes) for step in range(pairs + 1, HOPS + 1) for lanes in FEED_TURNS]
 
     def turn():
@@ -1803,14 +1879,17 @@
     for g in range(groups):
         rows = slice(g * 256, (g + 1) * 256)
         total = nt_dot(dk[rows, :], wk_ref[...]) + nt_dot(dv[rows, :], wv_ref[...])
-        if g == 0:
-            first_out[...] = total.astype(BF)
-        elif g == groups - 1:
-            last_out[...] = total
+        if g == groups - 1:
+            near_last[...] = total
         else:
-            near_out[(g - 1) * 256 : g * 256, :] = total.astype(BF)
+            near_low[rows, :] = total.astype(BF)
         if g % 2 == 1:
             turn()
+    stores += [
+        moves.start(near_low.at[:256], first_out),
+        moves.start(near_low.at[256:], near_out),
+        moves.start(near_last, last_out),
+    ]
     for c in range(near_ref.shape[1] // WIDE):
         lanes = slice(c * WIDE, (c + 1) * WIDE)
         first = before_ref[:, lanes].astype(F32).T.astype(BF)
@@ -1820,33 +1899,52 @@
             out_ref[lanes, :] = total.astype(BF)
         if c % 2 == 1:
             turn()
+    stores += [moves.start(dwk_ref, dwk_out), moves.start(dwv_ref, dwv_out)]
     while calls:
         turn()
+    near.wait_recv()
+    over.wait_recv()
+    fed_out[...] = fed_ref[...] + in_mate[...].astype(F32) + x_in[...].astype(F32)
+    for copy in (cross, near, over):
+        copy.wait_send()
     for lane in range(2):
         feed_out[lane] = share[lane, ring.chunk(lane, 1)]
     ring.finish(lambda lane: share.at[FEED_LANES[lane][0], 0, FEED_LANES[lane][2]])
-
-
-def middle(keep, query, dmixed, keys, values, before, near, wk, wv, fin, fout):
+    wait_all(stores)
+
+
+def middle(keep, query, dmixed, keys, values, before, near, wk, wv, fed, fed_parts, fin, fout):
     many, width = keys.shape
     wide = near.shape[1]
+    rows = query.shape[0]
     low = functools.partial(jax.ShapeDtypeStruct, dtype=BF)
     dma = pltpu.SemaphoreType.DMA
+    any_spec = pl.BlockSpec(memory_space=pl.ANY)
     pad = pltpu.VMEM((many // 256 * SPAN, WIDE), F32)
-    return pl.pallas_call(
+    feed_part, fed, *others = pl.pallas_call(
         middle_kernel,
         out_shape=(
+            low((2, *FEED[1:])),
+            jax.ShapeDtypeStruct(fed.shape, F32),
             low(query.shape),
             low(wk.shape),
             low(wv.shape),
             low((256, wide)),
             low((many - 512, wide)),
             jax.ShapeDtypeStruct((256, wide), F32),
-            low((2, *FEED[1:])),
         ),
-        in_specs=vmem(9) + [pl.BlockSpec(memory_space=pl.ANY)] * 2,
-        out_specs=tuple(vmem(7)),
+        in_specs=vmem(3) + [any_spec] * 10,
+        out_specs=tuple(vmem(2) + [any_spec] * 6),
         scratch_shapes=[
+            *[pltpu.VMEM((rows, width), BF)] * 2,
+            *[pltpu.VMEM((many, width), BF)] * 2,
+            pltpu.VMEM((256, wide), BF),
+            pltpu.VMEM((many - 256, wide), BF),
+            *[pltpu.VMEM(wk.shape, BF)] * 2,
+            pltpu.VMEM((rows, width), BF),
+            *[pltpu.VMEM(wk.shape, BF)] * 2,
+            pltpu.VMEM((many - 256, wide), BF),
+            pltpu.VMEM((256, wide), F32),
             pltpu.VMEM((many, width), BF),
             pltpu.VMEM((many, width), BF),
             pad,
@@ -1854,16 +1952,23 @@
             pad,
             pltpu.VMEM((2, *FEED), BF),
             pltpu.VMEM((2, HOPS, *FEED[1:]), BF),
-            dma((2,)),
+            *[pltpu.VMEM(fed.shape, BF)] * 4,
+            dma((16,)),
             dma((len(FEED_LANES), HOPS)),
             dma((len(FEED_LANES), HOPS)),
+            dma((3,)),
+            dma((3,)),
         ],
         compiler_params=pltpu.CompilerParams(
-            collective_id=5, has_side_effects=True, vmem_limit_bytes=56 << 20
+            collective_id=5, has_side_effects=True, vmem_limit_bytes=60 << 20
         ),
         cost_estimate=lasting(38),
         name="middle",
-    )(keep, query, dmixed, keys, values, before, near, wk, wv, fin.reshape(FEED), fout.reshape(FEED))
+    )(
+        keep, fed, fed_parts, query, dmixed, keys, values, before, near, wk, wv,
+        fin.reshape(FEED), fout.reshape(FEED),
+    )
+    return *others, feed_part, fed
 
 
 NAMES_OF_WEIGHTS = (
@@ -1944,10 +2049,9 @@
     normed_feed, back_feed = jax.vjp(root_norm, hidden_two, small_of["feednorm"])
     feed_low = normed_feed.astype(BF)
     bias_row = given["feedbias"].astype(F32)[None]
-    fed, grad_feed, fin, fout, bias_sums = ffn(
-        feed_low, upstream_all, feed_in, given["feedout"], bias_row
-    )
-    result = (hidden_two + fed + small_of["outbias"]).astype(BF)
+    fed, fed_parts, grad_feed, fin, fout, bias_sums = ffn(
+        split_heads, feed_low, upstream_all, feed_in, given["feedout"], bias_row
+    )
     grad_two_part, grad_feednorm = back_feed(grad_feed)
     grad_two = upstream + grad_two_part
     two_low = grad_two.astype(BF)
@@ -1955,7 +2059,7 @@
     grad_mixed = back_product(two_low, full["crossout"]).astype(BF)
     early = {}
     if split_heads:
-        grad_query_cross, early["ck"], early["cv"], first, near_low, near_last, feed_part = middle(
+        grad_query_cross, early["ck"], early["cv"], first, near_low, near_last, feed_part, fed = middle(
             keep,
             query_cross,
             grad_mixed,
@@ -1965,6 +2069,8 @@
             own_rows,
             full["crosskey"],
             full["crossvalue"],
+            fed,
+            fed_parts,
             fin,
             fout,
         )
@@ -1979,6 +2085,7 @@
         near_low = near_grads[span_rows:-span_rows].astype(BF)
         early["ck"] = outer_product(near_rows, dkeys).astype(BF)
         early["cv"] = outer_product(near_rows, dvalues).astype(BF)
+    result = (hidden_two + fed + small_of["outbias"]).astype(BF)
     back = passed_along(first, "ctx", -1).astype(F32)
     grad_hidden_part, grad_crossnorm = back_cross(
         back_product(grad_query_cross, full["crossquery"])
@@ -1986,12 +2093,15 @@
     grad_hidden = grad_two + grad_hidden_part
     hidden_low = grad_hidden.astype(BF)
     dout_low = back_product(hidden_low, full["selfout"]).astype(BF)
-    early["cq"] = outer_product(cross_in, grad_query_cross).astype(BF)
-    early["co"] = outer_product(mixed_low, two_low).astype(BF)
-    early["so"] = outer_product(attended_low, hidden_low).astype(BF)
+    sides = {
+        "cq": (cross_in, grad_query_cross),
+        "co": (mixed_low, two_low),
+        "so": (attended_low, hidden_low),
+    }
     if split_heads:
+        parts = [early["ck"], early["cv"], *(side for name in MADE for side in sides[name])]
         dquery_low, dkey_low, dvalue_low, grad_biastable, shares = heads_backward(
-            attention_state, dout_low, [early[name] for name in EARLY], feed_part
+            attention_state, dout_low, parts, feed_part
         )
         *shares, fin, fout = shares
     else:
@@ -2008,11 +2118,7 @@
         jnp.concatenate([near_low, (near_last + back).astype(BF)], 0)
         .reshape(neighbours.shape)
     )
-    late = {
-        "q": outer_product(normed_low, dquery_low).astype(BF),
-        "k": outer_product(normed_low, dkey_low).astype(BF),
-        "v": outer_product(normed_low, dvalue_low).astype(BF),
-    }
+    late_grads = (dquery_low, dkey_low, dvalue_low)
     wa, owners = lax.axis_index("wa"), lax.axis_size("wa")
     bias_grad = jnp.sum(bias_sums, axis=0)
     placed = lax.dynamic_update_slice(
@@ -2023,12 +2129,16 @@
     packed = jnp.pad(packed, ((0, 0), (0, LINE * 2 - packed.shape[1]))).reshape(-1, WIDE)
     if split_heads:
         *reduced, packed, fin = reduce_grads(
-            *shares, packed, [late[name] for name in LATE], fin
+            *shares, packed, normed_low, late_grads, fin
         )
         grads = unfold(dict(zip((*NAMES, *LATE), reduced, strict=True)))
         fout = fout.reshape(given["feedout"].shape)
     else:
-        grads, packed = reduce_plain(early | late, packed)
+        for name, grad in zip(LATE, late_grads, strict=True):
+            sides[name] = (normed_low, grad)
+        for name, (left, right) in sides.items():
+            early[name] = outer_product(left, right).astype(BF)
+        grads, packed = reduce_plain(early, packed)
         fin, fout = lax.psum((fin, fout), "ctx")
         fin = lax.all_to_all(fin, "wa", 0, 1, tiled=True)
     grads["fin"], grads["fout"] = fin.astype(F32), fout.astype(F32)

time: 481 us -> 455 us (0.946)
  Pallas kernels: 402 us -> 389 us
  matrix products: 27.8 us -> 15.8 us
    pallas_call x1, Pallas kernels: 115 us -> 96.4 us  [attn_forward(): pl.pallas_call(functools.partial(attn_forward_kernel, n), out_shape=(*who...]
    dot_general x6 -> x0, matrix products: 11.6 us -> none  [outer_product(): lax.dot_general(left_side, right_side, (((0,), (0,)), ((), ())), preferre...]
  transfers between devices with their start and end apart: 1 -> 1, of which waited for: 0 -> 0; matrix products, arithmetic and copies ran while one was open for 9% -> 7% of each run, Pallas kernels for 40% -> 43%
where the time goes in v5:
time: 455 us; the launch traced here: 447 us
  Pallas kernels  389 us (85%)
  other arithmetic  25.8 us (6%)
  matrix products  15.8 us (3%)
  local copies, waits for them, and re-layouts  13.7 us (3%)
    pallas_call x1, Pallas kernels, attn_backward(): pl.pallas_call(functools.partial(attn_backward_kernel, n), out_shape=(gra...  97.1 us
    pallas_call x1, Pallas kernels, reduce_grads(): pl.pallas_call(reduce_kernel, out_shape=(*(jax.ShapeDtypeStruct(BUFFERS[b...  96.5 us
    pallas_call x1, Pallas kernels, attn_forward(): pl.pallas_call(functools.partial(attn_forward_kernel, n), out_shape=(*who...  96.4 us
    pallas_call x1, Pallas kernels, ffn(): pl.pallas_call(functools.partial(ffn_kernel, late), out_shape=(jax.ShapeD...  45.5 us
    pallas_call x1, Pallas kernels, middle(): pl.pallas_call(middle_kernel, out_shape=(low((2, *FEED[1:])), jax.ShapeDt...  43.7 us
    dot_general x6, matrix products, back_product(): lax.dot_general(grad_low, weight, (((1,), (1,)), ((), ())), preferred_ele...  10.2 us
    pallas_call x1, Pallas kernels, cross_forward(): pl.pallas_call(functools.partial(cross_forward_kernel, groups), grid=(wid...  9.64 us
  transfers between devices with their start and end apart: 1, of which 0 were waited for; matrix products, arithmetic and copies ran while one was open for 7% of the time, Pallas kernels for 43%

profile of v5, /device:TPU:0, one launch (start us, length us, event | category | flops | bytes accessed | tf_op | source)
XLA Modules:
  0.0 446.8 jit_solution(10432640474174006543)
XLA Ops:
  1.6 1.3 reshape.217.bias_ref
  4.5 96.4 %attn_forward.1 = (bf16[896,1024]{1,0:T(8,128)(2,1)}, bf16[896,1024]{1,0:T(8,128)(2,1)}, bf16[896,1024]{1,0:T(8,128)(2,1)}, bf16[1024,896]{1,0:T(8,128)(2,1)}, b...) custom-call(bf16[256,896]{1,0:T(8,128)(2,1)} %bitcast.60, ...), custom_call_target="tpu_custom_call" | custom-call | bytes 255000000 | tf_op jit(solution)/shard_map/attn_forward/pallas_call | solution.py:821
  100.9 0.9 slice_reduce_fusion.1
  101.9 2.6 multiply_reduce_fusion.5
  106.3 1.5 convolution_convert_fusion.2.q_ref.q_far
  107.8 1.7 copy-done.3
  109.6 1.0 copy-done.5
  110.6 9.6 %cross_forward.1.rest_4_ = bf16[256,1024]{1,0:T(8,128)(2,1)S(1)} custom-call(f32[8,128]{1,0:T(8,128)S(1)} %broadcast_in_dim.53.keep_ref, bf16[256,1024]{1,0:T(8,128)(2,1)S(1)} %copy-done.5, bf16[1280,1024]{1,0:T(8,128)(2,1)S(1)} %copy-done.2, bf16[1280,1024]{1,0:T(8,128)(2,1)S(1)} %copy-done.3), custom_call_target="tpu_custom_call" | custom-call | bytes 27000000 | tf_op jit(solution)/shard_map/cross_forward/pallas_call | solution.py:1565
  122.0 45.5 %feed_forward.1 = (f32[256,896]{1,0:T(8,128)}, bf16[3,256,896]{2,1,0:T(8,128)(2,1)}, f32[256,896]{1,0:T(8,128)}, bf16[896,896]{1,0:T(8,128)(2,1)}, bf16[896,896]{1,0:T(8,128)(2,1)}, /*index=5*/f32[8,896]{1,0:T(8,128)}) custom-call(bf16[256,896]{1,0:T(8,128)(2,1)} %multiply_convert_fusion.f_ref, bf16[4,256,896]{2,1,0:T(8,128)(2,1)} %bitcast.65, ...), custom_call_target="tpu_custom_call" | custom-call | bytes 132000000 | tf_op jit(solution)/shard_map/feed_forward/pallas_call | solution.py:1493
  167.6 1.6 multiply_reduce_fusion
  169.5 1.5 convolution_convert_fusion.1.dx_far
  171.1 43.7 %middle.1 = (bf16[2,112,896]{2,1,0:T(8,128)(2,1)}, f32[256,896]{1,0:T(8,128)}, bf16[256,1024]{1,0:T(8,128)(2,1)}, bf16[896,1024]{1,0:T(8,128)(2,1)}, bf16[896,10...) custom-call(f32[8,128]{1,0:T(8,128)} %copy-done.6, ...), custom_call_target="tpu_custom_call" | custom-call | bytes 114000000 | tf_op jit(solution)/shard_map/middle/pallas_call | solution.py:1924
  214.8 1.3 collective-permute-start
  217.0 3.4 multiply_reduce_fusion.1
  220.6 3.4 fusion.29
  223.9 1.5 convolution_convert_fusion.do_ref
  225.5 97.1 %attn_backward.1 = (bf16[256,1024]{1,0:T(8,128)(2,1)}, bf16[256,1024]{1,0:T(8,128)(2,1)}, bf16[256,1024]{1,0:T(8,128)(2,1)}, f32[8,1024]{1,0:T(8,128)}, bf16[448...) custom-call(bf16[256,1024]{1,0:T(8,128)(2,1)} %convolution_convert_f, ...), custom_call_target="tpu_custom_call" | custom-call | bytes 300000000 | tf_op jit(solution)/shard_map/attn_backward/pallas_call | solution.py:1054
  322.6 1.9 fusion.32
  326.3 1.0 fusion.7
  329.4 96.5 %reduce_grads.1 = (bf16[224,1024]{1,0:T(8,128)(2,1)}, bf16[224,1024]{1,0:T(8,128)(2,1)}, bf16[224,1024]{1,0:T(8,128)(2,1)}, bf16[8,32,896]{2,1,0:T(8,128)(2,1)},...) custom-call(bf16[448,1024]{1,0:T(8,128)(2,1)} %get-tuple-element.110, ...), custom_call_target="tpu_custom_call" | custom-call | bytes 270000000 | tf_op jit(solution)/shard_map/reduce_grads/pallas_call | solution.py:1338
  427.5 2.1 convert_element_type.187
  429.6 2.1 convert_element_type.188
  431.7 1.0 convert_element_type.189
  432.8 1.0 convert_element_type.190
  433.8 1.0 convert_element_type.191
  434.9 1.4 bitcast_convert_fusion.1
  436.3 1.1 fusion.10
  437.4 1.0 convert_element_type.192
  438.4 2.1 convert_element_type.193
  441.8 2.0 bitcast_convert_fusion
  443.8 1.2 add_convert_fusion
  445.3 1.4 pad_maximum_fusion
  (125 shorter events, 14.4 us)
Async XLA Ops:
  0.7 2.9 copy-start
  4.5 97.3 %copy-start.10 = (bf16[1,256,896]{2,1,0:T(8,128)(2,1)S(1)}, bf16[1,256,896]{2,1,0:T(8,128)(2,1)}, u32[]{:S(2)}) copy-start(bf16[1,256,896]{2,1,0:T(8,128)(2,1)} %param.19) | copy-start | bytes 1376260
  101.9 4.5 copy-start.23
  105.5 2.3 copy-start.2
  107.8 12.4 %copy-start.6 = (f32[8,128]{1,0:T(8,128)}, f32[8,128]{1,0:T(8,128)S(1)}, u32[]{:S(2)}) copy-start(f32[8,128]{1,0:T(8,128)S(1)} %broadcast_in_dim.53.keep_ref) | copy-start | bytes 12292
  107.8 1.7 copy-start.3
  110.6 9.7 %copy-start.8 = (f32[256,896]{1,0:T(8,128)S(1)}, f32[256,896]{1,0:T(8,128)}, u32[]{:S(2)}) copy-start(f32[256,896]{1,0:T(8,128)} %copy-done.7) | copy-start | bytes 2752516
  110.6 9.7 %copy-start.19 = (bf16[1024,896]{1,0:T(8,128)(2,1)S(1)}, bf16[1024,896]{1,0:T(8,128)(2,1)}, u32[]{:S(2)}) copy-start(bf16[1024,896]{1,0:T(8,128)(2,1)} %get-tuple-element.80) | copy-start | bytes 5505028
  167.6 1.6 copy-start.12
  167.6 1.6 copy-start.13
  169.5 1.6 copy-start.24
  171.1 45.0 %copy-start.11 = (bf16[1,256,896]{2,1,0:T(8,128)(2,1)S(1)}, bf16[1,256,896]{2,1,0:T(8,128)(2,1)}, u32[]{:S(2)}) copy-start(bf16[1,256,896]{2,1,0:T(8,128)(2,1)} %param.19) | copy-start | bytes 1376260
  171.1 45.2 %copy-start.37 = (f32[32,1024]{1,0:T(8,128)S(1)}, f32[32,1024]{1,0:T(8,128)}, u32[]{:S(2)}) copy-start(f32[32,1024]{1,0:T(8,128)} %get-tuple-element.76) | copy-start | bytes 393220
  171.1 45.8 %copy-start.38 = (f32[8,896]{1,0:T(8,128)S(1)}, f32[8,896]{1,0:T(8,128)}, u32[]{:S(2)}) copy-start(f32[8,896]{1,0:T(8,128)} %get-tuple-element.114) | copy-start | bytes 86020
  171.1 46.0 %copy-start.9 = (f32[256,896]{1,0:T(8,128)S(1)}, f32[256,896]{1,0:T(8,128)}, u32[]{:S(2)}) copy-start(f32[256,896]{1,0:T(8,128)} %copy-done.7) | copy-start | bytes 2752516
  214.8 229.0 %collective-permute-start = (bf16[256,896]{1,0:T(8,128)(2,1)}, bf16[256,896]{1,0:T(8,128)(2,1)}, u32[]{:S(2)}, u32[]{:S(2)}) collective-permute-start(bf16[256,896]{1,0:T(8,128)(2,1)} %get-tuple-element.109), channel_id=1, source_target_pairs={{4,0},{8,4},{12,8},{16,12},{20,16},{24,20},{28,24},{5,1},{9,5},{13... | collective-permute-start | bytes 1376264 | tf_op jit(solution)/shard_map/ppermute | solution.py:32
  220.6 3.4 copy-start.22
  223.9 1.6 copy-start.17
  225.5 97.1 %copy-start.18 = (bf16[896,1024]{1,0:T(8,128)(2,1)S(1)}, bf16[896,1024]{1,0:T(8,128)(2,1)}, u32[]{:S(2)}) copy-start(bf16[896,1024]{1,0:T(8,128)(2,1)} %get-tuple-element.102) | copy-start | bytes 5505028
  322.6 2.0 copy-start.15
  322.6 2.0 copy-start.21
  324.6 1.7 copy-start.20
  425.9 5.8 %copy-start.34 = (bf16[224,1024]{1,0:T(8,128)(2,1)S(1)}, bf16[224,1024]{1,0:T(8,128)(2,1)}, u32[]{:S(2)}) copy-start(bf16[224,1024]{1,0:T(8,128)(2,1)} %get-tuple-element.120) | copy-start | bytes 1376260
  427.5 5.2 %copy-start.33 = (bf16[224,1024]{1,0:T(8,128)(2,1)S(1)}, bf16[224,1024]{1,0:T(8,128)(2,1)}, u32[]{:S(2)}) copy-start(bf16[224,1024]{1,0:T(8,128)(2,1)} %get-tuple-element.123) | copy-start | bytes 1376260
  429.6 4.2 copy-start.32
  431.7 3.1 copy-start.35
  431.7 3.1 copy-start.36
  432.8 2.1 copy-start.31
  436.3 2.1 copy-start.27
  438.4 3.4 copy-start.26
  441.8 2.0 copy-start.29
  445.0 1.6 copy-start.1
  (9 other events, 9.8 us)

commit v6 on v5

--- a/solution.py
+++ b/solution.py
@@ -876,20 +876,23 @@
     )(tokens, small, near, *shards, feed)
 
 
-def attn_backward_kernel(
-    n, do_ref, qh, kh, vh, ot_ref, lse_ref, bias_ref, *rest
-):
-    given = dict(zip(MADE, zip(rest[2:8:2], rest[3:8:2], strict=True), strict=True))
-    feed_part = rest[8]
-    dq_ref, dk_ref, dv_ref, line_ref, tall_pair, tall_one, flat_out = rest[9:16]
-    feed_full = rest[16:18]
+def attn_backward_kernel(n, do_ref, lse_ref, bias_ref, feed_part, *rest):
+    far = rest[:10]
+    sides_far = far[4:]
+    line_ref, *outs = rest[12:21]
+    near = rest[21:31]
+    kh, qh, ot_ref, vh = near[:4]
+    given = dict(zip(MADE, zip(near[4::2], near[5::2], strict=True), strict=True))
+    tall_pair, tall_one, flat_out, *feed_full, move_sem = rest[31:37]
     (
         doh, kt, stage, land, dk_acc, dv_acc, dq_acc, q_masked, do_masked, delta, tiles, dtiles,
         send, recv, gsend, grecv, ring_send, ring_recv,
-    ) = rest[18:36]
-    made = dict(zip(MADE, rest[36:39], strict=True))
-    parts = dict(zip(EARLY, (rest[0], rest[1], *made.values()), strict=True))
-    extra = rest[39:]
+    ) = rest[37:55]
+    made = dict(zip(MADE, rest[55:58], strict=True))
+    parts = dict(zip(EARLY, (rest[10], rest[11], *made.values()), strict=True))
+    extra = rest[58:]
+    moves = Moves(move_sem)
+    loads = [moves.start(*pair) for pair in zip(far, near, strict=True)]
     fold_wa = Folding(EARLY, parts, (extra[0:4], extra[4:8], extra[8:13]))
     ring = Ring(FEED_LANES, ring_send, ring_recv, full=feed_full)
     for lane in range(2):
@@ -900,6 +903,7 @@
     spread(n, me, pairs, send, recv, 0)
     fold_wa.start("ck", "cv")
     bias_tiles(bias_ref, me, tiles)
+    loads[0].wait()
     for j in range(n):
         part = slice(j * BLOCK, (j + 1) * BLOCK)
         kt[:, part] = (kh[part, :].astype(F32) * HD**-0.5).T.astype(BF)
@@ -908,6 +912,7 @@
         fold_wa.send(name)
     ring.gather(jnp.int32(0), FEED_TURNS[0])
     ring.gather(jnp.int32(0), FEED_TURNS[1])
+    wait_all(loads[1:])
     for name in MADE:
         product_into(made[name], *given[name])
         fold_wa.start(name)
@@ -1013,11 +1018,17 @@
 
     lax.fori_loop(0, n, dq_block, 0)
     ring.finish(lambda lane: feed_full[FEED_LANES[lane][0]].at[0, FEED_LANES[lane][2]])
+    stores = [moves.start(full, out) for full, out in zip(feed_full, outs[6:8], strict=True)]
     tall_pair[:224, :] = fold_wa.total("cq")
     tall_pair[224:, :] = fold_wa.total("ck")
     tall_one[...] = fold_wa.total("cv")
     for at, name in ((0, "co"), (32, "so")):
         flat_out[:, at : at + 32, :] = fold_wa.total(name).reshape(8, 32, 896)
+    stores += [
+        moves.start(tall_pair, outs[3]),
+        moves.start(tall_one, outs[4]),
+        moves.start(flat_out, outs[5]),
+    ]
     fold_wa.finish()
     for h in range(2):
         line = jnp.concatenate(
@@ -1042,31 +1053,26 @@
             )
             back.wait_send()
             back.wait_recv()
-    dq_ref[...] = land[0]
-    dk_ref[...] = land[1]
-    dv_ref[...] = land[2]
+    wait_all(stores + [moves.start(land.at[t], outs[t]) for t in range(3)])
 
 
 def attn_backward(n, dout, qh, kh, vh, ot, lse, bias_lines, parts, feed_part):
     rows, seq = dout.shape[0], n * dout.shape[0]
     grads = jax.ShapeDtypeStruct(dout.shape, BF)
     feed = jax.ShapeDtypeStruct(FEED, BF)
-    return pl.pallas_call(
+    low = functools.partial(jax.ShapeDtypeStruct, dtype=BF)
+    any_spec = pl.BlockSpec(memory_space=pl.ANY)
+    far = (kh, qh, ot, vh, *parts[2:])
+    shares = (low((448, 1024)), low((224, 1024)), low((8, 64, 896)))
+    line, *outs = pl.pallas_call(
         functools.partial(attn_backward_kernel, n),
-        out_shape=(
-            grads,
-            grads,
-            grads,
-            jax.ShapeDtypeStruct((8, LINE), F32),
-            jax.ShapeDtypeStruct((448, 1024), BF),
-            jax.ShapeDtypeStruct((224, 1024), BF),
-            jax.ShapeDtypeStruct((8, 64, 896), BF),
-            feed,
-            feed,
-        ),
-        in_specs=vmem(7) + [pl.BlockSpec(memory_space=pl.ANY)] * 2 + vmem(7),
-        out_specs=tuple(vmem(9)),
+        out_shape=(jax.ShapeDtypeStruct((8, LINE), F32), grads, grads, grads, *shares, feed, feed),
+        in_specs=vmem(4) + [any_spec] * 12,
+        out_specs=tuple(vmem(1) + [any_spec] * 8),
         scratch_shapes=[
+            *(pltpu.VMEM(v.shape, v.dtype) for v in far),
+            *(pltpu.VMEM(v.shape, v.dtype) for v in (*shares, feed, feed)),
+            pltpu.SemaphoreType.DMA((18,)),
             pltpu.VMEM((seq, WIDE), BF),
             pltpu.VMEM((WIDE, seq), BF),
             pltpu.VMEM((3, seq, WIDE), BF),
@@ -1095,7 +1101,8 @@
         ),
         cost_estimate=lasting(100),
         name="attn_backward",
-    )(dout, qh, kh, vh, ot, lse, bias_lines, *parts, feed_part)
+    )(dout, lse, bias_lines, feed_part, *far, *parts[:2])
+    return *outs[:3], line, *outs[3:]
 
 
 BUFFERS = {
@@ -1186,21 +1193,38 @@
 
 
 def reduce_kernel(*refs):
-    ca_ref, cb_ref, out_ref, small_ref, low_ref = refs[:5]
-    given = dict(zip(LATE, refs[5:8], strict=True))
-    fin_ref = refs[8]
+    small_ref, ca_far, cb_far, out_far = refs[:4]
+    sides_far, fin_ref = refs[4:8], refs[8]
     count = len(NAMES)
-    full = dict(zip(NAMES, refs[9 : 9 + count], strict=True))
-    refs = refs[9 + count :]
-    late_full = dict(zip(LATE, refs[:3], strict=True))
-    small_out, fin_out = refs[3:5]
-    refs = refs[5:]
+    small_out = refs[9]
+    full_out = dict(zip((*NAMES, *LATE), refs[10 : 13 + count], strict=True))
+    fin_out = refs[13 + count]
+    refs = refs[14 + count :]
+    low_ref, *sides = refs[:4]
+    given = dict(zip(LATE, sides, strict=True))
+    full = dict(zip((*NAMES, *LATE), refs[4 : 7 + count], strict=True))
+    late_full = full
+    move_sem = refs[7 + count]
+    refs = refs[8 + count :]
     share = dict(zip(NAMES, refs[:count], strict=True))
     hold = dict(zip(NAMES, refs[count : 2 * count], strict=True))
     refs = refs[2 * count :]
     grid_share, half_in, half, quarters, small_in, small_mid, small_beside, small_column = refs[:8]
     small_send, small_recv, ring_send, ring_recv, grid_send, grid_recv, fin_send, fin_recv = refs[8:16]
     made, turned = refs[16:18]
+    moves = Moves(move_sem)
+    share_loads = [
+        moves.start(*pair)
+        for pair in (
+            (ca_far.at[:224], share["cq"]),
+            (cb_far, share["cv"]),
+            (ca_far.at[224:], share["ck"]),
+            (out_far.at[:, :32], share["co"]),
+            (out_far.at[:, 32:48], share["so0"]),
+            (out_far.at[:, 48:], share["so1"]),
+        )
+    ]
+    side_loads = [moves.start(*pair) for pair in zip(sides_far, (low_ref, *sides), strict=True)]
     parts = {name: made.at[u] for u, name in enumerate(LATE)}
     extra = refs[18:]
     fold_wa = Folding(LATE, parts, (extra[0:4], None, extra[4:9]))
@@ -1232,12 +1256,7 @@
         remote(fin_ref.at[peer], fin_out.at[:, columns_of(wa)], fin_send.at[d], fin_recv.at[d], wa=peer)
         for d, peer in enumerate((fold_wa.across, both, fold_wa.mate))
     ]
-    share["cq"][...] = ca_ref[:224]
-    share["ck"][...] = ca_ref[224:]
-    share["cv"][...] = cb_ref[...]
-    share["co"][...] = out_ref[:, :32]
-    share["so0"][...] = out_ref[:, 32:48]
-    share["so1"][...] = out_ref[:, 48:]
+    wait_all(share_loads)
     copies = {}
 
     def ring_step(b, name, step):
@@ -1287,6 +1306,7 @@
         fold_wa.start(name)
 
     def make_all():
+        wait_all(side_loads)
         turned[...] = low_ref[...].astype(F32).T.astype(BF)
         make("q")
         make("k")
@@ -1311,6 +1331,7 @@
             ring_step(b, name, tick)
         for event in events.get(tick, ()):
             event()
+    stores = [moves.start(full[name], full_out[name]) for name in NAMES]
     for copy in columns:
         copy.wait_recv()
     total = small_column[0]
@@ -1319,12 +1340,14 @@
     small_out[...] = total
     for name in LATE:
         grids[name].finish()
+        stores.append(moves.start(full[name], full_out[name]))
     fold_wa.finish()
     for copy in (near, over, beside, *columns, *copies.values()):
         copy.wait_send()
     own_fin.wait()
     for copy in fin_copies:
         copy.wait()
+    wait_all(stores)
 
 
 def columns_of(owner):
@@ -1335,17 +1358,21 @@
     dma = pltpu.SemaphoreType.DMA
     any_spec = pl.BlockSpec(memory_space=pl.ANY)
     late = len(LATE)
-    return pl.pallas_call(
+    shapes = [*(BUFFERS[b][1] for b in NAMES), *[TALL] * late]
+    small, *others = pl.pallas_call(
         reduce_kernel,
         out_shape=(
-            *(jax.ShapeDtypeStruct(BUFFERS[b][1], BF) for b in NAMES),
-            *[jax.ShapeDtypeStruct(TALL, BF)] * late,
             jax.ShapeDtypeStruct(small.shape, F32),
+            *(jax.ShapeDtypeStruct(shape, BF) for shape in shapes),
             jax.ShapeDtypeStruct((224, 3584), BF),
         ),
-        in_specs=vmem(8) + [any_spec],
-        out_specs=(*vmem(len(NAMES) + late + 1), any_spec),
+        in_specs=vmem(1) + [any_spec] * 8,
+        out_specs=tuple(vmem(1) + [any_spec] * (len(shapes) + 1)),
         scratch_shapes=[
+            pltpu.VMEM(low.shape, BF),
+            *(pltpu.VMEM(grad.shape, BF) for grad in grads),
+            *(pltpu.VMEM(shape, BF) for shape in shapes),
+            dma((10 + len(shapes),)),
             *(pltpu.VMEM(BUFFERS[b][1], BF) for b in NAMES),
             *(pltpu.VMEM((HOPS, *chunk_shape(b)), BF) for b in NAMES),
             pltpu.VMEM((late, *TALL), BF),
@@ -1373,7 +1400,8 @@
         ),
         cost_estimate=lasting(90),
         name="reduce_grads",
-    )(pair, one, flat, small, low, *grads, fin.reshape(4, 224, 896))
+    )(small, pair, one, flat, low, *grads, fin.reshape(4, 224, 896))
+    return *others[:-1], small, others[-1]
 
 
 def unfold(full):
@@ -1389,10 +1417,14 @@
 
 
 def ffn_kernel(
-    late, f_ref, cot_ref, win_ref, wout_ref, bias_ref, res_ref, parts_ref, df_ref, dwin_ref, dwout_ref, dbias_ref,
-    f_all, g_all, dul_all, ahead, own, kept, out_mate, out_cross, in_mate, in_cross, x_out, x_in,
+    late, f_ref, bias_ref, win_far, cot_far, wout_far, df_ref, dbias_ref, res_out, parts_out, dwin_out, dwout_out,
+    win_ref, cot_ref, wout_ref, res_ref, parts_ref, dwin_ref, dwout_ref, move_sem, f_all, g_all, dul_all, ahead, own, kept, out_mate, out_cross, in_mate, in_cross, x_out, x_in,
     f_send, f_recv, p_send, p_recv,
 ):
+    moves = Moves(move_sem)
+    load_in, load_cot, load_out = (
+        moves.start(*pair) for pair in ((win_far, win_ref), (cot_far, cot_ref), (wout_far, wout_ref))
+    )
     me = lax.axis_index("wa")
     mate, across = other_wa(me, 1), other_wa(me, 2)
     both = other_wa(across, 1)
@@ -1408,6 +1440,7 @@
     f_all[me] = f_ref[...]
     order = (me, mate, across, both)
     dbias_ref[...] = jnp.zeros_like(dbias_ref)
+    load_in.wait()
     for k, s in enumerate(order):
         if k == 1:
             to_mate.wait_recv()
@@ -1422,6 +1455,9 @@
         square = u * u
         t = jnp.tanh(GELU * (u + 0.044715 * (square * u)))
         g_all[s] = (0.5 * u * (1.0 + t)).astype(BF)
+        if k == 0:
+            load_cot.wait()
+            load_out.wait()
         slope = 0.5 * (1.0 + t) + 0.5 * u * (1.0 - t * t) * (GELU * (1.0 + 3 * 0.044715 * square))
         du = (nt_dot(cot_ref[s], wout_ref[...]) if k < 2 else ahead[k - 2]) * slope
         dbias_ref[...] += jnp.sum(du.reshape(32, 8, du.shape[1]), axis=0)
@@ -1464,6 +1500,9 @@
     else:
         res_copies = scatter(1, lambda s: nn_dot(g_all[s], wout_ref[...]))
         parts_ref[...] = jnp.zeros_like(parts_ref)
+    stores = []
+    if late:
+        stores += [moves.start(res_ref, res_out), moves.start(parts_ref, parts_out)]
     width = f_ref.shape[1]
 
     def outer(left_all, right, out_ref):
@@ -1477,10 +1516,14 @@
             out_ref[lanes, :] = total.astype(BF)
 
     outer(f_all, dul_all, dwin_ref)
+    stores.append(moves.start(dwin_ref, dwin_out))
     outer(g_all, cot_ref, dwout_ref)
+    stores.append(moves.start(dwout_ref, dwout_out))
     finish(0, df_copies, df_ref)
     if not late:
         finish(1, res_copies, res_ref)
+        stores += [moves.start(res_ref, res_out), moves.start(parts_ref, parts_out)]
+    wait_all(stores)
     for copy in (to_mate, to_across, forward):
         copy.wait_send()
 
@@ -1490,19 +1533,28 @@
     hidden = win.shape[1]
     dma = pltpu.SemaphoreType.DMA
     block = (rows, width)
-    return pl.pallas_call(
+    any_spec = pl.BlockSpec(memory_space=pl.ANY)
+    df, dbias, *others = pl.pallas_call(
         functools.partial(ffn_kernel, late),
         out_shape=(
             jax.ShapeDtypeStruct(block, F32),
+            jax.ShapeDtypeStruct((8, hidden), F32),
+            jax.ShapeDtypeStruct(block, F32),
             jax.ShapeDtypeStruct((3, *block), BF),
-            jax.ShapeDtypeStruct(block, F32),
             jax.ShapeDtypeStruct(win.shape, BF),
             jax.ShapeDtypeStruct(wout.shape, BF),
-            jax.ShapeDtypeStruct((8, hidden), F32),
         ),
-        in_specs=vmem(5),
-        out_specs=tuple(vmem(6)),
+        in_specs=vmem(2) + [any_spec] * 3,
+        out_specs=tuple(vmem(2) + [any_spec] * 4),
         scratch_shapes=[
+            pltpu.VMEM(win.shape, BF),
+            pltpu.VMEM((4, *block), BF),
+            pltpu.VMEM(wout.shape, BF),
+            pltpu.VMEM(block, F32),
+            pltpu.VMEM((3, *block), BF),
+            pltpu.VMEM(win.shape, BF),
+            pltpu.VMEM(wout.shape, BF),
+            dma((7,)),
             pltpu.VMEM((4, *block), BF),
             pltpu.VMEM((4, rows, hidden), BF),
             pltpu.VMEM((4, rows, hidden), BF),
@@ -1516,11 +1568,13 @@
             dma((2, 3)),
         ],
         compiler_params=pltpu.CompilerParams(
-            collective_id=4, has_side_effects=True, vmem_limit_bytes=56 << 20
+            collective_id=4, has_side_effects=True, vmem_limit_bytes=60 << 20
         ),
         cost_estimate=lasting(44),
         name="feed_forward",
-    )(f_low, cot_all, win, wout, bias)
+    )(f_low, bias, win, cot_all, wout)
+    res, parts, dwin, dwout = others
+    return res, parts, df, dwin, dwout, dbias
 
 
 def padded_rows(pad, values):

time: 455 us -> 450 us (0.989)
  Pallas kernels: 389 us -> 382 us
where the time goes in v6:
time: 450 us; the launch traced here: 441 us
  Pallas kernels  382 us (85%)
  other arithmetic  25.8 us (6%)
  matrix products  15.8 us (4%)
  local copies, waits for them, and re-layouts  14.7 us (3%)
    pallas_call x1, Pallas kernels, attn_forward(): pl.pallas_call(functools.partial(attn_forward_kernel, n), out_shape=(*who...  96.3 us
    pallas_call x1, Pallas kernels, reduce_grads(): pl.pallas_call(reduce_kernel, out_shape=(jax.ShapeDtypeStruct(small.shape...  94.8 us
    pallas_call x1, Pallas kernels, attn_backward(): pl.pallas_call(functools.partial(attn_backward_kernel, n), out_shape=(jax...  94.5 us
    pallas_call x1, Pallas kernels, middle(): pl.pallas_call(middle_kernel, out_shape=(low((2, *FEED[1:])), jax.ShapeDt...  43.7 us
    pallas_call x1, Pallas kernels, ffn(): pl.pallas_call(functools.partial(ffn_kernel, late), out_shape=(jax.ShapeD...  43.4 us
    dot_general x6, matrix products, back_product(): lax.dot_general(grad_low, weight, (((1,), (1,)), ((), ())), preferred_ele...  10.2 us
    pallas_call x1, Pallas kernels, cross_forward(): pl.pallas_call(functools.partial(cross_forward_kernel, groups), grid=(wid...  9.64 us
  transfers between devices with their start and end apart: 1, of which 0 were waited for; matrix products, arithmetic and copies ran while one was open for 7% of the time, Pallas kernels for 43%

profile of v6, /device:TPU:0, one launch (start us, length us, event | category | flops | bytes accessed | tf_op | source)
XLA Modules:
  0.0 441.4 jit_solution(13958766985066916832)
XLA Ops:
  1.6 1.3 reshape.217.bias_ref
  4.5 96.3 %attn_forward.1 = (bf16[896,1024]{1,0:T(8,128)(2,1)}, bf16[896,1024]{1,0:T(8,128)(2,1)}, bf16[896,1024]{1,0:T(8,128)(2,1)}, bf16[1024,896]{1,0:T(8,128)(2,1)}, b...) custom-call(bf16[256,896]{1,0:T(8,128)(2,1)} %bitcast.60, ...), custom_call_target="tpu_custom_call" | custom-call | bytes 255000000 | tf_op jit(solution)/shard_map/attn_forward/pallas_call | solution.py:821
  101.8 2.6 multiply_reduce_fusion.5
  106.3 1.5 convolution_convert_fusion.2.q_ref.q_far
  107.8 1.7 copy-done.3
  109.5 1.0 copy-done.5
  110.6 9.6 %cross_forward.1.rest_6_ = bf16[256,1024]{1,0:T(8,128)(2,1)S(1)} custom-call(f32[8,128]{1,0:T(8,128)S(1)} %broadcast_in_dim.53.keep_ref, bf16[256,1024]{1,0:T(8,128)(2,1)S(1)} %copy-done.5, bf16[1280,1024]{1,0:T(8,128)(2,1)S(1)} %copy-done.2, bf16[1280,1024]{1,0:T(8,128)(2,1)S(1)} %copy-done.3), custom_call_target="tpu_custom_call" | custom-call | bytes 27000000 | tf_op jit(solution)/shard_map/cross_forward/pallas_call | solution.py:1619
  122.0 43.4 %feed_forward.1 = (f32[256,896]{1,0:T(8,128)}, f32[8,896]{1,0:T(8,128)}, f32[256,896]{1,0:T(8,128)}, bf16[3,256,896]{2,1,0:T(8,128)(2,1)}, bf16[896,896]{1,0:T(8,128)(2,1)}, /*index=5*/bf16[896,896]{1,0:T(8,128)(2,1)}) custom-call(bf16[256,896]{1,0:T(8,128)(2,1)} %multiply_convert_fusion.f_ref, f32[1,896]{1,0:T(1,128)} %reshape.217.bias_ref, ...), custom_call_target="tpu_custom_call" | custom-call | bytes 132000000 | tf_op jit(solution)/shard_map/feed_forward/pallas_call | solution.py:1537
  165.5 1.6 multiply_reduce_fusion
  167.4 1.2 copy-done.20
  168.6 1.5 convolution_convert_fusion.1.dx_far
  170.1 43.7 %middle.1 = (bf16[2,112,896]{2,1,0:T(8,128)(2,1)}, f32[256,896]{1,0:T(8,128)}, bf16[256,1024]{1,0:T(8,128)(2,1)}, bf16[896,1024]{1,0:T(8,128)(2,1)}, bf16[896,10...) custom-call(f32[8,128]{1,0:T(8,128)} %copy-done.6, ...), custom_call_target="tpu_custom_call" | custom-call | bytes 114000000 | tf_op jit(solution)/shard_map/middle/pallas_call | solution.py:1978
  213.8 1.3 collective-permute-start
  216.1 3.4 multiply_reduce_fusion.1
  219.6 3.4 fusion.29
  223.0 1.5 convolution_convert_fusion.do_ref
  224.5 94.5 %attn_backward.1 = (f32[8,1024]{1,0:T(8,128)}, bf16[256,1024]{1,0:T(8,128)(2,1)}, bf16[256,1024]{1,0:T(8,128)(2,1)}, bf16[256,1024]{1,0:T(8,128)(2,1)}, bf16[448...) custom-call(bf16[256,1024]{1,0:T(8,128)(2,1)} %convolution_convert_f, ...), custom_call_target="tpu_custom_call" | custom-call | bytes 300000000 | tf_op jit(solution)/shard_map/attn_backward/pallas_call | solution.py:1067
  319.0 1.9 fusion.32
  322.7 1.0 fusion.7
  325.6 94.8 %reduce_grads.1 = (f32[64,128]{1,0:T(8,128)}, bf16[224,1024]{1,0:T(8,128)(2,1)}, bf16[224,1024]{1,0:T(8,128)(2,1)}, bf16[224,1024]{1,0:T(8,128)(2,1)}, bf16[8,32...) custom-call(f32[64,128]{1,0:T(8,128)} %reshape.209.refs_0_, ...), custom_call_target="tpu_custom_call" | custom-call | bytes 270000000 | tf_op jit(solution)/shard_map/reduce_grads/pallas_call | solution.py:1362
  422.1 2.1 convert_element_type.187
  424.2 2.1 convert_element_type.188
  426.3 1.0 convert_element_type.189
  427.3 1.0 convert_element_type.190
  428.3 1.0 convert_element_type.191
  429.4 1.4 bitcast_convert_fusion.1
  430.8 1.1 fusion.10
  431.9 1.0 convert_element_type.192
  432.9 2.1 convert_element_type.193
  436.3 2.0 bitcast_convert_fusion
  438.3 1.2 add_convert_fusion
  439.8 1.4 pad_maximum_fusion
  (127 shorter events, 15.2 us)
Async XLA Ops:
  0.7 2.9 copy-start
  4.5 97.3 %copy-start.10 = (bf16[1,256,896]{2,1,0:T(8,128)(2,1)S(1)}, bf16[1,256,896]{2,1,0:T(8,128)(2,1)}, u32[]{:S(2)}) copy-start(bf16[1,256,896]{2,1,0:T(8,128)(2,1)} %param.19) | copy-start | bytes 1376260
  101.8 4.5 %copy-start.24 = (bf16[896,1024]{1,0:T(8,128)(2,1)S(1)}, bf16[896,1024]{1,0:T(8,128)(2,1)}, u32[]{:S(2)}) copy-start(bf16[896,1024]{1,0:T(8,128)(2,1)} %get-tuple-element.77) | copy-start | bytes 5505028
  105.5 2.3 copy-start.2
  107.8 12.4 %copy-start.6 = (f32[8,128]{1,0:T(8,128)}, f32[8,128]{1,0:T(8,128)S(1)}, u32[]{:S(2)}) copy-start(f32[8,128]{1,0:T(8,128)S(1)} %broadcast_in_dim.53.keep_ref) | copy-start | bytes 12292
  107.8 1.7 copy-start.3
  110.6 9.7 %copy-start.8 = (f32[256,896]{1,0:T(8,128)S(1)}, f32[256,896]{1,0:T(8,128)}, u32[]{:S(2)}) copy-start(f32[256,896]{1,0:T(8,128)} %copy-done.7) | copy-start | bytes 2752516
  110.6 9.7 %copy-start.19 = (bf16[1024,896]{1,0:T(8,128)(2,1)S(1)}, bf16[1024,896]{1,0:T(8,128)(2,1)}, u32[]{:S(2)}) copy-start(bf16[1024,896]{1,0:T(8,128)(2,1)} %get-tuple-element.80) | copy-start | bytes 5505028
  165.5 1.6 copy-start.12
  165.5 1.6 copy-start.13
  168.6 1.5 copy-start.25
  170.1 45.0 %copy-start.11 = (bf16[1,256,896]{2,1,0:T(8,128)(2,1)S(1)}, bf16[1,256,896]{2,1,0:T(8,128)(2,1)}, u32[]{:S(2)}) copy-start(bf16[1,256,896]{2,1,0:T(8,128)(2,1)} %param.19) | copy-start | bytes 1376260
  170.1 45.2 %copy-start.38 = (f32[32,1024]{1,0:T(8,128)S(1)}, f32[32,1024]{1,0:T(8,128)}, u32[]{:S(2)}) copy-start(f32[32,1024]{1,0:T(8,128)} %get-tuple-element.76) | copy-start | bytes 393220
  170.1 45.8 %copy-start.39 = (f32[8,896]{1,0:T(8,128)S(1)}, f32[8,896]{1,0:T(8,128)}, u32[]{:S(2)}) copy-start(f32[8,896]{1,0:T(8,128)} %get-tuple-element.111) | copy-start | bytes 86020
  170.1 46.0 %copy-start.9 = (f32[256,896]{1,0:T(8,128)S(1)}, f32[256,896]{1,0:T(8,128)}, u32[]{:S(2)}) copy-start(f32[256,896]{1,0:T(8,128)} %copy-done.7) | copy-start | bytes 2752516
  213.8 224.5 %collective-permute-start = (bf16[256,896]{1,0:T(8,128)(2,1)}, bf16[256,896]{1,0:T(8,128)(2,1)}, u32[]{:S(2)}, u32[]{:S(2)}) collective-permute-start(bf16[256,896]{1,0:T(8,128)(2,1)} %get-tuple-element.109), channel_id=1, source_target_pairs={{4,0},{8,4},{12,8},{16,12},{20,16},{24,20},{28,24},{5,1},{9,5},{13... | collective-permute-start | bytes 1376264 | tf_op jit(solution)/shard_map/ppermute | solution.py:32
  219.6 3.4 copy-start.23
  223.0 1.6 copy-start.17
  224.5 94.5 %copy-start.18 = (bf16[896,1024]{1,0:T(8,128)(2,1)S(1)}, bf16[896,1024]{1,0:T(8,128)(2,1)}, u32[]{:S(2)}) copy-start(bf16[896,1024]{1,0:T(8,128)(2,1)} %get-tuple-element.102) | copy-start | bytes 5505028
  319.0 2.0 copy-start.15
  319.0 2.0 copy-start.22
  321.0 1.7 copy-start.21
  420.5 5.8 %copy-start.35 = (bf16[224,1024]{1,0:T(8,128)(2,1)S(1)}, bf16[224,1024]{1,0:T(8,128)(2,1)}, u32[]{:S(2)}) copy-start(bf16[224,1024]{1,0:T(8,128)(2,1)} %get-tuple-element.120) | copy-start | bytes 1376260
  422.1 5.2 %copy-start.34 = (bf16[224,1024]{1,0:T(8,128)(2,1)S(1)}, bf16[224,1024]{1,0:T(8,128)(2,1)}, u32[]{:S(2)}) copy-start(bf16[224,1024]{1,0:T(8,128)(2,1)} %get-tuple-element.123) | copy-start | bytes 1376260
  424.2 4.2 copy-start.33
  426.3 3.1 copy-start.36
  426.3 3.1 copy-start.37
  427.3 2.1 copy-start.32
  430.8 2.1 copy-start.28
  432.9 3.4 copy-start.27
  436.3 2.0 copy-start.30
  439.6 1.6 copy-start.1
  (10 other events, 11.3 us)

commit v7 on v6

--- a/solution.py
+++ b/solution.py
@@ -1404,13 +1404,63 @@
     return *others[:-1], small, others[-1]
 
 
-def unfold(full):
-    wide = {name: value.astype(F32) for name, value in full.items()}
-    return {
-        "co": wide["co"].reshape(FLAT),
-        "so": jnp.concatenate([wide["so0"], wide["so1"]], 1).reshape(FLAT),
-        **{name: wide[name] for name in ("cq", "ck", "cv", *LATE)},
+WIDENED = ("cq", "ck", "cv", "q", "k", "v", "co", "fin", "fout")
+
+
+def widen_kernel(*refs):
+    count = len(WIDENED)
+    so0, so1, near, last, back = refs[count : count + 5]
+    outs = refs[count + 5 :]
+    for src, dst in zip(refs[:count], outs[:count], strict=True):
+        dst[...] = src[...].astype(F32)
+    for c in range(so0.shape[0]):
+        outs[count][c * 32 : c * 32 + 16, :] = so0[c].astype(F32)
+        outs[count][c * 32 + 16 : c * 32 + 32, :] = so1[c].astype(F32)
+    span = pl.program_id(0)
+
+    @pl.when(span < 3)
+    def _():
+        outs[count + 1][...] = near[...]
+
+    @pl.when(span == 3)
+    def _():
+        outs[count + 1][...] = (last[...] + back[...].astype(F32)).astype(BF)
+
+
+def widen(full, near, last, back):
+    values = [full[name] for name in WIDENED]
+    blocks = {
+        (224, 1024): ((224, 256), lambda i: (0, i)),
+        (256, 896): ((64, 896), lambda i: (i, 0)),
+        (224, 3584): ((224, 896), lambda i: (0, i)),
+        (896, 896): ((224, 896), lambda i: (i, 0)),
     }
+    specs = [pl.BlockSpec(*blocks[v.shape]) for v in values]
+    halves = pl.BlockSpec((2, 16, 896), lambda i: (i, 0, 0))
+    span = (256, 896)
+    still = pl.BlockSpec(span, lambda i: (0, 0))
+    moving = pl.BlockSpec(span, lambda i: (i, 0))
+    *wide, neighbour = pl.pallas_call(
+        widen_kernel,
+        grid=(4,),
+        out_shape=(
+            *(jax.ShapeDtypeStruct(v.shape, F32) for v in values),
+            jax.ShapeDtypeStruct(FLAT, F32),
+            jax.ShapeDtypeStruct((1024, 896), BF),
+        ),
+        in_specs=[
+            *specs,
+            halves,
+            halves,
+            pl.BlockSpec(span, lambda i: (jnp.minimum(i, 2), 0)),
+            still,
+            still,
+        ],
+        out_specs=(*specs, pl.BlockSpec((64, 896), lambda i: (i, 0)), moving),
+        compiler_params=pltpu.CompilerParams(vmem_limit_bytes=60 << 20),
+        name="widen",
+    )(*values, full["so0"], full["so1"], near, last, back)
+    return dict(zip((*WIDENED, "so"), wide, strict=True)), neighbour
 
 
 GELU = (2.0 / math.pi) ** 0.5
@@ -1595,16 +1645,15 @@
 
 def cross_forward_kernel(groups, keep_ref, q_ref, k_ref, v_ref, x_ref, q_pad, x_pad):
     padded_rows(q_pad, q_ref[...])
-    for g in range(groups):
-        rows = slice(g * 256, (g + 1) * 256)
-        query = both_heads(q_pad, g) * BF(HD**-0.5)
-        scores = nt_dot(query, k_ref[rows, :])
-        weights = jnp.exp(scores - jnp.max(scores, axis=1, keepdims=True))
-        weights = weights / jnp.sum(weights, axis=1, keepdims=True)
-        mixed = join_heads(nn_dot(weights.astype(BF), v_ref[rows, :]))
-        if g == 0:
-            mixed = mixed * keep_ref[0:1, :]
-        x_pad[g * SPAN : (g + 1) * SPAN, :] = mixed
+    spans = range(groups)
+    rows = [slice(g * 256, (g + 1) * 256) for g in spans]
+    scores = [nt_dot(both_heads(q_pad, g) * BF(HD**-0.5), k_ref[rows[g], :]) for g in spans]
+    weights = [jnp.exp(v - jnp.max(v, axis=1, keepdims=True)) for v in scores]
+    weights = [v / jnp.sum(v, axis=1, keepdims=True) for v in weights]
+    mixed = [join_heads(nn_dot(weights[g].astype(BF), v_ref[rows[g], :])) for g in spans]
+    mixed[0] = mixed[0] * keep_ref[0:1, :]
+    for g in spans:
+        x_pad[g * SPAN : (g + 1) * SPAN, :] = mixed[g]
     x_ref[...] = x_pad[1 : x_ref.shape[0] + 1, :].astype(BF)
 
 
@@ -2140,7 +2189,7 @@
         early["ck"] = outer_product(near_rows, dkeys).astype(BF)
         early["cv"] = outer_product(near_rows, dvalues).astype(BF)
     result = (hidden_two + fed + small_of["outbias"]).astype(BF)
-    back = passed_along(first, "ctx", -1).astype(F32)
+    back = passed_along(first, "ctx", -1)
     grad_hidden_part, grad_crossnorm = back_cross(
         back_product(grad_query_cross, full["crossquery"])
     )
@@ -2168,10 +2217,6 @@
     grad_input_part, grad_selfnorm = back_self(grad_normed)
     grad_inputs = (grad_hidden + grad_input_part).astype(BF)
 
-    grad_neigh = (
-        jnp.concatenate([near_low, (near_last + back).astype(BF)], 0)
-        .reshape(neighbours.shape)
-    )
     late_grads = (dquery_low, dkey_low, dvalue_low)
     wa, owners = lax.axis_index("wa"), lax.axis_size("wa")
     bias_grad = jnp.sum(bias_sums, axis=0)
@@ -2185,8 +2230,10 @@
         *reduced, packed, fin = reduce_grads(
             *shares, packed, normed_low, late_grads, fin
         )
-        grads = unfold(dict(zip((*NAMES, *LATE), reduced, strict=True)))
-        fout = fout.reshape(given["feedout"].shape)
+        reduced = dict(zip((*NAMES, *LATE), reduced, strict=True))
+        reduced["co"] = reduced["co"].reshape(FLAT)
+        reduced |= {"fin": fin, "fout": fout.reshape(given["feedout"].shape)}
+        grads, grad_neigh = widen(reduced, near_low, near_last, back)
     else:
         for name, grad in zip(LATE, late_grads, strict=True):
             sides[name] = (normed_low, grad)
@@ -2195,7 +2242,9 @@
         grads, packed = reduce_plain(early, packed)
         fin, fout = lax.psum((fin, fout), "ctx")
         fin = lax.all_to_all(fin, "wa", 0, 1, tiled=True)
-    grads["fin"], grads["fout"] = fin.astype(F32), fout.astype(F32)
+        grads["fin"], grads["fout"] = fin.astype(F32), fout.astype(F32)
+        grad_neigh = jnp.concatenate([near_low, (near_last + back.astype(F32)).astype(BF)], 0)
+    grad_neigh = grad_neigh.reshape(neighbours.shape)
     mine = lax.dynamic_index_in_dim(packed.reshape(owners, -1), wa, 0, keepdims=False)
     cuts, start = [], 0
     for v in (*sums, placed):

time: 450 us -> 438 us (0.973)
  other arithmetic: 25.8 us -> 8.54 us
  Pallas kernels: 382 us -> 390 us
    convert_element_type x9 -> x0, other arithmetic: 13.6 us -> none  [the longest x6 8.27 us: unfold(): wide = {name: value.astype(F32) for name, value in full.items()}]
    pallas_call x0 -> x1, Pallas kernels: none -> 9.87 us  [widen(): pl.pallas_call(widen_kernel, grid=(4,), out_shape=(*(jax.ShapeDtypeStruct...]
  transfers between devices with their start and end apart: 1 -> 1, of which waited for: 0 -> 0; matrix products, arithmetic and copies ran while one was open for 7% -> 4% of each run, Pallas kernels for 43% -> 44%
where the time goes in v7:
time: 438 us; the launch traced here: 430 us
  Pallas kernels  390 us (89%)
  local copies, waits for them, and re-layouts  14.4 us (3%)
  matrix products  14.1 us (3%)
  other arithmetic  8.54 us (2%)
    pallas_call x1, Pallas kernels, attn_forward(): pl.pallas_call(functools.partial(attn_forward_kernel, n), out_shape=(*who...  96.4 us
    pallas_call x1, Pallas kernels, reduce_grads(): pl.pallas_call(reduce_kernel, out_shape=(jax.ShapeDtypeStruct(small.shape...  95 us
    pallas_call x1, Pallas kernels, attn_backward(): pl.pallas_call(functools.partial(attn_backward_kernel, n), out_shape=(jax...  94.4 us
    pallas_call x1, Pallas kernels, middle(): pl.pallas_call(middle_kernel, out_shape=(low((2, *FEED[1:])), jax.ShapeDt...  43.7 us
    pallas_call x1, Pallas kernels, ffn(): pl.pallas_call(functools.partial(ffn_kernel, late), out_shape=(jax.ShapeD...  43.4 us
    pallas_call x1, Pallas kernels, widen(): pl.pallas_call(widen_kernel, grid=(4,), out_shape=(*(jax.ShapeDtypeStruct...  9.87 us
    dot_general x6, matrix products, back_product(): lax.dot_general(grad_low, weight, (((1,), (1,)), ((), ())), preferred_ele...  9.31 us
  transfers between devices with their start and end apart: 1, of which 0 were waited for; matrix products, arithmetic and copies ran while one was open for 4% of the time, Pallas kernels for 44%

profile of v7, /device:TPU:0, one launch (start us, length us, event | category | flops | bytes accessed | tf_op | source)
XLA Modules:
  0.0 429.5 jit_solution(15039851607813281743)
XLA Ops:
  0.7 0.8 pad_maximum_fusion.1
  1.6 1.3 reshape.206.bias_ref
  4.5 96.4 %attn_forward.1 = (bf16[896,1024]{1,0:T(8,128)(2,1)}, bf16[896,1024]{1,0:T(8,128)(2,1)}, bf16[896,1024]{1,0:T(8,128)(2,1)}, bf16[1024,896]{1,0:T(8,128)(2,1)}, b...) custom-call(bf16[256,896]{1,0:T(8,128)(2,1)} %bitcast.53, ...), custom_call_target="tpu_custom_call" | custom-call | bytes 255000000 | tf_op jit(solution)/shard_map/attn_forward/pallas_call | solution.py:821
  100.9 0.9 slice_reduce_fusion.1
  101.9 2.6 multiply_reduce_fusion.5
  104.7 0.7 copy-done.7
  105.4 0.8 copy-done.26
  106.2 0.7 convolution_convert_fusion.2.q_ref.q_far
  107.3 1.7 copy-done.3
  109.1 7.0 %cross_forward.1.rest_6_ = bf16[256,1024]{1,0:T(8,128)(2,1)S(1)} custom-call(f32[8,128]{1,0:T(8,128)S(1)} %broadcast_in_dim.53.keep_ref, bf16[256,1024]{1,0:T(8,128)(2,1)S(1)} %convolution_convert_fusion.2.q_ref.q_far, bf16[1280,1024]{1,0:T(8,128)(2,1)S(1)} %copy-done.2, bf16[1280,1024]{1,0:T(8,128)(2,1)S(1)} %copy-done.3), custom_call_target="tpu_custom_call" | custom-call | bytes 27000000 | tf_op jit(solution)/shard_map/cross_forward/pallas_call | solution.py:1668
  116.2 0.8 multiply_reduce_fusion.4
  117.0 0.9 multiply_convert_fusion.f_ref
  117.9 43.4 %feed_forward.1 = (f32[256,896]{1,0:T(8,128)}, f32[8,896]{1,0:T(8,128)}, f32[256,896]{1,0:T(8,128)}, bf16[3,256,896]{2,1,0:T(8,128)(2,1)}, bf16[896,896]{1,0:T(8,128)(2,1)}, /*index=5*/bf16[896,896]{1,0:T(8,128)(2,1)}) custom-call(bf16[256,896]{1,0:T(8,128)(2,1)} %multiply_convert_fusion.f_ref, f32[1,896]{1,0:T(1,128)} %reshape.206.bias_ref, ...), custom_call_target="tpu_custom_call" | custom-call | bytes 132000000 | tf_op jit(solution)/shard_map/feed_forward/pallas_call | solution.py:1587
  161.4 1.6 multiply_reduce_fusion
  163.3 1.2 copy-done.20
  164.4 1.6 convolution_convert_fusion.1.dx_far
  166.0 43.7 %middle.1 = (bf16[2,112,896]{2,1,0:T(8,128)(2,1)}, f32[256,896]{1,0:T(8,128)}, bf16[256,1024]{1,0:T(8,128)(2,1)}, bf16[896,1024]{1,0:T(8,128)(2,1)}, bf16[896,10...) custom-call(f32[8,128]{1,0:T(8,128)} %copy-done.6, ...), custom_call_target="tpu_custom_call" | custom-call | bytes 114000000 | tf_op jit(solution)/shard_map/middle/pallas_call | solution.py:2027
  209.7 1.3 collective-permute-start
  211.9 2.7 multiply_reduce_fusion.1
  214.6 1.6 fusion.29
  216.2 0.8 copy-done.17
  217.0 1.5 convolution_convert_fusion.do_ref
  218.5 94.4 %attn_backward.1 = (f32[8,1024]{1,0:T(8,128)}, bf16[256,1024]{1,0:T(8,128)(2,1)}, bf16[256,1024]{1,0:T(8,128)(2,1)}, bf16[256,1024]{1,0:T(8,128)(2,1)}, bf16[448...) custom-call(bf16[256,1024]{1,0:T(8,128)(2,1)} %convolution_convert_f, ...), custom_call_target="tpu_custom_call" | custom-call | bytes 300000000 | tf_op jit(solution)/shard_map/attn_backward/pallas_call | solution.py:1067
  313.0 1.0 slice_reduce_fusion
  314.0 1.8 fusion.32
  316.3 0.7 convolution_add_fusion.1
  317.9 1.0 fusion.7
  320.6 95.0 %reduce_grads.1 = (f32[64,128]{1,0:T(8,128)}, bf16[224,1024]{1,0:T(8,128)(2,1)}, bf16[224,1024]{1,0:T(8,128)(2,1)}, bf16[224,1024]{1,0:T(8,128)(2,1)}, bf16[8,32...) custom-call(f32[64,128]{1,0:T(8,128)} %reshape.199.refs_0_, ...), custom_call_target="tpu_custom_call" | custom-call | bytes 270000000 | tf_op jit(solution)/shard_map/reduce_grads/pallas_call | solution.py:1362
  415.5 0.8 reshape.204
  417.1 0.7 dynamic-slice_reduce_fusion
  418.4 1.1 fusion.10
  419.5 9.9 %widen.1 = (f32[224,1024]{1,0:T(8,128)}, f32[224,1024]{1,0:T(8,128)}, f32[224,1024]{1,0:T(8,128)}, f32[224,1024]{1,0:T(8,128)}, f32[224,1024]{1,0:T(8,128)}, /*i...) custom-call(bf16[224,1024]{1,0:T(8,128)(2,1)} %get-tuple-element.125, ...), custom_call_target="tpu_custom_call" | custom-call | tf_op jit(solution)/shard_map/widen/pallas_call | solution.py:1443
  (96 shorter events, 7.8 us)
Async XLA Ops:
  0.7 2.9 copy-start
  4.5 97.3 %copy-start.10 = (bf16[1,256,896]{2,1,0:T(8,128)(2,1)S(1)}, bf16[1,256,896]{2,1,0:T(8,128)(2,1)}, u32[]{:S(2)}) copy-start(bf16[1,256,896]{2,1,0:T(8,128)(2,1)} %param.19) | copy-start | bytes 1376260
  101.9 4.3 %copy-start.24 = (bf16[896,1024]{1,0:T(8,128)(2,1)S(1)}, bf16[896,1024]{1,0:T(8,128)(2,1)}, u32[]{:S(2)}) copy-start(bf16[896,1024]{1,0:T(8,128)(2,1)} %get-tuple-element.88) | copy-start | bytes 5505028
  104.5 0.9 copy-start.7
  105.4 0.8 copy-start.26
  105.4 1.9 copy-start.2
  106.9 9.2 %copy-start.5 = (bf16[256,1024]{1,0:T(8,128)(2,1)}, bf16[256,1024]{1,0:T(8,128)(2,1)S(1)}, u32[]{:S(2)}) copy-start(bf16[256,1024]{1,0:T(8,128)(2,1)S(1)} %convolution_convert_fusion.2.q_ref.q_far) | copy-start | bytes 1572868
  106.9 9.2 %copy-start.6 = (f32[8,128]{1,0:T(8,128)}, f32[8,128]{1,0:T(8,128)S(1)}, u32[]{:S(2)}) copy-start(f32[8,128]{1,0:T(8,128)S(1)} %broadcast_in_dim.53.keep_ref) | copy-start | bytes 12292
  107.3 1.7 copy-start.3
  109.1 7.1 %copy-start.8 = (f32[256,896]{1,0:T(8,128)S(1)}, f32[256,896]{1,0:T(8,128)}, u32[]{:S(2)}) copy-start(f32[256,896]{1,0:T(8,128)} %copy-done.7) | copy-start | bytes 2752516
  109.1 7.1 %copy-start.19 = (bf16[1024,896]{1,0:T(8,128)(2,1)S(1)}, bf16[1024,896]{1,0:T(8,128)(2,1)}, u32[]{:S(2)}) copy-start(bf16[1024,896]{1,0:T(8,128)(2,1)} %get-tuple-element.91) | copy-start | bytes 5505028
  116.1 0.8 copy-start.4
  161.3 1.6 copy-start.12
  161.3 1.6 copy-start.13
  162.9 1.5 copy-start.20
  164.4 1.6 copy-start.25
  166.0 45.1 %copy-start.11 = (bf16[1,256,896]{2,1,0:T(8,128)(2,1)S(1)}, bf16[1,256,896]{2,1,0:T(8,128)(2,1)}, u32[]{:S(2)}) copy-start(bf16[1,256,896]{2,1,0:T(8,128)(2,1)} %param.19) | copy-start | bytes 1376260
  166.0 45.2 %copy-start.28 = (f32[32,1024]{1,0:T(8,128)S(1)}, f32[32,1024]{1,0:T(8,128)}, u32[]{:S(2)}) copy-start(f32[32,1024]{1,0:T(8,128)} %get-tuple-element.87) | copy-start | bytes 393220
  166.0 45.9 %copy-start.9 = (f32[256,896]{1,0:T(8,128)S(1)}, f32[256,896]{1,0:T(8,128)}, u32[]{:S(2)}) copy-start(f32[256,896]{1,0:T(8,128)} %copy-done.7) | copy-start | bytes 2752516
  209.7 209.7 %collective-permute-start = (bf16[256,896]{1,0:T(8,128)(2,1)}, bf16[256,896]{1,0:T(8,128)(2,1)}, u32[]{:S(2)}, u32[]{:S(2)}) collective-permute-start(bf16[256,896]{1,0:T(8,128)(2,1)} %get-tuple-element.138), channel_id=1, source_target_pairs={{4,0},{8,4},{12,8},{16,12},{20,16},{24,20},{28,24},{5,1},{9,5},{13... | collective-permute-start | bytes 1376264 | tf_op jit(solution)/shard_map/ppermute | solution.py:32
  211.9 2.7 copy-start.27
  214.6 2.4 copy-start.23
  216.2 0.8 copy-start.17
  218.5 95.5 %copy-start.18 = (bf16[896,1024]{1,0:T(8,128)(2,1)S(1)}, bf16[896,1024]{1,0:T(8,128)(2,1)}, u32[]{:S(2)}) copy-start(bf16[896,1024]{1,0:T(8,128)(2,1)} %get-tuple-element.113) | copy-start | bytes 5505028
  313.0 2.9 copy-start.30
  313.0 3.2 copy-start.15
  313.0 3.2 copy-start.22
  316.3 1.0 copy-start.16
  316.3 1.7 copy-start.21
  317.9 1.0 copy-start.29
  320.6 97.8 %copy-start.14 = (f32[256,896]{1,0:T(8,128)S(1)}, f32[256,896]{1,0:T(8,128)}, u32[]{:S(2)}) copy-start(f32[256,896]{1,0:T(8,128)} %get-tuple-element.162) | copy-start | bytes 2752516
  419.5 9.9 %copy-start.1 = (bf16[8,16]{1,0:T(8,128)(2,1)S(1)}, bf16[8,16]{1,0:T(8,128)(2,1)}, u32[]{:S(2)}) copy-start(bf16[8,16]{1,0:T(8,128)(2,1)} %param.27) | copy-start | bytes 772
